TPU v7x, 32 devices: a whole 2x2x4 slice. The times are simulated.
32 devices in a mesh: box: 8 (over y, x, core), samp: 4 (over z).
Axes of the slice: x: 2, y: 2, z: 4, core: 2. Of those that a mesh axis runs over, the one named last changes fastest.
Arguments:
- xvec: bfloat16 [512, 2, 4, 128], P(('box', 'samp')), may hold values from -6 to 6
- near_blocks: bfloat16 [512, 8, 2, 128, 128], P(('box', 'samp')), may hold values from -0.1875 to 0.1875
- neighbours: int32 [512, 8], P(('box', 'samp')), may hold values from 0 to 511, as said below
- lift: bfloat16 [512, 2, 128, 128], P(('box', 'samp')), may hold values from -0.5 to 0.5
- place: bfloat16 [512, 2, 128, 128], P(('box', 'samp')), may hold values from -0.25 to 0.25
- interp: bfloat16 [2048, 128], replicated, may hold values from -0.5 to 0.5
- phases: float32 [8, 2, 2048], replicated, may hold values from -1 to 1, as said below
- octant: int32 [512], P(('box', 'samp')), may hold values from 0 to 7, as said below
- leaf_parent_index: int32 [512], P(('box', 'samp')), may hold values from 0 to 63, as said below
- translators: float32 [64, 2, 2048], P(None, None, 'samp'), may hold values from -0.5 to 0.5
- inter_list: int32 [64, 14], P('box'), may hold values from 0 to 63, as said below
- trans_id: int32 [64, 14], P('box'), may hold values from 0 to 63
Outputs:
- product: float32 [512, 2, 4, 128], P(('box', 'samp'))
Inputs may be any that keep to these rules, and one draw needn't show every extreme that they name: `neighbours`: row n starts with n itself; its other entries are distinct and lie within 8 boxes of n in cyclic order over all 512 leaf boxes (the texture is periodic). `leaf_parent_index`: leaf box n belongs to box group g = n // 64 and its parent is one of that group's upper-level boxes g * 8 to g * 8 + 7; every upper-level box has exactly 8 children. `octant`: the 8 children of an upper-level box have 8 distinct octants. `inter_list`: entries of row p are distinct, each equal to p + d modulo 64 with 2 <= |d| <= 8 (the periodic tree's interaction zone). `phases`: each entry has magnitude one: real part squared plus imaginary part squared is 1.
All inputs are finite; a program needn't handle non-finite values.
Results may differ from a plain program's by a relative error of at most 0.0065.
Values may be sent and summed in bfloat16 or wider, within the bound.
No kernel may reach another device: no remote copies, remote signals or barrier semaphores. Data moves between devices by JAX's collectives and lax.ppermute only.
A program may use at most 64 MiB of HBM per device.

v0:
```python
import jax
import jax.numpy as jnp
from jax import lax
from jax.sharding import PartitionSpec as P


def with_halo(cells, sides, width):
    for axis, dim in sides:
        count = lax.axis_size(axis)
        head = lax.slice_in_dim(cells, 0, width, axis=dim)
        tail = lax.slice_in_dim(cells, cells.shape[dim] - width, cells.shape[dim], axis=dim)
        cells = jnp.concatenate(
            [
                lax.ppermute(tail, axis, [(i, (i + 1) % count) for i in range(count)]),
                cells,
                lax.ppermute(head, axis, [((i + 1) % count, i) for i in range(count)]),
            ],
            axis=dim,
        )
    return cells


def cmul(ar, ai, br, bi):
    return (ar * br - ai * bi, ar * bi + ai * br)


def on_device(
    xvec,
    near_blocks,
    neighbours,
    lift,
    place,
    interp,
    phases,
    octant,
    leaf_parent_index,
    translators,
    inter_list,
    trans_id,
):
    f32 = jnp.float32
    bf16 = jnp.bfloat16
    finest_precision = lax.Precision.HIGHEST
    boxes = xvec.shape[0]
    nsamp = lax.axis_size("samp")
    nboxaxis = lax.axis_size("box")
    box_index = lax.axis_index("box")
    samp_index = lax.axis_index("samp")
    compute_unit = box_index * nsamp + samp_index
    total = boxes * nsamp * nboxaxis
    reach = boxes // 2
    parents_here = boxes * nsamp // 8
    all_parents = parents_here * nboxaxis
    sample_share = interp.shape[0] // nsamp
    rhs_count = xvec.shape[2]
    widened = with_halo(xvec, ((("box", "samp"), 0),), reach)
    local_index = jnp.mod(neighbours - compute_unit * boxes + reach, total)
    near_x = jnp.take(widened, local_index, axis=0)

    def apply(a, b):
        return jnp.einsum("bkpq,bkrq->brp", a, b, preferred_element_type=f32)

    near_r = apply(near_blocks[:, :, 0], near_x[:, :, 0]) - apply(
        near_blocks[:, :, 1], near_x[:, :, 1]
    )
    near_i = apply(near_blocks[:, :, 0], near_x[:, :, 1]) + apply(
        near_blocks[:, :, 1], near_x[:, :, 0]
    )

    def radiate(a, b):
        return jnp.einsum("bqu,bru->brq", a, b, preferred_element_type=f32)

    pat_r = radiate(lift[:, 0], xvec[:, 0]) - radiate(lift[:, 1], xvec[:, 1])
    pat_i = radiate(lift[:, 0], xvec[:, 1]) + radiate(lift[:, 1], xvec[:, 0])
    pattern = jnp.stack([pat_r, pat_i], 1).astype(bf16)

    def phase_rows(octs):
        indicator_matrix = (octs[:, None] == jnp.arange(8, dtype=jnp.int32)[None, :]).astype(f32)
        return jnp.einsum("ex,xwf->ewf", indicator_matrix, phases, precision=finest_precision)

    def parent_table(pars):
        local = pars - box_index * parents_here
        return local[:, None] == jnp.arange(parents_here, dtype=jnp.int32)[None, :]

    rows_i = interp
    raised_terms = jnp.einsum("sq,bcrq->bcrs", rows_i, pattern, preferred_element_type=f32)
    shift = phase_rows(octant)
    cr, ci = cmul(
        shift[:, 0][:, None, :], shift[:, 1][:, None, :], raised_terms[:, 0], raised_terms[:, 1]
    )
    owner = parent_table(leaf_parent_index).astype(f32)
    sum_r = jnp.einsum("bp,brs->prs", owner, cr, precision=finest_precision)
    sum_i = jnp.einsum("bp,brs->prs", owner, ci, precision=finest_precision)
    term = jnp.stack([sum_r, sum_i], 1)
    term = term.reshape(parents_here, 2, rhs_count, 1 * lax.axis_size("samp"), sample_share)
    upward = lax.psum_scatter(
        jnp.transpose(term, (3, 0, 1, 2, 4)), "samp", scatter_dimension=0, tiled=True
    )[0]
    parent_pat = upward.astype(bf16)
    table_count = translators.shape[0]
    selector_index = (
        trans_id[:, :, None] == jnp.arange(table_count, dtype=jnp.int32)[None, None, :]
    ).astype(f32)
    operator_list = jnp.einsum(
        "yaw,wjt->yajt", selector_index, translators, precision=finest_precision
    )
    bordered = with_halo(parent_pat, (("box", 0),), parents_here)
    window_index = jnp.mod(inter_list - box_index * parents_here + parents_here, all_parents)
    select = (
        window_index[:, :, None] == jnp.arange(3 * parents_here, dtype=jnp.int32)[None, None, :]
    ).astype(bf16)
    fetched = jnp.einsum("pkj,jcrs->pkcrs", select, bordered, preferred_element_type=f32)
    tr_r = operator_list[:, :, 0][:, :, None, :]
    tr_i = operator_list[:, :, 1][:, :, None, :]
    add_r, add_i = cmul(tr_r, tr_i, fetched[:, :, 0], fetched[:, :, 1])
    incoming = jnp.stack([add_r.sum(1), add_i.sum(1)], 1).astype(bf16)
    owner = parent_table(leaf_parent_index).astype(bf16)
    chosen = jnp.einsum(
        "ei,ihfz->ehfz",
        owner,
        lax.all_gather(incoming, "samp", axis=3, tiled=True),
        preferred_element_type=f32,
    )
    shift = phase_rows(octant)
    sr, si = cmul(shift[:, 0][:, None, :], shift[:, 1][:, None, :], chosen[:, 0], chosen[:, 1])
    shifted = jnp.stack([sr, si], 1).astype(bf16)
    rows_i = interp
    field = jnp.einsum("bcrs,sq->bcrq", shifted, rows_i, preferred_element_type=f32)
    field = field.astype(bf16)

    def receive(a, b):
        return jnp.einsum("buq,brq->bru", a, b, preferred_element_type=f32)

    far_r = receive(place[:, 0], field[:, 0]) - receive(place[:, 1], field[:, 1])
    far_i = receive(place[:, 0], field[:, 1]) + receive(place[:, 1], field[:, 0])
    return jnp.stack([near_r + far_r, near_i + far_i], 1)


def solution(mesh):
    in_specs = (
        P(("box", "samp"), None, None, None),
        P(("box", "samp"), None, None, None, None),
        P(("box", "samp"), None),
        P(("box", "samp"), None, None, None),
        P(("box", "samp"), None, None, None),
        P(),
        P(),
        P(("box", "samp")),
        P(("box", "samp")),
        P(None, None, "samp"),
        P("box", None),
        P("box", None),
    )
    out_specs = P(("box", "samp"), None, None, None)
    return jax.shard_map(
        on_device, mesh=mesh, in_specs=in_specs, out_specs=out_specs, check_vma=False
    )
```

profile of v0, /device:TPU:0, one launch (start us, length us, event | category | flops | bytes accessed | tf_op | source)
XLA Modules:
  0.0 82.8 jit_solution(6061716258988634404)
XLA Ops:
  0.0 1.5 %fusion.53 = f32[16,4,128]{2,1,0:T(4,128)S(1)} fusion(bf16[16,2,128,128]{3,2,1,0:T(8,128)(2,1)} %param.15, bf16[16,2,4,128]{3,2,1,0:T(4,128)(2,1)} %param.12), kind=kOutput, calls=%fused_computation.56 | convolution fusion | flops 2097152 | bytes 573440 | tf_op jit(solution)/shard_map/bqu,bru->brq/dot_general | solution.py:71
  1.5 1.4 %fusion.55 = f32[16,4,128]{2,1,0:T(4,128)S(1)} fusion(bf16[16,2,128,128]{3,2,1,0:T(8,128)(2,1)} %param.15, bf16[16,2,4,128]{3,2,1,0:T(4,128)(2,1)} %param.12), kind=kOutput, calls=%fused_computation.58 | convolution fusion | flops 2097152 | bytes 573440 | tf_op jit(solution)/shard_map/bqu,bru->brq/dot_general | solution.py:71
  2.9 1.4 %fusion.36 = bf16[16,1,4,128]{3,2,0,1:T(4,128)(2,1)S(1)} fusion(f32[16,4,128]{2,1,0:T(4,128)S(1)} %fusion.53, bf16[16,2,128,128]{3,2,1,0:T(8,128)(2,1)} %param.15, bf16[16,2,4,128]{3,2,1,0:T(4,128)(2,1)} %param.12), kind=kOutput, calls=%fused_computation.32 | convolution fusion | flops 2113536 | bytes 589824 | tf_op jit(solution)/shard_map/bqu,bru->brq/dot_general | solution.py:71
  4.4 1.4 %fusion.37 = bf16[16,1,4,128]{3,2,0,1:T(4,128)(2,1)S(1)} fusion(f32[16,4,128]{2,1,0:T(4,128)S(1)} %fusion.55, bf16[16,2,128,128]{3,2,1,0:T(8,128)(2,1)} %param.15, bf16[16,2,4,128]{3,2,1,0:T(4,128)(2,1)} %param.12), kind=kOutput, calls=%fused_computation.33 | convolution fusion | flops 2113536 | bytes 589824 | tf_op jit(solution)/shard_map/bqu,bru->brq/dot_general | solution.py:71
  5.8 1.3 %fusion.77 = f32[16,2,2048]{2,0,1:T(8,128)S(1)} fusion(f32[8,2,2048]{2,1,0:T(2,128)} %param.18, s32[16]{0:T(128)} %param.19), kind=kOutput, calls=%fused_computation.93 | convolution fusion | flops 6291584 | bytes 393280 | tf_op jit(solution)/shard_map/ex,xwf->ewf/dot_general | solution.py:79
  7.2 0.7 broadcast_subtract_fusion
  7.9 0.3 fusion.58
  8.4 0.3 convolution_bitcast_fusion.1
  8.7 0.3 convolution_bitcast_fusion
  9.0 32.1 %all-reduce.2 = bf16[4,8,2,4,512]{4,1,0,3,2:T(8,128)(2,1)S(1)} all-reduce(f32[4,8,2,4,512]{4,1,0,3,2:T(8,128)S(1)} %maximum_bitcast_fusion), channel_id=2, replica_groups=mesh['box'=8,'samp'=4] {'samp'}, use_global_device_ids=true, to_apply=%region_0.1.clone | all-reduce | flops 131072 | bytes 786432
  41.1 0.6 dynamic-slice
  41.7 0.7 fusion.79
  42.4 0.5 collective-permute-start.2
  43.0 5.3 %collective-permute-start.1 = (bf16[8,2,4,128]{3,2,1,0:T(4,128)(2,1)S(1)}, bf16[8,2,4,128]{3,2,1,0:T(4,128)(2,1)S(1)}, u32[]{:S(2)}, u32[]{:S(2)}) collective-permute-start(bf16[8,2,4,128]{3,2,1,0:T(4,128)(2,1)S(1)} %get-tuple-element.20), channel_id=1, source_target_pairs={{1,0},{2,1},{3,2},{4,3},{5,4},{6,5},{7,6},{8,7},{9,8},{10,9},{11,1... | collective-permute-start | bytes 49160 | tf_op jit(solution)/shard_map/ppermute | solution.py:16
  48.6 0.4 fusion.68
  49.2 0.6 collective-permute-done
  49.8 0.8 %gather_fusion = bf16[128,2,4,128]{3,2,1,0:T(4,128)(2,1)S(1)} fusion(bf16[32,2,4,128]{3,2,1,0:T(4,128)(2,1)S(1)} %pad_maximum_fusion, s32[1024]{0:T(1024)S(1)} %pad_clamp_fusion), kind=kCustom, calls=%fused_computation | custom fusion | bytes 524800 | tf_op jit(solution)/shard_map/jit(_take)/gather | solution.py:58
  50.8 0.2 broadcast_select_fusion
  51.0 3.4 %fusion.15 = f32[16,4,128]{2,1,0:T(4,128)S(1)} fusion(bf16[16,8,2,128,128]{4,3,2,1,0:T(8,128)(2,1)} %param.13, bf16[16,8,2,4,128]{4,3,1,0,2:T(4,128)(2,1)S(1)} %broadcast_select_fusion), kind=kOutput, calls=%fused_computation.17 | convolution fusion | flops 16777216 | bytes 4358144 | tf_op jit(solution)/shard_map/bkpq,bkrq->brp/dot_general | solution.py:61
  54.4 3.4 %fusion.12 = f32[16,4,128]{2,1,0:T(4,128)S(1)} fusion(bf16[16,8,2,128,128]{4,3,2,1,0:T(8,128)(2,1)} %param.13, bf16[16,8,2,4,128]{4,3,1,0,2:T(4,128)(2,1)S(1)} %broadcast_select_fusion), kind=kOutput, calls=%fused_computation.16 | convolution fusion | flops 16777216 | bytes 4358144 | tf_op jit(solution)/shard_map/bkpq,bkrq->brp/dot_general | solution.py:61
  57.8 3.4 %fusion.28 = f32[16,4,128]{2,1,0:T(4,128)S(1)} fusion(f32[16,4,128]{2,1,0:T(4,128)S(1)} %fusion.15, bf16[16,8,2,128,128]{4,3,2,1,0:T(8,128)(2,1)} %param.13, bf16[16,8,2,4,128]{4,3,1,0,2:T(4,128)(2,1)S(1)} %broadcast_select_fusion), kind=kOutput, calls=%fused_computation.28 | convolution fusion | flops 16785408 | bytes 4390912 | tf_op jit(solution)/shard_map/bkpq,bkrq->brp/dot_general | solution.py:61
  61.2 3.4 %fusion.31 = f32[16,4,128]{2,1,0:T(4,128)S(1)} fusion(f32[16,4,128]{2,1,0:T(4,128)S(1)} %fusion.12, bf16[16,8,2,128,128]{4,3,2,1,0:T(8,128)(2,1)} %param.13, bf16[16,8,2,4,128]{4,3,1,0,2:T(4,128)(2,1)S(1)} %broadcast_select_fusion), kind=kOutput, calls=%fused_computation.29 | convolution fusion | flops 16785408 | bytes 4390912 | tf_op jit(solution)/shard_map/bkpq,bkrq->brp/dot_general | solution.py:61
  64.7 0.5 fusion.71
  65.2 0.6 subtract_reduce_fusion
  65.8 13.9 %all_gather.3 = bf16[8,2,4,2048]{3,0,2,1:T(8,128)(2,1)S(1)} all-gather(bf16[8,2,4,512]{3,0,2,1:T(8,128)(2,1)S(1)} %pad_maximum_fusion.1), channel_id=1, replica_groups=mesh['box'=8,'samp'=4] {'samp'}, dimensions={3}, use_global_device_ids=true | all-gather | bytes 327680 | tf_op jit(solution)/shard_map/all_gather | solution.py:121
  79.8 0.3 fusion.106
  80.3 0.3 convolution_convert_fusion
  80.6 0.4 fusion.49
  81.0 0.4 fusion.47
  81.3 0.4 fusion.27
  81.7 0.4 fusion.25
  82.1 0.6 copy.81
  (40 shorter events, 1.1 us)
Async XLA Ops:
  0.0 7.9 %copy-start = (bf16[2048,128]{1,0:T(8,128)(2,1)S(1)}, bf16[2048,128]{1,0:T(8,128)(2,1)}, u32[]{:S(2)}) copy-start(bf16[2048,128]{1,0:T(8,128)(2,1)} %param.17) | copy-start | bytes 1572868
  5.8 35.3 %copy-start.7 = (u32[32]{0:T(128)S(1)}, u32[32]{0:T(128)}, u32[]{:S(2)}) copy-start(u32[32]{0:T(128)} %constant.72) | copy-start | bytes 388
  5.8 37.1 %copy-start.2 = (bf16[16,2,4,128]{3,2,1,0:T(4,128)(2,1)S(1)}, bf16[16,2,4,128]{3,2,1,0:T(4,128)(2,1)}, u32[]{:S(2)}) copy-start(bf16[16,2,4,128]{3,2,1,0:T(4,128)(2,1)} %param.12) | copy-start | bytes 98308
  7.1 41.2 %copy-start.5 = (s32[8,14]{1,0:T(8,128)S(1)}, s32[8,14]{1,0:T(8,128)}, u32[]{:S(2)}) copy-start(s32[8,14]{1,0:T(8,128)} %param.22) | copy-start | bytes 1348
  7.1 41.2 %copy-start.6 = (s32[16,8]{0,1:T(8,128)S(1)}, s32[16,8]{0,1:T(8,128)}, u32[]{:S(2)}) copy-start(s32[16,8]{0,1:T(8,128)} %param.14) | copy-start | bytes 1540
  7.1 41.4 %copy-start.3 = (f32[64,2,512]{2,1,0:T(2,128)S(1)}, f32[64,2,512]{2,1,0:T(2,128)}, u32[]{:S(2)}) copy-start(f32[64,2,512]{2,1,0:T(2,128)} %param.21) | copy-start | bytes 786436
  7.1 41.4 %copy-start.4 = (s32[8,14]{1,0:T(8,128)S(1)}, s32[8,14]{1,0:T(8,128)}, u32[]{:S(2)}) copy-start(s32[8,14]{1,0:T(8,128)} %param.23) | copy-start | bytes 1348
  42.4 22.3 %collective-permute-start.3 = (bf16[8,2,4,512]{3,0,2,1:T(8,128)(2,1)S(1)}, bf16[8,2,4,512]{3,0,2,1:T(8,128)(2,1)S(1)}, u32[]{:S(2)}, u32[]{:S(2)}) collective-permute-start(bf16[8,2,4,512]{3,0,2,1:T(8,128)(2,1)S(1)} %fusion.79), channel_id=1, source_target_pairs={{4,0},{8,4},{12,8},{16,12},{20,16},{24,20},{28,24},{0,28},{5,1},{9... | collective-permute-start | bytes 196616 | tf_op jit(solution)/shard_map/ppermute | solution.py:16
  42.4 22.2 %collective-permute-start.2 = (bf16[8,2,4,512]{3,0,2,1:T(8,128)(2,1)S(1)}, bf16[8,2,4,512]{3,0,2,1:T(8,128)(2,1)S(1)}, u32[]{:S(2)}, u32[]{:S(2)}) collective-permute-start(bf16[8,2,4,512]{3,0,2,1:T(8,128)(2,1)S(1)} %fusion.79), channel_id=1, source_target_pairs={{0,4},{4,8},{8,12},{12,16},{16,20},{20,24},{24,28},{28,0},{1,5},{5... | collective-permute-start | bytes 196616 | tf_op jit(solution)/shard_map/ppermute | solution.py:14
  42.9 6.8 %collective-permute-start = (bf16[8,2,4,128]{3,2,1,0:T(4,128)(2,1)S(1)}, bf16[8,2,4,128]{3,2,1,0:T(4,128)(2,1)S(1)}, u32[]{:S(2)}, u32[]{:S(2)}) collective-permute-start(bf16[8,2,4,128]{3,2,1,0:T(4,128)(2,1)S(1)} %get-tuple-element.19), channel_id=1, source_target_pairs={{0,1},{1,2},{2,3},{3,4},{4,5},{5,6},{6,7},{7,8},{8,9},{9,10},{10,1... | collective-permute-start | bytes 49160 | tf_op jit(solution)/shard_map/ppermute | solution.py:14
  43.0 6.8 %collective-permute-start.1 = (bf16[8,2,4,128]{3,2,1,0:T(4,128)(2,1)S(1)}, bf16[8,2,4,128]{3,2,1,0:T(4,128)(2,1)S(1)}, u32[]{:S(2)}, u32[]{:S(2)}) collective-permute-start(bf16[8,2,4,128]{3,2,1,0:T(4,128)(2,1)S(1)} %get-tuple-element.20), channel_id=1, source_target_pairs={{1,0},{2,1},{3,2},{4,3},{5,4},{6,5},{7,6},{8,7},{9,8},{10,9},{11,1... | collective-permute-start | bytes 49160 | tf_op jit(solution)/shard_map/ppermute | solution.py:16
  65.2 15.4 %copy-start.1 = (bf16[16,2,128,128]{3,2,1,0:T(8,128)(2,1)S(1)}, bf16[16,2,128,128]{3,2,1,0:T(8,128)(2,1)}, u32[]{:S(2)}) copy-start(bf16[16,2,128,128]{3,2,1,0:T(8,128)(2,1)} %param.16) | copy-start | bytes 3145732
where the time goes:
time: 83.2 us; the launch traced here: 82.8 us
  blocking collectives  46 us (55%)
  matrix products  24.7 us (30%)
  starting transfers between devices  5.95 us (7%)
  local copies, waits for them, and re-layouts  3.19 us (4%)
  other arithmetic  1.97 us (2%)
    unnamed x1, blocking collectives  32.1 us
    all_gather x1, blocking collectives, on_device(): lax.all_gather(incoming, 'samp', axis=3, tiled=True)  13.9 us
    dot_general x4, matrix products, apply(): return jnp.einsum('bkpq,bkrq->brp', a, b, preferred_element_type=f32)  13.7 us
    dot_general x4, matrix products, radiate(): return jnp.einsum('bqu,bru->brq', a, b, preferred_element_type=f32)  5.81 us
    ppermute x2, starting transfers between devices, with_halo(): lax.ppermute(head, axis, [((i + 1) % count, i) for i in range(count)])  5.39 us
  transfers between devices with their start and end apart: 4, of which 1 were waited for; matrix products, arithmetic and copies ran while one was open for 19% of the time, Pallas kernels for 0%

commit v1 on v0

v1 whole, which is shorter than its diff:
```python
import jax
import jax.numpy as jnp
from jax import lax
from jax.experimental import pallas as pl
from jax.experimental.pallas import tpu as pltpu
from jax.sharding import PartitionSpec as P

F32 = jnp.float32
BF16 = jnp.bfloat16
LANES = 128


def nt_dot(a, b):
    return lax.dot_general(a, b, (((1,), (1,)), ((), ())), preferred_element_type=F32)


def nn_dot(a, b):
    return lax.dot_general(a, b, (((1,), (0,)), ((), ())), preferred_element_type=F32)


def times_i(v):
    half = v.shape[0] // 2
    return jnp.concatenate([-v[half:], v[:half]], axis=0)


def widen(ref, n):
    v = jnp.concatenate([ref[n, 0].astype(F32), ref[n, 1].astype(F32)], axis=0)
    return jnp.concatenate([v, times_i(v)], axis=1)


def leaf_kernel(first_parent, octant, parent, x_ref, lift_ref, out_ref, rows, *, parents):
    step = pl.program_id(0)
    per_step = lift_ref.shape[0]
    boxes = x_ref.shape[0]
    parts = x_ref.shape[1] * x_ref.shape[2]
    for i in range(per_step):
        n = step * per_step + i
        xw = widen(x_ref, n).astype(BF16)
        mat = jnp.concatenate([lift_ref[i, 0], lift_ref[i, 1]], axis=1)
        rows[pl.ds(n, parts, stride=boxes), :] = nt_dot(xw, mat)

    @pl.when(step == pl.num_programs(0) - 1)
    def _():
        out_ref[: parts * boxes] = rows[...].astype(BF16)
        lane = lax.rem(lax.broadcasted_iota(jnp.int32, (boxes, LANES), 1), boxes)
        row = lax.broadcasted_iota(jnp.int32, (boxes, LANES), 0)
        across = jnp.zeros((boxes, LANES), F32)
        down = jnp.zeros((boxes, LANES), F32)
        for n in range(boxes):
            slot = (octant[n] * parents + parent[n] - first_parent[0]).astype(F32)
            across = jnp.where(lane == n, slot, across)
            down = jnp.where(row == n, slot, down)
        out_ref[parts * boxes : (parts + 1) * boxes] = across.astype(BF16)
        out_ref[(parts + 1) * boxes : (parts + 2) * boxes] = down.astype(BF16)


def up_kernel(*refs, pieces, boxes, parents, parts):
    msgs = refs[:pieces]
    interp_ref, phase_ref, out_ref, place_ref, raised, folded = refs[pieces:]
    leaves = pieces * boxes
    slots = 8 * parents
    samples = interp_ref.shape[0]
    per_tile = LANES // boxes
    at = parts * boxes
    tiles = []
    for t in range(0, pieces, per_tile):
        lane = lax.broadcasted_iota(jnp.int32, (boxes, LANES), 1) // boxes
        code = msgs[t][at : at + boxes].astype(F32)
        for d in range(1, min(per_tile, pieces - t)):
            code = jnp.where(lane == d, msgs[t + d][at : at + boxes].astype(F32), code)
        code = jnp.concatenate([code] * (slots // boxes), axis=0)
        want = lax.broadcasted_iota(jnp.int32, (slots, LANES), 0).astype(F32)
        width = min(per_tile, pieces - t) * boxes
        tiles.append(jnp.where(code == want, 1.0, 0.0)[:, :width])
    sorter = jnp.concatenate(tiles, axis=1).astype(BF16)
    code = jnp.concatenate([m[at + boxes : at + 2 * boxes].astype(F32) for m in msgs], axis=0)
    tiles = []
    for t in range(0, slots, LANES):
        width = min(LANES, slots - t)
        want = (lax.broadcasted_iota(jnp.int32, (leaves, LANES), 1) + t).astype(F32)
        tiles.append(jnp.where(code == want, 1.0, 0.0)[:, :width])
    place_ref[...] = jnp.concatenate(tiles, axis=1).astype(BF16)
    pats = jnp.concatenate(
        [
            jnp.concatenate([m[c * boxes : (c + 1) * boxes] for m in msgs], axis=0)
            for c in range(parts)
        ],
        axis=1,
    )
    ordered = nn_dot(sorter, pats).astype(BF16)
    for c in range(parts):
        raised[c * slots : (c + 1) * slots] = nt_dot(
            ordered[:, c * LANES : (c + 1) * LANES], interp_ref[...]
        )
    half = parts // 2
    for t in range(samples // LANES):
        lanes = slice(t * LANES, (t + 1) * LANES)
        for r in range(half):
            re = im = None
            for o in range(8):
                ph_r = phase_ref[o, 0:1, lanes]
                ph_i = phase_ref[o, 1:2, lanes]
                base_r = r * slots + o * parents
                base_i = (half + r) * slots + o * parents
                xr = raised[base_r : base_r + parents, lanes]
                xi = raised[base_i : base_i + parents, lanes]
                dr = ph_r * xr - ph_i * xi
                di = ph_r * xi + ph_i * xr
                re = dr if re is None else re + dr
                im = di if im is None else im + di
            folded[t, r * parents : (r + 1) * parents] = re
            folded[t, (half + r) * parents : (half + r + 1) * parents] = im
        for p in range(0, parents, 2):
            both = jnp.concatenate(
                [folded[t, pl.ds(p + e, parts, stride=parents), :] for e in range(2)], axis=0
            )
            out_ref[p * parts : (p + 2) * parts, lanes] = both.astype(BF16)


def down_kernel(
    first_parent, inter, trans, own, left, right, table, interp_ref, phase_ref, place_ref, *refs,
    pieces, boxes, parents, total, parts,
):
    outs = refs[:pieces]
    window, incoming, shifted = refs[pieces:]
    samples = interp_ref.shape[0]
    slots = 8 * parents
    half = parts // 2
    for i, src in enumerate((left, own, right)):
        window[i * parents : (i + 1) * parents] = (
            src[...].astype(F32).reshape(parents, parts, samples)
        )
    base = first_parent[0]

    def one(p, carry):
        acc_r = jnp.zeros((parts, samples), F32)
        acc_i = jnp.zeros((parts, samples), F32)
        for k in range(inter.shape[1]):
            j = lax.rem(inter[p, k] - base + parents + total, total)
            m = trans[p, k]
            x = window[j]
            acc_r += table[m, 0:1, :] * x
            acc_i += table[m, 1:2, :] * x
        got = (acc_r + times_i(acc_i)).astype(BF16).astype(F32)
        for t in range(samples // LANES):
            incoming[t, pl.ds(p * parts, parts), :] = got[:, t * LANES : (t + 1) * LANES]
        return carry

    lax.fori_loop(0, parents, one, 0)
    for t in range(samples // LANES):
        lanes = slice(t * LANES, (t + 1) * LANES)
        for r in range(half):
            ir = incoming[t, pl.ds(r, parents, stride=parts), :]
            ii = incoming[t, pl.ds(half + r, parents, stride=parts), :]
            re, im = [], []
            for o in range(8):
                ph_r = phase_ref[o, 0:1, lanes]
                ph_i = phase_ref[o, 1:2, lanes]
                re.append(ph_r * ir - ph_i * ii)
                im.append(ph_r * ii + ph_i * ir)
            shifted[r * slots : (r + 1) * slots, lanes] = jnp.concatenate(re, axis=0).astype(BF16)
            shifted[(half + r) * slots : (half + r + 1) * slots, lanes] = jnp.concatenate(
                im, axis=0
            ).astype(BF16)
    field = nn_dot(shifted[...], interp_ref[...]).astype(BF16)
    spread = jnp.concatenate([field[c * slots : (c + 1) * slots] for c in range(parts)], axis=1)
    leaves = nn_dot(place_ref[...], spread).astype(BF16)
    for d in range(pieces):
        for c in range(parts):
            outs[d][c * boxes : (c + 1) * boxes] = leaves[
                d * boxes : (d + 1) * boxes, c * LANES : (c + 1) * LANES
            ]


def near_kernel(first_box, neighbours, left, own, right, mats, out_ref, window, *, total):
    step = pl.program_id(0)
    per_step, near_count = mats.shape[:2]
    reach = left.shape[0]
    boxes = own.shape[0]

    @pl.when(step == 0)
    def _():
        for i in range(reach):
            window[i] = widen(left, i)
            window[reach + boxes + i] = widen(right, i)
        for i in range(boxes):
            window[reach + i] = widen(own, i)

    for i in range(per_step):
        n = step * per_step + i
        acc = None
        for k in range(near_count):
            j = lax.rem(neighbours[n, k] - first_box[0] + reach + total, total)
            mat = jnp.concatenate([mats[i, k, 0], mats[i, k, 1]], axis=1)
            y = nt_dot(window[j].astype(BF16), mat)
            acc = y if acc is None else acc + y
        out_ref[i] = acc


def final_kernel(*refs, pieces):
    parts_in = refs[:pieces]
    near_ref, mats, out_ref, field = refs[pieces:]
    boxes, halves, rhs = out_ref.shape[:3]
    parts = halves * rhs
    total = parts_in[0][...].astype(F32)
    for m in parts_in[1:]:
        total += m[...].astype(F32)
    field[...] = total.astype(BF16).astype(F32)
    for n in range(boxes):
        v = field[pl.ds(n, parts, stride=boxes), :]
        wide = jnp.concatenate([v, times_i(v)], axis=1).astype(BF16)
        y = nt_dot(wide, jnp.concatenate([mats[n, 0], mats[n, 1]], axis=1)) + near_ref[n]
        out_ref[n, 0] = y[:rhs]
        out_ref[n, 1] = y[rhs:]


def whole_in(kind):
    return pl.BlockSpec(memory_space=kind)


VM = pltpu.VMEM
SM = pltpu.SMEM
PARAMS = pltpu.CompilerParams(vmem_limit_bytes=24 * 1024 * 1024)


def on_device(
    xvec,
    near_blocks,
    neighbours,
    lift,
    place,
    interp,
    phases,
    octant,
    leaf_parent_index,
    translators,
    inter_list,
    trans_id,
):
    boxes, halves, rhs, unknowns = xvec.shape
    parts = halves * rhs
    nsamp = lax.axis_size("samp")
    nbox = lax.axis_size("box")
    box_index = lax.axis_index("box").astype(jnp.int32)
    samp_index = lax.axis_index("samp").astype(jnp.int32)
    total = boxes * nsamp * nbox
    reach = boxes // 2
    parents = boxes * nsamp // 8
    all_parents = parents * nbox
    samples = interp.shape[0] // nsamp
    slots = 8 * parents
    leaves = boxes * nsamp
    first_parent = (box_index * parents).reshape(1)
    first_box = ((box_index * nsamp + samp_index) * boxes).reshape(1)
    units = nsamp * nbox

    up_ring = [(i, (i + 1) % units) for i in range(units)]
    down_ring = [((i + 1) % units, i) for i in range(units)]
    x_left = lax.ppermute(xvec[boxes - reach :], ("box", "samp"), up_ring)
    x_right = lax.ppermute(xvec[:reach], ("box", "samp"), down_ring)

    lift_steps = 4
    message_rows = (parts + 2) * boxes
    message = pl.pallas_call(
        lambda *refs: leaf_kernel(*refs, parents=parents),
        grid_spec=pltpu.PrefetchScalarGridSpec(
            num_scalar_prefetch=3,
            grid=(lift_steps,),
            in_specs=[
                pl.BlockSpec(xvec.shape, lambda i, *_: (0, 0, 0, 0)),
                pl.BlockSpec(
                    (boxes // lift_steps,) + lift.shape[1:], lambda i, *_: (i, 0, 0, 0)
                ),
            ],
            out_specs=pl.BlockSpec((message_rows, LANES), lambda i, *_: (0, 0)),
            scratch_shapes=[VM((parts * boxes, LANES), F32)],
        ),
        out_shape=jax.ShapeDtypeStruct((message_rows, LANES), BF16),
        compiler_params=PARAMS,
        name="leaf",
    )(first_parent, octant, leaf_parent_index, xvec, lift)

    messages = [message] + [
        lax.ppermute(message, "samp", [(i, (i + d) % nsamp) for i in range(nsamp)])
        for d in range(1, nsamp)
    ]

    near_steps = boxes // 2
    near = pl.pallas_call(
        lambda *refs: near_kernel(*refs, total=total),
        grid_spec=pltpu.PrefetchScalarGridSpec(
            num_scalar_prefetch=2,
            grid=(near_steps,),
            in_specs=[
                pl.BlockSpec(x_left.shape, lambda i, *_: (0, 0, 0, 0)),
                pl.BlockSpec(xvec.shape, lambda i, *_: (0, 0, 0, 0)),
                pl.BlockSpec(x_right.shape, lambda i, *_: (0, 0, 0, 0)),
                pl.BlockSpec(
                    (boxes // near_steps,) + near_blocks.shape[1:],
                    lambda i, *_: (i, 0, 0, 0, 0),
                ),
            ],
            out_specs=pl.BlockSpec(
                (boxes // near_steps, parts, unknowns), lambda i, *_: (i, 0, 0)
            ),
            scratch_shapes=[VM((boxes + 2 * reach, parts, 2 * unknowns), F32)],
        ),
        out_shape=jax.ShapeDtypeStruct((boxes, parts, unknowns), F32),
        compiler_params=PARAMS,
        cost_estimate=pl.CostEstimate(
            flops=2 * parts * near_blocks.size,
            bytes_accessed=2 * near_blocks.size,
            transcendentals=0,
        ),
        name="near",
    )(first_box, neighbours, x_left, xvec, x_right, near_blocks)

    my_interp = lax.dynamic_slice_in_dim(interp, samp_index * samples, samples, axis=0)
    my_phases = lax.dynamic_slice_in_dim(phases, samp_index * samples, samples, axis=2)

    parent_pat, place_onehot = pl.pallas_call(
        lambda *refs: up_kernel(
            *refs, pieces=nsamp, boxes=boxes, parents=parents, parts=parts
        ),
        in_specs=[whole_in(VM)] * (nsamp + 2),
        out_specs=[whole_in(VM)] * 2,
        out_shape=[
            jax.ShapeDtypeStruct((parents * parts, samples), BF16),
            jax.ShapeDtypeStruct((leaves, slots), BF16),
        ],
        scratch_shapes=[
            VM((parts * slots, samples), F32),
            VM((samples // LANES, parts * parents, LANES), F32),
        ],
        compiler_params=PARAMS,
        name="up",
    )(*messages, my_interp, my_phases)

    from_left = lax.ppermute(parent_pat, "box", [(i, (i + 1) % nbox) for i in range(nbox)])
    from_right = lax.ppermute(parent_pat, "box", [((i + 1) % nbox, i) for i in range(nbox)])

    fields = pl.pallas_call(
        lambda *refs: down_kernel(
            *refs, pieces=nsamp, boxes=boxes, parents=parents, total=all_parents, parts=parts
        ),
        in_specs=[whole_in(SM)] * 3 + [whole_in(VM)] * 7,
        out_specs=[whole_in(VM)] * nsamp,
        out_shape=[jax.ShapeDtypeStruct((parts * boxes, LANES), BF16)] * nsamp,
        scratch_shapes=[
            VM((3 * parents, parts, samples), F32),
            VM((samples // LANES, parents * parts, LANES), F32),
            VM((parts * slots, samples), BF16),
        ],
        compiler_params=PARAMS,
        name="down",
    )(
        first_parent,
        inter_list,
        trans_id,
        parent_pat,
        from_left,
        from_right,
        translators,
        my_interp,
        my_phases,
        place_onehot,
    )

    partial = [fields[0]] + [
        lax.ppermute(fields[d], "samp", [((i + d) % nsamp, i) for i in range(nsamp)])
        for d in range(1, nsamp)
    ]

    return pl.pallas_call(
        lambda *refs: final_kernel(*refs, pieces=nsamp),
        in_specs=[whole_in(VM)] * (nsamp + 2),
        out_specs=whole_in(VM),
        out_shape=jax.ShapeDtypeStruct(xvec.shape, F32),
        scratch_shapes=[VM((parts * boxes, LANES), F32)],
        compiler_params=PARAMS,
        name="final",
    )(*partial, near, place)


def solution(mesh):
    in_specs = (
        P(("box", "samp"), None, None, None),
        P(("box", "samp"), None, None, None, None),
        P(("box", "samp"), None),
        P(("box", "samp"), None, None, None),
        P(("box", "samp"), None, None, None),
        P(),
        P(),
        P(("box", "samp")),
        P(("box", "samp")),
        P(None, None, "samp"),
        P("box", None),
        P("box", None),
    )
    out_specs = P(("box", "samp"), None, None, None)
    return jax.shard_map(
        on_device, mesh=mesh, in_specs=in_specs, out_specs=out_specs, check_vma=False
    )
```

time: 83.2 us -> 44.9 us (0.54)
  blocking collectives: 46 us -> 0 us
  matrix products: 24.7 us -> 0 us
  starting transfers between devices: 5.95 us -> 18.9 us
  local copies, waits for them, and re-layouts: 3.19 us -> 12.2 us
  Pallas kernels: 0 us -> 8.56 us
  waiting for transfers between devices: 0.64 us -> 4.61 us
  other arithmetic: 1.97 us -> 0 us
    unnamed x1 -> x0, blocking collectives: 32.1 us -> none
    dot_general x20 -> x0, matrix products: 24.7 us -> none  [the longest x4 13.7 us: apply(): return jnp.einsum('bkpq,bkrq->brp', a, b, preferred_element_type=f32)]
    all_gather x1 -> x0, blocking collectives: 13.9 us -> none  [on_device(): lax.all_gather(incoming, 'samp', axis=3, tiled=True)]
    ppermute x4 -> x10, starting transfers between devices: 5.95 us -> 18.9 us  [the longest x3 7.01 us: on_device(): lax.ppermute(message, 'samp', [(i, (i + d) % nsamp) for i in range(nsamp)])]
    unnamed x17 -> x23, local copies, waits for them, and re-layouts: 0.63 us -> 10.6 us
    pallas_call x0 -> x5, Pallas kernels: none -> 8.56 us  [the longest x1 3.79 us: on_device(): pl.pallas_call(lambda *refs: near_kernel(*refs, total=total), grid_spec=p...]
    ppermute x4 -> x10, waiting for transfers between devices: 0.64 us -> 4.61 us  [the longest x1 1.94 us: on_device(): lax.ppermute(parent_pat, 'box', [(i, (i + 1) % nbox) for i in range(nbox)])]
    gather x2 -> x0, local copies, waits for them, and re-layouts: 0.92 us -> none  [on_device(): near_x = jnp.take(widened, local_index, axis=0)]
  transfers between devices with their start and end apart: 4 -> 10, of which waited for: 1 -> 4; matrix products, arithmetic and copies ran while one was open for 19% -> 5% of each run, Pallas kernels for 0% -> 9%
where the time goes in v1:
time: 44.9 us; the launch traced here: 44.4 us
  starting transfers between devices  18.9 us (42%)
  local copies, waits for them, and re-layouts  12.2 us (27%)
  Pallas kernels  8.56 us (19%)
  waiting for transfers between devices  4.61 us (10%)
    unnamed x23, local copies, waits for them, and re-layouts  10.6 us
    ppermute x3, starting transfers between devices, on_device(): lax.ppermute(message, 'samp', [(i, (i + d) % nsamp) for i in range(nsamp)])  7.01 us
    ppermute x3, starting transfers between devices, on_device(): lax.ppermute(fields[d], 'samp', [((i + d) % nsamp, i) for i in range(nsam...  3.84 us
    pallas_call x1, Pallas kernels, on_device(): pl.pallas_call(lambda *refs: near_kernel(*refs, total=total), grid_spec=p...  3.79 us
    ppermute x1, starting transfers between devices, on_device(): x_left = lax.ppermute(xvec[boxes - reach:], ('box', 'samp'), up_ring)  2.91 us
    ppermute x1, starting transfers between devices, on_device(): lax.ppermute(parent_pat, 'box', [((i + 1) % nbox, i) for i in range(nbox)])  2.63 us
    ppermute x1, starting transfers between devices, on_device(): x_right = lax.ppermute(xvec[:reach], ('box', 'samp'), down_ring)  2.5 us
    ppermute x1, waiting for transfers between devices, on_device(): lax.ppermute(parent_pat, 'box', [(i, (i + 1) % nbox) for i in range(nbox)])  1.94 us
  transfers between devices with their start and end apart: 10, of which 4 were waited for; matrix products, arithmetic and copies ran while one was open for 5% of the time, Pallas kernels for 9%

profile of v1, /device:TPU:0, one launch (start us, length us, event | category | flops | bytes accessed | tf_op | source)
XLA Modules:
  0.0 44.4 jit_solution(6228172949076073129)
XLA Ops:
  0.0 1.3 %copy-done.3 = bf16[16,2,128,128]{3,2,1,0:T(8,128)(2,1)S(1)} copy-done((bf16[16,2,128,128]{3,2,1,0:T(8,128)(2,1)S(1)}, bf16[16,2,128,128]{3,2,1,0:T(8,128)(2,1)}, u32[]{:S(2)}) %copy-start.3) | copy-done | bytes 1048600
  1.4 0.8 %copy-done.4 = bf16[16,2,4,128]{3,2,1,0:T(4,128)(2,1)S(1)} copy-done((bf16[16,2,4,128]{3,2,1,0:T(4,128)(2,1)S(1)}, bf16[16,2,4,128]{3,2,1,0:T(4,128)(2,1)}, u32[]{:S(2)}) %copy-start.4) | copy-done | bytes 32792
  2.1 0.7 %copy-done.9 = s32[16]{0:T(128)S(1)} copy-done((s32[16]{0:T(128)S(1)}, s32[16]{0:T(128)}, u32[]{:S(2)}) %copy-start.9) | copy-done | bytes 88
  2.8 0.7 %copy-done.10 = s32[16]{0:T(128)S(1)} copy-done((s32[16]{0:T(128)S(1)}, s32[16]{0:T(128)}, u32[]{:S(2)}) %copy-start.10) | copy-done | bytes 88
  3.4 1.3 %leaf.1.refs_0_ = bf16[160,128]{1,0:T(8,128)(2,1)S(1)} custom-call(s32[1]{0:T(128)} %bitcast.refs_0_, s32[16]{0:T(128)S(1)} %copy-done.9, s32[16]{0:T(128)S(1)} %copy-done.10, bf16[16,2,4,128]{3,2,1,0:T(4,128)(2,1)S(1)} %copy-done.4, bf16[16,2,128,128]{3,2,1,0:T(8,128)(2,1)S(1)} %copy-done.3), custom_call_target="tpu_custom_call" | custom-call | tf_op jit(solution)/shard_map/leaf/pallas_call | solution.py:264
  4.8 3.1 %collective-permute-start = (bf16[160,128]{1,0:T(8,128)(2,1)S(1)}, bf16[160,128]{1,0:T(8,128)(2,1)S(1)}, u32[]{:S(2)}, u32[]{:S(2)}) collective-permute-start(bf16[160,128]{1,0:T(8,128)(2,1)S(1)} %leaf.1.refs_0_), channel_id=1, source_target_pairs={{0,1},{1,2},{2,3},{3,0},{4,5},{5,6},{6,7},{7,4},{8,9},{9,10},{10,1... | collective-permute-start | bytes 122888 | tf_op jit(solution)/shard_map/ppermute | solution.py:284
  7.8 2.6 %collective-permute-start.1 = (bf16[160,128]{1,0:T(8,128)(2,1)S(1)}, bf16[160,128]{1,0:T(8,128)(2,1)S(1)}, u32[]{:S(2)}, u32[]{:S(2)}) collective-permute-start(bf16[160,128]{1,0:T(8,128)(2,1)S(1)} %leaf.1.refs_0_), channel_id=1, source_target_pairs={{0,2},{1,3},{2,0},{3,1},{4,6},{5,7},{6,4},{7,5},{8,10},{9,11},{10,... | collective-permute-start | bytes 122888 | tf_op jit(solution)/shard_map/ppermute | solution.py:284
  10.4 1.3 %collective-permute-start.2 = (bf16[160,128]{1,0:T(8,128)(2,1)S(1)}, bf16[160,128]{1,0:T(8,128)(2,1)S(1)}, u32[]{:S(2)}, u32[]{:S(2)}) collective-permute-start(bf16[160,128]{1,0:T(8,128)(2,1)S(1)} %leaf.1.refs_0_), channel_id=1, source_target_pairs={{0,3},{1,0},{2,1},{3,2},{4,7},{5,4},{6,5},{7,6},{8,11},{9,8},{10,9... | collective-permute-start | bytes 122888 | tf_op jit(solution)/shard_map/ppermute | solution.py:284
  11.8 0.8 %constant_dynamic-slice_fusion.refs_5_.refs_8_ = f32[8,2,512]{2,1,0:T(2,128)S(1)} fusion(f32[8,2,2048]{2,1,0:T(2,128)} %param.18, s32[]{:T(128)S(6)} %select_n.4), kind=kLoop, calls=%fused_computation | loop fusion | bytes 65540 | tf_op jit(solution)/shard_map/dynamic_slice | solution.py:319
  12.6 0.7 %collective-permute-done.1.refs_2_ = bf16[160,128]{1,0:T(8,128)(2,1)S(1)} collective-permute-done((bf16[160,128]{1,0:T(8,128)(2,1)S(1)}, bf16[160,128]{1,0:T(8,128)(2,1)S(1)}, u32[]{:S(2)}, u32[]{:S(2)}) %collective-permute-start.1) | collective-permute-done | bytes 40992 | tf_op jit(solution)/shard_map/ppermute | solution.py:284
  13.2 1.2 %collective-permute-done.2.refs_3_ = bf16[160,128]{1,0:T(8,128)(2,1)S(1)} collective-permute-done((bf16[160,128]{1,0:T(8,128)(2,1)S(1)}, bf16[160,128]{1,0:T(8,128)(2,1)S(1)}, u32[]{:S(2)}, u32[]{:S(2)}) %collective-permute-start.2) | collective-permute-done | bytes 40992 | tf_op jit(solution)/shard_map/ppermute | solution.py:284
  14.4 0.7 %up.1 = (bf16[64,512]{1,0:T(8,128)(2,1)S(1)}, bf16[64,64]{1,0:T(8,128)(2,1)S(1)}) custom-call(bf16[160,128]{1,0:T(8,128)(2,1)S(1)} %leaf.1.refs_0_, bf16[160,128]{1,0:T(8,128)(2,1)S(1)} %collective-permute-done.refs_1_, bf16[160,128]{1,0:T(8,128)(2,1)S(1)} %collective-permute-done.1.refs_2_, bf16[160,128]{1,0:T(8,128)(2,1)S(1)} %collective-permute-done.2.refs_3_, ...), custom_call_target="tpu_custom_call" | custom-call | tf_op jit(solution)/shard_map/up/pallas_call | solution.py:321
  15.1 0.1 collective-permute-start.3
  15.2 2.6 %collective-permute-start.4 = (bf16[64,512]{1,0:T(8,128)(2,1)S(1)}, bf16[64,512]{1,0:T(8,128)(2,1)S(1)}, u32[]{:S(2)}, u32[]{:S(2)}) collective-permute-start(bf16[64,512]{1,0:T(8,128)(2,1)S(1)} %get-tuple-element.11.refs_3_), channel_id=1, source_target_pairs={{4,0},{8,4},{12,8},{16,12},{20,16},{24,20},{28,24},{0,28},{5,1},{9... | collective-permute-start | bytes 196616 | tf_op jit(solution)/shard_map/ppermute | solution.py:340
  17.8 1.9 %collective-permute-done.3.refs_4_ = bf16[64,512]{1,0:T(8,128)(2,1)S(1)} collective-permute-done((bf16[64,512]{1,0:T(8,128)(2,1)S(1)}, bf16[64,512]{1,0:T(8,128)(2,1)S(1)}, u32[]{:S(2)}, u32[]{:S(2)}) %collective-permute-start.3) | collective-permute-done | bytes 65568 | tf_op jit(solution)/shard_map/ppermute | solution.py:339
  19.8 0.9 %copy-done.6 = f32[64,2,512]{2,1,0:T(2,128)S(1)} copy-done((f32[64,2,512]{2,1,0:T(2,128)S(1)}, f32[64,2,512]{2,1,0:T(2,128)}, u32[]{:S(2)}) %copy-start.6) | copy-done | bytes 262168
  20.7 0.7 %copy-done.7 = s32[8,14]{1,0:T(8,128)S(1)} copy-done((s32[8,14]{1,0:T(8,128)S(1)}, s32[8,14]{1,0:T(8,128)}, u32[]{:S(2)}) %copy-start.7) | copy-done | bytes 472
  21.4 0.7 %copy-done.8 = s32[8,14]{1,0:T(8,128)S(1)} copy-done((s32[8,14]{1,0:T(8,128)S(1)}, s32[8,14]{1,0:T(8,128)}, u32[]{:S(2)}) %copy-start.8) | copy-done | bytes 472
  22.1 1.7 %down.1 = (bf16[128,128]{1,0:T(8,128)(2,1)S(1)}, bf16[128,128]{1,0:T(8,128)(2,1)S(1)}, bf16[128,128]{1,0:T(8,128)(2,1)S(1)}, bf16[128,128]{1,0:T(8,128)(2,1)S(1)}) custom-call(s32[1]{0:T(128)} %bitcast.refs_0_, s32[8,14]{1,0:T(8,128)S(1)} %copy-done.7, s32[8,14]{1,0:T(8,128)S(1)} %copy-done.8, bf16[64,512]{1,0:T(8,128)(2,1)S(1)} %get-tuple-element.11.refs_3_, ...), custom_call_target="tpu_custom_call" | custom-call | tf_op jit(solution)/shard_map/down/pallas_call | solution.py:342
  23.8 3.2 %collective-permute-start.5 = (bf16[128,128]{1,0:T(8,128)(2,1)S(1)}, bf16[128,128]{1,0:T(8,128)(2,1)S(1)}, u32[]{:S(2)}, u32[]{:S(2)}) collective-permute-start(bf16[128,128]{1,0:T(8,128)(2,1)S(1)} %get-tuple-element.14), channel_id=1, source_target_pairs={{1,0},{2,1},{3,2},{0,3},{5,4},{6,5},{7,6},{4,7},{9,8},{10,9},{11,1... | collective-permute-start | bytes 98312 | tf_op jit(solution)/shard_map/ppermute | solution.py:370
  27.0 0.6 %collective-permute-start.7 = (bf16[128,128]{1,0:T(8,128)(2,1)S(1)}, bf16[128,128]{1,0:T(8,128)(2,1)S(1)}, u32[]{:S(2)}, u32[]{:S(2)}) collective-permute-start(bf16[128,128]{1,0:T(8,128)(2,1)S(1)} %get-tuple-element.16), channel_id=1, source_target_pairs={{3,0},{0,1},{1,2},{2,3},{7,4},{4,5},{5,6},{6,7},{11,8},{8,9},{9,10... | collective-permute-start | bytes 98312 | tf_op jit(solution)/shard_map/ppermute | solution.py:370
  27.7 0.7 %fusion = (bf16[8,2,4,128]{3,2,1,0:T(4,128)(2,1)S(1)}, bf16[8,2,4,128]{3,2,1,0:T(4,128)(2,1)S(1)}) fusion(bf16[16,2,4,128]{3,2,1,0:T(4,128)(2,1)} %refs_3_.3), kind=kLoop, calls=%fused_computation.2 | loop fusion | bytes 65536 | tf_op jit(solution)/shard_map/slice | solution.py:260
  28.4 2.9 %collective-permute-start.8 = (bf16[8,2,4,128]{3,2,1,0:T(4,128)(2,1)S(1)}, bf16[8,2,4,128]{3,2,1,0:T(4,128)(2,1)S(1)}, u32[]{:S(2)}, u32[]{:S(2)}) collective-permute-start(bf16[8,2,4,128]{3,2,1,0:T(4,128)(2,1)S(1)} %get-tuple-element.18), channel_id=1, source_target_pairs={{0,1},{1,2},{2,3},{3,4},{4,5},{5,6},{6,7},{7,8},{8,9},{9,10},{10,1... | collective-permute-start | bytes 49160 | tf_op jit(solution)/shard_map/ppermute | solution.py:259
  31.3 2.5 %collective-permute-start.9 = (bf16[8,2,4,128]{3,2,1,0:T(4,128)(2,1)S(1)}, bf16[8,2,4,128]{3,2,1,0:T(4,128)(2,1)S(1)}, u32[]{:S(2)}, u32[]{:S(2)}) collective-permute-start(bf16[8,2,4,128]{3,2,1,0:T(4,128)(2,1)S(1)} %get-tuple-element.17), channel_id=1, source_target_pairs={{1,0},{2,1},{3,2},{4,3},{5,4},{6,5},{7,6},{8,7},{9,8},{10,9},{11,1... | collective-permute-start | bytes 49160 | tf_op jit(solution)/shard_map/ppermute | solution.py:260
  33.8 0.8 %copy.13.refs_1_ = s32[16,8]{1,0:T(8,128)S(1)} copy(s32[16,8]{0,1:T(8,128)} %param.14) | data formatting | bytes 1024 | tf_op args[2]
  34.6 0.8 %collective-permute-done.8.refs_2_ = bf16[8,2,4,128]{3,2,1,0:T(4,128)(2,1)S(1)} collective-permute-done((bf16[8,2,4,128]{3,2,1,0:T(4,128)(2,1)S(1)}, bf16[8,2,4,128]{3,2,1,0:T(4,128)(2,1)S(1)}, u32[]{:S(2)}, u32[]{:S(2)}) %collective-permute-start.8) | collective-permute-done | bytes 16416 | tf_op jit(solution)/shard_map/ppermute | solution.py:259
  35.3 0.0 collective-permute-done.9.refs_4_
  35.4 3.4 %copy-done.1 = bf16[16,8,2,128,128]{4,3,2,1,0:T(8,128)(2,1)S(1)} copy-done((bf16[16,8,2,128,128]{4,3,2,1,0:T(8,128)(2,1)S(1)}, bf16[16,8,2,128,128]{4,3,2,1,0:T(8,128)(2,1)}, u32[]{:S(2)}) %copy-start.1) | copy-done | bytes 8388632
  38.7 0.8 %copy-done.5 = bf16[16,2,4,128]{3,2,1,0:T(4,128)(2,1)S(1)} copy-done((bf16[16,2,4,128]{3,2,1,0:T(4,128)(2,1)S(1)}, bf16[16,2,4,128]{3,2,1,0:T(4,128)(2,1)}, u32[]{:S(2)}) %copy-start.5) | copy-done | bytes 32792
  39.5 3.8 %near.1.refs_4_ = f32[16,8,128]{2,1,0:T(8,128)S(1)} custom-call(s32[1]{0:T(128)} %bitcast.1.refs_0_, s32[16,8]{1,0:T(8,128)S(1)} %copy.13.refs_1_, bf16[8,2,4,128]{3,2,1,0:T(4,128)(2,1)S(1)} %collective-permute-done.8.refs_2_, bf16[16,2,4,128]{3,2,1,0:T(4,128)(2,1)S(1)} %copy-done.5, bf16[8,2,4,128]{3,2,1,0:T(4,128)(2,1)S(1)} %collective-permute-done.9.refs_4_, ...), custom_call_target="tpu_custom_call" | custom-call | flops 67108864 | bytes 8388608 | tf_op jit(solution)/shard_map/near/pallas_call | solution.py:289
  43.3 0.0 collective-permute-done.7.refs_3_
  43.3 1.0 %final.1 = f32[16,2,4,128]{3,2,1,0:T(4,128)} custom-call(bf16[128,128]{1,0:T(8,128)(2,1)S(1)} %get-tuple-element.13.refs_0_, bf16[128,128]{1,0:T(8,128)(2,1)S(1)} %collective-permute-done.5.refs_1_, bf16[128,128]{1,0:T(8,128)(2,1)S(1)} %collective-permute-done.6.refs_2_, bf16[128,128]{1,0:T(8,128)(2,1)S(1)} %collective-permute-done.7.refs_3_, ...), custom_call_target="tpu_custom_call" | custom-call | tf_op jit(solution)/shard_map/final/pallas_call | solution.py:374
  (19 shorter events, 0.0 us)
Async XLA Ops:
  0.0 11.8 %copy-start = (bf16[2048,128]{1,0:T(8,128)(2,1)S(1)}, bf16[2048,128]{1,0:T(8,128)(2,1)}, u32[]{:S(2)}) copy-start(bf16[2048,128]{1,0:T(8,128)(2,1)} %param.17) | copy-start | bytes 1572868
  0.0 43.3 %copy-start.2 = (bf16[16,2,128,128]{3,2,1,0:T(8,128)(2,1)S(1)}, bf16[16,2,128,128]{3,2,1,0:T(8,128)(2,1)}, u32[]{:S(2)}) copy-start(bf16[16,2,128,128]{3,2,1,0:T(8,128)(2,1)} %refs_5_.3) | copy-start | bytes 3145732
  0.0 1.3 %copy-start.3 = (bf16[16,2,128,128]{3,2,1,0:T(8,128)(2,1)S(1)}, bf16[16,2,128,128]{3,2,1,0:T(8,128)(2,1)}, u32[]{:S(2)}) copy-start(bf16[16,2,128,128]{3,2,1,0:T(8,128)(2,1)} %refs_4_.1) | copy-start | bytes 3145732
  1.3 0.8 %copy-start.4 = (bf16[16,2,4,128]{3,2,1,0:T(4,128)(2,1)S(1)}, bf16[16,2,4,128]{3,2,1,0:T(4,128)(2,1)}, u32[]{:S(2)}) copy-start(bf16[16,2,4,128]{3,2,1,0:T(4,128)(2,1)} %refs_3_.3) | copy-start | bytes 98308
  2.1 0.7 %copy-start.9 = (s32[16]{0:T(128)S(1)}, s32[16]{0:T(128)}, u32[]{:S(2)}) copy-start(s32[16]{0:T(128)} %refs_1_.3) | copy-start | bytes 196
  2.8 0.7 %copy-start.10 = (s32[16]{0:T(128)S(1)}, s32[16]{0:T(128)}, u32[]{:S(2)}) copy-start(s32[16]{0:T(128)} %refs_2_.2) | copy-start | bytes 196
  4.8 7.8 %collective-permute-start = (bf16[160,128]{1,0:T(8,128)(2,1)S(1)}, bf16[160,128]{1,0:T(8,128)(2,1)S(1)}, u32[]{:S(2)}, u32[]{:S(2)}) collective-permute-start(bf16[160,128]{1,0:T(8,128)(2,1)S(1)} %leaf.1.refs_0_), channel_id=1, source_target_pairs={{0,1},{1,2},{2,3},{3,0},{4,5},{5,6},{6,7},{7,4},{8,9},{9,10},{10,1... | collective-permute-start | bytes 122888 | tf_op jit(solution)/shard_map/ppermute | solution.py:284
  7.8 5.4 %collective-permute-start.1 = (bf16[160,128]{1,0:T(8,128)(2,1)S(1)}, bf16[160,128]{1,0:T(8,128)(2,1)S(1)}, u32[]{:S(2)}, u32[]{:S(2)}) collective-permute-start(bf16[160,128]{1,0:T(8,128)(2,1)S(1)} %leaf.1.refs_0_), channel_id=1, source_target_pairs={{0,2},{1,3},{2,0},{3,1},{4,6},{5,7},{6,4},{7,5},{8,10},{9,11},{10,... | collective-permute-start | bytes 122888 | tf_op jit(solution)/shard_map/ppermute | solution.py:284
  10.4 4.0 %collective-permute-start.2 = (bf16[160,128]{1,0:T(8,128)(2,1)S(1)}, bf16[160,128]{1,0:T(8,128)(2,1)S(1)}, u32[]{:S(2)}, u32[]{:S(2)}) collective-permute-start(bf16[160,128]{1,0:T(8,128)(2,1)S(1)} %leaf.1.refs_0_), channel_id=1, source_target_pairs={{0,3},{1,0},{2,1},{3,2},{4,7},{5,4},{6,5},{7,6},{8,11},{9,8},{10,9... | collective-permute-start | bytes 122888 | tf_op jit(solution)/shard_map/ppermute | solution.py:284
  15.1 4.6 %collective-permute-start.3 = (bf16[64,512]{1,0:T(8,128)(2,1)S(1)}, bf16[64,512]{1,0:T(8,128)(2,1)S(1)}, u32[]{:S(2)}, u32[]{:S(2)}) collective-permute-start(bf16[64,512]{1,0:T(8,128)(2,1)S(1)} %get-tuple-element.11.refs_3_), channel_id=1, source_target_pairs={{0,4},{4,8},{8,12},{12,16},{16,20},{20,24},{24,28},{28,0},{1,5},{5... | collective-permute-start | bytes 196616 | tf_op jit(solution)/shard_map/ppermute | solution.py:339
  15.2 4.6 %collective-permute-start.4 = (bf16[64,512]{1,0:T(8,128)(2,1)S(1)}, bf16[64,512]{1,0:T(8,128)(2,1)S(1)}, u32[]{:S(2)}, u32[]{:S(2)}) collective-permute-start(bf16[64,512]{1,0:T(8,128)(2,1)S(1)} %get-tuple-element.11.refs_3_), channel_id=1, source_target_pairs={{4,0},{8,4},{12,8},{16,12},{20,16},{24,20},{28,24},{0,28},{5,1},{9... | collective-permute-start | bytes 196616 | tf_op jit(solution)/shard_map/ppermute | solution.py:340
  19.8 1.0 %copy-start.6 = (f32[64,2,512]{2,1,0:T(2,128)S(1)}, f32[64,2,512]{2,1,0:T(2,128)}, u32[]{:S(2)}) copy-start(f32[64,2,512]{2,1,0:T(2,128)} %refs_6_.1) | copy-start | bytes 786436
  20.7 0.7 %copy-start.7 = (s32[8,14]{1,0:T(8,128)S(1)}, s32[8,14]{1,0:T(8,128)}, u32[]{:S(2)}) copy-start(s32[8,14]{1,0:T(8,128)} %refs_1_.4) | copy-start | bytes 1348
  21.4 0.7 %copy-start.8 = (s32[8,14]{1,0:T(8,128)S(1)}, s32[8,14]{1,0:T(8,128)}, u32[]{:S(2)}) copy-start(s32[8,14]{1,0:T(8,128)} %refs_2_.3) | copy-start | bytes 1348
  23.8 19.5 %collective-permute-start.5 = (bf16[128,128]{1,0:T(8,128)(2,1)S(1)}, bf16[128,128]{1,0:T(8,128)(2,1)S(1)}, u32[]{:S(2)}, u32[]{:S(2)}) collective-permute-start(bf16[128,128]{1,0:T(8,128)(2,1)S(1)} %get-tuple-element.14), channel_id=1, source_target_pairs={{1,0},{2,1},{3,2},{0,3},{5,4},{6,5},{7,6},{4,7},{9,8},{10,9},{11,1... | collective-permute-start | bytes 98312 | tf_op jit(solution)/shard_map/ppermute | solution.py:370
  27.0 16.3 %collective-permute-start.6 = (bf16[128,128]{1,0:T(8,128)(2,1)S(1)}, bf16[128,128]{1,0:T(8,128)(2,1)S(1)}, u32[]{:S(2)}, u32[]{:S(2)}) collective-permute-start(bf16[128,128]{1,0:T(8,128)(2,1)S(1)} %get-tuple-element.15), channel_id=1, source_target_pairs={{2,0},{3,1},{0,2},{1,3},{6,4},{7,5},{4,6},{5,7},{10,8},{11,9},{8,1... | collective-permute-start | bytes 98312 | tf_op jit(solution)/shard_map/ppermute | solution.py:370
  27.0 16.3 %collective-permute-start.7 = (bf16[128,128]{1,0:T(8,128)(2,1)S(1)}, bf16[128,128]{1,0:T(8,128)(2,1)S(1)}, u32[]{:S(2)}, u32[]{:S(2)}) collective-permute-start(bf16[128,128]{1,0:T(8,128)(2,1)S(1)} %get-tuple-element.16), channel_id=1, source_target_pairs={{3,0},{0,1},{1,2},{2,3},{7,4},{4,5},{5,6},{6,7},{11,8},{8,9},{9,10... | collective-permute-start | bytes 98312 | tf_op jit(solution)/shard_map/ppermute | solution.py:370
  28.4 6.9 %collective-permute-start.8 = (bf16[8,2,4,128]{3,2,1,0:T(4,128)(2,1)S(1)}, bf16[8,2,4,128]{3,2,1,0:T(4,128)(2,1)S(1)}, u32[]{:S(2)}, u32[]{:S(2)}) collective-permute-start(bf16[8,2,4,128]{3,2,1,0:T(4,128)(2,1)S(1)} %get-tuple-element.18), channel_id=1, source_target_pairs={{0,1},{1,2},{2,3},{3,4},{4,5},{5,6},{6,7},{7,8},{8,9},{9,10},{10,1... | collective-permute-start | bytes 49160 | tf_op jit(solution)/shard_map/ppermute | solution.py:259
  31.3 4.0 %collective-permute-start.9 = (bf16[8,2,4,128]{3,2,1,0:T(4,128)(2,1)S(1)}, bf16[8,2,4,128]{3,2,1,0:T(4,128)(2,1)S(1)}, u32[]{:S(2)}, u32[]{:S(2)}) collective-permute-start(bf16[8,2,4,128]{3,2,1,0:T(4,128)(2,1)S(1)} %get-tuple-element.17), channel_id=1, source_target_pairs={{1,0},{2,1},{3,2},{4,3},{5,4},{6,5},{7,6},{8,7},{9,8},{10,9},{11,1... | collective-permute-start | bytes 49160 | tf_op jit(solution)/shard_map/ppermute | solution.py:260
  35.4 3.4 %copy-start.1 = (bf16[16,8,2,128,128]{4,3,2,1,0:T(8,128)(2,1)S(1)}, bf16[16,8,2,128,128]{4,3,2,1,0:T(8,128)(2,1)}, u32[]{:S(2)}) copy-start(bf16[16,8,2,128,128]{4,3,2,1,0:T(8,128)(2,1)} %refs_5_.2) | copy-start | bytes 25165828
  38.7 0.8 %copy-start.5 = (bf16[16,2,4,128]{3,2,1,0:T(4,128)(2,1)S(1)}, bf16[16,2,4,128]{3,2,1,0:T(4,128)(2,1)}, u32[]{:S(2)}) copy-start(bf16[16,2,4,128]{3,2,1,0:T(4,128)(2,1)} %refs_3_.3) | copy-start | bytes 98308

commit v2 on v1

v2 whole, which is shorter than its diff:
```python
import jax
import jax.numpy as jnp
from jax import lax
from jax.experimental import pallas as pl
from jax.experimental.pallas import tpu as pltpu
from jax.sharding import PartitionSpec as P

F32 = jnp.float32
BF16 = jnp.bfloat16
LANES = 128


def nt_dot(a, b):
    return lax.dot_general(a, b, (((1,), (1,)), ((), ())), preferred_element_type=F32)


def nn_dot(a, b):
    return lax.dot_general(a, b, (((1,), (0,)), ((), ())), preferred_element_type=F32)


def times_i(v):
    half = v.shape[0] // 2
    return jnp.concatenate([-v[half:], v[:half]], axis=0)


def widen(ref, n):
    v = jnp.concatenate([ref[n, 0].astype(F32), ref[n, 1].astype(F32)], axis=0)
    return jnp.concatenate([v, times_i(v)], axis=1)


def leaf_kernel(octant, parent, x_hbm, lift_hbm, out_ref, x_ref, rows, lift, oct_s, par_s, sems, *, parents):
    boxes, halves, rhs, _ = x_ref.shape
    parts = halves * rhs
    chunks = sems.shape[0] - 3
    per = boxes // chunks
    small = [
        pltpu.make_async_copy(x_hbm, x_ref, sems.at[chunks]),
        pltpu.make_async_copy(octant, oct_s, sems.at[chunks + 1]),
        pltpu.make_async_copy(parent, par_s, sems.at[chunks + 2]),
    ]
    big = [
        pltpu.make_async_copy(
            lift_hbm.at[pl.ds(i * per, per)], lift.at[pl.ds(i * per, per)], sems.at[i]
        )
        for i in range(chunks)
    ]
    small[0].start()
    for copy in big:
        copy.start()
    small[1].start()
    small[2].start()
    small[0].wait()
    for n in range(boxes):
        if n % per == 0:
            big[n // per].wait()
        xw = widen(x_ref, n).astype(BF16)
        mat = jnp.concatenate([lift[n, 0], lift[n, 1]], axis=1)
        rows[pl.ds(n, parts, stride=boxes), :] = nt_dot(xw, mat)
    out_ref[: parts * boxes] = rows[...].astype(BF16)
    small[1].wait()
    small[2].wait()
    lane = lax.rem(lax.broadcasted_iota(jnp.int32, (boxes, LANES), 1), boxes)
    across = jnp.zeros((boxes, LANES), F32)
    for n in range(boxes):
        slot = (oct_s[n] * parents + lax.rem(par_s[n], parents)).astype(F32)
        across = jnp.where(lane == n, slot, across)
    out_ref[parts * boxes :] = across.astype(BF16)


def up_kernel(*refs, pieces, boxes, parents, parts):
    msgs = refs[:pieces]
    interp_ref, phase_ref, out_ref, place_ref, raised, folded = refs[pieces:]
    slots = 8 * parents
    samples = interp_ref.shape[0]
    per_tile = LANES // boxes
    at = parts * boxes
    tiles = []
    for t in range(0, pieces, per_tile):
        lane = lax.broadcasted_iota(jnp.int32, (boxes, LANES), 1) // boxes
        code = msgs[t][at : at + boxes].astype(F32)
        for d in range(1, min(per_tile, pieces - t)):
            code = jnp.where(lane == d, msgs[t + d][at : at + boxes].astype(F32), code)
        code = jnp.concatenate([code] * (slots // boxes), axis=0)
        want = lax.broadcasted_iota(jnp.int32, (slots, LANES), 0).astype(F32)
        width = min(per_tile, pieces - t) * boxes
        tiles.append(jnp.where(code == want, 1.0, 0.0)[:, :width])
    sorter = jnp.concatenate(tiles, axis=1)
    place_ref[...] = sorter.T.astype(BF16)
    sorter = sorter.astype(BF16)
    pats = jnp.concatenate(
        [
            jnp.concatenate([m[c * boxes : (c + 1) * boxes] for m in msgs], axis=0)
            for c in range(parts)
        ],
        axis=1,
    )
    ordered = nn_dot(sorter, pats).astype(BF16)
    for c in range(parts):
        raised[c * slots : (c + 1) * slots] = nt_dot(
            ordered[:, c * LANES : (c + 1) * LANES], interp_ref[...]
        )
    half = parts // 2
    for t in range(samples // LANES):
        lanes = slice(t * LANES, (t + 1) * LANES)
        for r in range(half):
            re = im = None
            for o in range(8):
                ph_r = phase_ref[o, 0:1, lanes]
                ph_i = phase_ref[o, 1:2, lanes]
                base_r = r * slots + o * parents
                base_i = (half + r) * slots + o * parents
                xr = raised[base_r : base_r + parents, lanes]
                xi = raised[base_i : base_i + parents, lanes]
                dr = ph_r * xr - ph_i * xi
                di = ph_r * xi + ph_i * xr
                re = dr if re is None else re + dr
                im = di if im is None else im + di
            folded[t, r * parents : (r + 1) * parents] = re
            folded[t, (half + r) * parents : (half + r + 1) * parents] = im
        for p in range(0, parents, 2):
            both = jnp.concatenate(
                [folded[t, pl.ds(p + e, parts, stride=parents), :] for e in range(2)], axis=0
            )
            out_ref[p * parts : (p + 2) * parts, lanes] = both.astype(BF16)


def down_kernel(
    parity, own, across, beside, dense, interp_ref, phase_ref, place_ref, *refs, pieces, boxes, parents, parts
):
    outs = refs[:pieces]
    window, incoming, shifted = refs[pieces:]
    samples = interp_ref.shape[0]
    slots = 8 * parents
    half = parts // 2
    odd = parity[0]
    window[parents : 2 * parents] = own[...].astype(F32).reshape(parents, parts, samples)
    window[pl.ds(2 * parents * odd, parents)] = (
        across[...].astype(F32).reshape(parents, parts, samples)
    )
    window[pl.ds(2 * parents * (1 - odd), parents)] = (
        beside[...].astype(F32).reshape(parents, parts, samples)
    )
    offsets = zone(parents)

    def one(p):
        for t in range(samples // LANES):
            lanes = slice(t * LANES, (t + 1) * LANES)
            acc_r = acc_i = None
            for i, d in enumerate(offsets):
                x = window[parents + p + d, :, lanes]
                yr = dense[p, i, 0:1, lanes] * x
                yi = dense[p, i, 1:2, lanes] * x
                acc_r = yr if acc_r is None else acc_r + yr
                acc_i = yi if acc_i is None else acc_i + yi
            got = (acc_r + times_i(acc_i)).astype(BF16).astype(F32)
            incoming[t, pl.ds(p * parts, parts), :] = got

    if parents <= 8:
        for p in range(parents):
            one(p)
    else:
        lax.fori_loop(0, parents, lambda p, c: (one(p), c)[1], 0)
    for t in range(samples // LANES):
        lanes = slice(t * LANES, (t + 1) * LANES)
        for r in range(half):
            ir = incoming[t, pl.ds(r, parents, stride=parts), :]
            ii = incoming[t, pl.ds(half + r, parents, stride=parts), :]
            re, im = [], []
            for o in range(8):
                ph_r = phase_ref[o, 0:1, lanes]
                ph_i = phase_ref[o, 1:2, lanes]
                re.append(ph_r * ir - ph_i * ii)
                im.append(ph_r * ii + ph_i * ir)
            shifted[r * slots : (r + 1) * slots, lanes] = jnp.concatenate(re, axis=0).astype(BF16)
            shifted[(half + r) * slots : (half + r + 1) * slots, lanes] = jnp.concatenate(
                im, axis=0
            ).astype(BF16)
    field = nn_dot(shifted[...], interp_ref[...]).astype(BF16)
    spread = jnp.concatenate([field[c * slots : (c + 1) * slots] for c in range(parts)], axis=1)
    leaves = nn_dot(place_ref[...], spread).astype(BF16)
    for d in range(pieces):
        for c in range(parts):
            outs[d][c * boxes : (c + 1) * boxes] = leaves[
                d * boxes : (d + 1) * boxes, c * LANES : (c + 1) * LANES
            ]


def zone(parents):
    return [d for d in range(-parents, parents + 1) if abs(d) >= 2]


def near_kernel(
    where, neighbours, own, beside, across, mats_hbm, after, *refs, first, count, total, table_args
):
    step_in = refs[:3] if table_args else ()
    refs = refs[len(step_in) :]
    out_ref = refs[0]
    dense = refs[1] if table_args else None
    refs = refs[1 + bool(table_args) :]
    window, mats, nbr, sems = refs[:4]
    boxes = own.shape[0]
    reach = boxes // 2
    near_count = mats.shape[1]
    first_box, odd = where[0], where[1]
    list_copy = pltpu.make_async_copy(neighbours, nbr, sems.at[count])
    list_copy.start()
    copies = [
        pltpu.make_async_copy(mats_hbm.at[first + i], mats.at[i], sems.at[i]) for i in range(count)
    ]
    if table_args:
        parents, all_parents = table_args
        inter, trans, table_hbm = step_in
        inter_s, trans_s, table, more = refs[4:]
        extra = [
            pltpu.make_async_copy(inter, inter_s, more.at[0]),
            pltpu.make_async_copy(trans, trans_s, more.at[1]),
            pltpu.make_async_copy(table_hbm, table, more.at[2]),
        ]
        for copy in extra:
            copy.start()
    for copy in copies:
        copy.start()
    for i in range(boxes):
        window[reach + i] = widen(own, i)
    for i in range(reach):
        window[(reach + boxes) * (1 - odd) + i] = widen(beside, reach * odd + i)
        window[(reach + boxes) * odd + i] = widen(across, reach * (1 - odd) + i)
    if table_args:
        for copy in extra:
            copy.wait()
        if len(zone(parents)) > inter.shape[1]:
            dense[...] = jnp.zeros_like(dense)

        def fill(p, carry):
            for k in range(inter.shape[1]):
                rel = lax.rem(inter_s[p, k] - where[2] - p + parents + all_parents, all_parents)
                at = jnp.where(rel < parents, rel, rel - 3)
                dense[p, at] = table[trans_s[p, k]]
            return carry

        lax.fori_loop(0, parents, fill, 0)
    list_copy.wait()
    for i in range(count):
        copies[i].wait()
        xs, zs = [], []
        for k in range(near_count):
            j = lax.rem(nbr[k, first + i] - first_box + reach + total, total)
            xs.append(window[j])
            zs += [mats[i, k, 0], mats[i, k, 1]]
        out_ref[i] = nt_dot(
            jnp.concatenate(xs, axis=1).astype(BF16), jnp.concatenate(zs, axis=1)
        )


def final_kernel(*refs, pieces):
    parts_in = refs[:pieces]
    near_refs = refs[pieces : pieces + 2]
    mats, out_ref, field = refs[pieces + 2 :]
    nears = [(ref, i) for ref in near_refs for i in range(ref.shape[0])]
    boxes, halves, rhs = out_ref.shape[:3]
    parts = halves * rhs
    total = parts_in[0][...].astype(F32)
    for m in parts_in[1:]:
        total += m[...].astype(F32)
    field[...] = total.astype(BF16).astype(F32)
    for n in range(boxes):
        v = field[pl.ds(n, parts, stride=boxes), :]
        wide = jnp.concatenate([v, times_i(v)], axis=1).astype(BF16)
        y = nt_dot(wide, jnp.concatenate([mats[n, 0], mats[n, 1]], axis=1))
        ref, i = nears[n]
        y = y + ref[i]
        out_ref[n, 0] = y[:rhs]
        out_ref[n, 1] = y[rhs:]


def whole_in(kind):
    return pl.BlockSpec(memory_space=kind)


VM = pltpu.VMEM
SM = pltpu.SMEM
HBM = pltpu.HBM
DMA = pltpu.SemaphoreType.DMA
PARAMS = pltpu.CompilerParams(vmem_limit_bytes=24 * 1024 * 1024)


def swap(x, axis, pairs):
    return lax.ppermute(x, axis, pairs)


def on_device(
    xvec,
    near_blocks,
    neighbours,
    lift,
    place,
    interp,
    phases,
    octant,
    leaf_parent_index,
    translators,
    inter_list,
    trans_id,
):
    boxes, halves, rhs, unknowns = xvec.shape
    parts = halves * rhs
    nsamp = lax.axis_size("samp")
    nbox = lax.axis_size("box")
    box_index = lax.axis_index("box").astype(jnp.int32)
    samp_index = lax.axis_index("samp").astype(jnp.int32)
    total = boxes * nsamp * nbox
    reach = boxes // 2
    parents = boxes * nsamp // 8
    all_parents = parents * nbox
    samples = interp.shape[0] // nsamp
    slots = 8 * parents
    leaves = boxes * nsamp
    units = nsamp * nbox
    near_count = near_blocks.shape[1]
    where = jnp.stack(
        [(box_index * nsamp + samp_index) * boxes, samp_index % 2, box_index * parents]
    )
    parity = (box_index % 2).reshape(1)

    lift_chunks = 4
    message, x_here = pl.pallas_call(
        lambda *refs: leaf_kernel(*refs, parents=parents),
        in_specs=[whole_in(HBM)] * 4,
        out_specs=[whole_in(VM)] * 2,
        out_shape=[
            jax.ShapeDtypeStruct(((parts + 1) * boxes, LANES), BF16),
            jax.ShapeDtypeStruct(xvec.shape, BF16),
        ],
        scratch_shapes=[
            VM((parts * boxes, LANES), F32),
            VM(lift.shape, BF16),
            SM((boxes,), jnp.int32),
            SM((boxes,), jnp.int32),
            DMA((lift_chunks + 3,)),
        ],
        compiler_params=PARAMS,
        name="leaf",
    )(octant, leaf_parent_index, xvec, lift)

    messages = [message] + [None] * (nsamp - 1)
    for d in reversed(range(1, nsamp)):
        messages[d] = swap(message, "samp", [(i, i ^ d) for i in range(nsamp)])

    both = ("box", "samp")
    x_beside = swap(x_here, both, [(i, i ^ 1) for i in range(units)])
    x_across = swap(
        x_here, both, [(i, (i + (1 if i % 2 else -1)) % units) for i in range(units)]
    )

    my_interp = lax.dynamic_slice_in_dim(interp, samp_index * samples, samples, axis=0)
    my_phases = lax.dynamic_slice_in_dim(phases, samp_index * samples, samples, axis=2)

    parent_pat, place_onehot = pl.pallas_call(
        lambda *refs: up_kernel(
            *refs, pieces=nsamp, boxes=boxes, parents=parents, parts=parts
        ),
        in_specs=[whole_in(VM)] * (nsamp + 2),
        out_specs=[whole_in(VM)] * 2,
        out_shape=[
            jax.ShapeDtypeStruct((parents * parts, samples), BF16),
            jax.ShapeDtypeStruct((leaves, slots), BF16),
        ],
        scratch_shapes=[
            VM((parts * slots, samples), F32),
            VM((samples // LANES, parts * parents, LANES), F32),
        ],
        compiler_params=PARAMS,
        name="up",
    )(*messages, my_interp, my_phases)

    across = swap(
        parent_pat, "box", [(i, (i + (1 if i % 2 else -1)) % nbox) for i in range(nbox)]
    )
    beside = swap(parent_pat, "box", [(i, i ^ 1) for i in range(nbox)])

    def near_part(first, count, after, table):
        zone_size = len(zone(parents))
        out_shape = [jax.ShapeDtypeStruct((count, parts, unknowns), F32)]
        scratch = [
            VM((boxes + 2 * reach, parts, 2 * unknowns), F32),
            VM((count,) + near_blocks.shape[1:], BF16),
            SM((near_count, boxes), jnp.int32),
            DMA((count + 1,)),
        ]
        if table:
            out_shape.append(jax.ShapeDtypeStruct((parents, zone_size, 2, samples), F32))
            scratch += [
                SM(inter_list.shape, jnp.int32),
                SM(trans_id.shape, jnp.int32),
                VM(translators.shape, F32),
                DMA((3,)),
            ]
        return pl.pallas_call(
            lambda *refs: near_kernel(
                *refs,
                first=first,
                count=count,
                total=total,
                table_args=(parents, all_parents) if table else None,
            ),
            in_specs=[whole_in(SM), whole_in(HBM)]
            + [whole_in(VM)] * 3
            + [whole_in(HBM), whole_in(VM)]
            + [whole_in(HBM)] * len(table),
            out_specs=[whole_in(VM)] * len(out_shape),
            out_shape=out_shape,
            scratch_shapes=scratch,
            compiler_params=PARAMS,
            cost_estimate=pl.CostEstimate(
                flops=2 * parts * near_blocks.size * count // boxes,
                bytes_accessed=2 * near_blocks.size * count // boxes,
                transcendentals=0,
            ),
            name="near",
        )(where, neighbours.T, x_here, x_beside, x_across, near_blocks, after, *table)

    split = boxes // 2
    near_a, dense = near_part(0, split, place_onehot, (inter_list, trans_id, translators))

    fields = pl.pallas_call(
        lambda *refs: down_kernel(
            *refs, pieces=nsamp, boxes=boxes, parents=parents, parts=parts
        ),
        in_specs=[whole_in(SM)] + [whole_in(VM)] * 7,
        out_specs=[whole_in(VM)] * nsamp,
        out_shape=[jax.ShapeDtypeStruct((parts * boxes, LANES), BF16)] * nsamp,
        scratch_shapes=[
            VM((3 * parents, parts, samples), F32),
            VM((samples // LANES, parents * parts, LANES), F32),
            VM((parts * slots, samples), BF16),
        ],
        compiler_params=PARAMS,
        name="down",
    )(parity, parent_pat, across, beside, dense, my_interp, my_phases, place_onehot)

    partial = [fields[0]] + [None] * (nsamp - 1)
    for d in reversed(range(1, nsamp)):
        partial[d] = swap(fields[d], "samp", [(i, i ^ d) for i in range(nsamp)])

    (near_b,) = near_part(split, boxes - split, fields[0], ())

    return pl.pallas_call(
        lambda *refs: final_kernel(*refs, pieces=nsamp),
        in_specs=[whole_in(VM)] * (nsamp + 3),
        out_specs=whole_in(VM),
        out_shape=jax.ShapeDtypeStruct(xvec.shape, F32),
        scratch_shapes=[VM((parts * boxes, LANES), F32)],
        compiler_params=PARAMS,
        name="final",
    )(*partial, near_a, near_b, place)


def solution(mesh):
    in_specs = (
        P(("box", "samp"), None, None, None),
        P(("box", "samp"), None, None, None, None),
        P(("box", "samp"), None),
        P(("box", "samp"), None, None, None),
        P(("box", "samp"), None, None, None),
        P(),
        P(),
        P(("box", "samp")),
        P(("box", "samp")),
        P(None, None, "samp"),
        P("box", None),
        P("box", None),
    )
    out_specs = P(("box", "samp"), None, None, None)
    return jax.shard_map(
        on_device, mesh=mesh, in_specs=in_specs, out_specs=out_specs, check_vma=False
    )
```

time: 44.9 us -> 42.8 us (0.953)
  Pallas kernels: 8.56 us -> 12.9 us
  starting transfers between devices: 18.9 us -> 16.5 us
  waiting for transfers between devices: 4.61 us -> 2.29 us
  local copies, waits for them, and re-layouts: 12.2 us -> 10.5 us
    pallas_call x2 -> x3, Pallas kernels: 5.13 us -> 10.4 us  [the longest x2 9.44 us: near_part(): pl.pallas_call(lambda *refs: near_kernel(*refs, first=first, count=count,...]
    ppermute x10, starting transfers between devices: 18.9 us -> 16.5 us  [swap(): return lax.ppermute(x, axis, pairs)]
    ppermute x10, waiting for transfers between devices: 4.61 us -> 2.29 us  [swap(): return lax.ppermute(x, axis, pairs)]
    pallas_call x1, Pallas kernels: 1.74 us -> 0.82 us  [on_device(): pl.pallas_call(lambda *refs: down_kernel(*refs, pieces=nsamp, boxes=boxes...]
    unnamed x23 -> x26, local copies, waits for them, and re-layouts: 10.6 us -> 9.75 us
    slice x1 -> x0, local copies, waits for them, and re-layouts: 0.75 us -> none  [on_device(): x_right = lax.ppermute(xvec[:reach], ('box', 'samp'), down_ring)]
  transfers between devices with their start and end apart: 10 -> 10, of which waited for: 4 -> 3; matrix products, arithmetic and copies ran while one was open for 5% -> 2% of each run, Pallas kernels for 9% -> 24%
where the time goes in v2:
time: 42.8 us; the launch traced here: 42.4 us
  starting transfers between devices  16.5 us (39%)
  Pallas kernels  12.9 us (30%)
  local copies, waits for them, and re-layouts  10.5 us (25%)
  waiting for transfers between devices  2.29 us (5%)
    ppermute x10, starting transfers between devices, swap(): return lax.ppermute(x, axis, pairs)  16.5 us
    unnamed x26, local copies, waits for them, and re-layouts  9.75 us
    pallas_call x2, Pallas kernels, near_part(): pl.pallas_call(lambda *refs: near_kernel(*refs, first=first, count=count,...  9.44 us
    ppermute x10, waiting for transfers between devices, swap(): return lax.ppermute(x, axis, pairs)  2.29 us
    pallas_call x1, Pallas kernels, on_device(): pl.pallas_call(lambda *refs: final_kernel(*refs, pieces=nsamp), in_specs=...  1.03 us
    pallas_call x1, Pallas kernels, on_device(): pl.pallas_call(lambda *refs: leaf_kernel(*refs, parents=parents), in_spec...  0.97 us
  transfers between devices with their start and end apart: 10, of which 3 were waited for; matrix products, arithmetic and copies ran while one was open for 2% of the time, Pallas kernels for 24%

profile of v2, /device:TPU:0, one launch (start us, length us, event | category | flops | bytes accessed | tf_op | source)
XLA Modules:
  0.0 42.4 jit_solution(16521621059311732602)
XLA Ops:
  0.0 1.3 %copy-done.4 = bf16[16,2,128,128]{3,2,1,0:T(8,128)(2,1)S(1)} copy-done((bf16[16,2,128,128]{3,2,1,0:T(8,128)(2,1)S(1)}, bf16[16,2,128,128]{3,2,1,0:T(8,128)(2,1)}, u32[]{:S(2)}) %copy-start.4) | copy-done | bytes 1048600
  1.3 0.8 %copy-done.6 = bf16[16,2,4,128]{3,2,1,0:T(4,128)(2,1)S(1)} copy-done((bf16[16,2,4,128]{3,2,1,0:T(4,128)(2,1)S(1)}, bf16[16,2,4,128]{3,2,1,0:T(4,128)(2,1)}, u32[]{:S(2)}) %copy-start.6) | copy-done | bytes 32792
  2.0 0.7 %copy-done.11 = s32[16]{0:T(128)S(1)} copy-done((s32[16]{0:T(128)S(1)}, s32[16]{0:T(128)}, u32[]{:S(2)}) %copy-start.11) | copy-done | bytes 88
  2.7 0.7 %copy-done.12 = s32[16]{0:T(128)S(1)} copy-done((s32[16]{0:T(128)S(1)}, s32[16]{0:T(128)}, u32[]{:S(2)}) %copy-start.12) | copy-done | bytes 88
  3.4 1.0 %leaf.1 = (bf16[144,128]{1,0:T(8,128)(2,1)S(1)}, bf16[16,2,4,128]{3,2,1,0:T(4,128)(2,1)S(1)}) custom-call(s32[16]{0:T(128)S(1)} %copy-done.11, s32[16]{0:T(128)S(1)} %copy-done.12, bf16[16,2,4,128]{3,2,1,0:T(4,128)(2,1)S(1)} %copy-done.6, bf16[16,2,128,128]{3,2,1,0:T(8,128)(2,1)S(1)} %copy-done.4), custom_call_target="tpu_custom_call" | custom-call | tf_op jit(solution)/shard_map/leaf/pallas_call | solution.py:326
  4.3 6.4 %collective-permute-start.6 = (bf16[16,2,4,128]{3,2,1,0:T(4,128)(2,1)S(1)}, bf16[16,2,4,128]{3,2,1,0:T(4,128)(2,1)S(1)}, u32[]{:S(2)}, u32[]{:S(2)}) collective-permute-start(bf16[16,2,4,128]{3,2,1,0:T(4,128)(2,1)S(1)} %get-tuple-element.17.refs_2_), channel_id=1, source_target_pairs={{0,31},{1,2},{2,1},{3,4},{4,3},{5,6},{6,5},{7,8},{8,7},{9,10},{10,... | collective-permute-start | bytes 98312 | tf_op jit(solution)/shard_map/ppermute | solution.py:288
  10.8 3.5 %collective-permute-start.1 = (bf16[144,128]{1,0:T(8,128)(2,1)S(1)}, bf16[144,128]{1,0:T(8,128)(2,1)S(1)}, u32[]{:S(2)}, u32[]{:S(2)}) collective-permute-start(bf16[144,128]{1,0:T(8,128)(2,1)S(1)} %get-tuple-element.15.refs_0_), channel_id=1, source_target_pairs={{0,2},{1,3},{2,0},{3,1},{4,6},{5,7},{6,4},{7,5},{8,10},{9,11},{10,... | collective-permute-start | bytes 110600 | tf_op jit(solution)/shard_map/ppermute | solution.py:288
  14.3 0.9 %collective-permute-start = (bf16[144,128]{1,0:T(8,128)(2,1)S(1)}, bf16[144,128]{1,0:T(8,128)(2,1)S(1)}, u32[]{:S(2)}, u32[]{:S(2)}) collective-permute-start(bf16[144,128]{1,0:T(8,128)(2,1)S(1)} %get-tuple-element.15.refs_0_), channel_id=1, source_target_pairs={{0,1},{1,0},{2,3},{3,2},{4,5},{5,4},{6,7},{7,6},{8,9},{9,8},{10,11... | collective-permute-start | bytes 110600 | tf_op jit(solution)/shard_map/ppermute | solution.py:288
  15.2 0.8 %constant_dynamic-slice_fusion.refs_5_.refs_6_ = f32[8,2,512]{2,1,0:T(2,128)S(1)} fusion(f32[8,2,2048]{2,1,0:T(2,128)} %param.18, s32[]{:T(128)S(6)} %select_n.16), kind=kLoop, calls=%fused_computation.1 | loop fusion | bytes 65540 | tf_op jit(solution)/shard_map/dynamic_slice | solution.py:356
  16.0 0.7 %collective-permute-done.2.refs_3_ = bf16[144,128]{1,0:T(8,128)(2,1)S(1)} collective-permute-done((bf16[144,128]{1,0:T(8,128)(2,1)S(1)}, bf16[144,128]{1,0:T(8,128)(2,1)S(1)}, u32[]{:S(2)}, u32[]{:S(2)}) %collective-permute-start.2) | collective-permute-done | bytes 36896 | tf_op jit(solution)/shard_map/ppermute | solution.py:288
  16.6 0.7 %collective-permute-done.1.refs_2_ = bf16[144,128]{1,0:T(8,128)(2,1)S(1)} collective-permute-done((bf16[144,128]{1,0:T(8,128)(2,1)S(1)}, bf16[144,128]{1,0:T(8,128)(2,1)S(1)}, u32[]{:S(2)}, u32[]{:S(2)}) %collective-permute-start.1) | collective-permute-done | bytes 36896 | tf_op jit(solution)/shard_map/ppermute | solution.py:288
  17.4 0.8 %collective-permute-done.refs_1_ = bf16[144,128]{1,0:T(8,128)(2,1)S(1)} collective-permute-done((bf16[144,128]{1,0:T(8,128)(2,1)S(1)}, bf16[144,128]{1,0:T(8,128)(2,1)S(1)}, u32[]{:S(2)}, u32[]{:S(2)}) %collective-permute-start) | collective-permute-done | bytes 36896 | tf_op jit(solution)/shard_map/ppermute | solution.py:288
  18.2 0.7 %up.1 = (bf16[64,512]{1,0:T(8,128)(2,1)S(1)}, bf16[64,64]{1,0:T(8,128)(2,1)S(1)}) custom-call(bf16[144,128]{1,0:T(8,128)(2,1)S(1)} %get-tuple-element.15.refs_0_, bf16[144,128]{1,0:T(8,128)(2,1)S(1)} %collective-permute-done.refs_1_, bf16[144,128]{1,0:T(8,128)(2,1)S(1)} %collective-permute-done.1.refs_2_, ...), custom_call_target="tpu_custom_call" | custom-call | tf_op jit(solution)/shard_map/up/pallas_call | solution.py:358
  18.9 0.1 collective-permute-start.4
  19.0 1.1 %collective-permute-start.3 = (bf16[64,512]{1,0:T(8,128)(2,1)S(1)}, bf16[64,512]{1,0:T(8,128)(2,1)S(1)}, u32[]{:S(2)}, u32[]{:S(2)}) collective-permute-start(bf16[64,512]{1,0:T(8,128)(2,1)S(1)} %get-tuple-element.16.refs_1_), channel_id=1, source_target_pairs={{0,28},{4,8},{8,4},{12,16},{16,12},{20,24},{24,20},{28,0},{1,29},{... | collective-permute-start | bytes 196616 | tf_op jit(solution)/shard_map/ppermute | solution.py:288
  20.1 0.1 pad_add_fusion.refs_0_
  20.1 0.0 collective-permute-done.5.refs_3_
  20.2 3.4 %copy-done.1 = bf16[16,8,2,128,128]{4,3,2,1,0:T(8,128)(2,1)S(1)} copy-done((bf16[16,8,2,128,128]{4,3,2,1,0:T(8,128)(2,1)S(1)}, bf16[16,8,2,128,128]{4,3,2,1,0:T(8,128)(2,1)}, u32[]{:S(2)}) %copy-start.1) | copy-done | bytes 8388632
  23.5 0.9 %copy-done.5 = f32[64,2,512]{2,1,0:T(2,128)S(1)} copy-done((f32[64,2,512]{2,1,0:T(2,128)S(1)}, f32[64,2,512]{2,1,0:T(2,128)}, u32[]{:S(2)}) %copy-start.5) | copy-done | bytes 262168
  24.5 0.7 %copy-done.7 = s32[16,8]{0,1:T(8,128)S(1)} copy-done((s32[16,8]{0,1:T(8,128)S(1)}, s32[16,8]{0,1:T(8,128)}, u32[]{:S(2)}) %copy-start.7) | copy-done | bytes 536
  25.2 0.7 %copy-done.9 = s32[8,14]{1,0:T(8,128)S(1)} copy-done((s32[8,14]{1,0:T(8,128)S(1)}, s32[8,14]{1,0:T(8,128)}, u32[]{:S(2)}) %copy-start.9) | copy-done | bytes 472
  25.9 0.7 %copy-done.10 = s32[8,14]{1,0:T(8,128)S(1)} copy-done((s32[8,14]{1,0:T(8,128)S(1)}, s32[8,14]{1,0:T(8,128)}, u32[]{:S(2)}) %copy-start.10) | copy-done | bytes 472
  26.6 5.1 %near.2 = (f32[8,8,128]{2,1,0:T(8,128)S(1)}, f32[8,14,2,512]{3,2,1,0:T(2,128)S(1)}) custom-call(s32[3]{0:T(128)S(1)} %pad_add_fusion.refs_0_, s32[8,16]{1,0:T(8,128)S(1)} %bitcast.5, bf16[16,2,4,128]{3,2,1,0:T(4,128)(2,1)S(1)} %get-tuple-element.17.refs_2_, bf16[16,2,4,128]{3,2,1,0:T(4,128)(2,1)S(1)} %collective-permute-done.5.refs_3_, ...), custom_call_target="tpu_custom_call" | custom-call | flops 33554432 | bytes 4194304 | tf_op jit(solution)/shard_map/near/pallas_call | solution.py:398
  31.7 0.0 collective-permute-done.3.refs_2_
  31.7 0.8 %down.1 = (bf16[128,128]{1,0:T(8,128)(2,1)S(1)}, bf16[128,128]{1,0:T(8,128)(2,1)S(1)}, bf16[128,128]{1,0:T(8,128)(2,1)S(1)}, bf16[128,128]{1,0:T(8,128)(2,1)S(1)}) custom-call(s32[1]{0:T(128)} %bitcast.refs_0_, bf16[64,512]{1,0:T(8,128)(2,1)S(1)} %get-tuple-element.16.refs_1_, bf16[64,512]{1,0:T(8,128)(2,1)S(1)} %collective-permute-done.3.refs_2_, ...), custom_call_target="tpu_custom_call" | custom-call | tf_op jit(solution)/shard_map/down/pallas_call | solution.py:425
  32.5 0.6 %collective-permute-start.7 = (bf16[128,128]{1,0:T(8,128)(2,1)S(1)}, bf16[128,128]{1,0:T(8,128)(2,1)S(1)}, u32[]{:S(2)}, u32[]{:S(2)}) collective-permute-start(bf16[128,128]{1,0:T(8,128)(2,1)S(1)} %get-tuple-element.21), channel_id=1, source_target_pairs={{0,1},{1,0},{2,3},{3,2},{4,5},{5,4},{6,7},{7,6},{8,9},{9,8},{10,11... | collective-permute-start | bytes 98312 | tf_op jit(solution)/shard_map/ppermute | solution.py:288
  33.2 1.3 %collective-permute-start.8 = (bf16[128,128]{1,0:T(8,128)(2,1)S(1)}, bf16[128,128]{1,0:T(8,128)(2,1)S(1)}, u32[]{:S(2)}, u32[]{:S(2)}) collective-permute-start(bf16[128,128]{1,0:T(8,128)(2,1)S(1)} %get-tuple-element.22), channel_id=1, source_target_pairs={{0,2},{1,3},{2,0},{3,1},{4,6},{5,7},{6,4},{7,5},{8,10},{9,11},{10,... | collective-permute-start | bytes 98312 | tf_op jit(solution)/shard_map/ppermute | solution.py:288
  34.5 2.5 %collective-permute-start.9 = (bf16[128,128]{1,0:T(8,128)(2,1)S(1)}, bf16[128,128]{1,0:T(8,128)(2,1)S(1)}, u32[]{:S(2)}, u32[]{:S(2)}) collective-permute-start(bf16[128,128]{1,0:T(8,128)(2,1)S(1)} %get-tuple-element.23), channel_id=1, source_target_pairs={{0,3},{1,2},{2,1},{3,0},{4,7},{5,6},{6,5},{7,4},{8,11},{9,10},{10,... | collective-permute-start | bytes 98312 | tf_op jit(solution)/shard_map/ppermute | solution.py:288
  37.0 4.3 %near.3.refs_5_ = f32[8,8,128]{2,1,0:T(8,128)S(1)} custom-call(s32[3]{0:T(128)S(1)} %pad_add_fusion.refs_0_, s32[8,16]{1,0:T(8,128)S(1)} %bitcast.6, bf16[16,2,4,128]{3,2,1,0:T(4,128)(2,1)S(1)} %get-tuple-element.17.refs_2_, bf16[16,2,4,128]{3,2,1,0:T(4,128)(2,1)S(1)} %collective-permute-done.5.refs_3_, ...), custom_call_target="tpu_custom_call" | custom-call | flops 33554432 | bytes 4194304 | tf_op jit(solution)/shard_map/near/pallas_call | solution.py:398
  41.3 0.0 collective-permute-done.7.refs_1_
  41.3 0.0 collective-permute-done.8.refs_2_
  41.4 1.0 %final.1 = f32[16,2,4,128]{3,2,1,0:T(4,128)} custom-call(bf16[128,128]{1,0:T(8,128)(2,1)S(1)} %get-tuple-element.20.refs_6_.refs_0_, bf16[128,128]{1,0:T(8,128)(2,1)S(1)} %collective-permute-done.7.refs_1_, bf16[128,128]{1,0:T(8,128)(2,1)S(1)} %collective-permute-done.8.refs_2_, bf16[128,128]{1,0:T(8,128)(2,1)S(1)} %collective-permute-done.9.refs_3_, ...), custom_call_target="tpu_custom_call" | custom-call | tf_op jit(solution)/shard_map/final/pallas_call | solution.py:447
  (23 shorter events, 0.1 us)
Async XLA Ops:
  0.0 15.2 %copy-start = (bf16[2048,128]{1,0:T(8,128)(2,1)S(1)}, bf16[2048,128]{1,0:T(8,128)(2,1)}, u32[]{:S(2)}) copy-start(bf16[2048,128]{1,0:T(8,128)(2,1)} %param.17) | copy-start | bytes 1572868
  0.0 1.3 %copy-start.4 = (bf16[16,2,128,128]{3,2,1,0:T(8,128)(2,1)S(1)}, bf16[16,2,128,128]{3,2,1,0:T(8,128)(2,1)}, u32[]{:S(2)}) copy-start(bf16[16,2,128,128]{3,2,1,0:T(8,128)(2,1)} %refs_3_.1) | copy-start | bytes 3145732
  1.3 0.8 %copy-start.6 = (bf16[16,2,4,128]{3,2,1,0:T(4,128)(2,1)S(1)}, bf16[16,2,4,128]{3,2,1,0:T(4,128)(2,1)}, u32[]{:S(2)}) copy-start(bf16[16,2,4,128]{3,2,1,0:T(4,128)(2,1)} %refs_2_.1) | copy-start | bytes 98308
  2.0 0.7 %copy-start.11 = (s32[16]{0:T(128)S(1)}, s32[16]{0:T(128)}, u32[]{:S(2)}) copy-start(s32[16]{0:T(128)} %refs_0_.1) | copy-start | bytes 196
  2.7 0.7 %copy-start.12 = (s32[16]{0:T(128)S(1)}, s32[16]{0:T(128)}, u32[]{:S(2)}) copy-start(s32[16]{0:T(128)} %refs_1_.1) | copy-start | bytes 196
  3.4 33.6 %copy-start.8 = (s32[16,8]{0,1:T(8,128)S(1)}, s32[16,8]{0,1:T(8,128)}, u32[]{:S(2)}) copy-start(s32[16,8]{0,1:T(8,128)} %param.14) | copy-start | bytes 1540
  4.3 15.8 %collective-permute-start.6 = (bf16[16,2,4,128]{3,2,1,0:T(4,128)(2,1)S(1)}, bf16[16,2,4,128]{3,2,1,0:T(4,128)(2,1)S(1)}, u32[]{:S(2)}, u32[]{:S(2)}) collective-permute-start(bf16[16,2,4,128]{3,2,1,0:T(4,128)(2,1)S(1)} %get-tuple-element.17.refs_2_), channel_id=1, source_target_pairs={{0,31},{1,2},{2,1},{3,4},{4,3},{5,6},{6,5},{7,8},{8,7},{9,10},{10,... | collective-permute-start | bytes 98312 | tf_op jit(solution)/shard_map/ppermute | solution.py:288
  10.8 9.4 %collective-permute-start.5 = (bf16[16,2,4,128]{3,2,1,0:T(4,128)(2,1)S(1)}, bf16[16,2,4,128]{3,2,1,0:T(4,128)(2,1)S(1)}, u32[]{:S(2)}, u32[]{:S(2)}) collective-permute-start(bf16[16,2,4,128]{3,2,1,0:T(4,128)(2,1)S(1)} %get-tuple-element.17.refs_2_), channel_id=1, source_target_pairs={{0,1},{1,0},{2,3},{3,2},{4,5},{5,4},{6,7},{7,6},{8,9},{9,8},{10,11... | collective-permute-start | bytes 98312 | tf_op jit(solution)/shard_map/ppermute | solution.py:288
  10.8 5.9 %collective-permute-start.2 = (bf16[144,128]{1,0:T(8,128)(2,1)S(1)}, bf16[144,128]{1,0:T(8,128)(2,1)S(1)}, u32[]{:S(2)}, u32[]{:S(2)}) collective-permute-start(bf16[144,128]{1,0:T(8,128)(2,1)S(1)} %get-tuple-element.15.refs_0_), channel_id=1, source_target_pairs={{0,3},{1,2},{2,1},{3,0},{4,7},{5,6},{6,5},{7,4},{8,11},{9,10},{10,... | collective-permute-start | bytes 110600 | tf_op jit(solution)/shard_map/ppermute | solution.py:288
  10.8 6.6 %collective-permute-start.1 = (bf16[144,128]{1,0:T(8,128)(2,1)S(1)}, bf16[144,128]{1,0:T(8,128)(2,1)S(1)}, u32[]{:S(2)}, u32[]{:S(2)}) collective-permute-start(bf16[144,128]{1,0:T(8,128)(2,1)S(1)} %get-tuple-element.15.refs_0_), channel_id=1, source_target_pairs={{0,2},{1,3},{2,0},{3,1},{4,6},{5,7},{6,4},{7,5},{8,10},{9,11},{10,... | collective-permute-start | bytes 110600 | tf_op jit(solution)/shard_map/ppermute | solution.py:288
  14.3 4.0 %collective-permute-start = (bf16[144,128]{1,0:T(8,128)(2,1)S(1)}, bf16[144,128]{1,0:T(8,128)(2,1)S(1)}, u32[]{:S(2)}, u32[]{:S(2)}) collective-permute-start(bf16[144,128]{1,0:T(8,128)(2,1)S(1)} %get-tuple-element.15.refs_0_), channel_id=1, source_target_pairs={{0,1},{1,0},{2,3},{3,2},{4,5},{5,4},{6,7},{7,6},{8,9},{9,8},{10,11... | collective-permute-start | bytes 110600 | tf_op jit(solution)/shard_map/ppermute | solution.py:288
  18.9 12.8 %collective-permute-start.4 = (bf16[64,512]{1,0:T(8,128)(2,1)S(1)}, bf16[64,512]{1,0:T(8,128)(2,1)S(1)}, u32[]{:S(2)}, u32[]{:S(2)}) collective-permute-start(bf16[64,512]{1,0:T(8,128)(2,1)S(1)} %get-tuple-element.16.refs_1_), channel_id=1, source_target_pairs={{0,4},{4,0},{8,12},{12,8},{16,20},{20,16},{24,28},{28,24},{1,5},{5... | collective-permute-start | bytes 196616 | tf_op jit(solution)/shard_map/ppermute | solution.py:288
  19.0 12.7 %collective-permute-start.3 = (bf16[64,512]{1,0:T(8,128)(2,1)S(1)}, bf16[64,512]{1,0:T(8,128)(2,1)S(1)}, u32[]{:S(2)}, u32[]{:S(2)}) collective-permute-start(bf16[64,512]{1,0:T(8,128)(2,1)S(1)} %get-tuple-element.16.refs_1_), channel_id=1, source_target_pairs={{0,28},{4,8},{8,4},{12,16},{16,12},{20,24},{24,20},{28,0},{1,29},{... | collective-permute-start | bytes 196616 | tf_op jit(solution)/shard_map/ppermute | solution.py:288
  20.1 3.4 %copy-start.1 = (bf16[16,8,2,128,128]{4,3,2,1,0:T(8,128)(2,1)S(1)}, bf16[16,8,2,128,128]{4,3,2,1,0:T(8,128)(2,1)}, u32[]{:S(2)}) copy-start(bf16[16,8,2,128,128]{4,3,2,1,0:T(8,128)(2,1)} %refs_5_.3) | copy-start | bytes 25165828
  23.5 0.9 %copy-start.5 = (f32[64,2,512]{2,1,0:T(2,128)S(1)}, f32[64,2,512]{2,1,0:T(2,128)}, u32[]{:S(2)}) copy-start(f32[64,2,512]{2,1,0:T(2,128)} %refs_9_.1) | copy-start | bytes 786436
  24.5 0.7 %copy-start.7 = (s32[16,8]{0,1:T(8,128)S(1)}, s32[16,8]{0,1:T(8,128)}, u32[]{:S(2)}) copy-start(s32[16,8]{0,1:T(8,128)} %param.14) | copy-start | bytes 1540
  25.2 0.7 %copy-start.9 = (s32[8,14]{1,0:T(8,128)S(1)}, s32[8,14]{1,0:T(8,128)}, u32[]{:S(2)}) copy-start(s32[8,14]{1,0:T(8,128)} %refs_7_.1) | copy-start | bytes 1348
  25.9 0.7 %copy-start.10 = (s32[8,14]{1,0:T(8,128)S(1)}, s32[8,14]{1,0:T(8,128)}, u32[]{:S(2)}) copy-start(s32[8,14]{1,0:T(8,128)} %refs_8_.1) | copy-start | bytes 1348
  26.5 10.4 %copy-start.2 = (bf16[16,8,2,128,128]{4,3,2,1,0:T(8,128)(2,1)S(1)}, bf16[16,8,2,128,128]{4,3,2,1,0:T(8,128)(2,1)}, u32[]{:S(2)}) copy-start(bf16[16,8,2,128,128]{4,3,2,1,0:T(8,128)(2,1)} %refs_5_.3) | copy-start | bytes 25165828
  26.6 14.8 %copy-start.3 = (bf16[16,2,128,128]{3,2,1,0:T(8,128)(2,1)S(1)}, bf16[16,2,128,128]{3,2,1,0:T(8,128)(2,1)}, u32[]{:S(2)}) copy-start(bf16[16,2,128,128]{3,2,1,0:T(8,128)(2,1)} %refs_6_.1) | copy-start | bytes 3145732
  32.5 8.8 %collective-permute-start.7 = (bf16[128,128]{1,0:T(8,128)(2,1)S(1)}, bf16[128,128]{1,0:T(8,128)(2,1)S(1)}, u32[]{:S(2)}, u32[]{:S(2)}) collective-permute-start(bf16[128,128]{1,0:T(8,128)(2,1)S(1)} %get-tuple-element.21), channel_id=1, source_target_pairs={{0,1},{1,0},{2,3},{3,2},{4,5},{5,4},{6,7},{7,6},{8,9},{9,8},{10,11... | collective-permute-start | bytes 98312 | tf_op jit(solution)/shard_map/ppermute | solution.py:288
  33.2 8.2 %collective-permute-start.8 = (bf16[128,128]{1,0:T(8,128)(2,1)S(1)}, bf16[128,128]{1,0:T(8,128)(2,1)S(1)}, u32[]{:S(2)}, u32[]{:S(2)}) collective-permute-start(bf16[128,128]{1,0:T(8,128)(2,1)S(1)} %get-tuple-element.22), channel_id=1, source_target_pairs={{0,2},{1,3},{2,0},{3,1},{4,6},{5,7},{6,4},{7,5},{8,10},{9,11},{10,... | collective-permute-start | bytes 98312 | tf_op jit(solution)/shard_map/ppermute | solution.py:288
  34.5 6.9 %collective-permute-start.9 = (bf16[128,128]{1,0:T(8,128)(2,1)S(1)}, bf16[128,128]{1,0:T(8,128)(2,1)S(1)}, u32[]{:S(2)}, u32[]{:S(2)}) collective-permute-start(bf16[128,128]{1,0:T(8,128)(2,1)S(1)} %get-tuple-element.23), channel_id=1, source_target_pairs={{0,3},{1,2},{2,1},{3,0},{4,7},{5,6},{6,5},{7,4},{8,11},{9,10},{10,... | collective-permute-start | bytes 98312 | tf_op jit(solution)/shard_map/ppermute | solution.py:288

commit v3 on v2

--- a/solution.py
+++ b/solution.py
@@ -28,15 +28,23 @@
     return jnp.concatenate([v, times_i(v)], axis=1)
 
 
-def leaf_kernel(octant, parent, x_hbm, lift_hbm, out_ref, x_ref, rows, lift, oct_s, par_s, sems, *, parents):
+def leaf_kernel(
+    octant, parent, x_hbm, lift_hbm, interp_hbm, phase_hbm,
+    out_ref, x_ref, interp_ref, phase_ref,
+    rows, lift, oct_s, par_s, sems, *, parents, copies_out,
+):
     boxes, halves, rhs, _ = x_ref.shape
     parts = halves * rhs
-    chunks = sems.shape[0] - 3
+    chunks = sems.shape[0] - 5
+    samples = interp_ref.shape[0]
+    mine = pl.ds(pl.multiple_of(lax.axis_index("samp") * samples, samples), samples)
     per = boxes // chunks
     small = [
         pltpu.make_async_copy(x_hbm, x_ref, sems.at[chunks]),
         pltpu.make_async_copy(octant, oct_s, sems.at[chunks + 1]),
         pltpu.make_async_copy(parent, par_s, sems.at[chunks + 2]),
+        pltpu.make_async_copy(interp_hbm.at[mine], interp_ref, sems.at[chunks + 3]),
+        pltpu.make_async_copy(phase_hbm.at[:, :, mine], phase_ref, sems.at[chunks + 4]),
     ]
     big = [
         pltpu.make_async_copy(
@@ -47,8 +55,8 @@
     small[0].start()
     for copy in big:
         copy.start()
-    small[1].start()
-    small[2].start()
+    for copy in small[1:]:
+        copy.start()
     small[0].wait()
     for n in range(boxes):
         if n % per == 0:
@@ -56,20 +64,25 @@
         xw = widen(x_ref, n).astype(BF16)
         mat = jnp.concatenate([lift[n, 0], lift[n, 1]], axis=1)
         rows[pl.ds(n, parts, stride=boxes), :] = nt_dot(xw, mat)
-    out_ref[: parts * boxes] = rows[...].astype(BF16)
-    small[1].wait()
-    small[2].wait()
+    pattern = rows[...].astype(BF16)
+    for copy in small[1:]:
+        copy.wait()
     lane = lax.rem(lax.broadcasted_iota(jnp.int32, (boxes, LANES), 1), boxes)
     across = jnp.zeros((boxes, LANES), F32)
     for n in range(boxes):
         slot = (oct_s[n] * parents + lax.rem(par_s[n], parents)).astype(F32)
         across = jnp.where(lane == n, slot, across)
-    out_ref[parts * boxes :] = across.astype(BF16)
+    codes = across.astype(BF16)
+    for i in range(copies_out):
+        at = i * (parts + 1) * boxes
+        out_ref[at : at + parts * boxes] = pattern
+        out_ref[at + parts * boxes : at + (parts + 1) * boxes] = codes
 
 
 def up_kernel(*refs, pieces, boxes, parents, parts):
-    msgs = refs[:pieces]
-    interp_ref, phase_ref, out_ref, place_ref, raised, folded = refs[pieces:]
+    every, interp_ref, phase_ref, out_ref, place_ref, raised, folded = refs
+    rows_each = (parts + 1) * boxes
+    msgs = [every.at[d * rows_each : (d + 1) * rows_each] for d in range(pieces)]
     slots = 8 * parents
     samples = interp_ref.shape[0]
     per_tile = LANES // boxes
@@ -125,14 +138,13 @@
 
 
 def down_kernel(
-    parity, own, across, beside, dense, interp_ref, phase_ref, place_ref, *refs, pieces, boxes, parents, parts
+    own, across, beside, dense, interp_ref, phase_ref, place_ref, out_ref,
+    window, incoming, shifted, *, pieces, boxes, parents, parts
 ):
-    outs = refs[:pieces]
-    window, incoming, shifted = refs[pieces:]
     samples = interp_ref.shape[0]
     slots = 8 * parents
     half = parts // 2
-    odd = parity[0]
+    odd = lax.rem(lax.axis_index("box"), 2)
     window[parents : 2 * parents] = own[...].astype(F32).reshape(parents, parts, samples)
     window[pl.ds(2 * parents * odd, parents)] = (
         across[...].astype(F32).reshape(parents, parts, samples)
@@ -180,7 +192,8 @@
     leaves = nn_dot(place_ref[...], spread).astype(BF16)
     for d in range(pieces):
         for c in range(parts):
-            outs[d][c * boxes : (c + 1) * boxes] = leaves[
+            at = (d * parts + c) * boxes
+            out_ref[at : at + boxes] = leaves[
                 d * boxes : (d + 1) * boxes, c * LANES : (c + 1) * LANES
             ]
 
@@ -190,7 +203,7 @@
 
 
 def near_kernel(
-    where, neighbours, own, beside, across, mats_hbm, after, *refs, first, count, total, table_args
+    neighbours, own, beside, across, mats_hbm, after, *refs, first, count, total, table_args
 ):
     step_in = refs[:3] if table_args else ()
     refs = refs[len(step_in) :]
@@ -201,7 +214,10 @@
     boxes = own.shape[0]
     reach = boxes // 2
     near_count = mats.shape[1]
-    first_box, odd = where[0], where[1]
+    samp = lax.axis_index("samp")
+    box = lax.axis_index("box")
+    first_box = (box * lax.axis_size("samp") + samp) * boxes
+    odd = lax.rem(samp, 2)
     list_copy = pltpu.make_async_copy(neighbours, nbr, sems.at[count])
     list_copy.start()
     copies = [
@@ -233,7 +249,7 @@
 
         def fill(p, carry):
             for k in range(inter.shape[1]):
-                rel = lax.rem(inter_s[p, k] - where[2] - p + parents + all_parents, all_parents)
+                rel = lax.rem(inter_s[p, k] - box * parents - p + parents + all_parents, all_parents)
                 at = jnp.where(rel < parents, rel, rel - 3)
                 dense[p, at] = table[trans_s[p, k]]
             return carry
@@ -253,15 +269,14 @@
 
 
 def final_kernel(*refs, pieces):
-    parts_in = refs[:pieces]
-    near_refs = refs[pieces : pieces + 2]
-    mats, out_ref, field = refs[pieces + 2 :]
+    every, *near_refs, mats, out_ref, field = refs
     nears = [(ref, i) for ref in near_refs for i in range(ref.shape[0])]
     boxes, halves, rhs = out_ref.shape[:3]
     parts = halves * rhs
-    total = parts_in[0][...].astype(F32)
-    for m in parts_in[1:]:
-        total += m[...].astype(F32)
+    rows_each = field.shape[0]
+    total = every[:rows_each].astype(F32)
+    for d in range(1, pieces):
+        total += every[d * rows_each : (d + 1) * rows_each].astype(F32)
     field[...] = total.astype(BF16).astype(F32)
     for n in range(boxes):
         v = field[pl.ds(n, parts, stride=boxes), :]
@@ -286,6 +301,10 @@
 
 def swap(x, axis, pairs):
     return lax.ppermute(x, axis, pairs)
+
+
+def stay(x):
+    return pltpu.with_memory_space_constraint(x, HBM)
 
 
 def on_device(
@@ -306,8 +325,6 @@
     parts = halves * rhs
     nsamp = lax.axis_size("samp")
     nbox = lax.axis_size("box")
-    box_index = lax.axis_index("box").astype(jnp.int32)
-    samp_index = lax.axis_index("samp").astype(jnp.int32)
     total = boxes * nsamp * nbox
     reach = boxes // 2
     parents = boxes * nsamp // 8
@@ -317,34 +334,29 @@
     leaves = boxes * nsamp
     units = nsamp * nbox
     near_count = near_blocks.shape[1]
-    where = jnp.stack(
-        [(box_index * nsamp + samp_index) * boxes, samp_index % 2, box_index * parents]
-    )
-    parity = (box_index % 2).reshape(1)
-
     lift_chunks = 4
-    message, x_here = pl.pallas_call(
-        lambda *refs: leaf_kernel(*refs, parents=parents),
-        in_specs=[whole_in(HBM)] * 4,
-        out_specs=[whole_in(VM)] * 2,
+    message, x_here, my_interp, my_phases = pl.pallas_call(
+        lambda *refs: leaf_kernel(*refs, parents=parents, copies_out=nsamp),
+        in_specs=[whole_in(HBM)] * 6,
+        out_specs=[whole_in(VM)] * 4,
         out_shape=[
-            jax.ShapeDtypeStruct(((parts + 1) * boxes, LANES), BF16),
+            jax.ShapeDtypeStruct((nsamp * (parts + 1) * boxes, LANES), BF16),
             jax.ShapeDtypeStruct(xvec.shape, BF16),
+            jax.ShapeDtypeStruct((samples, LANES), BF16),
+            jax.ShapeDtypeStruct((8, 2, samples), F32),
         ],
         scratch_shapes=[
             VM((parts * boxes, LANES), F32),
             VM(lift.shape, BF16),
             SM((boxes,), jnp.int32),
             SM((boxes,), jnp.int32),
-            DMA((lift_chunks + 3,)),
+            DMA((lift_chunks + 5,)),
         ],
         compiler_params=PARAMS,
         name="leaf",
-    )(octant, leaf_parent_index, xvec, lift)
-
-    messages = [message] + [None] * (nsamp - 1)
-    for d in reversed(range(1, nsamp)):
-        messages[d] = swap(message, "samp", [(i, i ^ d) for i in range(nsamp)])
+    )(*[stay(a) for a in (octant, leaf_parent_index, xvec, lift, interp, phases)])
+
+    messages = lax.all_to_all(message, "samp", 0, 0, tiled=True)
 
     both = ("box", "samp")
     x_beside = swap(x_here, both, [(i, i ^ 1) for i in range(units)])
@@ -352,14 +364,11 @@
         x_here, both, [(i, (i + (1 if i % 2 else -1)) % units) for i in range(units)]
     )
 
-    my_interp = lax.dynamic_slice_in_dim(interp, samp_index * samples, samples, axis=0)
-    my_phases = lax.dynamic_slice_in_dim(phases, samp_index * samples, samples, axis=2)
-
     parent_pat, place_onehot = pl.pallas_call(
         lambda *refs: up_kernel(
             *refs, pieces=nsamp, boxes=boxes, parents=parents, parts=parts
         ),
-        in_specs=[whole_in(VM)] * (nsamp + 2),
+        in_specs=[whole_in(VM)] * 3,
         out_specs=[whole_in(VM)] * 2,
         out_shape=[
             jax.ShapeDtypeStruct((parents * parts, samples), BF16),
@@ -371,7 +380,7 @@
         ],
         compiler_params=PARAMS,
         name="up",
-    )(*messages, my_interp, my_phases)
+    )(messages, my_interp, my_phases)
 
     across = swap(
         parent_pat, "box", [(i, (i + (1 if i % 2 else -1)) % nbox) for i in range(nbox)]
@@ -403,7 +412,7 @@
                 total=total,
                 table_args=(parents, all_parents) if table else None,
             ),
-            in_specs=[whole_in(SM), whole_in(HBM)]
+            in_specs=[whole_in(HBM)]
             + [whole_in(VM)] * 3
             + [whole_in(HBM), whole_in(VM)]
             + [whole_in(HBM)] * len(table),
@@ -417,7 +426,15 @@
                 transcendentals=0,
             ),
             name="near",
-        )(where, neighbours.T, x_here, x_beside, x_across, near_blocks, after, *table)
+        )(
+            stay(neighbours.T),
+            x_here,
+            x_beside,
+            x_across,
+            stay(near_blocks),
+            after,
+            *[stay(a) for a in table],
+        )
 
     split = boxes // 2
     near_a, dense = near_part(0, split, place_onehot, (inter_list, trans_id, translators))
@@ -426,9 +443,9 @@
         lambda *refs: down_kernel(
             *refs, pieces=nsamp, boxes=boxes, parents=parents, parts=parts
         ),
-        in_specs=[whole_in(SM)] + [whole_in(VM)] * 7,
-        out_specs=[whole_in(VM)] * nsamp,
-        out_shape=[jax.ShapeDtypeStruct((parts * boxes, LANES), BF16)] * nsamp,
+        in_specs=[whole_in(VM)] * 7,
+        out_specs=whole_in(VM),
+        out_shape=jax.ShapeDtypeStruct((nsamp * parts * boxes, LANES), BF16),
         scratch_shapes=[
             VM((3 * parents, parts, samples), F32),
             VM((samples // LANES, parents * parts, LANES), F32),
@@ -436,23 +453,21 @@
         ],
         compiler_params=PARAMS,
         name="down",
-    )(parity, parent_pat, across, beside, dense, my_interp, my_phases, place_onehot)
-
-    partial = [fields[0]] + [None] * (nsamp - 1)
-    for d in reversed(range(1, nsamp)):
-        partial[d] = swap(fields[d], "samp", [(i, i ^ d) for i in range(nsamp)])
-
-    (near_b,) = near_part(split, boxes - split, fields[0], ())
+    )(parent_pat, across, beside, dense, my_interp, my_phases, place_onehot)
+
+    partial = lax.all_to_all(fields, "samp", 0, 0, tiled=True)
+
+    (near_b,) = near_part(split, boxes - split, fields, ())
 
     return pl.pallas_call(
         lambda *refs: final_kernel(*refs, pieces=nsamp),
-        in_specs=[whole_in(VM)] * (nsamp + 3),
+        in_specs=[whole_in(VM)] * 4,
         out_specs=whole_in(VM),
         out_shape=jax.ShapeDtypeStruct(xvec.shape, F32),
         scratch_shapes=[VM((parts * boxes, LANES), F32)],
         compiler_params=PARAMS,
         name="final",
-    )(*partial, near_a, near_b, place)
+    )(partial, near_a, near_b, place)
 
 
 def solution(mesh):

time: 42.8 us -> 42.9 us (level)
  blocking collectives: 0 us -> 12.8 us
  local copies, waits for them, and re-layouts: 10.5 us -> 0.01 us
  starting transfers between devices: 16.5 us -> 7.11 us
  waiting for transfers between devices: 2.29 us -> 6.51 us
  Pallas kernels: 12.9 us -> 16.1 us
    all_to_all x0 -> x1, blocking collectives: none -> 12.8 us  [on_device(): messages = lax.all_to_all(message, 'samp', 0, 0, tiled=True)]
    ppermute x10 -> x4, starting transfers between devices: 16.5 us -> 3.79 us  [swap(): return lax.ppermute(x, axis, pairs)]
    unnamed x26 -> x2, local copies, waits for them, and re-layouts: 9.75 us -> 0.01 us
    ppermute x10 -> x4, waiting for transfers between devices: 2.29 us -> 5.77 us  [swap(): return lax.ppermute(x, axis, pairs)]
    all_to_all x0 -> x1, starting transfers between devices: none -> 3.32 us  [on_device(): partial = lax.all_to_all(fields, 'samp', 0, 0, tiled=True)]
    pallas_call x2, Pallas kernels: 9.44 us -> 11.1 us  [near_part(): pl.pallas_call(lambda *refs: near_kernel(*refs, first=first, count=count,...]
    pallas_call x1, Pallas kernels: 0.97 us -> 1.86 us  [on_device(): pl.pallas_call(lambda *refs: leaf_kernel(*refs, parents=parents, copies_o...]
    dynamic_slice x2 -> x0, local copies, waits for them, and re-layouts: 0.78 us -> none  [the longest x1 0.77 us: on_device(): lax.dynamic_slice_in_dim(phases, samp_index * samples, samples, axis=2)]
  transfers between devices with their start and end apart: 10 -> 5, of which waited for: 3 -> 2; matrix products, arithmetic and copies ran while one was open for 2% -> 0% of each run, Pallas kernels for 24% -> 26%
where the time goes in v3:
time: 42.9 us; the launch traced here: 42.6 us
  Pallas kernels  16.1 us (38%)
  blocking collectives  12.8 us (30%)
  starting transfers between devices  7.11 us (17%)
  waiting for transfers between devices  6.51 us (15%)
    all_to_all x1, blocking collectives, on_device(): messages = lax.all_to_all(message, 'samp', 0, 0, tiled=True)  12.8 us
    pallas_call x2, Pallas kernels, near_part(): pl.pallas_call(lambda *refs: near_kernel(*refs, first=first, count=count,...  11.1 us
    ppermute x4, waiting for transfers between devices, swap(): return lax.ppermute(x, axis, pairs)  5.77 us
    ppermute x4, starting transfers between devices, swap(): return lax.ppermute(x, axis, pairs)  3.79 us
    all_to_all x1, starting transfers between devices, on_device(): partial = lax.all_to_all(fields, 'samp', 0, 0, tiled=True)  3.32 us
    pallas_call x1, Pallas kernels, on_device(): pl.pallas_call(lambda *refs: leaf_kernel(*refs, parents=parents, copies_o...  1.86 us
    pallas_call x1, Pallas kernels, on_device(): pl.pallas_call(lambda *refs: down_kernel(*refs, pieces=nsamp, boxes=boxes...  1.47 us
    pallas_call x1, Pallas kernels, on_device(): pl.pallas_call(lambda *refs: final_kernel(*refs, pieces=nsamp), in_specs=...  1.03 us
  transfers between devices with their start and end apart: 5, of which 2 were waited for; matrix products, arithmetic and copies ran while one was open for 0% of the time, Pallas kernels for 26%

profile of v3, /device:TPU:0, one launch (start us, length us, event | category | flops | bytes accessed | tf_op | source)
XLA Modules:
  0.0 42.6 jit_solution(1910395631824497357)
XLA Ops:
  0.0 1.9 %leaf.1 = (bf16[576,128]{1,0:T(8,128)(2,1)S(1)}, bf16[16,2,4,128]{3,2,1,0:T(4,128)(2,1)S(1)}, bf16[512,128]{1,0:T(8,128)(2,1)S(1)}, f32[8,2,512]{2,1,0:T(2,128)S(1)}) custom-call(s32[16]{0:T(128)} %refs_0_.1, s32[16]{0:T(128)} %refs_1_.1, bf16[16,2,4,128]{3,2,1,0:T(4,128)(2,1)} %refs_2_.1, bf16[16,2,128,128]{3,2,1,0:T(8,128)(2,1)} %refs_3_.2, ...), custom_call_target="tpu_custom_call" | custom-call | tf_op jit(solution)/shard_map/leaf/pallas_call | solution.py:338
  1.9 12.8 %all_to_all.22 = bf16[4,144,128]{2,1,0:T(8,128)(2,1)S(1)} all-to-all(bf16[4,144,128]{2,1,0:T(8,128)(2,1)S(1)} %bitcast.7), channel_id=1, replica_groups=mesh['box'=8,'samp'=4] {'samp'}, dimensions={0} | all-to-all | bytes 294912 | tf_op jit(solution)/shard_map/all_to_all | solution.py:359
  14.7 0.7 %up.1 = (bf16[64,512]{1,0:T(8,128)(2,1)S(1)}, bf16[64,64]{1,0:T(8,128)(2,1)S(1)}) custom-call(bf16[576,128]{1,0:T(8,128)(2,1)S(1)} %bitcast.5, bf16[512,128]{1,0:T(8,128)(2,1)S(1)} %get-tuple-element.14.refs_1_.refs_4_, f32[8,2,512]{2,1,0:T(2,128)S(1)} %get-tuple-element.15.refs_2_.refs_5_), custom_call_target="tpu_custom_call" | custom-call | tf_op jit(solution)/shard_map/up/pallas_call | solution.py:367
  15.3 0.1 collective-permute-start.1
  15.4 2.5 %collective-permute-start = (bf16[64,512]{1,0:T(8,128)(2,1)S(1)}, bf16[64,512]{1,0:T(8,128)(2,1)S(1)}, u32[]{:S(2)}, u32[]{:S(2)}) collective-permute-start(bf16[64,512]{1,0:T(8,128)(2,1)S(1)} %get-tuple-element.16.refs_0_), channel_id=1, source_target_pairs={{0,28},{4,8},{8,4},{12,16},{16,12},{20,24},{24,20},{28,0},{1,29},{... | collective-permute-start | bytes 196616 | tf_op jit(solution)/shard_map/ppermute | solution.py:303
  17.9 0.8 %collective-permute-start.3 = (bf16[16,2,4,128]{3,2,1,0:T(4,128)(2,1)S(1)}, bf16[16,2,4,128]{3,2,1,0:T(4,128)(2,1)S(1)}, u32[]{:S(2)}, u32[]{:S(2)}) collective-permute-start(bf16[16,2,4,128]{3,2,1,0:T(4,128)(2,1)S(1)} %get-tuple-element.17.refs_1_), channel_id=1, source_target_pairs={{0,31},{1,2},{2,1},{3,4},{4,3},{5,6},{6,5},{7,8},{8,7},{9,10},{10,... | collective-permute-start | bytes 98312 | tf_op jit(solution)/shard_map/ppermute | solution.py:303
  18.8 0.4 collective-permute-start.2
  19.1 5.8 %collective-permute-done.3.refs_3_ = bf16[16,2,4,128]{3,2,1,0:T(4,128)(2,1)S(1)} collective-permute-done((bf16[16,2,4,128]{3,2,1,0:T(4,128)(2,1)S(1)}, bf16[16,2,4,128]{3,2,1,0:T(4,128)(2,1)S(1)}, u32[]{:S(2)}, u32[]{:S(2)}) %collective-permute-start.3) | collective-permute-done | bytes 32800 | tf_op jit(solution)/shard_map/ppermute | solution.py:303
  24.9 0.0 collective-permute-done.2.refs_2_
  24.9 0.0 copy-start
  24.9 6.0 %near.2 = (f32[8,8,128]{2,1,0:T(8,128)S(1)}, f32[8,14,2,512]{3,2,1,0:T(2,128)S(1)}) custom-call(s32[8,16]{1,0:T(8,128)} %bitcast.8, bf16[16,2,4,128]{3,2,1,0:T(4,128)(2,1)S(1)} %get-tuple-element.17.refs_1_, bf16[16,2,4,128]{3,2,1,0:T(4,128)(2,1)S(1)} %collective-permute-done.2.refs_2_, bf16[16,2,4,128]{3,2,1,0:T(4,128)(2,1)S(1)} %collective-permute-done.3.refs_3_, ...), custom_call_target="tpu_custom_call" | custom-call | flops 33554432 | bytes 4194304 | tf_op jit(solution)/shard_map/near/pallas_call | solution.py:407
  30.9 0.0 collective-permute-done.1.refs_2_
  30.9 0.0 collective-permute-done.refs_1_
  30.9 1.5 %down.1.refs_5_ = bf16[512,128]{1,0:T(8,128)(2,1)} custom-call(bf16[64,512]{1,0:T(8,128)(2,1)S(1)} %get-tuple-element.16.refs_0_, bf16[64,512]{1,0:T(8,128)(2,1)S(1)} %collective-permute-done.refs_1_, bf16[64,512]{1,0:T(8,128)(2,1)S(1)} %collective-permute-done.1.refs_2_, f32[8,14,2,512]{3,2,1,0:T(2,128)S(1)} %get-tuple-element.19.refs_3_, ...), custom_call_target="tpu_custom_call" | custom-call | tf_op jit(solution)/shard_map/down/pallas_call | solution.py:442
  32.3 3.3 %all-to-all-start.1 = ((bf16[4,128,128]{2,1,0:T(8,128)(2,1)}), bf16[4,128,128]{2,1,0:T(8,128)(2,1)S(1)}, u32[]{:S(2)}, u32[]{:S(2)}) async-start(bf16[4,128,128]{2,1,0:T(8,128)(2,1)} %bitcast.3), calls=%async_computation.1 | async-start | bytes 262144 | tf_op jit(solution)/shard_map/all_to_all | solution.py:458
  35.7 5.1 %near.3.refs_2_ = f32[8,8,128]{2,1,0:T(8,128)S(1)} custom-call(s32[8,16]{1,0:T(8,128)} %bitcast.9, bf16[16,2,4,128]{3,2,1,0:T(4,128)(2,1)S(1)} %get-tuple-element.17.refs_1_, bf16[16,2,4,128]{3,2,1,0:T(4,128)(2,1)S(1)} %collective-permute-done.2.refs_2_, bf16[16,2,4,128]{3,2,1,0:T(4,128)(2,1)S(1)} %collective-permute-done.3.refs_3_, ...), custom_call_target="tpu_custom_call" | custom-call | flops 33554432 | bytes 4194304 | tf_op jit(solution)/shard_map/near/pallas_call | solution.py:407
  40.8 0.7 %all-to-all-done.1 = bf16[4,128,128]{2,1,0:T(8,128)(2,1)S(1)} async-done(((bf16[4,128,128]{2,1,0:T(8,128)(2,1)}), bf16[4,128,128]{2,1,0:T(8,128)(2,1)S(1)}, u32[]{:S(2)}, u32[]{:S(2)}) %all-to-all-start.1) | async-done | bytes 131104 | tf_op jit(solution)/shard_map/all_to_all | solution.py:458
  41.6 0.0 copy-done
  41.6 1.0 %final.1 = f32[16,2,4,128]{3,2,1,0:T(4,128)} custom-call(bf16[512,128]{1,0:T(8,128)(2,1)S(1)} %bitcast.6, f32[8,8,128]{2,1,0:T(8,128)S(1)} %get-tuple-element.20.refs_1_, f32[8,8,128]{2,1,0:T(8,128)S(1)} %near.3.refs_2_, bf16[16,2,128,128]{3,2,1,0:T(8,128)(2,1)S(1)} %copy-done), custom_call_target="tpu_custom_call" | custom-call | tf_op jit(solution)/shard_map/final/pallas_call | solution.py:462
Async XLA Ops:
  15.3 15.5 %collective-permute-start.1 = (bf16[64,512]{1,0:T(8,128)(2,1)S(1)}, bf16[64,512]{1,0:T(8,128)(2,1)S(1)}, u32[]{:S(2)}, u32[]{:S(2)}) collective-permute-start(bf16[64,512]{1,0:T(8,128)(2,1)S(1)} %get-tuple-element.16.refs_0_), channel_id=1, source_target_pairs={{0,4},{4,0},{8,12},{12,8},{16,20},{20,16},{24,28},{28,24},{1,5},{5... | collective-permute-start | bytes 196616 | tf_op jit(solution)/shard_map/ppermute | solution.py:303
  15.4 15.5 %collective-permute-start = (bf16[64,512]{1,0:T(8,128)(2,1)S(1)}, bf16[64,512]{1,0:T(8,128)(2,1)S(1)}, u32[]{:S(2)}, u32[]{:S(2)}) collective-permute-start(bf16[64,512]{1,0:T(8,128)(2,1)S(1)} %get-tuple-element.16.refs_0_), channel_id=1, source_target_pairs={{0,28},{4,8},{8,4},{12,16},{16,12},{20,24},{24,20},{28,0},{1,29},{... | collective-permute-start | bytes 196616 | tf_op jit(solution)/shard_map/ppermute | solution.py:303
  17.9 6.9 %collective-permute-start.3 = (bf16[16,2,4,128]{3,2,1,0:T(4,128)(2,1)S(1)}, bf16[16,2,4,128]{3,2,1,0:T(4,128)(2,1)S(1)}, u32[]{:S(2)}, u32[]{:S(2)}) collective-permute-start(bf16[16,2,4,128]{3,2,1,0:T(4,128)(2,1)S(1)} %get-tuple-element.17.refs_1_), channel_id=1, source_target_pairs={{0,31},{1,2},{2,1},{3,4},{4,3},{5,6},{6,5},{7,8},{8,7},{9,10},{10,... | collective-permute-start | bytes 98312 | tf_op jit(solution)/shard_map/ppermute | solution.py:303
  18.8 6.1 %collective-permute-start.2 = (bf16[16,2,4,128]{3,2,1,0:T(4,128)(2,1)S(1)}, bf16[16,2,4,128]{3,2,1,0:T(4,128)(2,1)S(1)}, u32[]{:S(2)}, u32[]{:S(2)}) collective-permute-start(bf16[16,2,4,128]{3,2,1,0:T(4,128)(2,1)S(1)} %get-tuple-element.17.refs_1_), channel_id=1, source_target_pairs={{0,1},{1,0},{2,3},{3,2},{4,5},{5,4},{6,7},{7,6},{8,9},{9,8},{10,11... | collective-permute-start | bytes 98312 | tf_op jit(solution)/shard_map/ppermute | solution.py:303
  24.9 16.7 %copy-start = (bf16[16,2,128,128]{3,2,1,0:T(8,128)(2,1)S(1)}, bf16[16,2,128,128]{3,2,1,0:T(8,128)(2,1)}, u32[]{:S(2)}) copy-start(bf16[16,2,128,128]{3,2,1,0:T(8,128)(2,1)} %refs_3_.3) | copy-start | bytes 3145732
  32.3 9.2 %all-to-all-start.1 = ((bf16[4,128,128]{2,1,0:T(8,128)(2,1)}), bf16[4,128,128]{2,1,0:T(8,128)(2,1)S(1)}, u32[]{:S(2)}, u32[]{:S(2)}) async-start(bf16[4,128,128]{2,1,0:T(8,128)(2,1)} %bitcast.3), calls=%async_computation.1 | async-start | bytes 262144 | tf_op jit(solution)/shard_map/all_to_all | solution.py:458

commit v4 on v2

v4 whole, which is shorter than its diff:
```python
import jax
import jax.numpy as jnp
from jax import lax
from jax.experimental import pallas as pl
from jax.experimental.pallas import tpu as pltpu
from jax.sharding import PartitionSpec as P

F32 = jnp.float32
BF16 = jnp.bfloat16
LANES = 128


def nt_dot(a, b):
    return lax.dot_general(a, b, (((1,), (1,)), ((), ())), preferred_element_type=F32)


def nn_dot(a, b):
    return lax.dot_general(a, b, (((1,), (0,)), ((), ())), preferred_element_type=F32)


def times_i(v):
    half = v.shape[0] // 2
    return jnp.concatenate([-v[half:], v[:half]], axis=0)


def widen(v):
    return jnp.concatenate([v, times_i(v)], axis=1)


def leaf_kernel(
    octant, parent, x_hbm, lift_hbm, plain, to_beside, to_far, x_rows,
    x_ref, rows, lift, oct_s, par_s, sems, *, parents,
):
    boxes, halves, rhs, _ = x_ref.shape
    parts = halves * rhs
    reach = boxes // 2
    chunks = sems.shape[0] - 3
    per = boxes // chunks
    small = [
        pltpu.make_async_copy(x_hbm, x_ref, sems.at[chunks]),
        pltpu.make_async_copy(octant, oct_s, sems.at[chunks + 1]),
        pltpu.make_async_copy(parent, par_s, sems.at[chunks + 2]),
    ]
    big = [
        pltpu.make_async_copy(
            lift_hbm.at[pl.ds(i * per, per)], lift.at[pl.ds(i * per, per)], sems.at[i]
        )
        for i in range(chunks)
    ]
    small[0].start()
    for copy in big:
        copy.start()
    small[1].start()
    small[2].start()
    small[0].wait()
    own = [
        jnp.concatenate([x_ref[n, 0].astype(F32), x_ref[n, 1].astype(F32)], axis=0)
        for n in range(boxes)
    ]
    for n in range(boxes):
        if n % per == 0:
            big[n // per].wait()
        mat = jnp.concatenate([lift[n, 0], lift[n, 1]], axis=1)
        rows[pl.ds(n, parts, stride=boxes), :] = nt_dot(widen(own[n]).astype(BF16), mat)
    small[1].wait()
    small[2].wait()
    lane = lax.rem(lax.broadcasted_iota(jnp.int32, (boxes, LANES), 1), boxes)
    across = jnp.zeros((boxes, LANES), F32)
    for n in range(boxes):
        slot = (oct_s[n] * parents + lax.rem(par_s[n], parents)).astype(F32)
        across = jnp.where(lane == n, slot, across)
    pattern = rows[...].astype(BF16)
    codes = across.astype(BF16)
    at = parts * boxes
    for ref in (plain, to_beside, to_far):
        ref[:at] = pattern
        ref[at : at + boxes] = codes
    at += boxes
    x_rows[...] = jnp.concatenate(own, axis=0).astype(BF16)
    first = jnp.concatenate(own[:reach], axis=0)
    last = jnp.concatenate(own[reach:], axis=0)
    odd = lax.rem(lax.axis_index("samp"), 2) == 1
    to_beside[at:] = jnp.where(odd, first, last).astype(BF16)
    to_far[at:] = jnp.where(odd, last, first).astype(BF16)


def up_kernel(*refs, pieces, boxes, parents, parts):
    msgs = refs[:pieces]
    interp_ref, phase_ref, out_ref, place_ref, raised, folded = refs[pieces:]
    forward = msgs[-1]
    slots = 8 * parents
    samples = interp_ref.shape[0]
    per_tile = LANES // boxes
    at = parts * boxes
    tiles = []
    for t in range(0, pieces, per_tile):
        lane = lax.broadcasted_iota(jnp.int32, (boxes, LANES), 1) // boxes
        code = msgs[t][at : at + boxes].astype(F32)
        for d in range(1, min(per_tile, pieces - t)):
            code = jnp.where(lane == d, msgs[t + d][at : at + boxes].astype(F32), code)
        code = jnp.concatenate([code] * (slots // boxes), axis=0)
        want = lax.broadcasted_iota(jnp.int32, (slots, LANES), 0).astype(F32)
        width = min(per_tile, pieces - t) * boxes
        tiles.append(jnp.where(code == want, 1.0, 0.0)[:, :width])
    sorter = jnp.concatenate(tiles, axis=1)
    place_ref[...] = sorter.T.astype(BF16)
    sorter = sorter.astype(BF16)
    pats = jnp.concatenate(
        [
            jnp.concatenate([m[c * boxes : (c + 1) * boxes] for m in msgs], axis=0)
            for c in range(parts)
        ],
        axis=1,
    )
    ordered = nn_dot(sorter, pats).astype(BF16)
    for c in range(parts):
        raised[c * slots : (c + 1) * slots] = nt_dot(
            ordered[:, c * LANES : (c + 1) * LANES], interp_ref[...]
        )
    half = parts // 2
    for t in range(samples // LANES):
        lanes = slice(t * LANES, (t + 1) * LANES)
        for r in range(half):
            re = im = None
            for o in range(8):
                ph_r = phase_ref[o, 0:1, lanes]
                ph_i = phase_ref[o, 1:2, lanes]
                base_r = r * slots + o * parents
                base_i = (half + r) * slots + o * parents
                xr = raised[base_r : base_r + parents, lanes]
                xi = raised[base_i : base_i + parents, lanes]
                dr = ph_r * xr - ph_i * xi
                di = ph_r * xi + ph_i * xr
                re = dr if re is None else re + dr
                im = di if im is None else im + di
            folded[t, r * parents : (r + 1) * parents] = re
            folded[t, (half + r) * parents : (half + r + 1) * parents] = im
        for p in range(0, parents, 2):
            both = jnp.concatenate(
                [folded[t, pl.ds(p + e, parts, stride=parents), :] for e in range(2)], axis=0
            )
            out_ref[p * parts : (p + 2) * parts, lanes] = both.astype(BF16)
        extra = out_ref.shape[0] - parents * parts
        start = forward.shape[0] - extra * (samples // LANES - t)
        out_ref[parents * parts :, lanes] = forward[start : start + extra]


def zone(parents):
    return [d for d in range(-parents, parents + 1) if abs(d) >= 2]


def prep_kernel(
    inter, trans, table_hbm, interp_hbm, phase_hbm, after, dense, interp_ref, phase_ref,
    inter_s, trans_s, table, sems, *, parents, all_parents,
):
    samples = interp_ref.shape[0]
    mine = pl.ds(pl.multiple_of(lax.axis_index("samp") * samples, samples), samples)
    copies = [
        pltpu.make_async_copy(inter, inter_s, sems.at[0]),
        pltpu.make_async_copy(trans, trans_s, sems.at[1]),
        pltpu.make_async_copy(table_hbm, table, sems.at[2]),
        pltpu.make_async_copy(interp_hbm.at[mine], interp_ref, sems.at[3]),
        pltpu.make_async_copy(phase_hbm.at[:, :, mine], phase_ref, sems.at[4]),
    ]
    for copy in copies:
        copy.start()
    for copy in copies:
        copy.wait()
    if len(zone(parents)) > inter.shape[1]:
        dense[...] = jnp.zeros_like(dense)
    first = lax.axis_index("box") * parents

    def fill(p, carry):
        for k in range(inter.shape[1]):
            rel = lax.rem(inter_s[p, k] - first - p + parents + all_parents, all_parents)
            at = jnp.where(rel < parents, rel, rel - 3)
            dense[p, at] = table[trans_s[p, k]]
        return carry

    lax.fori_loop(0, parents, fill, 0)


def down_kernel(
    own, across, beside, dense, interp_ref, phase_ref, place_ref, *refs, pieces, boxes, parents, parts
):
    outs = refs[:pieces]
    window, incoming, shifted = refs[pieces:]
    samples = interp_ref.shape[0]
    slots = 8 * parents
    half = parts // 2
    odd = lax.rem(lax.axis_index("box"), 2)
    rows = parents * parts
    window[parents : 2 * parents] = own[:rows].astype(F32).reshape(parents, parts, samples)
    window[pl.ds(2 * parents * odd, parents)] = (
        across[:rows].astype(F32).reshape(parents, parts, samples)
    )
    window[pl.ds(2 * parents * (1 - odd), parents)] = (
        beside[:rows].astype(F32).reshape(parents, parts, samples)
    )
    offsets = zone(parents)

    def one(p):
        for t in range(samples // LANES):
            lanes = slice(t * LANES, (t + 1) * LANES)
            acc_r = acc_i = None
            for i, d in enumerate(offsets):
                x = window[parents + p + d, :, lanes]
                yr = dense[p, i, 0:1, lanes] * x
                yi = dense[p, i, 1:2, lanes] * x
                acc_r = yr if acc_r is None else acc_r + yr
                acc_i = yi if acc_i is None else acc_i + yi
            got = (acc_r + times_i(acc_i)).astype(BF16).astype(F32)
            incoming[t, pl.ds(p * parts, parts), :] = got

    if parents <= 8:
        for p in range(parents):
            one(p)
    else:
        lax.fori_loop(0, parents, lambda p, c: (one(p), c)[1], 0)
    for t in range(samples // LANES):
        lanes = slice(t * LANES, (t + 1) * LANES)
        for r in range(half):
            ir = incoming[t, pl.ds(r, parents, stride=parts), :]
            ii = incoming[t, pl.ds(half + r, parents, stride=parts), :]
            re, im = [], []
            for o in range(8):
                ph_r = phase_ref[o, 0:1, lanes]
                ph_i = phase_ref[o, 1:2, lanes]
                re.append(ph_r * ir - ph_i * ii)
                im.append(ph_r * ii + ph_i * ir)
            shifted[r * slots : (r + 1) * slots, lanes] = jnp.concatenate(re, axis=0).astype(BF16)
            shifted[(half + r) * slots : (half + r + 1) * slots, lanes] = jnp.concatenate(
                im, axis=0
            ).astype(BF16)
    field = nn_dot(shifted[...], interp_ref[...]).astype(BF16)
    spread = jnp.concatenate([field[c * slots : (c + 1) * slots] for c in range(parts)], axis=1)
    leaves = nn_dot(place_ref[...], spread).astype(BF16)
    for d in range(pieces):
        for c in range(parts):
            outs[d][c * boxes : (c + 1) * boxes] = leaves[
                d * boxes : (d + 1) * boxes, c * LANES : (c + 1) * LANES
            ]


def near_kernel(
    neighbours, own, mats_hbm, after, *refs, late, nsamp, total, halo_rows, parent_rows
):
    far = nsamp.bit_length() - 2
    from_beside, from_far, refs = refs[0], refs[1 : 1 + far], refs[1 + far :]
    if late:
        across, beside, refs = refs[0], refs[1], refs[2:]
    out_ref, window, mats, nbr, sems = refs
    count, parts, unknowns = out_ref.shape
    boxes = own.shape[0] // parts
    near_count = mats.shape[1]
    samp = lax.axis_index("samp")
    box = lax.axis_index("box")
    odd = lax.rem(samp, 2) == 1
    final = samp == nsamp - 1
    upper = jnp.logical_not(final) if not late else final
    first = jnp.where(upper, boxes - count, 0)
    list_copy = pltpu.make_async_copy(neighbours, nbr, sems.at[count])
    list_copy.start()
    copies = [
        pltpu.make_async_copy(mats_hbm.at[first + i], mats.at[i], sems.at[i]) for i in range(count)
    ]
    for copy in copies:
        copy.start()

    def piece(ref):
        return ref[ref.shape[0] - halo_rows :].astype(F32)

    distant = piece(from_far[0])
    step = samp ^ (samp - 1) if late else samp ^ (samp + 1)
    for i in range(1, far):
        distant = jnp.where(step == (4 << i) - 1, piece(from_far[i]), distant)
    near_by = piece(from_beside)
    if late:
        def forwarded(ref):
            return jnp.concatenate(
                [
                    ref[parent_rows:, t * LANES : (t + 1) * LANES].astype(F32)
                    for t in range(ref.shape[1] // LANES)
                ],
                axis=0,
            )

        box_odd = lax.rem(box, 2) == 1
        from_left = samp == 0
        passed = jnp.where(box_odd == from_left, forwarded(beside), forwarded(across))
        halo = jnp.where(odd, near_by, distant)
        halo = jnp.where(jnp.logical_or(from_left, final), passed, halo)
    else:
        halo = jnp.where(jnp.logical_and(odd, jnp.logical_not(final)), distant, near_by)
    at = jnp.where(upper, boxes + count, 0)
    for i in range(count):
        window[at + i] = widen(halo[i * parts : (i + 1) * parts])
    mine = own[...].astype(F32)
    for i in range(boxes):
        window[count + i] = widen(mine[i * parts : (i + 1) * parts])
    list_copy.wait()
    base = (box * nsamp + samp) * boxes
    for i in range(count):
        copies[i].wait()
        acc = None
        for k in range(near_count):
            j = lax.rem(nbr[k, first + i] - base + count + total, total)
            mat = jnp.concatenate([mats[i, k, 0], mats[i, k, 1]], axis=1)
            y = nt_dot(window[j].astype(BF16), mat)
            acc = y if acc is None else acc + y
        out_ref[i] = acc


def final_kernel(*refs, pieces):
    parts_in = refs[:pieces]
    near_early, near_late, mats, out_ref, field = refs[pieces:]
    boxes, halves, rhs = out_ref.shape[:3]
    parts = halves * rhs
    half = boxes // 2
    flip = lax.axis_index("samp") == lax.axis_size("samp") - 1
    total = parts_in[0][...].astype(F32)
    for m in parts_in[1:]:
        total += m[...].astype(F32)
    field[...] = total.astype(BF16).astype(F32)
    for n in range(boxes):
        v = field[pl.ds(n, parts, stride=boxes), :]
        wide = jnp.concatenate([v, times_i(v)], axis=1).astype(BF16)
        y = nt_dot(wide, jnp.concatenate([mats[n, 0], mats[n, 1]], axis=1))
        i = n % half
        y = y + jnp.where(flip == (n < half), near_early[i], near_late[i])
        out_ref[n, 0] = y[:rhs]
        out_ref[n, 1] = y[rhs:]


def whole_in(kind):
    return pl.BlockSpec(memory_space=kind)


VM = pltpu.VMEM
SM = pltpu.SMEM
HBM = pltpu.HBM
DMA = pltpu.SemaphoreType.DMA
PARAMS = pltpu.CompilerParams(vmem_limit_bytes=24 * 1024 * 1024)


def stay(x):
    return pltpu.with_memory_space_constraint(x, HBM)


def on_device(
    xvec,
    near_blocks,
    neighbours,
    lift,
    place,
    interp,
    phases,
    octant,
    leaf_parent_index,
    translators,
    inter_list,
    trans_id,
):
    boxes, halves, rhs, unknowns = xvec.shape
    parts = halves * rhs
    nsamp = lax.axis_size("samp")
    nbox = lax.axis_size("box")
    total = boxes * nsamp * nbox
    reach = boxes // 2
    parents = boxes * nsamp // 8
    all_parents = parents * nbox
    samples = interp.shape[0] // nsamp
    slots = 8 * parents
    leaves = boxes * nsamp
    near_count = near_blocks.shape[1]
    halo_rows = reach * parts
    parent_rows = parents * parts
    plain_rows = (parts + 1) * boxes

    def shape(dims, dtype=BF16):
        return jax.ShapeDtypeStruct(dims, dtype)

    lift_chunks = 4
    plain, to_beside, to_far, x_rows = pl.pallas_call(
        lambda *refs: leaf_kernel(*refs, parents=parents),
        in_specs=[whole_in(HBM)] * 4,
        out_specs=[whole_in(VM)] * 4,
        out_shape=[
            shape((plain_rows, LANES)),
            shape((plain_rows + halo_rows, LANES)),
            shape((plain_rows + halo_rows, LANES)),
            shape((boxes * parts, LANES)),
        ],
        scratch_shapes=[
            VM(xvec.shape, BF16),
            VM((parts * boxes, LANES), F32),
            VM(lift.shape, BF16),
            SM((boxes,), jnp.int32),
            SM((boxes,), jnp.int32),
            DMA((lift_chunks + 3,)),
        ],
        compiler_params=PARAMS,
        name="leaf",
    )(*[stay(a) for a in (octant, leaf_parent_index, xvec, lift)])

    def exchange(x, d):
        return lax.ppermute(x, "samp", [(i, i ^ d) for i in range(nsamp)])

    messages = [plain] + [None] * (nsamp - 1)
    far = [(4 << i) - 1 for i in range(nsamp.bit_length() - 2)]
    for d in reversed(range(1, nsamp)):
        messages[d] = exchange(to_beside if d == 1 else to_far if d in far else plain, d)
    far_messages = [messages[d] for d in far]

    dense, my_interp, my_phases = pl.pallas_call(
        lambda *refs: prep_kernel(*refs, parents=parents, all_parents=all_parents),
        in_specs=[whole_in(HBM)] * 5 + [whole_in(VM)],
        out_specs=[whole_in(VM)] * 3,
        out_shape=[
            shape((parents, len(zone(parents)), 2, samples), F32),
            shape((samples, LANES)),
            shape((8, 2, samples), F32),
        ],
        scratch_shapes=[
            SM(inter_list.shape, jnp.int32),
            SM(trans_id.shape, jnp.int32),
            VM(translators.shape, F32),
            DMA((5,)),
        ],
        compiler_params=PARAMS,
        cost_estimate=pl.CostEstimate(
            flops=0, bytes_accessed=4 * 1024 * 1024, transcendentals=0
        ),
        name="prep",
    )(*[stay(a) for a in (inter_list, trans_id, translators, interp, phases)], x_rows)

    parent_pat, place_onehot = pl.pallas_call(
        lambda *refs: up_kernel(
            *refs, pieces=nsamp, boxes=boxes, parents=parents, parts=parts
        ),
        in_specs=[whole_in(VM)] * (nsamp + 2),
        out_specs=[whole_in(VM)] * 2,
        out_shape=[
            shape((parent_rows + halo_rows * LANES // samples, samples)),
            shape((leaves, slots)),
        ],
        scratch_shapes=[
            VM((parts * slots, samples), F32),
            VM((samples // LANES, parent_rows, LANES), F32),
        ],
        compiler_params=PARAMS,
        name="up",
    )(*messages, my_interp, my_phases)

    across = lax.ppermute(
        parent_pat, "box", [(i, (i + (1 if i % 2 else -1)) % nbox) for i in range(nbox)]
    )
    beside = lax.ppermute(parent_pat, "box", [(i, i ^ 1) for i in range(nbox)])

    def near_half(late, after, sources):
        return pl.pallas_call(
            lambda *refs: near_kernel(
                *refs,
                late=late,
                nsamp=nsamp,
                total=total,
                halo_rows=halo_rows,
                parent_rows=parent_rows,
            ),
            in_specs=[whole_in(HBM), whole_in(VM), whole_in(HBM), whole_in(VM)]
            + [whole_in(VM)] * len(sources),
            out_specs=whole_in(VM),
            out_shape=shape((reach, parts, unknowns), F32),
            scratch_shapes=[
                VM((boxes + 2 * reach, parts, 2 * unknowns), F32),
                VM((reach,) + near_blocks.shape[1:], BF16),
                SM((near_count, boxes), jnp.int32),
                DMA((reach + 1,)),
            ],
            compiler_params=PARAMS,
            cost_estimate=pl.CostEstimate(
                flops=parts * near_blocks.size,
                bytes_accessed=near_blocks.size,
                transcendentals=0,
            ),
            name="near",
        )(stay(neighbours.T), x_rows, stay(near_blocks), after, *sources)

    near_early = near_half(False, place_onehot, [messages[1], *far_messages])

    fields = pl.pallas_call(
        lambda *refs: down_kernel(
            *refs, pieces=nsamp, boxes=boxes, parents=parents, parts=parts
        ),
        in_specs=[whole_in(VM)] * 7,
        out_specs=[whole_in(VM)] * nsamp,
        out_shape=[shape((parts * boxes, LANES))] * nsamp,
        scratch_shapes=[
            VM((3 * parents, parts, samples), F32),
            VM((samples // LANES, parent_rows, LANES), F32),
            VM((parts * slots, samples), BF16),
        ],
        compiler_params=PARAMS,
        name="down",
    )(parent_pat, across, beside, dense, my_interp, my_phases, place_onehot)

    partial = [fields[0]] + [None] * (nsamp - 1)
    for d in reversed(range(1, nsamp)):
        partial[d] = exchange(fields[d], d)

    near_late = near_half(
        True, fields[0], [messages[1], *far_messages, across, beside]
    )

    return pl.pallas_call(
        lambda *refs: final_kernel(*refs, pieces=nsamp),
        in_specs=[whole_in(VM)] * (nsamp + 3),
        out_specs=whole_in(VM),
        out_shape=shape(xvec.shape, F32),
        scratch_shapes=[VM((parts * boxes, LANES), F32)],
        compiler_params=PARAMS,
        name="final",
    )(*partial, near_early, near_late, place)


def solution(mesh):
    in_specs = (
        P(("box", "samp"), None, None, None),
        P(("box", "samp"), None, None, None, None),
        P(("box", "samp"), None),
        P(("box", "samp"), None, None, None),
        P(("box", "samp"), None, None, None),
        P(),
        P(),
        P(("box", "samp")),
        P(("box", "samp")),
        P(None, None, "samp"),
        P("box", None),
        P("box", None),
    )
    out_specs = P(("box", "samp"), None, None, None)
    return jax.shard_map(
        on_device, mesh=mesh, in_specs=in_specs, out_specs=out_specs, check_vma=False
    )
```

time: 42.8 us -> 34.1 us (0.80)
  local copies, waits for them, and re-layouts: 10.5 us -> 0.01 us
  waiting for transfers between devices: 2.29 us -> 7.44 us
  starting transfers between devices: 16.5 us -> 11.8 us
  Pallas kernels: 12.9 us -> 14.6 us
    unnamed x26 -> x2, local copies, waits for them, and re-layouts: 9.75 us -> 0.01 us
    ppermute x10 -> x8, waiting for transfers between devices: 2.29 us -> 7.44 us  [the longest x1 3.94 us: on_device(): lax.ppermute(parent_pat, 'box', [(i, (i + (1 if i % 2 else -1)) % nbox) f...]
    ppermute x10 -> x8, starting transfers between devices: 16.5 us -> 11.8 us  [the longest x6 10.1 us: exchange(): return lax.ppermute(x, 'samp', [(i, i ^ d) for i in range(nsamp)])]
    pallas_call x1, Pallas kernels: 0.97 us -> 1.85 us  [on_device(): pl.pallas_call(lambda *refs: leaf_kernel(*refs, parents=parents), in_spec...]
    dynamic_slice x2 -> x0, local copies, waits for them, and re-layouts: 0.78 us -> none  [the longest x1 0.77 us: on_device(): lax.dynamic_slice_in_dim(phases, samp_index * samples, samples, axis=2)]
    pallas_call x2 -> x3, Pallas kernels: 9.44 us -> 10.2 us  [the longest x2 8.53 us: near_half(): pl.pallas_call(lambda *refs: near_kernel(*refs, late=late, nsamp=nsamp, t...]
  transfers between devices with their start and end apart: 10 -> 8, of which waited for: 3 -> 2; matrix products, arithmetic and copies ran while one was open for 2% -> 0% of each run, Pallas kernels for 24% -> 30%
where the time goes in v4:
time: 34.1 us; the launch traced here: 33.9 us
  Pallas kernels  14.6 us (43%)
  starting transfers between devices  11.8 us (35%)
  waiting for transfers between devices  7.44 us (22%)
    ppermute x6, starting transfers between devices, exchange(): return lax.ppermute(x, 'samp', [(i, i ^ d) for i in range(nsamp)])  10.1 us
    pallas_call x2, Pallas kernels, near_half(): pl.pallas_call(lambda *refs: near_kernel(*refs, late=late, nsamp=nsamp, t...  8.53 us
    ppermute x1, waiting for transfers between devices, on_device(): lax.ppermute(parent_pat, 'box', [(i, (i + (1 if i % 2 else -1)) % nbox) f...  3.94 us
    ppermute x6, waiting for transfers between devices, exchange(): return lax.ppermute(x, 'samp', [(i, i ^ d) for i in range(nsamp)])  3.5 us
    pallas_call x1, Pallas kernels, on_device(): pl.pallas_call(lambda *refs: leaf_kernel(*refs, parents=parents), in_spec...  1.85 us
    pallas_call x1, Pallas kernels, on_device(): pl.pallas_call(lambda *refs: prep_kernel(*refs, parents=parents, all_pare...  1.64 us
    pallas_call x1, Pallas kernels, on_device(): pl.pallas_call(lambda *refs: final_kernel(*refs, pieces=nsamp), in_specs=...  1.03 us
    ppermute x1, starting transfers between devices, on_device(): beside = lax.ppermute(parent_pat, 'box', [(i, i ^ 1) for i in range(nbox)])  0.84 us
  transfers between devices with their start and end apart: 8, of which 2 were waited for; matrix products, arithmetic and copies ran while one was open for 0% of the time, Pallas kernels for 30%

profile of v4, /device:TPU:0, one launch (start us, length us, event | category | flops | bytes accessed | tf_op | source)
XLA Modules:
  0.0 33.9 jit_solution(14062292217489226018)
XLA Ops:
  0.0 1.9 %leaf.1 = (bf16[144,128]{1,0:T(8,128)(2,1)S(1)}, bf16[208,128]{1,0:T(8,128)(2,1)S(1)}, bf16[208,128]{1,0:T(8,128)(2,1)S(1)}, bf16[128,128]{1,0:T(8,128)(2,1)S(1)}) custom-call(s32[16]{0:T(128)} %refs_0_.2, s32[16]{0:T(128)} %refs_1_.2, bf16[16,2,4,128]{3,2,1,0:T(4,128)(2,1)} %refs_2_.4, bf16[16,2,128,128]{3,2,1,0:T(8,128)(2,1)} %refs_3_.2), custom_call_target="tpu_custom_call" | custom-call | tf_op jit(solution)/shard_map/leaf/pallas_call | solution.py:384
  1.9 3.1 %collective-permute-start = (bf16[208,128]{1,0:T(8,128)(2,1)S(1)}, bf16[208,128]{1,0:T(8,128)(2,1)S(1)}, u32[]{:S(2)}, u32[]{:S(2)}) collective-permute-start(bf16[208,128]{1,0:T(8,128)(2,1)S(1)} %get-tuple-element.19), channel_id=1, source_target_pairs={{0,1},{1,0},{2,3},{3,2},{4,5},{5,4},{6,7},{7,6},{8,9},{9,8},{10,11... | collective-permute-start | bytes 159752 | tf_op jit(solution)/shard_map/ppermute | solution.py:407
  4.9 2.5 %collective-permute-start.2 = (bf16[208,128]{1,0:T(8,128)(2,1)S(1)}, bf16[208,128]{1,0:T(8,128)(2,1)S(1)}, u32[]{:S(2)}, u32[]{:S(2)}) collective-permute-start(bf16[208,128]{1,0:T(8,128)(2,1)S(1)} %get-tuple-element.20), channel_id=1, source_target_pairs={{0,3},{1,2},{2,1},{3,0},{4,7},{5,6},{6,5},{7,4},{8,11},{9,10},{10,... | collective-permute-start | bytes 159752 | tf_op jit(solution)/shard_map/ppermute | solution.py:407
  7.4 0.1 collective-permute-start.1
  7.5 1.6 %prep.1 = (f32[8,14,2,512]{3,2,1,0:T(2,128)S(1)}, bf16[512,128]{1,0:T(8,128)(2,1)S(1)}, f32[8,2,512]{2,1,0:T(2,128)S(1)}) custom-call(s32[8,14]{1,0:T(8,128)} %refs_0_.3, s32[8,14]{1,0:T(8,128)} %refs_1_.3, f32[64,2,512]{2,1,0:T(2,128)} %refs_2_.5, bf16[2048,128]{1,0:T(8,128)(2,1)} %refs_3_.3, f32[8,2,2048]{2,1,0:T(2,128)} %refs_4_.1, ...), custom_call_target="tpu_custom_call" | custom-call | bytes 4194304 | tf_op jit(solution)/shard_map/prep/pallas_call | solution.py:415
  9.2 3.5 %collective-permute-done.1.refs_2_ = bf16[144,128]{1,0:T(8,128)(2,1)S(1)} collective-permute-done((bf16[144,128]{1,0:T(8,128)(2,1)S(1)}, bf16[144,128]{1,0:T(8,128)(2,1)S(1)}, u32[]{:S(2)}, u32[]{:S(2)}) %collective-permute-start.1) | collective-permute-done | bytes 36896 | tf_op jit(solution)/shard_map/ppermute | solution.py:407
  12.7 0.0 collective-permute-done.refs_1_.refs_4_
  12.7 0.0 collective-permute-done.2.refs_3_.refs_5_
  12.7 0.7 %up.1 = (bf16[80,512]{1,0:T(8,128)(2,1)S(1)}, bf16[64,64]{1,0:T(8,128)(2,1)S(1)}) custom-call(bf16[144,128]{1,0:T(8,128)(2,1)S(1)} %get-tuple-element.18.refs_0_, bf16[208,128]{1,0:T(8,128)(2,1)S(1)} %collective-permute-done.refs_1_.refs_4_, bf16[144,128]{1,0:T(8,128)(2,1)S(1)} %collective-permute-done.1.refs_2_, ...), custom_call_target="tpu_custom_call" | custom-call | tf_op jit(solution)/shard_map/up/pallas_call | solution.py:437
  13.4 0.8 %collective-permute-start.3 = (bf16[80,512]{1,0:T(8,128)(2,1)S(1)}, bf16[80,512]{1,0:T(8,128)(2,1)S(1)}, u32[]{:S(2)}, u32[]{:S(2)}) collective-permute-start(bf16[80,512]{1,0:T(8,128)(2,1)S(1)} %get-tuple-element.24.refs_0_), channel_id=1, source_target_pairs={{0,28},{4,8},{8,4},{12,16},{16,12},{20,24},{24,20},{28,0},{1,29},{... | collective-permute-start | bytes 245768 | tf_op jit(solution)/shard_map/ppermute | solution.py:455
  14.2 0.8 %collective-permute-start.4 = (bf16[80,512]{1,0:T(8,128)(2,1)S(1)}, bf16[80,512]{1,0:T(8,128)(2,1)S(1)}, u32[]{:S(2)}, u32[]{:S(2)}) collective-permute-start(bf16[80,512]{1,0:T(8,128)(2,1)S(1)} %get-tuple-element.24.refs_0_), channel_id=1, source_target_pairs={{0,4},{4,0},{8,12},{12,8},{16,20},{20,16},{24,28},{28,24},{1,5},{5... | collective-permute-start | bytes 245768 | tf_op jit(solution)/shard_map/ppermute | solution.py:458
  15.0 3.9 %collective-permute-done.3.refs_1_.refs_6_ = bf16[80,512]{1,0:T(8,128)(2,1)S(1)} collective-permute-done((bf16[80,512]{1,0:T(8,128)(2,1)S(1)}, bf16[80,512]{1,0:T(8,128)(2,1)S(1)}, u32[]{:S(2)}, u32[]{:S(2)}) %collective-permute-start.3) | collective-permute-done | bytes 81952 | tf_op jit(solution)/shard_map/ppermute | solution.py:455
  19.0 0.0 collective-permute-done.4.refs_2_.refs_7_
  19.0 0.8 %down.1 = (bf16[128,128]{1,0:T(8,128)(2,1)S(1)}, bf16[128,128]{1,0:T(8,128)(2,1)S(1)}, bf16[128,128]{1,0:T(8,128)(2,1)S(1)}, bf16[128,128]{1,0:T(8,128)(2,1)S(1)}) custom-call(bf16[80,512]{1,0:T(8,128)(2,1)S(1)} %get-tuple-element.24.refs_0_, bf16[80,512]{1,0:T(8,128)(2,1)S(1)} %collective-permute-done.3.refs_1_.refs_6_, ...), custom_call_target="tpu_custom_call" | custom-call | tf_op jit(solution)/shard_map/down/pallas_call | solution.py:491
  19.8 0.4 %collective-permute-start.5 = (bf16[128,128]{1,0:T(8,128)(2,1)S(1)}, bf16[128,128]{1,0:T(8,128)(2,1)S(1)}, u32[]{:S(2)}, u32[]{:S(2)}) collective-permute-start(bf16[128,128]{1,0:T(8,128)(2,1)S(1)} %get-tuple-element.28), channel_id=1, source_target_pairs={{0,1},{1,0},{2,3},{3,2},{4,5},{5,4},{6,7},{7,6},{8,9},{9,8},{10,11... | collective-permute-start | bytes 98312 | tf_op jit(solution)/shard_map/ppermute | solution.py:407
  20.2 2.2 %collective-permute-start.6 = (bf16[128,128]{1,0:T(8,128)(2,1)S(1)}, bf16[128,128]{1,0:T(8,128)(2,1)S(1)}, u32[]{:S(2)}, u32[]{:S(2)}) collective-permute-start(bf16[128,128]{1,0:T(8,128)(2,1)S(1)} %get-tuple-element.29), channel_id=1, source_target_pairs={{0,2},{1,3},{2,0},{3,1},{4,6},{5,7},{6,4},{7,5},{8,10},{9,11},{10,... | collective-permute-start | bytes 98312 | tf_op jit(solution)/shard_map/ppermute | solution.py:407
  22.4 1.9 %collective-permute-start.7 = (bf16[128,128]{1,0:T(8,128)(2,1)S(1)}, bf16[128,128]{1,0:T(8,128)(2,1)S(1)}, u32[]{:S(2)}, u32[]{:S(2)}) collective-permute-start(bf16[128,128]{1,0:T(8,128)(2,1)S(1)} %get-tuple-element.30), channel_id=1, source_target_pairs={{0,3},{1,2},{2,1},{3,0},{4,7},{5,6},{6,5},{7,4},{8,11},{9,10},{10,... | collective-permute-start | bytes 98312 | tf_op jit(solution)/shard_map/ppermute | solution.py:407
  24.3 0.0 copy-start
  24.3 4.3 %near.2.refs_4_ = f32[8,8,128]{2,1,0:T(8,128)S(1)} custom-call(s32[8,16]{1,0:T(8,128)} %bitcast.1, bf16[128,128]{1,0:T(8,128)(2,1)S(1)} %get-tuple-element.21.refs_5_.refs_1_, bf16[16,8,2,128,128]{4,3,2,1,0:T(8,128)(2,1)} %refs_2_.7, bf16[64,64]{1,0:T(8,128)(2,1)S(1)} %get-tuple-element.26.refs_6_.refs_3_, ...), custom_call_target="tpu_custom_call" | custom-call | flops 33554432 | bytes 4194304 | tf_op jit(solution)/shard_map/near/pallas_call | solution.py:461
  28.6 4.2 %near.3.refs_5_ = f32[8,8,128]{2,1,0:T(8,128)S(1)} custom-call(s32[8,16]{1,0:T(8,128)} %bitcast.2, bf16[128,128]{1,0:T(8,128)(2,1)S(1)} %get-tuple-element.21.refs_5_.refs_1_, bf16[16,8,2,128,128]{4,3,2,1,0:T(8,128)(2,1)} %refs_2_.7, bf16[128,128]{1,0:T(8,128)(2,1)S(1)} %get-tuple-element.27.refs_3_.refs_0_, ...), custom_call_target="tpu_custom_call" | custom-call | flops 33554432 | bytes 4194304 | tf_op jit(solution)/shard_map/near/pallas_call | solution.py:461
  32.8 0.0 collective-permute-done.5.refs_1_
  32.8 0.0 collective-permute-done.6.refs_2_
  32.8 0.0 collective-permute-done.7.refs_3_
  32.8 0.0 copy-done
  32.8 1.0 %final.1 = f32[16,2,4,128]{3,2,1,0:T(4,128)} custom-call(bf16[128,128]{1,0:T(8,128)(2,1)S(1)} %get-tuple-element.27.refs_3_.refs_0_, bf16[128,128]{1,0:T(8,128)(2,1)S(1)} %collective-permute-done.5.refs_1_, bf16[128,128]{1,0:T(8,128)(2,1)S(1)} %collective-permute-done.6.refs_2_, bf16[128,128]{1,0:T(8,128)(2,1)S(1)} %collective-permute-done.7.refs_3_, ...), custom_call_target="tpu_custom_call" | custom-call | tf_op jit(solution)/shard_map/final/pallas_call | solution.py:515
Async XLA Ops:
  1.9 10.8 %collective-permute-start = (bf16[208,128]{1,0:T(8,128)(2,1)S(1)}, bf16[208,128]{1,0:T(8,128)(2,1)S(1)}, u32[]{:S(2)}, u32[]{:S(2)}) collective-permute-start(bf16[208,128]{1,0:T(8,128)(2,1)S(1)} %get-tuple-element.19), channel_id=1, source_target_pairs={{0,1},{1,0},{2,3},{3,2},{4,5},{5,4},{6,7},{7,6},{8,9},{9,8},{10,11... | collective-permute-start | bytes 159752 | tf_op jit(solution)/shard_map/ppermute | solution.py:407
  4.9 7.7 %collective-permute-start.2 = (bf16[208,128]{1,0:T(8,128)(2,1)S(1)}, bf16[208,128]{1,0:T(8,128)(2,1)S(1)}, u32[]{:S(2)}, u32[]{:S(2)}) collective-permute-start(bf16[208,128]{1,0:T(8,128)(2,1)S(1)} %get-tuple-element.20), channel_id=1, source_target_pairs={{0,3},{1,2},{2,1},{3,0},{4,7},{5,6},{6,5},{7,4},{8,11},{9,10},{10,... | collective-permute-start | bytes 159752 | tf_op jit(solution)/shard_map/ppermute | solution.py:407
  7.4 5.3 %collective-permute-start.1 = (bf16[144,128]{1,0:T(8,128)(2,1)S(1)}, bf16[144,128]{1,0:T(8,128)(2,1)S(1)}, u32[]{:S(2)}, u32[]{:S(2)}) collective-permute-start(bf16[144,128]{1,0:T(8,128)(2,1)S(1)} %get-tuple-element.18.refs_0_), channel_id=1, source_target_pairs={{0,2},{1,3},{2,0},{3,1},{4,6},{5,7},{6,4},{7,5},{8,10},{9,11},{10,... | collective-permute-start | bytes 110600 | tf_op jit(solution)/shard_map/ppermute | solution.py:407
  13.4 5.6 %collective-permute-start.3 = (bf16[80,512]{1,0:T(8,128)(2,1)S(1)}, bf16[80,512]{1,0:T(8,128)(2,1)S(1)}, u32[]{:S(2)}, u32[]{:S(2)}) collective-permute-start(bf16[80,512]{1,0:T(8,128)(2,1)S(1)} %get-tuple-element.24.refs_0_), channel_id=1, source_target_pairs={{0,28},{4,8},{8,4},{12,16},{16,12},{20,24},{24,20},{28,0},{1,29},{... | collective-permute-start | bytes 245768 | tf_op jit(solution)/shard_map/ppermute | solution.py:455
  14.2 4.8 %collective-permute-start.4 = (bf16[80,512]{1,0:T(8,128)(2,1)S(1)}, bf16[80,512]{1,0:T(8,128)(2,1)S(1)}, u32[]{:S(2)}, u32[]{:S(2)}) collective-permute-start(bf16[80,512]{1,0:T(8,128)(2,1)S(1)} %get-tuple-element.24.refs_0_), channel_id=1, source_target_pairs={{0,4},{4,0},{8,12},{12,8},{16,20},{20,16},{24,28},{28,24},{1,5},{5... | collective-permute-start | bytes 245768 | tf_op jit(solution)/shard_map/ppermute | solution.py:458
  19.8 13.0 %collective-permute-start.5 = (bf16[128,128]{1,0:T(8,128)(2,1)S(1)}, bf16[128,128]{1,0:T(8,128)(2,1)S(1)}, u32[]{:S(2)}, u32[]{:S(2)}) collective-permute-start(bf16[128,128]{1,0:T(8,128)(2,1)S(1)} %get-tuple-element.28), channel_id=1, source_target_pairs={{0,1},{1,0},{2,3},{3,2},{4,5},{5,4},{6,7},{7,6},{8,9},{9,8},{10,11... | collective-permute-start | bytes 98312 | tf_op jit(solution)/shard_map/ppermute | solution.py:407
  20.2 12.6 %collective-permute-start.6 = (bf16[128,128]{1,0:T(8,128)(2,1)S(1)}, bf16[128,128]{1,0:T(8,128)(2,1)S(1)}, u32[]{:S(2)}, u32[]{:S(2)}) collective-permute-start(bf16[128,128]{1,0:T(8,128)(2,1)S(1)} %get-tuple-element.29), channel_id=1, source_target_pairs={{0,2},{1,3},{2,0},{3,1},{4,6},{5,7},{6,4},{7,5},{8,10},{9,11},{10,... | collective-permute-start | bytes 98312 | tf_op jit(solution)/shard_map/ppermute | solution.py:407
  22.4 10.4 %collective-permute-start.7 = (bf16[128,128]{1,0:T(8,128)(2,1)S(1)}, bf16[128,128]{1,0:T(8,128)(2,1)S(1)}, u32[]{:S(2)}, u32[]{:S(2)}) collective-permute-start(bf16[128,128]{1,0:T(8,128)(2,1)S(1)} %get-tuple-element.30), channel_id=1, source_target_pairs={{0,3},{1,2},{2,1},{3,0},{4,7},{5,6},{6,5},{7,4},{8,11},{9,10},{10,... | collective-permute-start | bytes 98312 | tf_op jit(solution)/shard_map/ppermute | solution.py:407
  24.3 8.6 %copy-start = (bf16[16,2,128,128]{3,2,1,0:T(8,128)(2,1)S(1)}, bf16[16,2,128,128]{3,2,1,0:T(8,128)(2,1)}, u32[]{:S(2)}) copy-start(bf16[16,2,128,128]{3,2,1,0:T(8,128)(2,1)} %refs_6_.1) | copy-start | bytes 3145732

commit v5 on v4

--- a/solution.py
+++ b/solution.py
@@ -149,9 +149,15 @@
     return [d for d in range(-parents, parents + 1) if abs(d) >= 2]
 
 
+def half_of(mats, late):
+    count = mats.shape[0]
+    odd = lax.rem(lax.axis_index("samp"), 2)
+    return pl.ds(count * (odd if late else 1 - odd), count)
+
+
 def prep_kernel(
-    inter, trans, table_hbm, interp_hbm, phase_hbm, after, dense, interp_ref, phase_ref,
-    inter_s, trans_s, table, sems, *, parents, all_parents,
+    inter, trans, table_hbm, interp_hbm, phase_hbm, neighbours, mats_hbm, after,
+    dense, interp_ref, phase_ref, nbr, mats, inter_s, trans_s, table, sems, *, parents, all_parents,
 ):
     samples = interp_ref.shape[0]
     mine = pl.ds(pl.multiple_of(lax.axis_index("samp") * samples, samples), samples)
@@ -161,10 +167,12 @@
         pltpu.make_async_copy(table_hbm, table, sems.at[2]),
         pltpu.make_async_copy(interp_hbm.at[mine], interp_ref, sems.at[3]),
         pltpu.make_async_copy(phase_hbm.at[:, :, mine], phase_ref, sems.at[4]),
+        pltpu.make_async_copy(neighbours, nbr, sems.at[5]),
+        pltpu.make_async_copy(mats_hbm.at[half_of(mats, False)], mats, sems.at[6]),
     ]
     for copy in copies:
         copy.start()
-    for copy in copies:
+    for copy in copies[:3]:
         copy.wait()
     if len(zone(parents)) > inter.shape[1]:
         dense[...] = jnp.zeros_like(dense)
@@ -178,10 +186,12 @@
         return carry
 
     lax.fori_loop(0, parents, fill, 0)
+    for copy in copies[3:]:
+        copy.wait()
 
 
 def down_kernel(
-    own, across, beside, dense, interp_ref, phase_ref, place_ref, *refs, pieces, boxes, parents, parts
+    own, across, beside, dense, interp_ref, phase_ref, place_ref, after, *refs, pieces, boxes, parents, parts
 ):
     outs = refs[:pieces]
     window, incoming, shifted = refs[pieces:]
@@ -242,39 +252,26 @@
             ]
 
 
-def near_kernel(
-    neighbours, own, mats_hbm, after, *refs, late, nsamp, total, halo_rows, parent_rows
-):
-    far = nsamp.bit_length() - 2
-    from_beside, from_far, refs = refs[0], refs[1 : 1 + far], refs[1 + far :]
+def near_kernel(*refs, late, nsamp, total, halo_rows, parent_rows):
     if late:
-        across, beside, refs = refs[0], refs[1], refs[2:]
-    out_ref, window, mats, nbr, sems = refs
+        neighbours, own, mats, after, across, beside, *from_far, out_ref, window, nbr, sems = refs
+    else:
+        neighbours, own, mats, after, from_beside, mats_hbm, out_ref, more, window, nbr, sems = refs
+        fetch = pltpu.make_async_copy(mats_hbm.at[half_of(more, True)], more, sems.at[1])
+        fetch.start()
+    list_copy = pltpu.make_async_copy(neighbours, nbr, sems.at[0])
+    list_copy.start()
     count, parts, unknowns = out_ref.shape
     boxes = own.shape[0] // parts
     near_count = mats.shape[1]
     samp = lax.axis_index("samp")
     box = lax.axis_index("box")
-    odd = lax.rem(samp, 2) == 1
-    final = samp == nsamp - 1
-    upper = jnp.logical_not(final) if not late else final
-    first = jnp.where(upper, boxes - count, 0)
-    list_copy = pltpu.make_async_copy(neighbours, nbr, sems.at[count])
-    list_copy.start()
-    copies = [
-        pltpu.make_async_copy(mats_hbm.at[first + i], mats.at[i], sems.at[i]) for i in range(count)
-    ]
-    for copy in copies:
-        copy.start()
+    odd = lax.rem(samp, 2)
+    first = count * (odd if late else 1 - odd)
 
     def piece(ref):
         return ref[ref.shape[0] - halo_rows :].astype(F32)
 
-    distant = piece(from_far[0])
-    step = samp ^ (samp - 1) if late else samp ^ (samp + 1)
-    for i in range(1, far):
-        distant = jnp.where(step == (4 << i) - 1, piece(from_far[i]), distant)
-    near_by = piece(from_beside)
     if late:
         def forwarded(ref):
             return jnp.concatenate(
@@ -285,14 +282,17 @@
                 axis=0,
             )
 
+        partner = samp ^ (samp - 1 + 2 * odd)
+        halo = piece(from_far[0])
+        for i in range(1, len(from_far)):
+            halo = jnp.where(partner == (4 << i) - 1, piece(from_far[i]), halo)
         box_odd = lax.rem(box, 2) == 1
         from_left = samp == 0
         passed = jnp.where(box_odd == from_left, forwarded(beside), forwarded(across))
-        halo = jnp.where(odd, near_by, distant)
-        halo = jnp.where(jnp.logical_or(from_left, final), passed, halo)
+        halo = jnp.where(jnp.logical_or(from_left, samp == nsamp - 1), passed, halo)
     else:
-        halo = jnp.where(jnp.logical_and(odd, jnp.logical_not(final)), distant, near_by)
-    at = jnp.where(upper, boxes + count, 0)
+        halo = piece(from_beside)
+    at = jnp.where(first > 0, boxes + count, 0)
     for i in range(count):
         window[at + i] = widen(halo[i * parts : (i + 1) * parts])
     mine = own[...].astype(F32)
@@ -301,7 +301,6 @@
     list_copy.wait()
     base = (box * nsamp + samp) * boxes
     for i in range(count):
-        copies[i].wait()
         acc = None
         for k in range(near_count):
             j = lax.rem(nbr[k, first + i] - base + count + total, total)
@@ -309,6 +308,8 @@
             y = nt_dot(window[j].astype(BF16), mat)
             acc = y if acc is None else acc + y
         out_ref[i] = acc
+    if not late:
+        fetch.wait()
 
 
 def final_kernel(*refs, pieces):
@@ -317,7 +318,7 @@
     boxes, halves, rhs = out_ref.shape[:3]
     parts = halves * rhs
     half = boxes // 2
-    flip = lax.axis_index("samp") == lax.axis_size("samp") - 1
+    odd = lax.rem(lax.axis_index("samp"), 2) == 1
     total = parts_in[0][...].astype(F32)
     for m in parts_in[1:]:
         total += m[...].astype(F32)
@@ -327,7 +328,7 @@
         wide = jnp.concatenate([v, times_i(v)], axis=1).astype(BF16)
         y = nt_dot(wide, jnp.concatenate([mats[n, 0], mats[n, 1]], axis=1))
         i = n % half
-        y = y + jnp.where(flip == (n < half), near_early[i], near_late[i])
+        y = y + jnp.where(odd == (n < half), near_early[i], near_late[i])
         out_ref[n, 0] = y[:rhs]
         out_ref[n, 1] = y[rhs:]
 
@@ -412,27 +413,34 @@
         messages[d] = exchange(to_beside if d == 1 else to_far if d in far else plain, d)
     far_messages = [messages[d] for d in far]
 
-    dense, my_interp, my_phases = pl.pallas_call(
+    dense, my_interp, my_phases, near_list, mats_early = pl.pallas_call(
         lambda *refs: prep_kernel(*refs, parents=parents, all_parents=all_parents),
-        in_specs=[whole_in(HBM)] * 5 + [whole_in(VM)],
-        out_specs=[whole_in(VM)] * 3,
+        in_specs=[whole_in(HBM)] * 7 + [whole_in(VM)],
+        out_specs=[whole_in(VM)] * 5,
         out_shape=[
             shape((parents, len(zone(parents)), 2, samples), F32),
             shape((samples, LANES)),
             shape((8, 2, samples), F32),
+            shape((near_count, boxes), jnp.int32),
+            shape((reach,) + near_blocks.shape[1:]),
         ],
         scratch_shapes=[
             SM(inter_list.shape, jnp.int32),
             SM(trans_id.shape, jnp.int32),
             VM(translators.shape, F32),
-            DMA((5,)),
+            DMA((7,)),
         ],
         compiler_params=PARAMS,
         cost_estimate=pl.CostEstimate(
             flops=0, bytes_accessed=4 * 1024 * 1024, transcendentals=0
         ),
         name="prep",
-    )(*[stay(a) for a in (inter_list, trans_id, translators, interp, phases)], x_rows)
+    )(
+        *[stay(a) for a in (inter_list, trans_id, translators, interp, phases)],
+        stay(neighbours.T),
+        stay(near_blocks),
+        x_rows,
+    )
 
     parent_pat, place_onehot = pl.pallas_call(
         lambda *refs: up_kernel(
@@ -457,7 +465,12 @@
     )
     beside = lax.ppermute(parent_pat, "box", [(i, i ^ 1) for i in range(nbox)])
 
-    def near_half(late, after, sources):
+    def near_half(late, args):
+        out_shape = [shape((reach, parts, unknowns), F32)]
+        in_specs = [whole_in(VM)] * len(args)
+        if not late:
+            out_shape.append(shape(mats_early.shape))
+            in_specs[-1] = whole_in(HBM)
         return pl.pallas_call(
             lambda *refs: near_kernel(
                 *refs,
@@ -467,15 +480,13 @@
                 halo_rows=halo_rows,
                 parent_rows=parent_rows,
             ),
-            in_specs=[whole_in(HBM), whole_in(VM), whole_in(HBM), whole_in(VM)]
-            + [whole_in(VM)] * len(sources),
-            out_specs=whole_in(VM),
-            out_shape=shape((reach, parts, unknowns), F32),
+            in_specs=[whole_in(VM)] * 2 + in_specs,
+            out_specs=[whole_in(VM)] * len(out_shape),
+            out_shape=out_shape,
             scratch_shapes=[
                 VM((boxes + 2 * reach, parts, 2 * unknowns), F32),
-                VM((reach,) + near_blocks.shape[1:], BF16),
                 SM((near_count, boxes), jnp.int32),
-                DMA((reach + 1,)),
+                DMA((2,)),
             ],
             compiler_params=PARAMS,
             cost_estimate=pl.CostEstimate(
@@ -484,15 +495,17 @@
                 transcendentals=0,
             ),
             name="near",
-        )(stay(neighbours.T), x_rows, stay(near_blocks), after, *sources)
-
-    near_early = near_half(False, place_onehot, [messages[1], *far_messages])
+        )(near_list, x_rows, *args)
+
+    near_early, mats_late = near_half(
+        False, [mats_early, place_onehot, messages[1], stay(near_blocks)]
+    )
 
     fields = pl.pallas_call(
         lambda *refs: down_kernel(
             *refs, pieces=nsamp, boxes=boxes, parents=parents, parts=parts
         ),
-        in_specs=[whole_in(VM)] * 7,
+        in_specs=[whole_in(VM)] * 8,
         out_specs=[whole_in(VM)] * nsamp,
         out_shape=[shape((parts * boxes, LANES))] * nsamp,
         scratch_shapes=[
@@ -502,15 +515,13 @@
         ],
         compiler_params=PARAMS,
         name="down",
-    )(parent_pat, across, beside, dense, my_interp, my_phases, place_onehot)
+    )(parent_pat, across, beside, dense, my_interp, my_phases, place_onehot, near_early)
 
     partial = [fields[0]] + [None] * (nsamp - 1)
     for d in reversed(range(1, nsamp)):
         partial[d] = exchange(fields[d], d)
 
-    near_late = near_half(
-        True, fields[0], [messages[1], *far_messages, across, beside]
-    )
+    (near_late,) = near_half(True, [mats_late, fields[0], across, beside, *far_messages])
 
     return pl.pallas_call(
         lambda *refs: final_kernel(*refs, pieces=nsamp),

time: 34.1 us -> 28.9 us (0.85)
  Pallas kernels: 14.6 us -> 10.8 us
  waiting for transfers between devices: 7.44 us -> 5.01 us
  starting transfers between devices: 11.8 us -> 12.8 us
    pallas_call x2, Pallas kernels: 8.53 us -> 4.03 us  [near_half(): pl.pallas_call(lambda *refs: near_kernel(*refs, late=late, nsamp=nsamp, t...]
    ppermute x1, waiting for transfers between devices: 3.94 us -> 0.29 us  [on_device(): lax.ppermute(parent_pat, 'box', [(i, (i + (1 if i % 2 else -1)) % nbox) f...]
    ppermute x1, starting transfers between devices: 0.83 us -> 2.55 us  [on_device(): lax.ppermute(parent_pat, 'box', [(i, (i + (1 if i % 2 else -1)) % nbox) f...]
    ppermute x6, waiting for transfers between devices: 3.5 us -> 4.72 us  [exchange(): return lax.ppermute(x, 'samp', [(i, i ^ d) for i in range(nsamp)])]
    pallas_call x1, Pallas kernels: 1.64 us -> 2.44 us  [on_device(): pl.pallas_call(lambda *refs: prep_kernel(*refs, parents=parents, all_pare...]
    ppermute x1, starting transfers between devices: 0.84 us -> 0.07 us  [on_device(): beside = lax.ppermute(parent_pat, 'box', [(i, i ^ 1) for i in range(nbox)])]
  transfers between devices with their start and end apart: 8 -> 8, of which waited for: 2 -> 3; matrix products, arithmetic and copies ran while one was open for 0% -> 0% of each run, Pallas kernels for 30% -> 23%
where the time goes in v5:
time: 28.9 us; the launch traced here: 28.7 us
  starting transfers between devices  12.8 us (44%)
  Pallas kernels  10.8 us (37%)
  waiting for transfers between devices  5.01 us (17%)
    ppermute x6, starting transfers between devices, exchange(): return lax.ppermute(x, 'samp', [(i, i ^ d) for i in range(nsamp)])  10.1 us
    ppermute x6, waiting for transfers between devices, exchange(): return lax.ppermute(x, 'samp', [(i, i ^ d) for i in range(nsamp)])  4.72 us
    pallas_call x2, Pallas kernels, near_half(): pl.pallas_call(lambda *refs: near_kernel(*refs, late=late, nsamp=nsamp, t...  4.03 us
    ppermute x1, starting transfers between devices, on_device(): lax.ppermute(parent_pat, 'box', [(i, (i + (1 if i % 2 else -1)) % nbox) f...  2.55 us
    pallas_call x1, Pallas kernels, on_device(): pl.pallas_call(lambda *refs: prep_kernel(*refs, parents=parents, all_pare...  2.44 us
    pallas_call x1, Pallas kernels, on_device(): pl.pallas_call(lambda *refs: leaf_kernel(*refs, parents=parents), in_spec...  1.85 us
    pallas_call x1, Pallas kernels, on_device(): pl.pallas_call(lambda *refs: final_kernel(*refs, pieces=nsamp), in_specs=...  1.03 us
    pallas_call x1, Pallas kernels, on_device(): pl.pallas_call(lambda *refs: down_kernel(*refs, pieces=nsamp, boxes=boxes...  0.82 us
  transfers between devices with their start and end apart: 8, of which 3 were waited for; matrix products, arithmetic and copies ran while one was open for 0% of the time, Pallas kernels for 23%

profile of v5, /device:TPU:0, one launch (start us, length us, event | category | flops | bytes accessed | tf_op | source)
XLA Modules:
  0.0 28.7 jit_solution(1730799642581921792)
XLA Ops:
  0.0 1.9 %leaf.1 = (bf16[144,128]{1,0:T(8,128)(2,1)S(1)}, bf16[208,128]{1,0:T(8,128)(2,1)S(1)}, bf16[208,128]{1,0:T(8,128)(2,1)S(1)}, bf16[128,128]{1,0:T(8,128)(2,1)S(1)}) custom-call(s32[16]{0:T(128)} %refs_0_.2, s32[16]{0:T(128)} %refs_1_.2, bf16[16,2,4,128]{3,2,1,0:T(4,128)(2,1)} %refs_2_.2, bf16[16,2,128,128]{3,2,1,0:T(8,128)(2,1)} %refs_3_.2), custom_call_target="tpu_custom_call" | custom-call | tf_op jit(solution)/shard_map/leaf/pallas_call | solution.py:385
  1.9 3.1 %collective-permute-start = (bf16[208,128]{1,0:T(8,128)(2,1)S(1)}, bf16[208,128]{1,0:T(8,128)(2,1)S(1)}, u32[]{:S(2)}, u32[]{:S(2)}) collective-permute-start(bf16[208,128]{1,0:T(8,128)(2,1)S(1)} %get-tuple-element.23), channel_id=1, source_target_pairs={{0,1},{1,0},{2,3},{3,2},{4,5},{5,4},{6,7},{7,6},{8,9},{9,8},{10,11... | collective-permute-start | bytes 159752 | tf_op jit(solution)/shard_map/ppermute | solution.py:408
  4.9 2.5 %collective-permute-start.2 = (bf16[208,128]{1,0:T(8,128)(2,1)S(1)}, bf16[208,128]{1,0:T(8,128)(2,1)S(1)}, u32[]{:S(2)}, u32[]{:S(2)}) collective-permute-start(bf16[208,128]{1,0:T(8,128)(2,1)S(1)} %get-tuple-element.24), channel_id=1, source_target_pairs={{0,3},{1,2},{2,1},{3,0},{4,7},{5,6},{6,5},{7,4},{8,11},{9,10},{10,... | collective-permute-start | bytes 159752 | tf_op jit(solution)/shard_map/ppermute | solution.py:408
  7.4 0.1 collective-permute-start.1
  7.5 2.4 %prep.1 = (f32[8,14,2,512]{3,2,1,0:T(2,128)S(1)}, bf16[512,128]{1,0:T(8,128)(2,1)S(1)}, f32[8,2,512]{2,1,0:T(2,128)S(1)}, s32[8,16]{1,0:T(8,128)S(1)}, bf16[8,8,2,128,128]{4,3,2,1,0:T(8,128)(2,1)S(1)}) custom-call(s32[8,14]{1,0:T(8,128)} %refs_0_.3, s32[8,14]{1,0:T(8,128)} %refs_1_.3, f32[64,2,512]{2,1,0:T(2,128)} %refs_2_.3, bf16[2048,128]{1,0:T(8,128)(2,1)} %refs_3_.3, ...), custom_call_target="tpu_custom_call" | custom-call | bytes 4194304 | tf_op jit(solution)/shard_map/prep/pallas_call | solution.py:416
  10.0 2.7 %collective-permute-done.1.refs_2_ = bf16[144,128]{1,0:T(8,128)(2,1)S(1)} collective-permute-done((bf16[144,128]{1,0:T(8,128)(2,1)S(1)}, bf16[144,128]{1,0:T(8,128)(2,1)S(1)}, u32[]{:S(2)}, u32[]{:S(2)}) %collective-permute-start.1) | collective-permute-done | bytes 36896 | tf_op jit(solution)/shard_map/ppermute | solution.py:408
  12.7 0.0 collective-permute-done.refs_1_.refs_4_
  12.7 0.0 collective-permute-done.2.refs_3_.refs_6_
  12.7 0.7 %up.1 = (bf16[80,512]{1,0:T(8,128)(2,1)S(1)}, bf16[64,64]{1,0:T(8,128)(2,1)S(1)}) custom-call(bf16[144,128]{1,0:T(8,128)(2,1)S(1)} %get-tuple-element.22.refs_0_, bf16[208,128]{1,0:T(8,128)(2,1)S(1)} %collective-permute-done.refs_1_.refs_4_, bf16[144,128]{1,0:T(8,128)(2,1)S(1)} %collective-permute-done.1.refs_2_, ...), custom_call_target="tpu_custom_call" | custom-call | tf_op jit(solution)/shard_map/up/pallas_call | solution.py:445
  13.4 0.1 collective-permute-start.4
  13.4 2.5 %collective-permute-start.3 = (bf16[80,512]{1,0:T(8,128)(2,1)S(1)}, bf16[80,512]{1,0:T(8,128)(2,1)S(1)}, u32[]{:S(2)}, u32[]{:S(2)}) collective-permute-start(bf16[80,512]{1,0:T(8,128)(2,1)S(1)} %get-tuple-element.28.refs_0_), channel_id=1, source_target_pairs={{0,28},{4,8},{8,4},{12,16},{16,12},{20,24},{24,20},{28,0},{1,29},{... | collective-permute-start | bytes 245768 | tf_op jit(solution)/shard_map/ppermute | solution.py:463
  16.0 2.2 %near.2 = (f32[8,8,128]{2,1,0:T(8,128)S(1)}, bf16[8,8,2,128,128]{4,3,2,1,0:T(8,128)(2,1)S(1)}) custom-call(s32[8,16]{1,0:T(8,128)S(1)} %get-tuple-element.31.refs_0_, bf16[128,128]{1,0:T(8,128)(2,1)S(1)} %get-tuple-element.25.refs_7_.refs_1_, bf16[8,8,2,128,128]{4,3,2,1,0:T(8,128)(2,1)S(1)} %get-tuple-element.32.refs_2_, ...), custom_call_target="tpu_custom_call" | custom-call | flops 33554432 | bytes 4194304 | tf_op jit(solution)/shard_map/near/pallas_call | solution.py:474
  18.2 0.0 copy-start
  18.2 0.0 collective-permute-done.4.refs_2_.refs_5_
  18.2 0.3 %collective-permute-done.3.refs_1_.refs_4_ = bf16[80,512]{1,0:T(8,128)(2,1)S(1)} collective-permute-done((bf16[80,512]{1,0:T(8,128)(2,1)S(1)}, bf16[80,512]{1,0:T(8,128)(2,1)S(1)}, u32[]{:S(2)}, u32[]{:S(2)}) %collective-permute-start.3) | collective-permute-done | bytes 81952 | tf_op jit(solution)/shard_map/ppermute | solution.py:463
  18.5 0.8 %down.1 = (bf16[128,128]{1,0:T(8,128)(2,1)S(1)}, bf16[128,128]{1,0:T(8,128)(2,1)S(1)}, bf16[128,128]{1,0:T(8,128)(2,1)S(1)}, bf16[128,128]{1,0:T(8,128)(2,1)S(1)}) custom-call(bf16[80,512]{1,0:T(8,128)(2,1)S(1)} %get-tuple-element.28.refs_0_, bf16[80,512]{1,0:T(8,128)(2,1)S(1)} %collective-permute-done.3.refs_1_.refs_4_, ...), custom_call_target="tpu_custom_call" | custom-call | tf_op jit(solution)/shard_map/down/pallas_call | solution.py:504
  19.4 0.4 %collective-permute-start.5 = (bf16[128,128]{1,0:T(8,128)(2,1)S(1)}, bf16[128,128]{1,0:T(8,128)(2,1)S(1)}, u32[]{:S(2)}, u32[]{:S(2)}) collective-permute-start(bf16[128,128]{1,0:T(8,128)(2,1)S(1)} %get-tuple-element.35), channel_id=1, source_target_pairs={{0,1},{1,0},{2,3},{3,2},{4,5},{5,4},{6,7},{7,6},{8,9},{9,8},{10,11... | collective-permute-start | bytes 98312 | tf_op jit(solution)/shard_map/ppermute | solution.py:408
  19.8 2.2 %collective-permute-start.6 = (bf16[128,128]{1,0:T(8,128)(2,1)S(1)}, bf16[128,128]{1,0:T(8,128)(2,1)S(1)}, u32[]{:S(2)}, u32[]{:S(2)}) collective-permute-start(bf16[128,128]{1,0:T(8,128)(2,1)S(1)} %get-tuple-element.36), channel_id=1, source_target_pairs={{0,2},{1,3},{2,0},{3,1},{4,6},{5,7},{6,4},{7,5},{8,10},{9,11},{10,... | collective-permute-start | bytes 98312 | tf_op jit(solution)/shard_map/ppermute | solution.py:408
  22.0 1.8 %collective-permute-start.7 = (bf16[128,128]{1,0:T(8,128)(2,1)S(1)}, bf16[128,128]{1,0:T(8,128)(2,1)S(1)}, u32[]{:S(2)}, u32[]{:S(2)}) collective-permute-start(bf16[128,128]{1,0:T(8,128)(2,1)S(1)} %get-tuple-element.37), channel_id=1, source_target_pairs={{0,3},{1,2},{2,1},{3,0},{4,7},{5,6},{6,5},{7,4},{8,11},{9,10},{10,... | collective-permute-start | bytes 98312 | tf_op jit(solution)/shard_map/ppermute | solution.py:408
  23.8 1.8 %near.3.refs_5_ = f32[8,8,128]{2,1,0:T(8,128)S(1)} custom-call(s32[8,16]{1,0:T(8,128)S(1)} %get-tuple-element.31.refs_0_, bf16[128,128]{1,0:T(8,128)(2,1)S(1)} %get-tuple-element.25.refs_7_.refs_1_, bf16[8,8,2,128,128]{4,3,2,1,0:T(8,128)(2,1)S(1)} %get-tuple-element.38.refs_2_, bf16[128,128]{1,0:T(8,128)(2,1)S(1)} %get-tuple-element.34.refs_3_.refs_0_, ...), custom_call_target="tpu_custom_call" | custom-call | flops 33554432 | bytes 4194304 | tf_op jit(solution)/shard_map/near/pallas_call | solution.py:474
  25.6 0.0 collective-permute-done.5.refs_1_
  25.6 0.0 collective-permute-done.6.refs_2_
  25.7 2.0 %collective-permute-done.7.refs_3_ = bf16[128,128]{1,0:T(8,128)(2,1)S(1)} collective-permute-done((bf16[128,128]{1,0:T(8,128)(2,1)S(1)}, bf16[128,128]{1,0:T(8,128)(2,1)S(1)}, u32[]{:S(2)}, u32[]{:S(2)}) %collective-permute-start.7) | collective-permute-done | bytes 32800 | tf_op jit(solution)/shard_map/ppermute | solution.py:408
  27.7 0.0 copy-done
  27.7 1.0 %final.1 = f32[16,2,4,128]{3,2,1,0:T(4,128)} custom-call(bf16[128,128]{1,0:T(8,128)(2,1)S(1)} %get-tuple-element.34.refs_3_.refs_0_, bf16[128,128]{1,0:T(8,128)(2,1)S(1)} %collective-permute-done.5.refs_1_, bf16[128,128]{1,0:T(8,128)(2,1)S(1)} %collective-permute-done.6.refs_2_, bf16[128,128]{1,0:T(8,128)(2,1)S(1)} %collective-permute-done.7.refs_3_, ...), custom_call_target="tpu_custom_call" | custom-call | tf_op jit(solution)/shard_map/final/pallas_call | solution.py:526
Async XLA Ops:
  1.9 10.8 %collective-permute-start = (bf16[208,128]{1,0:T(8,128)(2,1)S(1)}, bf16[208,128]{1,0:T(8,128)(2,1)S(1)}, u32[]{:S(2)}, u32[]{:S(2)}) collective-permute-start(bf16[208,128]{1,0:T(8,128)(2,1)S(1)} %get-tuple-element.23), channel_id=1, source_target_pairs={{0,1},{1,0},{2,3},{3,2},{4,5},{5,4},{6,7},{7,6},{8,9},{9,8},{10,11... | collective-permute-start | bytes 159752 | tf_op jit(solution)/shard_map/ppermute | solution.py:408
  4.9 7.7 %collective-permute-start.2 = (bf16[208,128]{1,0:T(8,128)(2,1)S(1)}, bf16[208,128]{1,0:T(8,128)(2,1)S(1)}, u32[]{:S(2)}, u32[]{:S(2)}) collective-permute-start(bf16[208,128]{1,0:T(8,128)(2,1)S(1)} %get-tuple-element.24), channel_id=1, source_target_pairs={{0,3},{1,2},{2,1},{3,0},{4,7},{5,6},{6,5},{7,4},{8,11},{9,10},{10,... | collective-permute-start | bytes 159752 | tf_op jit(solution)/shard_map/ppermute | solution.py:408
  7.4 5.3 %collective-permute-start.1 = (bf16[144,128]{1,0:T(8,128)(2,1)S(1)}, bf16[144,128]{1,0:T(8,128)(2,1)S(1)}, u32[]{:S(2)}, u32[]{:S(2)}) collective-permute-start(bf16[144,128]{1,0:T(8,128)(2,1)S(1)} %get-tuple-element.22.refs_0_), channel_id=1, source_target_pairs={{0,2},{1,3},{2,0},{3,1},{4,6},{5,7},{6,4},{7,5},{8,10},{9,11},{10,... | collective-permute-start | bytes 110600 | tf_op jit(solution)/shard_map/ppermute | solution.py:408
  13.4 4.9 %collective-permute-start.4 = (bf16[80,512]{1,0:T(8,128)(2,1)S(1)}, bf16[80,512]{1,0:T(8,128)(2,1)S(1)}, u32[]{:S(2)}, u32[]{:S(2)}) collective-permute-start(bf16[80,512]{1,0:T(8,128)(2,1)S(1)} %get-tuple-element.28.refs_0_), channel_id=1, source_target_pairs={{0,4},{4,0},{8,12},{12,8},{16,20},{20,16},{24,28},{28,24},{1,5},{5... | collective-permute-start | bytes 245768 | tf_op jit(solution)/shard_map/ppermute | solution.py:466
  13.4 5.1 %collective-permute-start.3 = (bf16[80,512]{1,0:T(8,128)(2,1)S(1)}, bf16[80,512]{1,0:T(8,128)(2,1)S(1)}, u32[]{:S(2)}, u32[]{:S(2)}) collective-permute-start(bf16[80,512]{1,0:T(8,128)(2,1)S(1)} %get-tuple-element.28.refs_0_), channel_id=1, source_target_pairs={{0,28},{4,8},{8,4},{12,16},{16,12},{20,24},{24,20},{28,0},{1,29},{... | collective-permute-start | bytes 245768 | tf_op jit(solution)/shard_map/ppermute | solution.py:463
  18.2 9.5 %copy-start = (bf16[16,2,128,128]{3,2,1,0:T(8,128)(2,1)S(1)}, bf16[16,2,128,128]{3,2,1,0:T(8,128)(2,1)}, u32[]{:S(2)}) copy-start(bf16[16,2,128,128]{3,2,1,0:T(8,128)(2,1)} %refs_6_.3) | copy-start | bytes 3145732
  19.4 6.3 %collective-permute-start.5 = (bf16[128,128]{1,0:T(8,128)(2,1)S(1)}, bf16[128,128]{1,0:T(8,128)(2,1)S(1)}, u32[]{:S(2)}, u32[]{:S(2)}) collective-permute-start(bf16[128,128]{1,0:T(8,128)(2,1)S(1)} %get-tuple-element.35), channel_id=1, source_target_pairs={{0,1},{1,0},{2,3},{3,2},{4,5},{5,4},{6,7},{7,6},{8,9},{9,8},{10,11... | collective-permute-start | bytes 98312 | tf_op jit(solution)/shard_map/ppermute | solution.py:408
  19.8 5.8 %collective-permute-start.6 = (bf16[128,128]{1,0:T(8,128)(2,1)S(1)}, bf16[128,128]{1,0:T(8,128)(2,1)S(1)}, u32[]{:S(2)}, u32[]{:S(2)}) collective-permute-start(bf16[128,128]{1,0:T(8,128)(2,1)S(1)} %get-tuple-element.36), channel_id=1, source_target_pairs={{0,2},{1,3},{2,0},{3,1},{4,6},{5,7},{6,4},{7,5},{8,10},{9,11},{10,... | collective-permute-start | bytes 98312 | tf_op jit(solution)/shard_map/ppermute | solution.py:408
  22.0 5.7 %collective-permute-start.7 = (bf16[128,128]{1,0:T(8,128)(2,1)S(1)}, bf16[128,128]{1,0:T(8,128)(2,1)S(1)}, u32[]{:S(2)}, u32[]{:S(2)}) collective-permute-start(bf16[128,128]{1,0:T(8,128)(2,1)S(1)} %get-tuple-element.37), channel_id=1, source_target_pairs={{0,3},{1,2},{2,1},{3,0},{4,7},{5,6},{6,5},{7,4},{8,11},{9,10},{10,... | collective-permute-start | bytes 98312 | tf_op jit(solution)/shard_map/ppermute | solution.py:408

commit v6 on v5

--- a/solution.py
+++ b/solution.py
@@ -28,7 +28,7 @@
 
 
 def leaf_kernel(
-    octant, parent, x_hbm, lift_hbm, plain, to_beside, to_far, x_rows,
+    octant, parent, x_hbm, lift_hbm, to_far, plain, to_beside, x_rows,
     x_ref, rows, lift, oct_s, par_s, sems, *, parents,
 ):
     boxes, halves, rhs, _ = x_ref.shape
@@ -47,47 +47,43 @@
         )
         for i in range(chunks)
     ]
-    small[0].start()
-    for copy in big:
+    for copy in small + big:
         copy.start()
-    small[1].start()
-    small[2].start()
-    small[0].wait()
+    for copy in small:
+        copy.wait()
     own = [
         jnp.concatenate([x_ref[n, 0].astype(F32), x_ref[n, 1].astype(F32)], axis=0)
         for n in range(boxes)
     ]
+    lane = lax.rem(lax.broadcasted_iota(jnp.int32, (boxes, LANES), 1), boxes)
+    codes = jnp.zeros((boxes, LANES), F32)
+    for n in range(boxes):
+        slot = (oct_s[n] * parents + lax.rem(par_s[n], parents)).astype(F32)
+        codes = jnp.where(lane == n, slot, codes)
+    codes = codes.astype(BF16)
+    x_rows[...] = jnp.concatenate(own, axis=0).astype(BF16)
+    first = jnp.concatenate(own[:reach], axis=0)
+    last = jnp.concatenate(own[reach:], axis=0)
+    odd = lax.rem(lax.axis_index("samp"), 2) == 1
+    at = parts * boxes
+    to_beside[at + boxes :] = jnp.where(odd, first, last).astype(BF16)
+    to_far[at + boxes :] = jnp.where(odd, last, first).astype(BF16)
+    for ref in (plain, to_beside, to_far):
+        ref[at : at + boxes] = codes
     for n in range(boxes):
         if n % per == 0:
             big[n // per].wait()
         mat = jnp.concatenate([lift[n, 0], lift[n, 1]], axis=1)
         rows[pl.ds(n, parts, stride=boxes), :] = nt_dot(widen(own[n]).astype(BF16), mat)
-    small[1].wait()
-    small[2].wait()
-    lane = lax.rem(lax.broadcasted_iota(jnp.int32, (boxes, LANES), 1), boxes)
-    across = jnp.zeros((boxes, LANES), F32)
-    for n in range(boxes):
-        slot = (oct_s[n] * parents + lax.rem(par_s[n], parents)).astype(F32)
-        across = jnp.where(lane == n, slot, across)
     pattern = rows[...].astype(BF16)
-    codes = across.astype(BF16)
-    at = parts * boxes
     for ref in (plain, to_beside, to_far):
         ref[:at] = pattern
-        ref[at : at + boxes] = codes
-    at += boxes
-    x_rows[...] = jnp.concatenate(own, axis=0).astype(BF16)
-    first = jnp.concatenate(own[:reach], axis=0)
-    last = jnp.concatenate(own[reach:], axis=0)
-    odd = lax.rem(lax.axis_index("samp"), 2) == 1
-    to_beside[at:] = jnp.where(odd, first, last).astype(BF16)
-    to_far[at:] = jnp.where(odd, last, first).astype(BF16)
 
 
 def up_kernel(*refs, pieces, boxes, parents, parts):
     msgs = refs[:pieces]
-    interp_ref, phase_ref, out_ref, place_ref, raised, folded = refs[pieces:]
-    forward = msgs[-1]
+    interp_ref, phase_ref, out_ref, out_copy, place_ref, raised, folded = refs[pieces:]
+    forward = msgs[1]
     slots = 8 * parents
     samples = interp_ref.shape[0]
     per_tile = LANES // boxes
@@ -139,10 +135,13 @@
             both = jnp.concatenate(
                 [folded[t, pl.ds(p + e, parts, stride=parents), :] for e in range(2)], axis=0
             )
-            out_ref[p * parts : (p + 2) * parts, lanes] = both.astype(BF16)
+            both = both.astype(BF16)
+            for ref in (out_ref, out_copy):
+                ref[p * parts : (p + 2) * parts, lanes] = both
         extra = out_ref.shape[0] - parents * parts
         start = forward.shape[0] - extra * (samples // LANES - t)
-        out_ref[parents * parts :, lanes] = forward[start : start + extra]
+        for ref in (out_ref, out_copy):
+            ref[parents * parts :, lanes] = forward[start : start + extra]
 
 
 def zone(parents):
@@ -382,13 +381,13 @@
         return jax.ShapeDtypeStruct(dims, dtype)
 
     lift_chunks = 4
-    plain, to_beside, to_far, x_rows = pl.pallas_call(
+    to_far, plain, to_beside, x_rows = pl.pallas_call(
         lambda *refs: leaf_kernel(*refs, parents=parents),
         in_specs=[whole_in(HBM)] * 4,
         out_specs=[whole_in(VM)] * 4,
         out_shape=[
+            shape((plain_rows + halo_rows, LANES)),
             shape((plain_rows, LANES)),
-            shape((plain_rows + halo_rows, LANES)),
             shape((plain_rows + halo_rows, LANES)),
             shape((boxes * parts, LANES)),
         ],
@@ -407,9 +406,10 @@
     def exchange(x, d):
         return lax.ppermute(x, "samp", [(i, i ^ d) for i in range(nsamp)])
 
-    messages = [plain] + [None] * (nsamp - 1)
+    order = [0, *reversed(range(1, nsamp))]
     far = [(4 << i) - 1 for i in range(nsamp.bit_length() - 2)]
-    for d in reversed(range(1, nsamp)):
+    messages = {0: plain}
+    for d in order[1:]:
         messages[d] = exchange(to_beside if d == 1 else to_far if d in far else plain, d)
     far_messages = [messages[d] for d in far]
 
@@ -442,13 +442,14 @@
         x_rows,
     )
 
-    parent_pat, place_onehot = pl.pallas_call(
+    to_across, parent_pat, place_onehot = pl.pallas_call(
         lambda *refs: up_kernel(
             *refs, pieces=nsamp, boxes=boxes, parents=parents, parts=parts
         ),
         in_specs=[whole_in(VM)] * (nsamp + 2),
-        out_specs=[whole_in(VM)] * 2,
+        out_specs=[whole_in(VM)] * 3,
         out_shape=[
+            shape((parent_rows + halo_rows * LANES // samples, samples)),
             shape((parent_rows + halo_rows * LANES // samples, samples)),
             shape((leaves, slots)),
         ],
@@ -458,10 +459,10 @@
         ],
         compiler_params=PARAMS,
         name="up",
-    )(*messages, my_interp, my_phases)
+    )(*[messages[d] for d in order], my_interp, my_phases)
 
     across = lax.ppermute(
-        parent_pat, "box", [(i, (i + (1 if i % 2 else -1)) % nbox) for i in range(nbox)]
+        to_across, "box", [(i, (i + (1 if i % 2 else -1)) % nbox) for i in range(nbox)]
     )
     beside = lax.ppermute(parent_pat, "box", [(i, i ^ 1) for i in range(nbox)])
 
@@ -517,9 +518,7 @@
         name="down",
     )(parent_pat, across, beside, dense, my_interp, my_phases, place_onehot, near_early)
 
-    partial = [fields[0]] + [None] * (nsamp - 1)
-    for d in reversed(range(1, nsamp)):
-        partial[d] = exchange(fields[d], d)
+    partial = [fields[0]] + [exchange(x, d) for x, d in zip(fields[1:], order[1:])]
 
     (near_late,) = near_half(True, [mats_late, fields[0], across, beside, *far_messages])
 

time: 28.9 us -> 27.6 us (0.955)
  starting transfers between devices: 12.8 us -> 11.9 us
  waiting for transfers between devices: 5.01 us -> 4.65 us
    ppermute x1, starting transfers between devices: 2.55 us -> 0.36 us  [on_device(): lax.ppermute(to_across, 'box', [(i, (i + (1 if i % 2 else -1)) % nbox) fo...]
    ppermute x6, waiting for transfers between devices: 4.72 us -> 2.95 us  [exchange(): return lax.ppermute(x, 'samp', [(i, i ^ d) for i in range(nsamp)])]
    ppermute x1, waiting for transfers between devices: 0.29 us -> 1.69 us  [on_device(): lax.ppermute(to_across, 'box', [(i, (i + (1 if i % 2 else -1)) % nbox) fo...]
    ppermute x1, starting transfers between devices: 0.07 us -> 1.31 us  [on_device(): beside = lax.ppermute(parent_pat, 'box', [(i, i ^ 1) for i in range(nbox)])]
  transfers between devices with their start and end apart: 8 -> 8, of which waited for: 3 -> 4; matrix products, arithmetic and copies ran while one was open for 0% -> 0% of each run, Pallas kernels for 23% -> 24%
where the time goes in v6:
time: 27.6 us; the launch traced here: 27.4 us
  starting transfers between devices  11.9 us (43%)
  Pallas kernels  10.8 us (39%)
  waiting for transfers between devices  4.65 us (17%)
    ppermute x6, starting transfers between devices, exchange(): return lax.ppermute(x, 'samp', [(i, i ^ d) for i in range(nsamp)])  10.2 us
    pallas_call x2, Pallas kernels, near_half(): pl.pallas_call(lambda *refs: near_kernel(*refs, late=late, nsamp=nsamp, t...  4.03 us
    ppermute x6, waiting for transfers between devices, exchange(): return lax.ppermute(x, 'samp', [(i, i ^ d) for i in range(nsamp)])  2.95 us
    pallas_call x1, Pallas kernels, on_device(): pl.pallas_call(lambda *refs: prep_kernel(*refs, parents=parents, all_pare...  2.44 us
    pallas_call x1, Pallas kernels, on_device(): pl.pallas_call(lambda *refs: leaf_kernel(*refs, parents=parents), in_spec...  1.78 us
    ppermute x1, waiting for transfers between devices, on_device(): lax.ppermute(to_across, 'box', [(i, (i + (1 if i % 2 else -1)) % nbox) fo...  1.69 us
    ppermute x1, starting transfers between devices, on_device(): beside = lax.ppermute(parent_pat, 'box', [(i, i ^ 1) for i in range(nbox)])  1.31 us
    pallas_call x1, Pallas kernels, on_device(): pl.pallas_call(lambda *refs: final_kernel(*refs, pieces=nsamp), in_specs=...  1.03 us
  transfers between devices with their start and end apart: 8, of which 4 were waited for; matrix products, arithmetic and copies ran while one was open for 0% of the time, Pallas kernels for 24%

profile of v6, /device:TPU:0, one launch (start us, length us, event | category | flops | bytes accessed | tf_op | source)
XLA Modules:
  0.0 27.4 jit_solution(6498126655413614629)
XLA Ops:
  0.0 1.8 %leaf.1 = (bf16[208,128]{1,0:T(8,128)(2,1)S(1)}, bf16[144,128]{1,0:T(8,128)(2,1)S(1)}, bf16[208,128]{1,0:T(8,128)(2,1)S(1)}, bf16[128,128]{1,0:T(8,128)(2,1)S(1)}) custom-call(s32[16]{0:T(128)} %refs_0_.2, s32[16]{0:T(128)} %refs_1_.2, bf16[16,2,4,128]{3,2,1,0:T(4,128)(2,1)} %refs_2_.2, bf16[16,2,128,128]{3,2,1,0:T(8,128)(2,1)} %refs_3_.2), custom_call_target="tpu_custom_call" | custom-call | tf_op jit(solution)/shard_map/leaf/pallas_call | solution.py:384
  1.8 5.1 %collective-permute-start = (bf16[208,128]{1,0:T(8,128)(2,1)S(1)}, bf16[208,128]{1,0:T(8,128)(2,1)S(1)}, u32[]{:S(2)}, u32[]{:S(2)}) collective-permute-start(bf16[208,128]{1,0:T(8,128)(2,1)S(1)} %get-tuple-element.24), channel_id=1, source_target_pairs={{0,3},{1,2},{2,1},{3,0},{4,7},{5,6},{6,5},{7,4},{8,11},{9,10},{10,... | collective-permute-start | bytes 159752 | tf_op jit(solution)/shard_map/ppermute | solution.py:407
  6.9 0.0 collective-permute-start.2
  6.9 0.6 %collective-permute-start.1 = (bf16[144,128]{1,0:T(8,128)(2,1)S(1)}, bf16[144,128]{1,0:T(8,128)(2,1)S(1)}, u32[]{:S(2)}, u32[]{:S(2)}) collective-permute-start(bf16[144,128]{1,0:T(8,128)(2,1)S(1)} %get-tuple-element.23.refs_0_), channel_id=1, source_target_pairs={{0,2},{1,3},{2,0},{3,1},{4,6},{5,7},{6,4},{7,5},{8,10},{9,11},{10,... | collective-permute-start | bytes 110600 | tf_op jit(solution)/shard_map/ppermute | solution.py:407
  7.5 2.4 %prep.1 = (f32[8,14,2,512]{3,2,1,0:T(2,128)S(1)}, bf16[512,128]{1,0:T(8,128)(2,1)S(1)}, f32[8,2,512]{2,1,0:T(2,128)S(1)}, s32[8,16]{1,0:T(8,128)S(1)}, bf16[8,8,2,128,128]{4,3,2,1,0:T(8,128)(2,1)S(1)}) custom-call(s32[8,14]{1,0:T(8,128)} %refs_0_.3, s32[8,14]{1,0:T(8,128)} %refs_1_.3, f32[64,2,512]{2,1,0:T(2,128)} %refs_2_.3, bf16[2048,128]{1,0:T(8,128)(2,1)} %refs_3_.3, ...), custom_call_target="tpu_custom_call" | custom-call | bytes 4194304 | tf_op jit(solution)/shard_map/prep/pallas_call | solution.py:416
  10.0 1.9 %collective-permute-done.1.refs_2_ = bf16[144,128]{1,0:T(8,128)(2,1)S(1)} collective-permute-done((bf16[144,128]{1,0:T(8,128)(2,1)S(1)}, bf16[144,128]{1,0:T(8,128)(2,1)S(1)}, u32[]{:S(2)}, u32[]{:S(2)}) %collective-permute-start.1) | collective-permute-done | bytes 36896 | tf_op jit(solution)/shard_map/ppermute | solution.py:407
  11.9 0.0 collective-permute-done.refs_1_.refs_6_
  11.9 0.0 collective-permute-done.2.refs_3_.refs_4_
  11.9 0.7 %up.1 = (bf16[80,512]{1,0:T(8,128)(2,1)S(1)}, bf16[80,512]{1,0:T(8,128)(2,1)S(1)}, bf16[64,64]{1,0:T(8,128)(2,1)S(1)}) custom-call(bf16[144,128]{1,0:T(8,128)(2,1)S(1)} %get-tuple-element.23.refs_0_, bf16[208,128]{1,0:T(8,128)(2,1)S(1)} %collective-permute-done.refs_1_.refs_6_, bf16[144,128]{1,0:T(8,128)(2,1)S(1)} %collective-permute-done.1.refs_2_, ...), custom_call_target="tpu_custom_call" | custom-call | tf_op jit(solution)/shard_map/up/pallas_call | solution.py:445
  12.6 0.4 %collective-permute-start.3 = (bf16[80,512]{1,0:T(8,128)(2,1)S(1)}, bf16[80,512]{1,0:T(8,128)(2,1)S(1)}, u32[]{:S(2)}, u32[]{:S(2)}) collective-permute-start(bf16[80,512]{1,0:T(8,128)(2,1)S(1)} %get-tuple-element.30), channel_id=1, source_target_pairs={{0,28},{4,8},{8,4},{12,16},{16,12},{20,24},{24,20},{28,0},{1,29},{... | collective-permute-start | bytes 245768 | tf_op jit(solution)/shard_map/ppermute | solution.py:464
  13.0 1.3 %collective-permute-start.4 = (bf16[80,512]{1,0:T(8,128)(2,1)S(1)}, bf16[80,512]{1,0:T(8,128)(2,1)S(1)}, u32[]{:S(2)}, u32[]{:S(2)}) collective-permute-start(bf16[80,512]{1,0:T(8,128)(2,1)S(1)} %get-tuple-element.29.refs_0_), channel_id=1, source_target_pairs={{0,4},{4,0},{8,12},{12,8},{16,20},{20,16},{24,28},{28,24},{1,5},{5... | collective-permute-start | bytes 245768 | tf_op jit(solution)/shard_map/ppermute | solution.py:467
  14.3 2.2 %near.2 = (f32[8,8,128]{2,1,0:T(8,128)S(1)}, bf16[8,8,2,128,128]{4,3,2,1,0:T(8,128)(2,1)S(1)}) custom-call(s32[8,16]{1,0:T(8,128)S(1)} %get-tuple-element.33.refs_0_, bf16[128,128]{1,0:T(8,128)(2,1)S(1)} %get-tuple-element.26.refs_7_.refs_1_, bf16[8,8,2,128,128]{4,3,2,1,0:T(8,128)(2,1)S(1)} %get-tuple-element.34.refs_2_, ...), custom_call_target="tpu_custom_call" | custom-call | flops 33554432 | bytes 4194304 | tf_op jit(solution)/shard_map/near/pallas_call | solution.py:475
  16.5 0.0 copy-start
  16.5 1.7 %collective-permute-done.3.refs_1_.refs_4_ = bf16[80,512]{1,0:T(8,128)(2,1)S(1)} collective-permute-done((bf16[80,512]{1,0:T(8,128)(2,1)S(1)}, bf16[80,512]{1,0:T(8,128)(2,1)S(1)}, u32[]{:S(2)}, u32[]{:S(2)}) %collective-permute-start.3) | collective-permute-done | bytes 81952 | tf_op jit(solution)/shard_map/ppermute | solution.py:464
  18.2 0.0 collective-permute-done.4.refs_2_.refs_5_
  18.2 0.8 %down.1 = (bf16[128,128]{1,0:T(8,128)(2,1)S(1)}, bf16[128,128]{1,0:T(8,128)(2,1)S(1)}, bf16[128,128]{1,0:T(8,128)(2,1)S(1)}, bf16[128,128]{1,0:T(8,128)(2,1)S(1)}) custom-call(bf16[80,512]{1,0:T(8,128)(2,1)S(1)} %get-tuple-element.29.refs_0_, bf16[80,512]{1,0:T(8,128)(2,1)S(1)} %collective-permute-done.3.refs_1_.refs_4_, ...), custom_call_target="tpu_custom_call" | custom-call | tf_op jit(solution)/shard_map/down/pallas_call | solution.py:505
  19.1 1.9 %collective-permute-start.5 = (bf16[128,128]{1,0:T(8,128)(2,1)S(1)}, bf16[128,128]{1,0:T(8,128)(2,1)S(1)}, u32[]{:S(2)}, u32[]{:S(2)}) collective-permute-start(bf16[128,128]{1,0:T(8,128)(2,1)S(1)} %get-tuple-element.37), channel_id=1, source_target_pairs={{0,3},{1,2},{2,1},{3,0},{4,7},{5,6},{6,5},{7,4},{8,11},{9,10},{10,... | collective-permute-start | bytes 98312 | tf_op jit(solution)/shard_map/ppermute | solution.py:407
  21.0 1.5 %collective-permute-start.6 = (bf16[128,128]{1,0:T(8,128)(2,1)S(1)}, bf16[128,128]{1,0:T(8,128)(2,1)S(1)}, u32[]{:S(2)}, u32[]{:S(2)}) collective-permute-start(bf16[128,128]{1,0:T(8,128)(2,1)S(1)} %get-tuple-element.38), channel_id=1, source_target_pairs={{0,2},{1,3},{2,0},{3,1},{4,6},{5,7},{6,4},{7,5},{8,10},{9,11},{10,... | collective-permute-start | bytes 98312 | tf_op jit(solution)/shard_map/ppermute | solution.py:407
  22.4 1.1 %collective-permute-start.7 = (bf16[128,128]{1,0:T(8,128)(2,1)S(1)}, bf16[128,128]{1,0:T(8,128)(2,1)S(1)}, u32[]{:S(2)}, u32[]{:S(2)}) collective-permute-start(bf16[128,128]{1,0:T(8,128)(2,1)S(1)} %get-tuple-element.39), channel_id=1, source_target_pairs={{0,1},{1,0},{2,3},{3,2},{4,5},{5,4},{6,7},{7,6},{8,9},{9,8},{10,11... | collective-permute-start | bytes 98312 | tf_op jit(solution)/shard_map/ppermute | solution.py:407
  23.5 1.8 %near.3.refs_5_ = f32[8,8,128]{2,1,0:T(8,128)S(1)} custom-call(s32[8,16]{1,0:T(8,128)S(1)} %get-tuple-element.33.refs_0_, bf16[128,128]{1,0:T(8,128)(2,1)S(1)} %get-tuple-element.26.refs_7_.refs_1_, bf16[8,8,2,128,128]{4,3,2,1,0:T(8,128)(2,1)S(1)} %get-tuple-element.40.refs_2_, bf16[128,128]{1,0:T(8,128)(2,1)S(1)} %get-tuple-element.36.refs_3_.refs_0_, ...), custom_call_target="tpu_custom_call" | custom-call | flops 33554432 | bytes 4194304 | tf_op jit(solution)/shard_map/near/pallas_call | solution.py:475
  25.3 0.0 collective-permute-done.5.refs_1_
  25.3 0.4 %collective-permute-done.6.refs_2_ = bf16[128,128]{1,0:T(8,128)(2,1)S(1)} collective-permute-done((bf16[128,128]{1,0:T(8,128)(2,1)S(1)}, bf16[128,128]{1,0:T(8,128)(2,1)S(1)}, u32[]{:S(2)}, u32[]{:S(2)}) %collective-permute-start.6) | collective-permute-done | bytes 32800 | tf_op jit(solution)/shard_map/ppermute | solution.py:407
  25.8 0.6 %collective-permute-done.7.refs_3_ = bf16[128,128]{1,0:T(8,128)(2,1)S(1)} collective-permute-done((bf16[128,128]{1,0:T(8,128)(2,1)S(1)}, bf16[128,128]{1,0:T(8,128)(2,1)S(1)}, u32[]{:S(2)}, u32[]{:S(2)}) %collective-permute-start.7) | collective-permute-done | bytes 32800 | tf_op jit(solution)/shard_map/ppermute | solution.py:407
  26.4 0.0 copy-done
  26.4 1.0 %final.1 = f32[16,2,4,128]{3,2,1,0:T(4,128)} custom-call(bf16[128,128]{1,0:T(8,128)(2,1)S(1)} %get-tuple-element.36.refs_3_.refs_0_, bf16[128,128]{1,0:T(8,128)(2,1)S(1)} %collective-permute-done.5.refs_1_, bf16[128,128]{1,0:T(8,128)(2,1)S(1)} %collective-permute-done.6.refs_2_, bf16[128,128]{1,0:T(8,128)(2,1)S(1)} %collective-permute-done.7.refs_3_, ...), custom_call_target="tpu_custom_call" | custom-call | tf_op jit(solution)/shard_map/final/pallas_call | solution.py:525
Async XLA Ops:
  1.8 10.1 %collective-permute-start = (bf16[208,128]{1,0:T(8,128)(2,1)S(1)}, bf16[208,128]{1,0:T(8,128)(2,1)S(1)}, u32[]{:S(2)}, u32[]{:S(2)}) collective-permute-start(bf16[208,128]{1,0:T(8,128)(2,1)S(1)} %get-tuple-element.24), channel_id=1, source_target_pairs={{0,3},{1,2},{2,1},{3,0},{4,7},{5,6},{6,5},{7,4},{8,11},{9,10},{10,... | collective-permute-start | bytes 159752 | tf_op jit(solution)/shard_map/ppermute | solution.py:407
  6.9 5.0 %collective-permute-start.2 = (bf16[208,128]{1,0:T(8,128)(2,1)S(1)}, bf16[208,128]{1,0:T(8,128)(2,1)S(1)}, u32[]{:S(2)}, u32[]{:S(2)}) collective-permute-start(bf16[208,128]{1,0:T(8,128)(2,1)S(1)} %get-tuple-element.25), channel_id=1, source_target_pairs={{0,1},{1,0},{2,3},{3,2},{4,5},{5,4},{6,7},{7,6},{8,9},{9,8},{10,11... | collective-permute-start | bytes 159752 | tf_op jit(solution)/shard_map/ppermute | solution.py:407
  6.9 5.0 %collective-permute-start.1 = (bf16[144,128]{1,0:T(8,128)(2,1)S(1)}, bf16[144,128]{1,0:T(8,128)(2,1)S(1)}, u32[]{:S(2)}, u32[]{:S(2)}) collective-permute-start(bf16[144,128]{1,0:T(8,128)(2,1)S(1)} %get-tuple-element.23.refs_0_), channel_id=1, source_target_pairs={{0,2},{1,3},{2,0},{3,1},{4,6},{5,7},{6,4},{7,5},{8,10},{9,11},{10,... | collective-permute-start | bytes 110600 | tf_op jit(solution)/shard_map/ppermute | solution.py:407
  12.6 5.6 %collective-permute-start.3 = (bf16[80,512]{1,0:T(8,128)(2,1)S(1)}, bf16[80,512]{1,0:T(8,128)(2,1)S(1)}, u32[]{:S(2)}, u32[]{:S(2)}) collective-permute-start(bf16[80,512]{1,0:T(8,128)(2,1)S(1)} %get-tuple-element.30), channel_id=1, source_target_pairs={{0,28},{4,8},{8,4},{12,16},{16,12},{20,24},{24,20},{28,0},{1,29},{... | collective-permute-start | bytes 245768 | tf_op jit(solution)/shard_map/ppermute | solution.py:464
  13.0 5.2 %collective-permute-start.4 = (bf16[80,512]{1,0:T(8,128)(2,1)S(1)}, bf16[80,512]{1,0:T(8,128)(2,1)S(1)}, u32[]{:S(2)}, u32[]{:S(2)}) collective-permute-start(bf16[80,512]{1,0:T(8,128)(2,1)S(1)} %get-tuple-element.29.refs_0_), channel_id=1, source_target_pairs={{0,4},{4,0},{8,12},{12,8},{16,20},{20,16},{24,28},{28,24},{1,5},{5... | collective-permute-start | bytes 245768 | tf_op jit(solution)/shard_map/ppermute | solution.py:467
  16.5 9.8 %copy-start = (bf16[16,2,128,128]{3,2,1,0:T(8,128)(2,1)S(1)}, bf16[16,2,128,128]{3,2,1,0:T(8,128)(2,1)}, u32[]{:S(2)}) copy-start(bf16[16,2,128,128]{3,2,1,0:T(8,128)(2,1)} %refs_6_.3) | copy-start | bytes 3145732
  19.1 6.3 %collective-permute-start.5 = (bf16[128,128]{1,0:T(8,128)(2,1)S(1)}, bf16[128,128]{1,0:T(8,128)(2,1)S(1)}, u32[]{:S(2)}, u32[]{:S(2)}) collective-permute-start(bf16[128,128]{1,0:T(8,128)(2,1)S(1)} %get-tuple-element.37), channel_id=1, source_target_pairs={{0,3},{1,2},{2,1},{3,0},{4,7},{5,6},{6,5},{7,4},{8,11},{9,10},{10,... | collective-permute-start | bytes 98312 | tf_op jit(solution)/shard_map/ppermute | solution.py:407
  21.0 4.8 %collective-permute-start.6 = (bf16[128,128]{1,0:T(8,128)(2,1)S(1)}, bf16[128,128]{1,0:T(8,128)(2,1)S(1)}, u32[]{:S(2)}, u32[]{:S(2)}) collective-permute-start(bf16[128,128]{1,0:T(8,128)(2,1)S(1)} %get-tuple-element.38), channel_id=1, source_target_pairs={{0,2},{1,3},{2,0},{3,1},{4,6},{5,7},{6,4},{7,5},{8,10},{9,11},{10,... | collective-permute-start | bytes 98312 | tf_op jit(solution)/shard_map/ppermute | solution.py:407
  22.4 3.9 %collective-permute-start.7 = (bf16[128,128]{1,0:T(8,128)(2,1)S(1)}, bf16[128,128]{1,0:T(8,128)(2,1)S(1)}, u32[]{:S(2)}, u32[]{:S(2)}) collective-permute-start(bf16[128,128]{1,0:T(8,128)(2,1)S(1)} %get-tuple-element.39), channel_id=1, source_target_pairs={{0,1},{1,0},{2,3},{3,2},{4,5},{5,4},{6,7},{7,6},{8,9},{9,8},{10,11... | collective-permute-start | bytes 98312 | tf_op jit(solution)/shard_map/ppermute | solution.py:407

commit v7 on v6

--- a/solution.py
+++ b/solution.py
@@ -82,10 +82,12 @@
 
 def up_kernel(*refs, pieces, boxes, parents, parts):
     msgs = refs[:pieces]
-    interp_ref, phase_ref, out_ref, out_copy, place_ref, raised, folded = refs[pieces:]
+    interp_ref, phase_ref, after, out_ref, out_copy, place_ref, raised, folded = refs[pieces:]
     forward = msgs[1]
     slots = 8 * parents
-    samples = interp_ref.shape[0]
+    samples = raised.shape[1]
+    first = lax.axis_index("samp") * samples
+    mine = interp_ref[pl.ds(pl.multiple_of(first, samples), samples)]
     per_tile = LANES // boxes
     at = parts * boxes
     tiles = []
@@ -111,16 +113,17 @@
     ordered = nn_dot(sorter, pats).astype(BF16)
     for c in range(parts):
         raised[c * slots : (c + 1) * slots] = nt_dot(
-            ordered[:, c * LANES : (c + 1) * LANES], interp_ref[...]
+            ordered[:, c * LANES : (c + 1) * LANES], mine
         )
     half = parts // 2
     for t in range(samples // LANES):
         lanes = slice(t * LANES, (t + 1) * LANES)
+        here = pl.ds(pl.multiple_of(first + t * LANES, LANES), LANES)
         for r in range(half):
             re = im = None
             for o in range(8):
-                ph_r = phase_ref[o, 0:1, lanes]
-                ph_i = phase_ref[o, 1:2, lanes]
+                ph_r = phase_ref[o, 0:1, here]
+                ph_i = phase_ref[o, 1:2, here]
                 base_r = r * slots + o * parents
                 base_i = (half + r) * slots + o * parents
                 xr = raised[base_r : base_r + parents, lanes]
@@ -148,26 +151,15 @@
     return [d for d in range(-parents, parents + 1) if abs(d) >= 2]
 
 
-def half_of(mats, late):
-    count = mats.shape[0]
-    odd = lax.rem(lax.axis_index("samp"), 2)
-    return pl.ds(count * (odd if late else 1 - odd), count)
-
-
 def prep_kernel(
-    inter, trans, table_hbm, interp_hbm, phase_hbm, neighbours, mats_hbm, after,
-    dense, interp_ref, phase_ref, nbr, mats, inter_s, trans_s, table, sems, *, parents, all_parents,
+    inter, trans, neighbours, table_hbm, mats_hbm, after, dense, nbr, inter_s, trans_s, table, sems,
+    *, parents, all_parents,
 ):
-    samples = interp_ref.shape[0]
-    mine = pl.ds(pl.multiple_of(lax.axis_index("samp") * samples, samples), samples)
     copies = [
         pltpu.make_async_copy(inter, inter_s, sems.at[0]),
         pltpu.make_async_copy(trans, trans_s, sems.at[1]),
         pltpu.make_async_copy(table_hbm, table, sems.at[2]),
-        pltpu.make_async_copy(interp_hbm.at[mine], interp_ref, sems.at[3]),
-        pltpu.make_async_copy(phase_hbm.at[:, :, mine], phase_ref, sems.at[4]),
-        pltpu.make_async_copy(neighbours, nbr, sems.at[5]),
-        pltpu.make_async_copy(mats_hbm.at[half_of(mats, False)], mats, sems.at[6]),
+        pltpu.make_async_copy(neighbours, nbr, sems.at[3]),
     ]
     for copy in copies:
         copy.start()
@@ -185,8 +177,7 @@
         return carry
 
     lax.fori_loop(0, parents, fill, 0)
-    for copy in copies[3:]:
-        copy.wait()
+    copies[3].wait()
 
 
 def down_kernel(
@@ -194,7 +185,9 @@
 ):
     outs = refs[:pieces]
     window, incoming, shifted = refs[pieces:]
-    samples = interp_ref.shape[0]
+    samples = window.shape[2]
+    first = lax.axis_index("samp") * samples
+    mine = interp_ref[pl.ds(pl.multiple_of(first, samples), samples)]
     slots = 8 * parents
     half = parts // 2
     odd = lax.rem(lax.axis_index("box"), 2)
@@ -228,20 +221,21 @@
         lax.fori_loop(0, parents, lambda p, c: (one(p), c)[1], 0)
     for t in range(samples // LANES):
         lanes = slice(t * LANES, (t + 1) * LANES)
+        here = pl.ds(pl.multiple_of(first + t * LANES, LANES), LANES)
         for r in range(half):
             ir = incoming[t, pl.ds(r, parents, stride=parts), :]
             ii = incoming[t, pl.ds(half + r, parents, stride=parts), :]
             re, im = [], []
             for o in range(8):
-                ph_r = phase_ref[o, 0:1, lanes]
-                ph_i = phase_ref[o, 1:2, lanes]
+                ph_r = phase_ref[o, 0:1, here]
+                ph_i = phase_ref[o, 1:2, here]
                 re.append(ph_r * ir - ph_i * ii)
                 im.append(ph_r * ii + ph_i * ir)
             shifted[r * slots : (r + 1) * slots, lanes] = jnp.concatenate(re, axis=0).astype(BF16)
             shifted[(half + r) * slots : (half + r + 1) * slots, lanes] = jnp.concatenate(
                 im, axis=0
             ).astype(BF16)
-    field = nn_dot(shifted[...], interp_ref[...]).astype(BF16)
+    field = nn_dot(shifted[...], mine).astype(BF16)
     spread = jnp.concatenate([field[c * slots : (c + 1) * slots] for c in range(parts)], axis=1)
     leaves = nn_dot(place_ref[...], spread).astype(BF16)
     for d in range(pieces):
@@ -252,12 +246,11 @@
 
 
 def near_kernel(*refs, late, nsamp, total, halo_rows, parent_rows):
+    neighbours, own, mats, after, *halos, out_ref, window, nbr, sems = refs
     if late:
-        neighbours, own, mats, after, across, beside, *from_far, out_ref, window, nbr, sems = refs
+        across, beside, *from_far = halos
     else:
-        neighbours, own, mats, after, from_beside, mats_hbm, out_ref, more, window, nbr, sems = refs
-        fetch = pltpu.make_async_copy(mats_hbm.at[half_of(more, True)], more, sems.at[1])
-        fetch.start()
+        (from_beside,) = halos
     list_copy = pltpu.make_async_copy(neighbours, nbr, sems.at[0])
     list_copy.start()
     count, parts, unknowns = out_ref.shape
@@ -303,12 +296,10 @@
         acc = None
         for k in range(near_count):
             j = lax.rem(nbr[k, first + i] - base + count + total, total)
-            mat = jnp.concatenate([mats[i, k, 0], mats[i, k, 1]], axis=1)
+            mat = jnp.concatenate([mats[first + i, k, 0], mats[first + i, k, 1]], axis=1)
             y = nt_dot(window[j].astype(BF16), mat)
             acc = y if acc is None else acc + y
         out_ref[i] = acc
-    if not late:
-        fetch.wait()
 
 
 def final_kernel(*refs, pieces):
@@ -406,38 +397,37 @@
     def exchange(x, d):
         return lax.ppermute(x, "samp", [(i, i ^ d) for i in range(nsamp)])
 
-    order = [0, *reversed(range(1, nsamp))]
+    order = [0, nsamp - 1, *range(1, nsamp - 1)]
     far = [(4 << i) - 1 for i in range(nsamp.bit_length() - 2)]
     messages = {0: plain}
     for d in order[1:]:
         messages[d] = exchange(to_beside if d == 1 else to_far if d in far else plain, d)
     far_messages = [messages[d] for d in far]
 
-    dense, my_interp, my_phases, near_list, mats_early = pl.pallas_call(
+    dense, near_list = pl.pallas_call(
         lambda *refs: prep_kernel(*refs, parents=parents, all_parents=all_parents),
-        in_specs=[whole_in(HBM)] * 7 + [whole_in(VM)],
-        out_specs=[whole_in(VM)] * 5,
+        in_specs=[whole_in(HBM)] * 5 + [whole_in(VM)],
+        out_specs=[whole_in(VM)] * 2,
         out_shape=[
             shape((parents, len(zone(parents)), 2, samples), F32),
-            shape((samples, LANES)),
-            shape((8, 2, samples), F32),
             shape((near_count, boxes), jnp.int32),
-            shape((reach,) + near_blocks.shape[1:]),
         ],
         scratch_shapes=[
             SM(inter_list.shape, jnp.int32),
             SM(trans_id.shape, jnp.int32),
             VM(translators.shape, F32),
-            DMA((7,)),
+            DMA((4,)),
         ],
         compiler_params=PARAMS,
         cost_estimate=pl.CostEstimate(
-            flops=0, bytes_accessed=4 * 1024 * 1024, transcendentals=0
+            flops=0, bytes_accessed=2 * near_blocks.size, transcendentals=0
         ),
         name="prep",
     )(
-        *[stay(a) for a in (inter_list, trans_id, translators, interp, phases)],
+        stay(inter_list),
+        stay(trans_id),
         stay(neighbours.T),
+        stay(translators),
         stay(near_blocks),
         x_rows,
     )
@@ -446,7 +436,7 @@
         lambda *refs: up_kernel(
             *refs, pieces=nsamp, boxes=boxes, parents=parents, parts=parts
         ),
-        in_specs=[whole_in(VM)] * (nsamp + 2),
+        in_specs=[whole_in(VM)] * (nsamp + 3),
         out_specs=[whole_in(VM)] * 3,
         out_shape=[
             shape((parent_rows + halo_rows * LANES // samples, samples)),
@@ -459,7 +449,7 @@
         ],
         compiler_params=PARAMS,
         name="up",
-    )(*[messages[d] for d in order], my_interp, my_phases)
+    )(*[messages[d] for d in order], interp, phases, near_list)
 
     across = lax.ppermute(
         to_across, "box", [(i, (i + (1 if i % 2 else -1)) % nbox) for i in range(nbox)]
@@ -467,11 +457,6 @@
     beside = lax.ppermute(parent_pat, "box", [(i, i ^ 1) for i in range(nbox)])
 
     def near_half(late, args):
-        out_shape = [shape((reach, parts, unknowns), F32)]
-        in_specs = [whole_in(VM)] * len(args)
-        if not late:
-            out_shape.append(shape(mats_early.shape))
-            in_specs[-1] = whole_in(HBM)
         return pl.pallas_call(
             lambda *refs: near_kernel(
                 *refs,
@@ -481,13 +466,13 @@
                 halo_rows=halo_rows,
                 parent_rows=parent_rows,
             ),
-            in_specs=[whole_in(VM)] * 2 + in_specs,
-            out_specs=[whole_in(VM)] * len(out_shape),
-            out_shape=out_shape,
+            in_specs=[whole_in(VM)] * (3 + len(args)),
+            out_specs=whole_in(VM),
+            out_shape=shape((reach, parts, unknowns), F32),
             scratch_shapes=[
                 VM((boxes + 2 * reach, parts, 2 * unknowns), F32),
                 SM((near_count, boxes), jnp.int32),
-                DMA((2,)),
+                DMA((1,)),
             ],
             compiler_params=PARAMS,
             cost_estimate=pl.CostEstimate(
@@ -496,11 +481,9 @@
                 transcendentals=0,
             ),
             name="near",
-        )(near_list, x_rows, *args)
-
-    near_early, mats_late = near_half(
-        False, [mats_early, place_onehot, messages[1], stay(near_blocks)]
-    )
+        )(near_list, x_rows, near_blocks, *args)
+
+    near_early = near_half(False, [place_onehot, messages[1]])
 
     fields = pl.pallas_call(
         lambda *refs: down_kernel(
@@ -516,11 +499,12 @@
         ],
         compiler_params=PARAMS,
         name="down",
-    )(parent_pat, across, beside, dense, my_interp, my_phases, place_onehot, near_early)
-
-    partial = [fields[0]] + [exchange(x, d) for x, d in zip(fields[1:], order[1:])]
-
-    (near_late,) = near_half(True, [mats_late, fields[0], across, beside, *far_messages])
+    )(parent_pat, across, beside, dense, interp, phases, place_onehot, near_early)
+
+    pieces = dict(zip(order, fields))
+    partial = [pieces[0]] + [exchange(pieces[d], d) for d in reversed(range(1, nsamp))]
+
+    near_late = near_half(True, [fields[0], across, beside, *far_messages])
 
     return pl.pallas_call(
         lambda *refs: final_kernel(*refs, pieces=nsamp),

time: 27.6 us -> 27.7 us (level)
  waiting for transfers between devices: 4.65 us -> 5.92 us
  Pallas kernels: 10.8 us -> 9.67 us
    ppermute x6, waiting for transfers between devices: 2.95 us -> 3.8 us  [exchange(): return lax.ppermute(x, 'samp', [(i, i ^ d) for i in range(nsamp)])]
    pallas_call x1, Pallas kernels: 2.44 us -> 1.6 us  [on_device(): pl.pallas_call(lambda *refs: prep_kernel(*refs, parents=parents, all_pare...]
    ppermute x1, waiting for transfers between devices: 1.69 us -> 2.11 us  [on_device(): lax.ppermute(to_across, 'box', [(i, (i + (1 if i % 2 else -1)) % nbox) fo...]
    pallas_call x2, Pallas kernels: 4.03 us -> 3.62 us  [near_half(): pl.pallas_call(lambda *refs: near_kernel(*refs, late=late, nsamp=nsamp, t...]
  transfers between devices with their start and end apart: 8 -> 8, of which waited for: 4 -> 4; matrix products, arithmetic and copies ran while one was open for 0% -> 0% of each run, Pallas kernels for 24% -> 19%
where the time goes in v7:
time: 27.7 us; the launch traced here: 27.6 us
  starting transfers between devices  11.9 us (43%)
  Pallas kernels  9.67 us (35%)
  waiting for transfers between devices  5.92 us (21%)
    ppermute x6, starting transfers between devices, exchange(): return lax.ppermute(x, 'samp', [(i, i ^ d) for i in range(nsamp)])  10.2 us
    ppermute x6, waiting for transfers between devices, exchange(): return lax.ppermute(x, 'samp', [(i, i ^ d) for i in range(nsamp)])  3.8 us
    pallas_call x2, Pallas kernels, near_half(): pl.pallas_call(lambda *refs: near_kernel(*refs, late=late, nsamp=nsamp, t...  3.62 us
    ppermute x1, waiting for transfers between devices, on_device(): lax.ppermute(to_across, 'box', [(i, (i + (1 if i % 2 else -1)) % nbox) fo...  2.11 us
    pallas_call x1, Pallas kernels, on_device(): pl.pallas_call(lambda *refs: leaf_kernel(*refs, parents=parents), in_spec...  1.93 us
    pallas_call x1, Pallas kernels, on_device(): pl.pallas_call(lambda *refs: prep_kernel(*refs, parents=parents, all_pare...  1.6 us
    ppermute x1, starting transfers between devices, on_device(): beside = lax.ppermute(parent_pat, 'box', [(i, i ^ 1) for i in range(nbox)])  1.31 us
    pallas_call x1, Pallas kernels, on_device(): pl.pallas_call(lambda *refs: final_kernel(*refs, pieces=nsamp), in_specs=...  1.03 us
  transfers between devices with their start and end apart: 8, of which 4 were waited for; matrix products, arithmetic and copies ran while one was open for 0% of the time, Pallas kernels for 19%

profile of v7, /device:TPU:0, one launch (start us, length us, event | category | flops | bytes accessed | tf_op | source)
XLA Modules:
  0.0 27.6 jit_solution(5594097901506353026)
XLA Ops:
  0.0 0.0 copy-start
  0.0 0.0 copy-start.3
  0.0 0.0 copy-start.1
  0.0 1.9 %leaf.1 = (bf16[208,128]{1,0:T(8,128)(2,1)S(1)}, bf16[144,128]{1,0:T(8,128)(2,1)S(1)}, bf16[208,128]{1,0:T(8,128)(2,1)S(1)}, bf16[128,128]{1,0:T(8,128)(2,1)S(1)}) custom-call(s32[16]{0:T(128)} %refs_0_.2, s32[16]{0:T(128)} %refs_1_.2, bf16[16,2,4,128]{3,2,1,0:T(4,128)(2,1)} %refs_2_.3, bf16[16,2,128,128]{3,2,1,0:T(8,128)(2,1)} %refs_3_.2), custom_call_target="tpu_custom_call" | custom-call | tf_op jit(solution)/shard_map/leaf/pallas_call | solution.py:375
  1.9 5.1 %collective-permute-start = (bf16[208,128]{1,0:T(8,128)(2,1)S(1)}, bf16[208,128]{1,0:T(8,128)(2,1)S(1)}, u32[]{:S(2)}, u32[]{:S(2)}) collective-permute-start(bf16[208,128]{1,0:T(8,128)(2,1)S(1)} %get-tuple-element.19), channel_id=1, source_target_pairs={{0,3},{1,2},{2,1},{3,0},{4,7},{5,6},{6,5},{7,4},{8,11},{9,10},{10,... | collective-permute-start | bytes 159752 | tf_op jit(solution)/shard_map/ppermute | solution.py:398
  7.1 0.0 collective-permute-start.1
  7.1 0.6 %collective-permute-start.2 = (bf16[144,128]{1,0:T(8,128)(2,1)S(1)}, bf16[144,128]{1,0:T(8,128)(2,1)S(1)}, u32[]{:S(2)}, u32[]{:S(2)}) collective-permute-start(bf16[144,128]{1,0:T(8,128)(2,1)S(1)} %get-tuple-element.18.refs_0_), channel_id=1, source_target_pairs={{0,2},{1,3},{2,0},{3,1},{4,6},{5,7},{6,4},{7,5},{8,10},{9,11},{10,... | collective-permute-start | bytes 110600 | tf_op jit(solution)/shard_map/ppermute | solution.py:398
  7.7 1.6 %prep.1 = (f32[8,14,2,512]{3,2,1,0:T(2,128)S(1)}, s32[8,16]{1,0:T(8,128)S(1)}) custom-call(s32[8,14]{1,0:T(8,128)} %refs_0_.3, s32[8,14]{1,0:T(8,128)} %refs_1_.3, s32[8,16]{1,0:T(8,128)} %bitcast.1, f32[64,2,512]{2,1,0:T(2,128)} %refs_3_.3, bf16[16,8,2,128,128]{4,3,2,1,0:T(8,128)(2,1)} %refs_2_.5, bf16[128,128]{1,0:T(8,128)(2,1)S(1)} %get-tuple-element.21.refs_5_.refs_1_), custom_call_target="tpu_custom_call" | custom-call | bytes 8388608 | tf_op jit(solution)/shard_map/prep/pallas_call | solution.py:407
  9.3 2.8 %collective-permute-done.2.refs_3_ = bf16[144,128]{1,0:T(8,128)(2,1)S(1)} collective-permute-done((bf16[144,128]{1,0:T(8,128)(2,1)S(1)}, bf16[144,128]{1,0:T(8,128)(2,1)S(1)}, u32[]{:S(2)}, u32[]{:S(2)}) %collective-permute-start.2) | collective-permute-done | bytes 36896 | tf_op jit(solution)/shard_map/ppermute | solution.py:398
  12.1 0.0 collective-permute-done.refs_1_.refs_6_
  12.1 0.0 collective-permute-done.1.refs_2_.refs_4_
  12.1 0.0 copy-done.3
  12.1 0.0 copy-done.1
  12.1 0.7 %up.1 = (bf16[80,512]{1,0:T(8,128)(2,1)S(1)}, bf16[80,512]{1,0:T(8,128)(2,1)S(1)}, bf16[64,64]{1,0:T(8,128)(2,1)S(1)}) custom-call(bf16[144,128]{1,0:T(8,128)(2,1)S(1)} %get-tuple-element.18.refs_0_, bf16[208,128]{1,0:T(8,128)(2,1)S(1)} %collective-permute-done.refs_1_.refs_6_, bf16[208,128]{1,0:T(8,128)(2,1)S(1)} %collective-permute-done.1.refs_2_.refs_4_, ...), custom_call_target="tpu_custom_call" | custom-call | tf_op jit(solution)/shard_map/up/pallas_call | solution.py:435
  12.8 0.4 %collective-permute-start.3 = (bf16[80,512]{1,0:T(8,128)(2,1)S(1)}, bf16[80,512]{1,0:T(8,128)(2,1)S(1)}, u32[]{:S(2)}, u32[]{:S(2)}) collective-permute-start(bf16[80,512]{1,0:T(8,128)(2,1)S(1)} %get-tuple-element.24), channel_id=1, source_target_pairs={{0,28},{4,8},{8,4},{12,16},{16,12},{20,24},{24,20},{28,0},{1,29},{... | collective-permute-start | bytes 245768 | tf_op jit(solution)/shard_map/ppermute | solution.py:454
  13.2 1.3 %collective-permute-start.4 = (bf16[80,512]{1,0:T(8,128)(2,1)S(1)}, bf16[80,512]{1,0:T(8,128)(2,1)S(1)}, u32[]{:S(2)}, u32[]{:S(2)}) collective-permute-start(bf16[80,512]{1,0:T(8,128)(2,1)S(1)} %get-tuple-element.23.refs_0_), channel_id=1, source_target_pairs={{0,4},{4,0},{8,12},{12,8},{16,20},{20,16},{24,28},{28,24},{1,5},{5... | collective-permute-start | bytes 245768 | tf_op jit(solution)/shard_map/ppermute | solution.py:457
  14.5 0.0 copy-done
  14.5 0.0 copy-start.2
  14.5 1.8 %near.2.refs_7_.refs_4_ = f32[8,8,128]{2,1,0:T(8,128)S(1)} custom-call(s32[8,16]{1,0:T(8,128)S(1)} %get-tuple-element.22.refs_6_.refs_0_, bf16[128,128]{1,0:T(8,128)(2,1)S(1)} %get-tuple-element.21.refs_5_.refs_1_, bf16[16,8,2,128,128]{4,3,2,1,0:T(8,128)(2,1)S(1)} %copy-done, bf16[64,64]{1,0:T(8,128)(2,1)S(1)} %get-tuple-element.26.refs_3_.refs_6_, ...), custom_call_target="tpu_custom_call" | custom-call | flops 33554432 | bytes 4194304 | tf_op jit(solution)/shard_map/near/pallas_call | solution.py:460
  16.3 2.1 %collective-permute-done.3.refs_1_.refs_4_ = bf16[80,512]{1,0:T(8,128)(2,1)S(1)} collective-permute-done((bf16[80,512]{1,0:T(8,128)(2,1)S(1)}, bf16[80,512]{1,0:T(8,128)(2,1)S(1)}, u32[]{:S(2)}, u32[]{:S(2)}) %collective-permute-start.3) | collective-permute-done | bytes 81952 | tf_op jit(solution)/shard_map/ppermute | solution.py:454
  18.4 0.0 collective-permute-done.4.refs_2_.refs_5_
  18.4 0.8 %down.1 = (bf16[128,128]{1,0:T(8,128)(2,1)S(1)}, bf16[128,128]{1,0:T(8,128)(2,1)S(1)}, bf16[128,128]{1,0:T(8,128)(2,1)S(1)}, bf16[128,128]{1,0:T(8,128)(2,1)S(1)}) custom-call(bf16[80,512]{1,0:T(8,128)(2,1)S(1)} %get-tuple-element.23.refs_0_, bf16[80,512]{1,0:T(8,128)(2,1)S(1)} %collective-permute-done.3.refs_1_.refs_4_, ...), custom_call_target="tpu_custom_call" | custom-call | tf_op jit(solution)/shard_map/down/pallas_call | solution.py:488
  19.2 1.8 %collective-permute-start.5 = (bf16[128,128]{1,0:T(8,128)(2,1)S(1)}, bf16[128,128]{1,0:T(8,128)(2,1)S(1)}, u32[]{:S(2)}, u32[]{:S(2)}) collective-permute-start(bf16[128,128]{1,0:T(8,128)(2,1)S(1)} %get-tuple-element.28), channel_id=1, source_target_pairs={{0,3},{1,2},{2,1},{3,0},{4,7},{5,6},{6,5},{7,4},{8,11},{9,10},{10,... | collective-permute-start | bytes 98312 | tf_op jit(solution)/shard_map/ppermute | solution.py:398
  21.0 1.6 %collective-permute-start.6 = (bf16[128,128]{1,0:T(8,128)(2,1)S(1)}, bf16[128,128]{1,0:T(8,128)(2,1)S(1)}, u32[]{:S(2)}, u32[]{:S(2)}) collective-permute-start(bf16[128,128]{1,0:T(8,128)(2,1)S(1)} %get-tuple-element.29), channel_id=1, source_target_pairs={{0,2},{1,3},{2,0},{3,1},{4,6},{5,7},{6,4},{7,5},{8,10},{9,11},{10,... | collective-permute-start | bytes 98312 | tf_op jit(solution)/shard_map/ppermute | solution.py:398
  22.6 1.1 %collective-permute-start.7 = (bf16[128,128]{1,0:T(8,128)(2,1)S(1)}, bf16[128,128]{1,0:T(8,128)(2,1)S(1)}, u32[]{:S(2)}, u32[]{:S(2)}) collective-permute-start(bf16[128,128]{1,0:T(8,128)(2,1)S(1)} %get-tuple-element.30), channel_id=1, source_target_pairs={{0,1},{1,0},{2,3},{3,2},{4,5},{5,4},{6,7},{7,6},{8,9},{9,8},{10,11... | collective-permute-start | bytes 98312 | tf_op jit(solution)/shard_map/ppermute | solution.py:398
  23.7 1.8 %near.3.refs_5_ = f32[8,8,128]{2,1,0:T(8,128)S(1)} custom-call(s32[8,16]{1,0:T(8,128)S(1)} %get-tuple-element.22.refs_6_.refs_0_, bf16[128,128]{1,0:T(8,128)(2,1)S(1)} %get-tuple-element.21.refs_5_.refs_1_, bf16[16,8,2,128,128]{4,3,2,1,0:T(8,128)(2,1)S(1)} %copy-done, bf16[128,128]{1,0:T(8,128)(2,1)S(1)} %get-tuple-element.27.refs_3_.refs_0_, ...), custom_call_target="tpu_custom_call" | custom-call | flops 33554432 | bytes 4194304 | tf_op jit(solution)/shard_map/near/pallas_call | solution.py:460
  25.5 0.0 collective-permute-done.5.refs_1_
  25.5 0.3 %collective-permute-done.6.refs_2_ = bf16[128,128]{1,0:T(8,128)(2,1)S(1)} collective-permute-done((bf16[128,128]{1,0:T(8,128)(2,1)S(1)}, bf16[128,128]{1,0:T(8,128)(2,1)S(1)}, u32[]{:S(2)}, u32[]{:S(2)}) %collective-permute-start.6) | collective-permute-done | bytes 32800 | tf_op jit(solution)/shard_map/ppermute | solution.py:398
  25.8 0.7 %collective-permute-done.7.refs_3_ = bf16[128,128]{1,0:T(8,128)(2,1)S(1)} collective-permute-done((bf16[128,128]{1,0:T(8,128)(2,1)S(1)}, bf16[128,128]{1,0:T(8,128)(2,1)S(1)}, u32[]{:S(2)}, u32[]{:S(2)}) %collective-permute-start.7) | collective-permute-done | bytes 32800 | tf_op jit(solution)/shard_map/ppermute | solution.py:398
  26.5 0.0 copy-done.2
  26.5 1.0 %final.1 = f32[16,2,4,128]{3,2,1,0:T(4,128)} custom-call(bf16[128,128]{1,0:T(8,128)(2,1)S(1)} %get-tuple-element.27.refs_3_.refs_0_, bf16[128,128]{1,0:T(8,128)(2,1)S(1)} %collective-permute-done.5.refs_1_, bf16[128,128]{1,0:T(8,128)(2,1)S(1)} %collective-permute-done.6.refs_2_, bf16[128,128]{1,0:T(8,128)(2,1)S(1)} %collective-permute-done.7.refs_3_, ...), custom_call_target="tpu_custom_call" | custom-call | tf_op jit(solution)/shard_map/final/pallas_call | solution.py:509
Async XLA Ops:
  0.0 14.5 %copy-start = (bf16[16,8,2,128,128]{4,3,2,1,0:T(8,128)(2,1)S(1)}, bf16[16,8,2,128,128]{4,3,2,1,0:T(8,128)(2,1)}, u32[]{:S(2)}) copy-start(bf16[16,8,2,128,128]{4,3,2,1,0:T(8,128)(2,1)} %refs_2_.5) | copy-start | bytes 25165828
  0.0 12.1 %copy-start.3 = (f32[8,2,2048]{2,1,0:T(2,128)S(1)}, f32[8,2,2048]{2,1,0:T(2,128)}, u32[]{:S(2)}) copy-start(f32[8,2,2048]{2,1,0:T(2,128)} %refs_5_.3) | copy-start | bytes 393220
  0.0 12.1 %copy-start.1 = (bf16[2048,128]{1,0:T(8,128)(2,1)S(1)}, bf16[2048,128]{1,0:T(8,128)(2,1)}, u32[]{:S(2)}) copy-start(bf16[2048,128]{1,0:T(8,128)(2,1)} %refs_4_.5) | copy-start | bytes 1572868
  1.9 10.1 %collective-permute-start = (bf16[208,128]{1,0:T(8,128)(2,1)S(1)}, bf16[208,128]{1,0:T(8,128)(2,1)S(1)}, u32[]{:S(2)}, u32[]{:S(2)}) collective-permute-start(bf16[208,128]{1,0:T(8,128)(2,1)S(1)} %get-tuple-element.19), channel_id=1, source_target_pairs={{0,3},{1,2},{2,1},{3,0},{4,7},{5,6},{6,5},{7,4},{8,11},{9,10},{10,... | collective-permute-start | bytes 159752 | tf_op jit(solution)/shard_map/ppermute | solution.py:398
  7.1 5.0 %collective-permute-start.1 = (bf16[208,128]{1,0:T(8,128)(2,1)S(1)}, bf16[208,128]{1,0:T(8,128)(2,1)S(1)}, u32[]{:S(2)}, u32[]{:S(2)}) collective-permute-start(bf16[208,128]{1,0:T(8,128)(2,1)S(1)} %get-tuple-element.20), channel_id=1, source_target_pairs={{0,1},{1,0},{2,3},{3,2},{4,5},{5,4},{6,7},{7,6},{8,9},{9,8},{10,11... | collective-permute-start | bytes 159752 | tf_op jit(solution)/shard_map/ppermute | solution.py:398
  7.1 5.0 %collective-permute-start.2 = (bf16[144,128]{1,0:T(8,128)(2,1)S(1)}, bf16[144,128]{1,0:T(8,128)(2,1)S(1)}, u32[]{:S(2)}, u32[]{:S(2)}) collective-permute-start(bf16[144,128]{1,0:T(8,128)(2,1)S(1)} %get-tuple-element.18.refs_0_), channel_id=1, source_target_pairs={{0,2},{1,3},{2,0},{3,1},{4,6},{5,7},{6,4},{7,5},{8,10},{9,11},{10,... | collective-permute-start | bytes 110600 | tf_op jit(solution)/shard_map/ppermute | solution.py:398
  12.8 5.6 %collective-permute-start.3 = (bf16[80,512]{1,0:T(8,128)(2,1)S(1)}, bf16[80,512]{1,0:T(8,128)(2,1)S(1)}, u32[]{:S(2)}, u32[]{:S(2)}) collective-permute-start(bf16[80,512]{1,0:T(8,128)(2,1)S(1)} %get-tuple-element.24), channel_id=1, source_target_pairs={{0,28},{4,8},{8,4},{12,16},{16,12},{20,24},{24,20},{28,0},{1,29},{... | collective-permute-start | bytes 245768 | tf_op jit(solution)/shard_map/ppermute | solution.py:454
  13.2 5.2 %collective-permute-start.4 = (bf16[80,512]{1,0:T(8,128)(2,1)S(1)}, bf16[80,512]{1,0:T(8,128)(2,1)S(1)}, u32[]{:S(2)}, u32[]{:S(2)}) collective-permute-start(bf16[80,512]{1,0:T(8,128)(2,1)S(1)} %get-tuple-element.23.refs_0_), channel_id=1, source_target_pairs={{0,4},{4,0},{8,12},{12,8},{16,20},{20,16},{24,28},{28,24},{1,5},{5... | collective-permute-start | bytes 245768 | tf_op jit(solution)/shard_map/ppermute | solution.py:457
  14.5 12.1 %copy-start.2 = (bf16[16,2,128,128]{3,2,1,0:T(8,128)(2,1)S(1)}, bf16[16,2,128,128]{3,2,1,0:T(8,128)(2,1)}, u32[]{:S(2)}) copy-start(bf16[16,2,128,128]{3,2,1,0:T(8,128)(2,1)} %refs_6_.1) | copy-start | bytes 3145732
  19.2 6.3 %collective-permute-start.5 = (bf16[128,128]{1,0:T(8,128)(2,1)S(1)}, bf16[128,128]{1,0:T(8,128)(2,1)S(1)}, u32[]{:S(2)}, u32[]{:S(2)}) collective-permute-start(bf16[128,128]{1,0:T(8,128)(2,1)S(1)} %get-tuple-element.28), channel_id=1, source_target_pairs={{0,3},{1,2},{2,1},{3,0},{4,7},{5,6},{6,5},{7,4},{8,11},{9,10},{10,... | collective-permute-start | bytes 98312 | tf_op jit(solution)/shard_map/ppermute | solution.py:398
  21.0 4.8 %collective-permute-start.6 = (bf16[128,128]{1,0:T(8,128)(2,1)S(1)}, bf16[128,128]{1,0:T(8,128)(2,1)S(1)}, u32[]{:S(2)}, u32[]{:S(2)}) collective-permute-start(bf16[128,128]{1,0:T(8,128)(2,1)S(1)} %get-tuple-element.29), channel_id=1, source_target_pairs={{0,2},{1,3},{2,0},{3,1},{4,6},{5,7},{6,4},{7,5},{8,10},{9,11},{10,... | collective-permute-start | bytes 98312 | tf_op jit(solution)/shard_map/ppermute | solution.py:398
  22.6 3.9 %collective-permute-start.7 = (bf16[128,128]{1,0:T(8,128)(2,1)S(1)}, bf16[128,128]{1,0:T(8,128)(2,1)S(1)}, u32[]{:S(2)}, u32[]{:S(2)}) collective-permute-start(bf16[128,128]{1,0:T(8,128)(2,1)S(1)} %get-tuple-element.30), channel_id=1, source_target_pairs={{0,1},{1,0},{2,3},{3,2},{4,5},{5,4},{6,7},{7,6},{8,9},{9,8},{10,11... | collective-permute-start | bytes 98312 | tf_op jit(solution)/shard_map/ppermute | solution.py:398

commit v8 on v7

--- a/solution.py
+++ b/solution.py
@@ -8,6 +8,7 @@
 F32 = jnp.float32
 BF16 = jnp.bfloat16
 LANES = 128
+CODE_ROWS = 8
 
 
 def nt_dot(a, b):
@@ -28,7 +29,7 @@
 
 
 def leaf_kernel(
-    octant, parent, x_hbm, lift_hbm, to_far, plain, to_beside, x_rows,
+    octant, parent, x_hbm, lift_hbm, mats_hbm, to_far, plain, x_beside, x_rows,
     x_ref, rows, lift, oct_s, par_s, sems, *, parents,
 ):
     boxes, halves, rhs, _ = x_ref.shape
@@ -60,29 +61,29 @@
     for n in range(boxes):
         slot = (oct_s[n] * parents + lax.rem(par_s[n], parents)).astype(F32)
         codes = jnp.where(lane == n, slot, codes)
-    codes = codes.astype(BF16)
+    codes = codes[:CODE_ROWS].astype(BF16)
     x_rows[...] = jnp.concatenate(own, axis=0).astype(BF16)
     first = jnp.concatenate(own[:reach], axis=0)
     last = jnp.concatenate(own[reach:], axis=0)
     odd = lax.rem(lax.axis_index("samp"), 2) == 1
     at = parts * boxes
-    to_beside[at + boxes :] = jnp.where(odd, first, last).astype(BF16)
-    to_far[at + boxes :] = jnp.where(odd, last, first).astype(BF16)
-    for ref in (plain, to_beside, to_far):
-        ref[at : at + boxes] = codes
+    x_beside[...] = jnp.where(odd, first, last).astype(BF16)
+    to_far[at + CODE_ROWS :] = jnp.where(odd, last, first).astype(BF16)
+    for ref in (plain, to_far):
+        ref[at : at + CODE_ROWS] = codes
     for n in range(boxes):
         if n % per == 0:
             big[n // per].wait()
         mat = jnp.concatenate([lift[n, 0], lift[n, 1]], axis=1)
         rows[pl.ds(n, parts, stride=boxes), :] = nt_dot(widen(own[n]).astype(BF16), mat)
     pattern = rows[...].astype(BF16)
-    for ref in (plain, to_beside, to_far):
+    for ref in (plain, to_far):
         ref[:at] = pattern
 
 
 def up_kernel(*refs, pieces, boxes, parents, parts):
     msgs = refs[:pieces]
-    interp_ref, phase_ref, after, out_ref, out_copy, place_ref, raised, folded = refs[pieces:]
+    interp_ref, phase_ref, out_ref, out_copy, place_ref, raised, folded = refs[pieces:]
     forward = msgs[1]
     slots = 8 * parents
     samples = raised.shape[1]
@@ -92,11 +93,11 @@
     at = parts * boxes
     tiles = []
     for t in range(0, pieces, per_tile):
-        lane = lax.broadcasted_iota(jnp.int32, (boxes, LANES), 1) // boxes
-        code = msgs[t][at : at + boxes].astype(F32)
+        lane = lax.broadcasted_iota(jnp.int32, (CODE_ROWS, LANES), 1) // boxes
+        code = msgs[t][at : at + CODE_ROWS].astype(F32)
         for d in range(1, min(per_tile, pieces - t)):
-            code = jnp.where(lane == d, msgs[t + d][at : at + boxes].astype(F32), code)
-        code = jnp.concatenate([code] * (slots // boxes), axis=0)
+            code = jnp.where(lane == d, msgs[t + d][at : at + CODE_ROWS].astype(F32), code)
+        code = jnp.concatenate([code] * (slots // CODE_ROWS), axis=0)
         want = lax.broadcasted_iota(jnp.int32, (slots, LANES), 0).astype(F32)
         width = min(per_tile, pieces - t) * boxes
         tiles.append(jnp.where(code == want, 1.0, 0.0)[:, :width])
@@ -366,20 +367,20 @@
     near_count = near_blocks.shape[1]
     halo_rows = reach * parts
     parent_rows = parents * parts
-    plain_rows = (parts + 1) * boxes
+    plain_rows = parts * boxes + CODE_ROWS
 
     def shape(dims, dtype=BF16):
         return jax.ShapeDtypeStruct(dims, dtype)
 
     lift_chunks = 4
-    to_far, plain, to_beside, x_rows = pl.pallas_call(
+    to_far, plain, x_beside, x_rows = pl.pallas_call(
         lambda *refs: leaf_kernel(*refs, parents=parents),
-        in_specs=[whole_in(HBM)] * 4,
+        in_specs=[whole_in(HBM)] * 5,
         out_specs=[whole_in(VM)] * 4,
         out_shape=[
             shape((plain_rows + halo_rows, LANES)),
             shape((plain_rows, LANES)),
-            shape((plain_rows + halo_rows, LANES)),
+            shape((halo_rows, LANES)),
             shape((boxes * parts, LANES)),
         ],
         scratch_shapes=[
@@ -392,7 +393,7 @@
         ],
         compiler_params=PARAMS,
         name="leaf",
-    )(*[stay(a) for a in (octant, leaf_parent_index, xvec, lift)])
+    )(*[stay(a) for a in (octant, leaf_parent_index, xvec, lift, near_blocks)])
 
     def exchange(x, d):
         return lax.ppermute(x, "samp", [(i, i ^ d) for i in range(nsamp)])
@@ -401,8 +402,33 @@
     far = [(4 << i) - 1 for i in range(nsamp.bit_length() - 2)]
     messages = {0: plain}
     for d in order[1:]:
-        messages[d] = exchange(to_beside if d == 1 else to_far if d in far else plain, d)
+        messages[d] = exchange(to_far if d in far else plain, d)
     far_messages = [messages[d] for d in far]
+    halo_beside = exchange(x_beside, 1)
+
+    to_across, parent_pat, place_onehot = pl.pallas_call(
+        lambda *refs: up_kernel(
+            *refs, pieces=nsamp, boxes=boxes, parents=parents, parts=parts
+        ),
+        in_specs=[whole_in(VM)] * (nsamp + 2),
+        out_specs=[whole_in(VM)] * 3,
+        out_shape=[
+            shape((parent_rows + halo_rows * LANES // samples, samples)),
+            shape((parent_rows + halo_rows * LANES // samples, samples)),
+            shape((leaves, slots)),
+        ],
+        scratch_shapes=[
+            VM((parts * slots, samples), F32),
+            VM((samples // LANES, parent_rows, LANES), F32),
+        ],
+        compiler_params=PARAMS,
+        name="up",
+    )(*[messages[d] for d in order], interp, phases)
+
+    across = lax.ppermute(
+        to_across, "box", [(i, (i + (1 if i % 2 else -1)) % nbox) for i in range(nbox)]
+    )
+    beside = lax.ppermute(parent_pat, "box", [(i, i ^ 1) for i in range(nbox)])
 
     dense, near_list = pl.pallas_call(
         lambda *refs: prep_kernel(*refs, parents=parents, all_parents=all_parents),
@@ -429,32 +455,8 @@
         stay(neighbours.T),
         stay(translators),
         stay(near_blocks),
-        x_rows,
-    )
-
-    to_across, parent_pat, place_onehot = pl.pallas_call(
-        lambda *refs: up_kernel(
-            *refs, pieces=nsamp, boxes=boxes, parents=parents, parts=parts
-        ),
-        in_specs=[whole_in(VM)] * (nsamp + 3),
-        out_specs=[whole_in(VM)] * 3,
-        out_shape=[
-            shape((parent_rows + halo_rows * LANES // samples, samples)),
-            shape((parent_rows + halo_rows * LANES // samples, samples)),
-            shape((leaves, slots)),
-        ],
-        scratch_shapes=[
-            VM((parts * slots, samples), F32),
-            VM((samples // LANES, parent_rows, LANES), F32),
-        ],
-        compiler_params=PARAMS,
-        name="up",
-    )(*[messages[d] for d in order], interp, phases, near_list)
-
-    across = lax.ppermute(
-        to_across, "box", [(i, (i + (1 if i % 2 else -1)) % nbox) for i in range(nbox)]
-    )
-    beside = lax.ppermute(parent_pat, "box", [(i, i ^ 1) for i in range(nbox)])
+        place_onehot,
+    )
 
     def near_half(late, args):
         return pl.pallas_call(
@@ -483,7 +485,7 @@
             name="near",
         )(near_list, x_rows, near_blocks, *args)
 
-    near_early = near_half(False, [place_onehot, messages[1]])
+    near_early = near_half(False, [place_onehot, halo_beside])
 
     fields = pl.pallas_call(
         lambda *refs: down_kernel(

time: 27.7 us -> 28.6 us (1.032)
  waiting for transfers between devices: 5.92 us -> 6.58 us
    ppermute x6 -> x7, waiting for transfers between devices: 3.8 us -> 6.57 us  [exchange(): return lax.ppermute(x, 'samp', [(i, i ^ d) for i in range(nsamp)])]
    ppermute x1, waiting for transfers between devices: 2.11 us -> 0.01 us  [on_device(): lax.ppermute(to_across, 'box', [(i, (i + (1 if i % 2 else -1)) % nbox) fo...]
    ppermute x6 -> x7, starting transfers between devices: 10.2 us -> 10.4 us  [exchange(): return lax.ppermute(x, 'samp', [(i, i ^ d) for i in range(nsamp)])]
  transfers between devices with their start and end apart: 8 -> 9, of which waited for: 4 -> 4; matrix products, arithmetic and copies ran while one was open for 0% -> 0% of each run, Pallas kernels for 19% -> 18%
where the time goes in v8:
time: 28.6 us; the launch traced here: 28.4 us
  starting transfers between devices  12.1 us (42%)
  Pallas kernels  9.67 us (34%)
  waiting for transfers between devices  6.58 us (23%)
    ppermute x7, starting transfers between devices, exchange(): return lax.ppermute(x, 'samp', [(i, i ^ d) for i in range(nsamp)])  10.4 us
    ppermute x7, waiting for transfers between devices, exchange(): return lax.ppermute(x, 'samp', [(i, i ^ d) for i in range(nsamp)])  6.57 us
    pallas_call x2, Pallas kernels, near_half(): pl.pallas_call(lambda *refs: near_kernel(*refs, late=late, nsamp=nsamp, t...  3.62 us
    pallas_call x1, Pallas kernels, on_device(): pl.pallas_call(lambda *refs: leaf_kernel(*refs, parents=parents), in_spec...  1.93 us
    pallas_call x1, Pallas kernels, on_device(): pl.pallas_call(lambda *refs: prep_kernel(*refs, parents=parents, all_pare...  1.6 us
    ppermute x1, starting transfers between devices, on_device(): beside = lax.ppermute(parent_pat, 'box', [(i, i ^ 1) for i in range(nbox)])  1.16 us
    pallas_call x1, Pallas kernels, on_device(): pl.pallas_call(lambda *refs: final_kernel(*refs, pieces=nsamp), in_specs=...  1.03 us
    pallas_call x1, Pallas kernels, on_device(): pl.pallas_call(lambda *refs: down_kernel(*refs, pieces=nsamp, boxes=boxes...  0.82 us
  transfers between devices with their start and end apart: 9, of which 4 were waited for; matrix products, arithmetic and copies ran while one was open for 0% of the time, Pallas kernels for 18%

profile of v8, /device:TPU:0, one launch (start us, length us, event | category | flops | bytes accessed | tf_op | source)
XLA Modules:
  0.0 28.4 jit_solution(130689996505173703)
XLA Ops:
  0.0 0.0 copy-start.2
  0.0 0.0 copy-start
  0.0 1.9 %leaf.1 = (bf16[200,128]{1,0:T(8,128)(2,1)S(1)}, bf16[136,128]{1,0:T(8,128)(2,1)S(1)}, bf16[64,128]{1,0:T(8,128)(2,1)S(1)}, bf16[128,128]{1,0:T(8,128)(2,1)S(1)}) custom-call(s32[16]{0:T(128)} %refs_0_.2, s32[16]{0:T(128)} %refs_1_.2, bf16[16,2,4,128]{3,2,1,0:T(4,128)(2,1)} %refs_2_.3, bf16[16,2,128,128]{3,2,1,0:T(8,128)(2,1)} %refs_3_.2, ...), custom_call_target="tpu_custom_call" | custom-call | tf_op jit(solution)/shard_map/leaf/pallas_call | solution.py:376
  1.9 5.1 %collective-permute-start = (bf16[200,128]{1,0:T(8,128)(2,1)S(1)}, bf16[200,128]{1,0:T(8,128)(2,1)S(1)}, u32[]{:S(2)}, u32[]{:S(2)}) collective-permute-start(bf16[200,128]{1,0:T(8,128)(2,1)S(1)} %get-tuple-element.19), channel_id=1, source_target_pairs={{0,3},{1,2},{2,1},{3,0},{4,7},{5,6},{6,5},{7,4},{8,11},{9,10},{10,... | collective-permute-start | bytes 153608 | tf_op jit(solution)/shard_map/ppermute | solution.py:399
  7.1 0.0 collective-permute-start.2
  7.1 0.7 %collective-permute-start.1 = (bf16[136,128]{1,0:T(8,128)(2,1)S(1)}, bf16[136,128]{1,0:T(8,128)(2,1)S(1)}, u32[]{:S(2)}, u32[]{:S(2)}) collective-permute-start(bf16[136,128]{1,0:T(8,128)(2,1)S(1)} %get-tuple-element.18.refs_0_), channel_id=1, source_target_pairs={{0,1},{1,0},{2,3},{3,2},{4,5},{5,4},{6,7},{7,6},{8,9},{9,8},{10,11... | collective-permute-start | bytes 104456 | tf_op jit(solution)/shard_map/ppermute | solution.py:399
  7.7 4.2 %collective-permute-done.2.refs_3_ = bf16[136,128]{1,0:T(8,128)(2,1)S(1)} collective-permute-done((bf16[136,128]{1,0:T(8,128)(2,1)S(1)}, bf16[136,128]{1,0:T(8,128)(2,1)S(1)}, u32[]{:S(2)}, u32[]{:S(2)}) %collective-permute-start.2) | collective-permute-done | bytes 34848 | tf_op jit(solution)/shard_map/ppermute | solution.py:399
  11.9 0.0 collective-permute-done.1.refs_2_
  11.9 0.0 collective-permute-done.refs_1_.refs_6_
  11.9 0.0 copy-done.2
  11.9 0.0 copy-done
  11.9 0.7 %up.1 = (bf16[80,512]{1,0:T(8,128)(2,1)S(1)}, bf16[80,512]{1,0:T(8,128)(2,1)S(1)}, bf16[64,64]{1,0:T(8,128)(2,1)S(1)}) custom-call(bf16[136,128]{1,0:T(8,128)(2,1)S(1)} %get-tuple-element.18.refs_0_, bf16[200,128]{1,0:T(8,128)(2,1)S(1)} %collective-permute-done.refs_1_.refs_6_, bf16[136,128]{1,0:T(8,128)(2,1)S(1)} %collective-permute-done.1.refs_2_, ...), custom_call_target="tpu_custom_call" | custom-call | tf_op jit(solution)/shard_map/up/pallas_call | solution.py:409
  12.6 0.5 %collective-permute-start.3 = (bf16[80,512]{1,0:T(8,128)(2,1)S(1)}, bf16[80,512]{1,0:T(8,128)(2,1)S(1)}, u32[]{:S(2)}, u32[]{:S(2)}) collective-permute-start(bf16[80,512]{1,0:T(8,128)(2,1)S(1)} %get-tuple-element.21), channel_id=1, source_target_pairs={{0,28},{4,8},{8,4},{12,16},{16,12},{20,24},{24,20},{28,0},{1,29},{... | collective-permute-start | bytes 245768 | tf_op jit(solution)/shard_map/ppermute | solution.py:428
  13.1 1.2 %collective-permute-start.4 = (bf16[80,512]{1,0:T(8,128)(2,1)S(1)}, bf16[80,512]{1,0:T(8,128)(2,1)S(1)}, u32[]{:S(2)}, u32[]{:S(2)}) collective-permute-start(bf16[80,512]{1,0:T(8,128)(2,1)S(1)} %get-tuple-element.20.refs_0_), channel_id=1, source_target_pairs={{0,4},{4,0},{8,12},{12,8},{16,20},{20,16},{24,28},{28,24},{1,5},{5... | collective-permute-start | bytes 245768 | tf_op jit(solution)/shard_map/ppermute | solution.py:431
  14.3 0.2 collective-permute-start.5
  14.5 1.6 %prep.1 = (f32[8,14,2,512]{3,2,1,0:T(2,128)S(1)}, s32[8,16]{1,0:T(8,128)S(1)}) custom-call(s32[8,14]{1,0:T(8,128)} %refs_0_.3, s32[8,14]{1,0:T(8,128)} %refs_1_.3, s32[8,16]{1,0:T(8,128)} %bitcast.3, f32[64,2,512]{2,1,0:T(2,128)} %refs_3_.3, bf16[16,8,2,128,128]{4,3,2,1,0:T(8,128)(2,1)} %refs_2_.5, bf16[64,64]{1,0:T(8,128)(2,1)S(1)} %get-tuple-element.22.refs_5_.refs_3_.refs_6_), custom_call_target="tpu_custom_call" | custom-call | bytes 8388608 | tf_op jit(solution)/shard_map/prep/pallas_call | solution.py:433
  16.1 2.0 %collective-permute-done.5.refs_4_ = bf16[64,128]{1,0:T(8,128)(2,1)S(1)} collective-permute-done((bf16[64,128]{1,0:T(8,128)(2,1)S(1)}, bf16[64,128]{1,0:T(8,128)(2,1)S(1)}, u32[]{:S(2)}, u32[]{:S(2)}) %collective-permute-start.5) | collective-permute-done | bytes 16416 | tf_op jit(solution)/shard_map/ppermute | solution.py:399
  18.0 0.0 slice-done
  18.0 0.0 slice-done.1
  18.0 1.8 %near.2.refs_7_.refs_4_ = f32[8,8,128]{2,1,0:T(8,128)S(1)} custom-call(s32[8,16]{1,0:T(8,128)S(1)} %get-tuple-element.24.refs_0_, bf16[128,128]{1,0:T(8,128)(2,1)S(1)} %get-tuple-element.25.refs_1_, bf16[16,8,2,128,128]{4,3,2,1,0:T(8,128)(2,1)S(1)} %bitcast.2, bf16[64,64]{1,0:T(8,128)(2,1)S(1)} %get-tuple-element.22.refs_5_.refs_3_.refs_6_, ...), custom_call_target="tpu_custom_call" | custom-call | flops 33554432 | bytes 4194304 | tf_op jit(solution)/shard_map/near/pallas_call | solution.py:462
  19.9 0.0 collective-permute-done.3.refs_1_.refs_4_
  19.9 0.0 collective-permute-done.4.refs_2_.refs_5_
  19.9 0.8 %down.1 = (bf16[128,128]{1,0:T(8,128)(2,1)S(1)}, bf16[128,128]{1,0:T(8,128)(2,1)S(1)}, bf16[128,128]{1,0:T(8,128)(2,1)S(1)}, bf16[128,128]{1,0:T(8,128)(2,1)S(1)}) custom-call(bf16[80,512]{1,0:T(8,128)(2,1)S(1)} %get-tuple-element.20.refs_0_, bf16[80,512]{1,0:T(8,128)(2,1)S(1)} %collective-permute-done.3.refs_1_.refs_4_, ...), custom_call_target="tpu_custom_call" | custom-call | tf_op jit(solution)/shard_map/down/pallas_call | solution.py:490
  20.7 1.8 %collective-permute-start.6 = (bf16[128,128]{1,0:T(8,128)(2,1)S(1)}, bf16[128,128]{1,0:T(8,128)(2,1)S(1)}, u32[]{:S(2)}, u32[]{:S(2)}) collective-permute-start(bf16[128,128]{1,0:T(8,128)(2,1)S(1)} %get-tuple-element.28), channel_id=1, source_target_pairs={{0,3},{1,2},{2,1},{3,0},{4,7},{5,6},{6,5},{7,4},{8,11},{9,10},{10,... | collective-permute-start | bytes 98312 | tf_op jit(solution)/shard_map/ppermute | solution.py:399
  22.5 0.4 %collective-permute-start.7 = (bf16[128,128]{1,0:T(8,128)(2,1)S(1)}, bf16[128,128]{1,0:T(8,128)(2,1)S(1)}, u32[]{:S(2)}, u32[]{:S(2)}) collective-permute-start(bf16[128,128]{1,0:T(8,128)(2,1)S(1)} %get-tuple-element.29), channel_id=1, source_target_pairs={{0,2},{1,3},{2,0},{3,1},{4,6},{5,7},{6,4},{7,5},{8,10},{9,11},{10,... | collective-permute-start | bytes 98312 | tf_op jit(solution)/shard_map/ppermute | solution.py:399
  22.9 2.3 %collective-permute-start.8 = (bf16[128,128]{1,0:T(8,128)(2,1)S(1)}, bf16[128,128]{1,0:T(8,128)(2,1)S(1)}, u32[]{:S(2)}, u32[]{:S(2)}) collective-permute-start(bf16[128,128]{1,0:T(8,128)(2,1)S(1)} %get-tuple-element.30), channel_id=1, source_target_pairs={{0,1},{1,0},{2,3},{3,2},{4,5},{5,4},{6,7},{7,6},{8,9},{9,8},{10,11... | collective-permute-start | bytes 98312 | tf_op jit(solution)/shard_map/ppermute | solution.py:399
  25.2 1.8 %near.3.refs_5_ = f32[8,8,128]{2,1,0:T(8,128)S(1)} custom-call(s32[8,16]{1,0:T(8,128)S(1)} %get-tuple-element.24.refs_0_, bf16[128,128]{1,0:T(8,128)(2,1)S(1)} %get-tuple-element.25.refs_1_, bf16[16,8,2,128,128]{4,3,2,1,0:T(8,128)(2,1)S(1)} %bitcast.2, bf16[128,128]{1,0:T(8,128)(2,1)S(1)} %get-tuple-element.27.refs_3_.refs_0_, ...), custom_call_target="tpu_custom_call" | custom-call | flops 33554432 | bytes 4194304 | tf_op jit(solution)/shard_map/near/pallas_call | solution.py:462
  27.0 0.0 collective-permute-done.6.refs_1_
  27.0 0.3 %collective-permute-done.7.refs_2_ = bf16[128,128]{1,0:T(8,128)(2,1)S(1)} collective-permute-done((bf16[128,128]{1,0:T(8,128)(2,1)S(1)}, bf16[128,128]{1,0:T(8,128)(2,1)S(1)}, u32[]{:S(2)}, u32[]{:S(2)}) %collective-permute-start.7) | collective-permute-done | bytes 32800 | tf_op jit(solution)/shard_map/ppermute | solution.py:399
  27.3 0.1 collective-permute-done.8.refs_3_
  27.4 0.0 copy-done.1
  27.4 1.0 %final.1 = f32[16,2,4,128]{3,2,1,0:T(4,128)} custom-call(bf16[128,128]{1,0:T(8,128)(2,1)S(1)} %get-tuple-element.27.refs_3_.refs_0_, bf16[128,128]{1,0:T(8,128)(2,1)S(1)} %collective-permute-done.6.refs_1_, bf16[128,128]{1,0:T(8,128)(2,1)S(1)} %collective-permute-done.7.refs_2_, bf16[128,128]{1,0:T(8,128)(2,1)S(1)} %collective-permute-done.8.refs_3_, ...), custom_call_target="tpu_custom_call" | custom-call | tf_op jit(solution)/shard_map/final/pallas_call | solution.py:511
  (4 shorter events, 0.0 us)
Async XLA Ops:
  0.0 18.0 %slice-start = ((s8[8388608]{0:T(1024)(128)(4,1)}), s8[4194304]{0:T(1024)(128)(4,1)S(1)}, s32[]{:S(2)}) async-start(s8[8388608]{0:T(1024)(128)(4,1)} %bitcast.1), calls=%async_computation | async-start | bytes 8388608
  0.0 11.9 %copy-start.2 = (f32[8,2,2048]{2,1,0:T(2,128)S(1)}, f32[8,2,2048]{2,1,0:T(2,128)}, u32[]{:S(2)}) copy-start(f32[8,2,2048]{2,1,0:T(2,128)} %refs_5_.3) | copy-start | bytes 393220
  0.0 11.9 %copy-start = (bf16[2048,128]{1,0:T(8,128)(2,1)S(1)}, bf16[2048,128]{1,0:T(8,128)(2,1)}, u32[]{:S(2)}) copy-start(bf16[2048,128]{1,0:T(8,128)(2,1)} %refs_4_.7) | copy-start | bytes 1572868
  1.9 10.0 %collective-permute-start = (bf16[200,128]{1,0:T(8,128)(2,1)S(1)}, bf16[200,128]{1,0:T(8,128)(2,1)S(1)}, u32[]{:S(2)}, u32[]{:S(2)}) collective-permute-start(bf16[200,128]{1,0:T(8,128)(2,1)S(1)} %get-tuple-element.19), channel_id=1, source_target_pairs={{0,3},{1,2},{2,1},{3,0},{4,7},{5,6},{6,5},{7,4},{8,11},{9,10},{10,... | collective-permute-start | bytes 153608 | tf_op jit(solution)/shard_map/ppermute | solution.py:399
  7.1 11.0 %slice-start.1 = ((s8[8388608]{0:T(1024)(128)(4,1)}), s8[4194304]{0:T(1024)(128)(4,1)S(1)}, s32[]{:S(2)}) async-start(s8[8388608]{0:T(1024)(128)(4,1)} %bitcast.1), calls=%async_computation.1 | async-start | bytes 8388608
  7.1 4.8 %collective-permute-start.2 = (bf16[136,128]{1,0:T(8,128)(2,1)S(1)}, bf16[136,128]{1,0:T(8,128)(2,1)S(1)}, u32[]{:S(2)}, u32[]{:S(2)}) collective-permute-start(bf16[136,128]{1,0:T(8,128)(2,1)S(1)} %get-tuple-element.18.refs_0_), channel_id=1, source_target_pairs={{0,2},{1,3},{2,0},{3,1},{4,6},{5,7},{6,4},{7,5},{8,10},{9,11},{10,... | collective-permute-start | bytes 104456 | tf_op jit(solution)/shard_map/ppermute | solution.py:399
  7.1 4.8 %collective-permute-start.1 = (bf16[136,128]{1,0:T(8,128)(2,1)S(1)}, bf16[136,128]{1,0:T(8,128)(2,1)S(1)}, u32[]{:S(2)}, u32[]{:S(2)}) collective-permute-start(bf16[136,128]{1,0:T(8,128)(2,1)S(1)} %get-tuple-element.18.refs_0_), channel_id=1, source_target_pairs={{0,1},{1,0},{2,3},{3,2},{4,5},{5,4},{6,7},{7,6},{8,9},{9,8},{10,11... | collective-permute-start | bytes 104456 | tf_op jit(solution)/shard_map/ppermute | solution.py:399
  12.6 7.2 %collective-permute-start.3 = (bf16[80,512]{1,0:T(8,128)(2,1)S(1)}, bf16[80,512]{1,0:T(8,128)(2,1)S(1)}, u32[]{:S(2)}, u32[]{:S(2)}) collective-permute-start(bf16[80,512]{1,0:T(8,128)(2,1)S(1)} %get-tuple-element.21), channel_id=1, source_target_pairs={{0,28},{4,8},{8,4},{12,16},{16,12},{20,24},{24,20},{28,0},{1,29},{... | collective-permute-start | bytes 245768 | tf_op jit(solution)/shard_map/ppermute | solution.py:428
  13.1 6.7 %collective-permute-start.4 = (bf16[80,512]{1,0:T(8,128)(2,1)S(1)}, bf16[80,512]{1,0:T(8,128)(2,1)S(1)}, u32[]{:S(2)}, u32[]{:S(2)}) collective-permute-start(bf16[80,512]{1,0:T(8,128)(2,1)S(1)} %get-tuple-element.20.refs_0_), channel_id=1, source_target_pairs={{0,4},{4,0},{8,12},{12,8},{16,20},{20,16},{24,28},{28,24},{1,5},{5... | collective-permute-start | bytes 245768 | tf_op jit(solution)/shard_map/ppermute | solution.py:431
  14.3 3.7 %collective-permute-start.5 = (bf16[64,128]{1,0:T(8,128)(2,1)S(1)}, bf16[64,128]{1,0:T(8,128)(2,1)S(1)}, u32[]{:S(2)}, u32[]{:S(2)}) collective-permute-start(bf16[64,128]{1,0:T(8,128)(2,1)S(1)} %get-tuple-element.26), channel_id=1, source_target_pairs={{0,1},{1,0},{2,3},{3,2},{4,5},{5,4},{6,7},{7,6},{8,9},{9,8},{10,11... | collective-permute-start | bytes 49160 | tf_op jit(solution)/shard_map/ppermute | solution.py:399
  18.0 9.4 %copy-start.1 = (bf16[16,2,128,128]{3,2,1,0:T(8,128)(2,1)S(1)}, bf16[16,2,128,128]{3,2,1,0:T(8,128)(2,1)}, u32[]{:S(2)}) copy-start(bf16[16,2,128,128]{3,2,1,0:T(8,128)(2,1)} %refs_6_.1) | copy-start | bytes 3145732
  20.7 6.3 %collective-permute-start.6 = (bf16[128,128]{1,0:T(8,128)(2,1)S(1)}, bf16[128,128]{1,0:T(8,128)(2,1)S(1)}, u32[]{:S(2)}, u32[]{:S(2)}) collective-permute-start(bf16[128,128]{1,0:T(8,128)(2,1)S(1)} %get-tuple-element.28), channel_id=1, source_target_pairs={{0,3},{1,2},{2,1},{3,0},{4,7},{5,6},{6,5},{7,4},{8,11},{9,10},{10,... | collective-permute-start | bytes 98312 | tf_op jit(solution)/shard_map/ppermute | solution.py:399
  22.5 4.9 %collective-permute-start.7 = (bf16[128,128]{1,0:T(8,128)(2,1)S(1)}, bf16[128,128]{1,0:T(8,128)(2,1)S(1)}, u32[]{:S(2)}, u32[]{:S(2)}) collective-permute-start(bf16[128,128]{1,0:T(8,128)(2,1)S(1)} %get-tuple-element.29), channel_id=1, source_target_pairs={{0,2},{1,3},{2,0},{3,1},{4,6},{5,7},{6,4},{7,5},{8,10},{9,11},{10,... | collective-permute-start | bytes 98312 | tf_op jit(solution)/shard_map/ppermute | solution.py:399
  22.9 4.5 %collective-permute-start.8 = (bf16[128,128]{1,0:T(8,128)(2,1)S(1)}, bf16[128,128]{1,0:T(8,128)(2,1)S(1)}, u32[]{:S(2)}, u32[]{:S(2)}) collective-permute-start(bf16[128,128]{1,0:T(8,128)(2,1)S(1)} %get-tuple-element.30), channel_id=1, source_target_pairs={{0,1},{1,0},{2,3},{3,2},{4,5},{5,4},{6,7},{7,6},{8,9},{9,8},{10,11... | collective-permute-start | bytes 98312 | tf_op jit(solution)/shard_map/ppermute | solution.py:399

commit v9 on v7

--- a/solution.py
+++ b/solution.py
@@ -8,6 +8,7 @@
 F32 = jnp.float32
 BF16 = jnp.bfloat16
 LANES = 128
+CODE_ROWS = 8
 
 
 def nt_dot(a, b):
@@ -60,16 +61,16 @@
     for n in range(boxes):
         slot = (oct_s[n] * parents + lax.rem(par_s[n], parents)).astype(F32)
         codes = jnp.where(lane == n, slot, codes)
-    codes = codes.astype(BF16)
+    codes = codes[:CODE_ROWS].astype(BF16)
     x_rows[...] = jnp.concatenate(own, axis=0).astype(BF16)
     first = jnp.concatenate(own[:reach], axis=0)
     last = jnp.concatenate(own[reach:], axis=0)
     odd = lax.rem(lax.axis_index("samp"), 2) == 1
     at = parts * boxes
-    to_beside[at + boxes :] = jnp.where(odd, first, last).astype(BF16)
-    to_far[at + boxes :] = jnp.where(odd, last, first).astype(BF16)
+    to_beside[at + CODE_ROWS :] = jnp.where(odd, first, last).astype(BF16)
+    to_far[at + CODE_ROWS :] = jnp.where(odd, last, first).astype(BF16)
     for ref in (plain, to_beside, to_far):
-        ref[at : at + boxes] = codes
+        ref[at : at + CODE_ROWS] = codes
     for n in range(boxes):
         if n % per == 0:
             big[n // per].wait()
@@ -82,21 +83,21 @@
 
 def up_kernel(*refs, pieces, boxes, parents, parts):
     msgs = refs[:pieces]
-    interp_ref, phase_ref, after, out_ref, out_copy, place_ref, raised, folded = refs[pieces:]
+    interp_ref, phase_ref, after, cross_a, cross_b, side_a, side_b, out_ref, place_ref, raised, folded = refs[pieces:]
     forward = msgs[1]
     slots = 8 * parents
     samples = raised.shape[1]
     first = lax.axis_index("samp") * samples
     mine = interp_ref[pl.ds(pl.multiple_of(first, samples), samples)]
     per_tile = LANES // boxes
-    at = parts * boxes
+    code_at = parts * boxes
     tiles = []
     for t in range(0, pieces, per_tile):
-        lane = lax.broadcasted_iota(jnp.int32, (boxes, LANES), 1) // boxes
-        code = msgs[t][at : at + boxes].astype(F32)
+        lane = lax.broadcasted_iota(jnp.int32, (CODE_ROWS, LANES), 1) // boxes
+        code = msgs[t][code_at : code_at + CODE_ROWS].astype(F32)
         for d in range(1, min(per_tile, pieces - t)):
-            code = jnp.where(lane == d, msgs[t + d][at : at + boxes].astype(F32), code)
-        code = jnp.concatenate([code] * (slots // boxes), axis=0)
+            code = jnp.where(lane == d, msgs[t + d][code_at : code_at + CODE_ROWS].astype(F32), code)
+        code = jnp.concatenate([code] * (slots // CODE_ROWS), axis=0)
         want = lax.broadcasted_iota(jnp.int32, (slots, LANES), 0).astype(F32)
         width = min(per_tile, pieces - t) * boxes
         tiles.append(jnp.where(code == want, 1.0, 0.0)[:, :width])
@@ -139,12 +140,16 @@
                 [folded[t, pl.ds(p + e, parts, stride=parents), :] for e in range(2)], axis=0
             )
             both = both.astype(BF16)
-            for ref in (out_ref, out_copy):
-                ref[p * parts : (p + 2) * parts, lanes] = both
-        extra = out_ref.shape[0] - parents * parts
+            at = p * parts
+            out_ref[at : at + 2 * parts, lanes] = both
+            split = parents * parts // 2
+            both_refs, at = ((cross_a, side_a), at) if at < split else ((cross_b, side_b), at - split)
+            for ref in both_refs:
+                ref[at : at + 2 * parts, lanes] = both
+        extra = cross_a.shape[0] - parents * parts // 2
         start = forward.shape[0] - extra * (samples // LANES - t)
-        for ref in (out_ref, out_copy):
-            ref[parents * parts :, lanes] = forward[start : start + extra]
+        for ref in (cross_a, cross_b, side_a, side_b):
+            ref[ref.shape[0] - extra :, lanes] = forward[start : start + extra]
 
 
 def zone(parents):
@@ -181,7 +186,7 @@
 
 
 def down_kernel(
-    own, across, beside, dense, interp_ref, phase_ref, place_ref, after, *refs, pieces, boxes, parents, parts
+    own, across_a, across_b, beside_a, beside_b, dense, interp_ref, phase_ref, place_ref, after, *refs, pieces, boxes, parents, parts
 ):
     outs = refs[:pieces]
     window, incoming, shifted = refs[pieces:]
@@ -193,12 +198,12 @@
     odd = lax.rem(lax.axis_index("box"), 2)
     rows = parents * parts
     window[parents : 2 * parents] = own[:rows].astype(F32).reshape(parents, parts, samples)
-    window[pl.ds(2 * parents * odd, parents)] = (
-        across[:rows].astype(F32).reshape(parents, parts, samples)
-    )
-    window[pl.ds(2 * parents * (1 - odd), parents)] = (
-        beside[:rows].astype(F32).reshape(parents, parts, samples)
-    )
+    some = parents // 2
+    for near_pair, side in (((across_a, across_b), odd), ((beside_a, beside_b), 1 - odd)):
+        for i, ref in enumerate(near_pair):
+            window[pl.ds(2 * parents * side + i * some, some)] = (
+                ref[: some * parts].astype(F32).reshape(some, parts, samples)
+            )
     offsets = zone(parents)
 
     def one(p):
@@ -245,7 +250,7 @@
             ]
 
 
-def near_kernel(*refs, late, nsamp, total, halo_rows, parent_rows):
+def near_kernel(*refs, late, nsamp, total, halo_rows, extra_rows):
     neighbours, own, mats, after, *halos, out_ref, window, nbr, sems = refs
     if late:
         across, beside, *from_far = halos
@@ -268,7 +273,7 @@
         def forwarded(ref):
             return jnp.concatenate(
                 [
-                    ref[parent_rows:, t * LANES : (t + 1) * LANES].astype(F32)
+                    ref[ref.shape[0] - extra_rows :, t * LANES : (t + 1) * LANES].astype(F32)
                     for t in range(ref.shape[1] // LANES)
                 ],
                 axis=0,
@@ -304,8 +309,8 @@
 
 def final_kernel(*refs, pieces):
     parts_in = refs[:pieces]
-    near_early, near_late, mats, out_ref, field = refs[pieces:]
-    boxes, halves, rhs = out_ref.shape[:3]
+    near_early, near_late, mats, out_hbm, field, out, sems = refs[pieces:]
+    boxes, halves, rhs = out.shape[:3]
     parts = halves * rhs
     half = boxes // 2
     odd = lax.rem(lax.axis_index("samp"), 2) == 1
@@ -313,14 +318,24 @@
     for m in parts_in[1:]:
         total += m[...].astype(F32)
     field[...] = total.astype(BF16).astype(F32)
+    copies = [
+        pltpu.make_async_copy(
+            out.at[pl.ds(i * half, half)], out_hbm.at[pl.ds(i * half, half)], sems.at[i]
+        )
+        for i in range(2)
+    ]
     for n in range(boxes):
         v = field[pl.ds(n, parts, stride=boxes), :]
         wide = jnp.concatenate([v, times_i(v)], axis=1).astype(BF16)
         y = nt_dot(wide, jnp.concatenate([mats[n, 0], mats[n, 1]], axis=1))
         i = n % half
         y = y + jnp.where(odd == (n < half), near_early[i], near_late[i])
-        out_ref[n, 0] = y[:rhs]
-        out_ref[n, 1] = y[rhs:]
+        out[n, 0] = y[:rhs]
+        out[n, 1] = y[rhs:]
+        if i == half - 1:
+            copies[n // half].start()
+    for copy in copies:
+        copy.wait()
 
 
 def whole_in(kind):
@@ -366,7 +381,7 @@
     near_count = near_blocks.shape[1]
     halo_rows = reach * parts
     parent_rows = parents * parts
-    plain_rows = (parts + 1) * boxes
+    plain_rows = parts * boxes + CODE_ROWS
 
     def shape(dims, dtype=BF16):
         return jax.ShapeDtypeStruct(dims, dtype)
@@ -432,15 +447,20 @@
         x_rows,
     )
 
-    to_across, parent_pat, place_onehot = pl.pallas_call(
+    half_rows = parent_rows // 2
+    extra_rows = halo_rows * LANES // samples
+    cross_a, cross_b, side_a, side_b, parent_pat, place_onehot = pl.pallas_call(
         lambda *refs: up_kernel(
             *refs, pieces=nsamp, boxes=boxes, parents=parents, parts=parts
         ),
         in_specs=[whole_in(VM)] * (nsamp + 3),
-        out_specs=[whole_in(VM)] * 3,
+        out_specs=[whole_in(VM)] * 6,
         out_shape=[
-            shape((parent_rows + halo_rows * LANES // samples, samples)),
-            shape((parent_rows + halo_rows * LANES // samples, samples)),
+            shape((half_rows + extra_rows, samples)),
+            shape((half_rows + extra_rows, samples)),
+            shape((half_rows + extra_rows, samples)),
+            shape((half_rows + extra_rows, samples)),
+            shape((parent_rows, samples)),
             shape((leaves, slots)),
         ],
         scratch_shapes=[
@@ -451,10 +471,12 @@
         name="up",
     )(*[messages[d] for d in order], interp, phases, near_list)
 
-    across = lax.ppermute(
-        to_across, "box", [(i, (i + (1 if i % 2 else -1)) % nbox) for i in range(nbox)]
-    )
-    beside = lax.ppermute(parent_pat, "box", [(i, i ^ 1) for i in range(nbox)])
+    cross = [(i, (i + (1 if i % 2 else -1)) % nbox) for i in range(nbox)]
+    across_a = lax.ppermute(cross_a, "box", cross)
+    across_b = lax.ppermute(cross_b, "box", cross)
+    pair = [(i, i ^ 1) for i in range(nbox)]
+    beside_a = lax.ppermute(side_a, "box", pair)
+    beside_b = lax.ppermute(side_b, "box", pair)
 
     def near_half(late, args):
         return pl.pallas_call(
@@ -464,7 +486,7 @@
                 nsamp=nsamp,
                 total=total,
                 halo_rows=halo_rows,
-                parent_rows=parent_rows,
+                extra_rows=extra_rows,
             ),
             in_specs=[whole_in(VM)] * (3 + len(args)),
             out_specs=whole_in(VM),
@@ -489,7 +511,7 @@
         lambda *refs: down_kernel(
             *refs, pieces=nsamp, boxes=boxes, parents=parents, parts=parts
         ),
-        in_specs=[whole_in(VM)] * 8,
+        in_specs=[whole_in(VM)] * 10,
         out_specs=[whole_in(VM)] * nsamp,
         out_shape=[shape((parts * boxes, LANES))] * nsamp,
         scratch_shapes=[
@@ -499,19 +521,23 @@
         ],
         compiler_params=PARAMS,
         name="down",
-    )(parent_pat, across, beside, dense, interp, phases, place_onehot, near_early)
+    )(parent_pat, across_a, across_b, beside_a, beside_b, dense, interp, phases, place_onehot, near_early)
 
     pieces = dict(zip(order, fields))
     partial = [pieces[0]] + [exchange(pieces[d], d) for d in reversed(range(1, nsamp))]
 
-    near_late = near_half(True, [fields[0], across, beside, *far_messages])
+    near_late = near_half(True, [fields[0], across_b, beside_b, *far_messages])
 
     return pl.pallas_call(
         lambda *refs: final_kernel(*refs, pieces=nsamp),
         in_specs=[whole_in(VM)] * (nsamp + 3),
-        out_specs=whole_in(VM),
+        out_specs=whole_in(HBM),
         out_shape=shape(xvec.shape, F32),
-        scratch_shapes=[VM((parts * boxes, LANES), F32)],
+        scratch_shapes=[
+            VM((parts * boxes, LANES), F32),
+            VM(xvec.shape, F32),
+            DMA((2,)),
+        ],
         compiler_params=PARAMS,
         name="final",
     )(*partial, near_early, near_late, place)

time: 27.7 us -> 27.7 us (level)
  waiting for transfers between devices: 5.92 us -> 4.35 us
  starting transfers between devices: 11.9 us -> 13.4 us
    ppermute x2 -> x4, waiting for transfers between devices: 2.11 us -> 0.49 us  [the longest x1 0.48 us: on_device(): across_b = lax.ppermute(cross_b, 'box', cross)]
    ppermute x2 -> x4, starting transfers between devices: 1.67 us -> 3.22 us  [the longest x1 2.33 us: on_device(): across_b = lax.ppermute(cross_b, 'box', cross)]
  transfers between devices with their start and end apart: 8 -> 10, of which waited for: 4 -> 4; matrix products, arithmetic and copies ran while one was open for 0% -> 0% of each run, Pallas kernels for 19% -> 19%
where the time goes in v9:
time: 27.7 us; the launch traced here: 27.6 us
  starting transfers between devices  13.4 us (48%)
  Pallas kernels  9.68 us (35%)
  waiting for transfers between devices  4.35 us (16%)
    ppermute x6, starting transfers between devices, exchange(): return lax.ppermute(x, 'samp', [(i, i ^ d) for i in range(nsamp)])  10.2 us
    ppermute x6, waiting for transfers between devices, exchange(): return lax.ppermute(x, 'samp', [(i, i ^ d) for i in range(nsamp)])  3.87 us
    pallas_call x2, Pallas kernels, near_half(): pl.pallas_call(lambda *refs: near_kernel(*refs, late=late, nsamp=nsamp, t...  3.62 us
    ppermute x1, starting transfers between devices, on_device(): across_b = lax.ppermute(cross_b, 'box', cross)  2.33 us
    pallas_call x1, Pallas kernels, on_device(): pl.pallas_call(lambda *refs: leaf_kernel(*refs, parents=parents), in_spec...  1.93 us
    pallas_call x1, Pallas kernels, on_device(): pl.pallas_call(lambda *refs: prep_kernel(*refs, parents=parents, all_pare...  1.6 us
    pallas_call x1, Pallas kernels, on_device(): pl.pallas_call(lambda *refs: final_kernel(*refs, pieces=nsamp), in_specs=...  1.03 us
    pallas_call x1, Pallas kernels, on_device(): pl.pallas_call(lambda *refs: down_kernel(*refs, pieces=nsamp, boxes=boxes...  0.82 us
  transfers between devices with their start and end apart: 10, of which 4 were waited for; matrix products, arithmetic and copies ran while one was open for 0% of the time, Pallas kernels for 19%

profile of v9, /device:TPU:0, one launch (start us, length us, event | category | flops | bytes accessed | tf_op | source)
XLA Modules:
  0.0 27.6 jit_solution(8159917952867737729)
XLA Ops:
  0.0 0.0 copy-start
  0.0 1.9 %leaf.1 = (bf16[200,128]{1,0:T(8,128)(2,1)S(1)}, bf16[136,128]{1,0:T(8,128)(2,1)S(1)}, bf16[200,128]{1,0:T(8,128)(2,1)S(1)}, bf16[128,128]{1,0:T(8,128)(2,1)S(1)}) custom-call(s32[16]{0:T(128)} %refs_0_.2, s32[16]{0:T(128)} %refs_1_.2, bf16[16,2,4,128]{3,2,1,0:T(4,128)(2,1)} %refs_2_.3, bf16[16,2,128,128]{3,2,1,0:T(8,128)(2,1)} %refs_3_.2), custom_call_target="tpu_custom_call" | custom-call | tf_op jit(solution)/shard_map/leaf/pallas_call | solution.py:390
  1.9 5.1 %collective-permute-start = (bf16[200,128]{1,0:T(8,128)(2,1)S(1)}, bf16[200,128]{1,0:T(8,128)(2,1)S(1)}, u32[]{:S(2)}, u32[]{:S(2)}) collective-permute-start(bf16[200,128]{1,0:T(8,128)(2,1)S(1)} %get-tuple-element.22), channel_id=1, source_target_pairs={{0,3},{1,2},{2,1},{3,0},{4,7},{5,6},{6,5},{7,4},{8,11},{9,10},{10,... | collective-permute-start | bytes 153608 | tf_op jit(solution)/shard_map/ppermute | solution.py:413
  7.1 0.0 collective-permute-start.1
  7.1 0.6 %collective-permute-start.2 = (bf16[136,128]{1,0:T(8,128)(2,1)S(1)}, bf16[136,128]{1,0:T(8,128)(2,1)S(1)}, u32[]{:S(2)}, u32[]{:S(2)}) collective-permute-start(bf16[136,128]{1,0:T(8,128)(2,1)S(1)} %get-tuple-element.21.refs_0_), channel_id=1, source_target_pairs={{0,2},{1,3},{2,0},{3,1},{4,6},{5,7},{6,4},{7,5},{8,10},{9,11},{10,... | collective-permute-start | bytes 104456 | tf_op jit(solution)/shard_map/ppermute | solution.py:413
  7.7 1.6 %prep.1 = (f32[8,14,2,512]{3,2,1,0:T(2,128)S(1)}, s32[8,16]{1,0:T(8,128)S(1)}) custom-call(s32[8,14]{1,0:T(8,128)} %refs_0_.3, s32[8,14]{1,0:T(8,128)} %refs_1_.3, s32[8,16]{1,0:T(8,128)} %bitcast.1, f32[64,2,512]{2,1,0:T(2,128)} %refs_3_.3, bf16[16,8,2,128,128]{4,3,2,1,0:T(8,128)(2,1)} %refs_2_.5, bf16[128,128]{1,0:T(8,128)(2,1)S(1)} %get-tuple-element.24.refs_5_.refs_1_), custom_call_target="tpu_custom_call" | custom-call | bytes 8388608 | tf_op jit(solution)/shard_map/prep/pallas_call | solution.py:422
  9.3 2.7 %collective-permute-done.2.refs_3_ = bf16[136,128]{1,0:T(8,128)(2,1)S(1)} collective-permute-done((bf16[136,128]{1,0:T(8,128)(2,1)S(1)}, bf16[136,128]{1,0:T(8,128)(2,1)S(1)}, u32[]{:S(2)}, u32[]{:S(2)}) %collective-permute-start.2) | collective-permute-done | bytes 34848 | tf_op jit(solution)/shard_map/ppermute | solution.py:413
  12.0 0.0 collective-permute-done.refs_1_.refs_6_
  12.0 0.0 collective-permute-done.1.refs_2_.refs_4_
  12.0 0.0 copy-done.3
  12.1 0.0 copy-done.1
  12.1 0.7 %up.1 = (bf16[48,512]{1,0:T(8,128)(2,1)S(1)}, bf16[48,512]{1,0:T(8,128)(2,1)S(1)}, bf16[48,512]{1,0:T(8,128)(2,1)S(1)}, bf16[48,512]{1,0:T(8,128)(2,1)S(1)}, bf1...) custom-call(bf16[136,128]{1,0:T(8,128)(2,1)S(1)} %get-tuple-element.21.refs_0_, ...), custom_call_target="tpu_custom_call" | custom-call | tf_op jit(solution)/shard_map/up/pallas_call | solution.py:452
  12.8 0.4 %collective-permute-start.3 = (bf16[48,512]{1,0:T(8,128)(2,1)S(1)}, bf16[48,512]{1,0:T(8,128)(2,1)S(1)}, u32[]{:S(2)}, u32[]{:S(2)}) collective-permute-start(bf16[48,512]{1,0:T(8,128)(2,1)S(1)} %get-tuple-element.27), channel_id=1, source_target_pairs={{0,28},{4,8},{8,4},{12,16},{16,12},{20,24},{24,20},{28,0},{1,29},{... | collective-permute-start | bytes 147464 | tf_op jit(solution)/shard_map/ppermute | solution.py:475
  13.1 2.3 %collective-permute-start.4 = (bf16[48,512]{1,0:T(8,128)(2,1)S(1)}, bf16[48,512]{1,0:T(8,128)(2,1)S(1)}, u32[]{:S(2)}, u32[]{:S(2)}) collective-permute-start(bf16[48,512]{1,0:T(8,128)(2,1)S(1)} %get-tuple-element.28), channel_id=1, source_target_pairs={{0,28},{4,8},{8,4},{12,16},{16,12},{20,24},{24,20},{28,0},{1,29},{... | collective-permute-start | bytes 147464 | tf_op jit(solution)/shard_map/ppermute | solution.py:476
  15.5 0.0 collective-permute-start.5
  15.5 0.5 %collective-permute-start.6 = (bf16[48,512]{1,0:T(8,128)(2,1)S(1)}, bf16[48,512]{1,0:T(8,128)(2,1)S(1)}, u32[]{:S(2)}, u32[]{:S(2)}) collective-permute-start(bf16[48,512]{1,0:T(8,128)(2,1)S(1)} %get-tuple-element.30), channel_id=1, source_target_pairs={{0,4},{4,0},{8,12},{12,8},{16,20},{20,16},{24,28},{28,24},{1,5},{5... | collective-permute-start | bytes 147464 | tf_op jit(solution)/shard_map/ppermute | solution.py:479
  16.0 0.0 copy-done
  16.0 1.8 %near.2.refs_9_.refs_4_ = f32[8,8,128]{2,1,0:T(8,128)S(1)} custom-call(s32[8,16]{1,0:T(8,128)S(1)} %get-tuple-element.25.refs_6_.refs_0_, bf16[128,128]{1,0:T(8,128)(2,1)S(1)} %get-tuple-element.24.refs_5_.refs_1_, bf16[16,8,2,128,128]{4,3,2,1,0:T(8,128)(2,1)S(1)} %copy-done, bf16[64,64]{1,0:T(8,128)(2,1)S(1)} %get-tuple-element.32.refs_3_.refs_8_, ...), custom_call_target="tpu_custom_call" | custom-call | flops 33554432 | bytes 4194304 | tf_op jit(solution)/shard_map/near/pallas_call | solution.py:482
  17.8 0.0 collective-permute-done.3.refs_1_
  17.8 0.5 %collective-permute-done.4.refs_2_.refs_4_ = bf16[48,512]{1,0:T(8,128)(2,1)S(1)} collective-permute-done((bf16[48,512]{1,0:T(8,128)(2,1)S(1)}, bf16[48,512]{1,0:T(8,128)(2,1)S(1)}, u32[]{:S(2)}, u32[]{:S(2)}) %collective-permute-start.4) | collective-permute-done | bytes 49184 | tf_op jit(solution)/shard_map/ppermute | solution.py:476
  18.3 0.0 collective-permute-done.5.refs_3_
  18.3 0.0 collective-permute-done.6.refs_4_.refs_5_
  18.3 0.8 %down.1 = (bf16[128,128]{1,0:T(8,128)(2,1)S(1)}, bf16[128,128]{1,0:T(8,128)(2,1)S(1)}, bf16[128,128]{1,0:T(8,128)(2,1)S(1)}, bf16[128,128]{1,0:T(8,128)(2,1)S(1)}) custom-call(bf16[64,512]{1,0:T(8,128)(2,1)S(1)} %get-tuple-element.26.refs_0_, bf16[48,512]{1,0:T(8,128)(2,1)S(1)} %collective-permute-done.3.refs_1_, ...), custom_call_target="tpu_custom_call" | custom-call | tf_op jit(solution)/shard_map/down/pallas_call | solution.py:510
  19.1 1.7 %collective-permute-start.7 = (bf16[128,128]{1,0:T(8,128)(2,1)S(1)}, bf16[128,128]{1,0:T(8,128)(2,1)S(1)}, u32[]{:S(2)}, u32[]{:S(2)}) collective-permute-start(bf16[128,128]{1,0:T(8,128)(2,1)S(1)} %get-tuple-element.34), channel_id=1, source_target_pairs={{0,3},{1,2},{2,1},{3,0},{4,7},{5,6},{6,5},{7,4},{8,11},{9,10},{10,... | collective-permute-start | bytes 98312 | tf_op jit(solution)/shard_map/ppermute | solution.py:413
  20.8 1.7 %collective-permute-start.8 = (bf16[128,128]{1,0:T(8,128)(2,1)S(1)}, bf16[128,128]{1,0:T(8,128)(2,1)S(1)}, u32[]{:S(2)}, u32[]{:S(2)}) collective-permute-start(bf16[128,128]{1,0:T(8,128)(2,1)S(1)} %get-tuple-element.35), channel_id=1, source_target_pairs={{0,2},{1,3},{2,0},{3,1},{4,6},{5,7},{6,4},{7,5},{8,10},{9,11},{10,... | collective-permute-start | bytes 98312 | tf_op jit(solution)/shard_map/ppermute | solution.py:413
  22.5 1.0 %collective-permute-start.9 = (bf16[128,128]{1,0:T(8,128)(2,1)S(1)}, bf16[128,128]{1,0:T(8,128)(2,1)S(1)}, u32[]{:S(2)}, u32[]{:S(2)}) collective-permute-start(bf16[128,128]{1,0:T(8,128)(2,1)S(1)} %get-tuple-element.36), channel_id=1, source_target_pairs={{0,1},{1,0},{2,3},{3,2},{4,5},{5,4},{6,7},{7,6},{8,9},{9,8},{10,11... | collective-permute-start | bytes 98312 | tf_op jit(solution)/shard_map/ppermute | solution.py:413
  23.6 1.8 %near.3.refs_5_ = f32[8,8,128]{2,1,0:T(8,128)S(1)} custom-call(s32[8,16]{1,0:T(8,128)S(1)} %get-tuple-element.25.refs_6_.refs_0_, bf16[128,128]{1,0:T(8,128)(2,1)S(1)} %get-tuple-element.24.refs_5_.refs_1_, bf16[16,8,2,128,128]{4,3,2,1,0:T(8,128)(2,1)S(1)} %copy-done, bf16[128,128]{1,0:T(8,128)(2,1)S(1)} %get-tuple-element.33.refs_3_.refs_0_, ...), custom_call_target="tpu_custom_call" | custom-call | flops 33554432 | bytes 4194304 | tf_op jit(solution)/shard_map/near/pallas_call | solution.py:482
  25.4 0.0 collective-permute-done.7.refs_1_
  25.4 0.8 %collective-permute-done.8.refs_2_ = bf16[128,128]{1,0:T(8,128)(2,1)S(1)} collective-permute-done((bf16[128,128]{1,0:T(8,128)(2,1)S(1)}, bf16[128,128]{1,0:T(8,128)(2,1)S(1)}, u32[]{:S(2)}, u32[]{:S(2)}) %collective-permute-start.8) | collective-permute-done | bytes 32800 | tf_op jit(solution)/shard_map/ppermute | solution.py:413
  26.2 0.3 %collective-permute-done.9.refs_3_ = bf16[128,128]{1,0:T(8,128)(2,1)S(1)} collective-permute-done((bf16[128,128]{1,0:T(8,128)(2,1)S(1)}, bf16[128,128]{1,0:T(8,128)(2,1)S(1)}, u32[]{:S(2)}, u32[]{:S(2)}) %collective-permute-start.9) | collective-permute-done | bytes 32800 | tf_op jit(solution)/shard_map/ppermute | solution.py:413
  26.5 0.0 copy-done.2
  26.5 1.0 %final.1 = f32[16,2,4,128]{3,2,1,0:T(4,128)} custom-call(bf16[128,128]{1,0:T(8,128)(2,1)S(1)} %get-tuple-element.33.refs_3_.refs_0_, bf16[128,128]{1,0:T(8,128)(2,1)S(1)} %collective-permute-done.7.refs_1_, bf16[128,128]{1,0:T(8,128)(2,1)S(1)} %collective-permute-done.8.refs_2_, bf16[128,128]{1,0:T(8,128)(2,1)S(1)} %collective-permute-done.9.refs_3_, ...), custom_call_target="tpu_custom_call" | custom-call | tf_op jit(solution)/shard_map/final/pallas_call | solution.py:531
  (3 shorter events, 0.0 us)
Async XLA Ops:
  0.0 16.0 %copy-start = (bf16[16,8,2,128,128]{4,3,2,1,0:T(8,128)(2,1)S(1)}, bf16[16,8,2,128,128]{4,3,2,1,0:T(8,128)(2,1)}, u32[]{:S(2)}) copy-start(bf16[16,8,2,128,128]{4,3,2,1,0:T(8,128)(2,1)} %refs_2_.5) | copy-start | bytes 25165828
  0.0 12.0 %copy-start.3 = (f32[8,2,2048]{2,1,0:T(2,128)S(1)}, f32[8,2,2048]{2,1,0:T(2,128)}, u32[]{:S(2)}) copy-start(f32[8,2,2048]{2,1,0:T(2,128)} %refs_7_.1) | copy-start | bytes 393220
  0.0 12.0 %copy-start.1 = (bf16[2048,128]{1,0:T(8,128)(2,1)S(1)}, bf16[2048,128]{1,0:T(8,128)(2,1)}, u32[]{:S(2)}) copy-start(bf16[2048,128]{1,0:T(8,128)(2,1)} %refs_6_.2) | copy-start | bytes 1572868
  1.9 10.1 %collective-permute-start = (bf16[200,128]{1,0:T(8,128)(2,1)S(1)}, bf16[200,128]{1,0:T(8,128)(2,1)S(1)}, u32[]{:S(2)}, u32[]{:S(2)}) collective-permute-start(bf16[200,128]{1,0:T(8,128)(2,1)S(1)} %get-tuple-element.22), channel_id=1, source_target_pairs={{0,3},{1,2},{2,1},{3,0},{4,7},{5,6},{6,5},{7,4},{8,11},{9,10},{10,... | collective-permute-start | bytes 153608 | tf_op jit(solution)/shard_map/ppermute | solution.py:413
  7.1 5.0 %collective-permute-start.1 = (bf16[200,128]{1,0:T(8,128)(2,1)S(1)}, bf16[200,128]{1,0:T(8,128)(2,1)S(1)}, u32[]{:S(2)}, u32[]{:S(2)}) collective-permute-start(bf16[200,128]{1,0:T(8,128)(2,1)S(1)} %get-tuple-element.23), channel_id=1, source_target_pairs={{0,1},{1,0},{2,3},{3,2},{4,5},{5,4},{6,7},{7,6},{8,9},{9,8},{10,11... | collective-permute-start | bytes 153608 | tf_op jit(solution)/shard_map/ppermute | solution.py:413
  7.1 5.0 %collective-permute-start.2 = (bf16[136,128]{1,0:T(8,128)(2,1)S(1)}, bf16[136,128]{1,0:T(8,128)(2,1)S(1)}, u32[]{:S(2)}, u32[]{:S(2)}) collective-permute-start(bf16[136,128]{1,0:T(8,128)(2,1)S(1)} %get-tuple-element.21.refs_0_), channel_id=1, source_target_pairs={{0,2},{1,3},{2,0},{3,1},{4,6},{5,7},{6,4},{7,5},{8,10},{9,11},{10,... | collective-permute-start | bytes 104456 | tf_op jit(solution)/shard_map/ppermute | solution.py:413
  12.8 5.0 %collective-permute-start.3 = (bf16[48,512]{1,0:T(8,128)(2,1)S(1)}, bf16[48,512]{1,0:T(8,128)(2,1)S(1)}, u32[]{:S(2)}, u32[]{:S(2)}) collective-permute-start(bf16[48,512]{1,0:T(8,128)(2,1)S(1)} %get-tuple-element.27), channel_id=1, source_target_pairs={{0,28},{4,8},{8,4},{12,16},{16,12},{20,24},{24,20},{28,0},{1,29},{... | collective-permute-start | bytes 147464 | tf_op jit(solution)/shard_map/ppermute | solution.py:475
  13.1 5.1 %collective-permute-start.4 = (bf16[48,512]{1,0:T(8,128)(2,1)S(1)}, bf16[48,512]{1,0:T(8,128)(2,1)S(1)}, u32[]{:S(2)}, u32[]{:S(2)}) collective-permute-start(bf16[48,512]{1,0:T(8,128)(2,1)S(1)} %get-tuple-element.28), channel_id=1, source_target_pairs={{0,28},{4,8},{8,4},{12,16},{16,12},{20,24},{24,20},{28,0},{1,29},{... | collective-permute-start | bytes 147464 | tf_op jit(solution)/shard_map/ppermute | solution.py:476
  15.5 2.8 %collective-permute-start.5 = (bf16[48,512]{1,0:T(8,128)(2,1)S(1)}, bf16[48,512]{1,0:T(8,128)(2,1)S(1)}, u32[]{:S(2)}, u32[]{:S(2)}) collective-permute-start(bf16[48,512]{1,0:T(8,128)(2,1)S(1)} %get-tuple-element.29), channel_id=1, source_target_pairs={{0,4},{4,0},{8,12},{12,8},{16,20},{20,16},{24,28},{28,24},{1,5},{5... | collective-permute-start | bytes 147464 | tf_op jit(solution)/shard_map/ppermute | solution.py:478
  15.5 2.8 %collective-permute-start.6 = (bf16[48,512]{1,0:T(8,128)(2,1)S(1)}, bf16[48,512]{1,0:T(8,128)(2,1)S(1)}, u32[]{:S(2)}, u32[]{:S(2)}) collective-permute-start(bf16[48,512]{1,0:T(8,128)(2,1)S(1)} %get-tuple-element.30), channel_id=1, source_target_pairs={{0,4},{4,0},{8,12},{12,8},{16,20},{20,16},{24,28},{28,24},{1,5},{5... | collective-permute-start | bytes 147464 | tf_op jit(solution)/shard_map/ppermute | solution.py:479
  16.0 10.6 %copy-start.2 = (bf16[16,2,128,128]{3,2,1,0:T(8,128)(2,1)S(1)}, bf16[16,2,128,128]{3,2,1,0:T(8,128)(2,1)}, u32[]{:S(2)}) copy-start(bf16[16,2,128,128]{3,2,1,0:T(8,128)(2,1)} %refs_6_.3) | copy-start | bytes 3145732
  19.1 6.3 %collective-permute-start.7 = (bf16[128,128]{1,0:T(8,128)(2,1)S(1)}, bf16[128,128]{1,0:T(8,128)(2,1)S(1)}, u32[]{:S(2)}, u32[]{:S(2)}) collective-permute-start(bf16[128,128]{1,0:T(8,128)(2,1)S(1)} %get-tuple-element.34), channel_id=1, source_target_pairs={{0,3},{1,2},{2,1},{3,0},{4,7},{5,6},{6,5},{7,4},{8,11},{9,10},{10,... | collective-permute-start | bytes 98312 | tf_op jit(solution)/shard_map/ppermute | solution.py:413
  20.8 5.4 %collective-permute-start.8 = (bf16[128,128]{1,0:T(8,128)(2,1)S(1)}, bf16[128,128]{1,0:T(8,128)(2,1)S(1)}, u32[]{:S(2)}, u32[]{:S(2)}) collective-permute-start(bf16[128,128]{1,0:T(8,128)(2,1)S(1)} %get-tuple-element.35), channel_id=1, source_target_pairs={{0,2},{1,3},{2,0},{3,1},{4,6},{5,7},{6,4},{7,5},{8,10},{9,11},{10,... | collective-permute-start | bytes 98312 | tf_op jit(solution)/shard_map/ppermute | solution.py:413
  22.5 4.0 %collective-permute-start.9 = (bf16[128,128]{1,0:T(8,128)(2,1)S(1)}, bf16[128,128]{1,0:T(8,128)(2,1)S(1)}, u32[]{:S(2)}, u32[]{:S(2)}) collective-permute-start(bf16[128,128]{1,0:T(8,128)(2,1)S(1)} %get-tuple-element.36), channel_id=1, source_target_pairs={{0,1},{1,0},{2,3},{3,2},{4,5},{5,4},{6,7},{7,6},{8,9},{9,8},{10,11... | collective-permute-start | bytes 98312 | tf_op jit(solution)/shard_map/ppermute | solution.py:413

commit v10 on v7

--- a/solution.py
+++ b/solution.py
@@ -8,6 +8,7 @@
 F32 = jnp.float32
 BF16 = jnp.bfloat16
 LANES = 128
+CODE_ROWS = 8
 
 
 def nt_dot(a, b):
@@ -60,16 +61,16 @@
     for n in range(boxes):
         slot = (oct_s[n] * parents + lax.rem(par_s[n], parents)).astype(F32)
         codes = jnp.where(lane == n, slot, codes)
-    codes = codes.astype(BF16)
+    codes = codes[:CODE_ROWS].astype(BF16)
     x_rows[...] = jnp.concatenate(own, axis=0).astype(BF16)
     first = jnp.concatenate(own[:reach], axis=0)
     last = jnp.concatenate(own[reach:], axis=0)
     odd = lax.rem(lax.axis_index("samp"), 2) == 1
     at = parts * boxes
-    to_beside[at + boxes :] = jnp.where(odd, first, last).astype(BF16)
-    to_far[at + boxes :] = jnp.where(odd, last, first).astype(BF16)
+    to_beside[at + CODE_ROWS :] = jnp.where(odd, first, last).astype(BF16)
+    to_far[at + CODE_ROWS :] = jnp.where(odd, last, first).astype(BF16)
     for ref in (plain, to_beside, to_far):
-        ref[at : at + boxes] = codes
+        ref[at : at + CODE_ROWS] = codes
     for n in range(boxes):
         if n % per == 0:
             big[n // per].wait()
@@ -82,7 +83,7 @@
 
 def up_kernel(*refs, pieces, boxes, parents, parts):
     msgs = refs[:pieces]
-    interp_ref, phase_ref, after, out_ref, out_copy, place_ref, raised, folded = refs[pieces:]
+    interp_ref, phase_ref, after, out_ref, out_copy, pass_a, pass_b, place_ref, raised, folded = refs[pieces:]
     forward = msgs[1]
     slots = 8 * parents
     samples = raised.shape[1]
@@ -92,11 +93,11 @@
     at = parts * boxes
     tiles = []
     for t in range(0, pieces, per_tile):
-        lane = lax.broadcasted_iota(jnp.int32, (boxes, LANES), 1) // boxes
-        code = msgs[t][at : at + boxes].astype(F32)
+        lane = lax.broadcasted_iota(jnp.int32, (CODE_ROWS, LANES), 1) // boxes
+        code = msgs[t][at : at + CODE_ROWS].astype(F32)
         for d in range(1, min(per_tile, pieces - t)):
-            code = jnp.where(lane == d, msgs[t + d][at : at + boxes].astype(F32), code)
-        code = jnp.concatenate([code] * (slots // boxes), axis=0)
+            code = jnp.where(lane == d, msgs[t + d][at : at + CODE_ROWS].astype(F32), code)
+        code = jnp.concatenate([code] * (slots // CODE_ROWS), axis=0)
         want = lax.broadcasted_iota(jnp.int32, (slots, LANES), 0).astype(F32)
         width = min(per_tile, pieces - t) * boxes
         tiles.append(jnp.where(code == want, 1.0, 0.0)[:, :width])
@@ -141,10 +142,8 @@
             both = both.astype(BF16)
             for ref in (out_ref, out_copy):
                 ref[p * parts : (p + 2) * parts, lanes] = both
-        extra = out_ref.shape[0] - parents * parts
-        start = forward.shape[0] - extra * (samples // LANES - t)
-        for ref in (out_ref, out_copy):
-            ref[parents * parts :, lanes] = forward[start : start + extra]
+    pass_a[...] = forward[forward.shape[0] - pass_a.shape[0] :]
+    pass_b[...] = forward[forward.shape[0] - pass_b.shape[0] :]
 
 
 def zone(parents):
@@ -181,10 +180,10 @@
 
 
 def down_kernel(
-    own, across, beside, dense, interp_ref, phase_ref, place_ref, after, *refs, pieces, boxes, parents, parts
+    own, across, beside, dense, interp_ref, phase_ref, place_ref, *refs, pieces, boxes, parents, parts
 ):
-    outs = refs[:pieces]
-    window, incoming, shifted = refs[pieces:]
+    outs = refs[3 : 3 + pieces]
+    window, incoming, shifted = refs[3 + pieces :]
     samples = window.shape[2]
     first = lax.axis_index("samp") * samples
     mine = interp_ref[pl.ds(pl.multiple_of(first, samples), samples)]
@@ -245,7 +244,7 @@
             ]
 
 
-def near_kernel(*refs, late, nsamp, total, halo_rows, parent_rows):
+def near_kernel(*refs, late, nsamp, total, halo_rows):
     neighbours, own, mats, after, *halos, out_ref, window, nbr, sems = refs
     if late:
         across, beside, *from_far = halos
@@ -265,22 +264,13 @@
         return ref[ref.shape[0] - halo_rows :].astype(F32)
 
     if late:
-        def forwarded(ref):
-            return jnp.concatenate(
-                [
-                    ref[parent_rows:, t * LANES : (t + 1) * LANES].astype(F32)
-                    for t in range(ref.shape[1] // LANES)
-                ],
-                axis=0,
-            )
-
         partner = samp ^ (samp - 1 + 2 * odd)
         halo = piece(from_far[0])
         for i in range(1, len(from_far)):
             halo = jnp.where(partner == (4 << i) - 1, piece(from_far[i]), halo)
         box_odd = lax.rem(box, 2) == 1
         from_left = samp == 0
-        passed = jnp.where(box_odd == from_left, forwarded(beside), forwarded(across))
+        passed = jnp.where(box_odd == from_left, piece(beside), piece(across))
         halo = jnp.where(jnp.logical_or(from_left, samp == nsamp - 1), passed, halo)
     else:
         halo = piece(from_beside)
@@ -366,12 +356,12 @@
     near_count = near_blocks.shape[1]
     halo_rows = reach * parts
     parent_rows = parents * parts
-    plain_rows = (parts + 1) * boxes
+    plain_rows = parts * boxes + CODE_ROWS
 
     def shape(dims, dtype=BF16):
         return jax.ShapeDtypeStruct(dims, dtype)
 
-    lift_chunks = 4
+    lift_chunks = 2
     to_far, plain, to_beside, x_rows = pl.pallas_call(
         lambda *refs: leaf_kernel(*refs, parents=parents),
         in_specs=[whole_in(HBM)] * 4,
@@ -432,15 +422,17 @@
         x_rows,
     )
 
-    to_across, parent_pat, place_onehot = pl.pallas_call(
+    to_across, parent_pat, pass_a, pass_b, place_onehot = pl.pallas_call(
         lambda *refs: up_kernel(
             *refs, pieces=nsamp, boxes=boxes, parents=parents, parts=parts
         ),
         in_specs=[whole_in(VM)] * (nsamp + 3),
-        out_specs=[whole_in(VM)] * 3,
+        out_specs=[whole_in(VM)] * 5,
         out_shape=[
-            shape((parent_rows + halo_rows * LANES // samples, samples)),
-            shape((parent_rows + halo_rows * LANES // samples, samples)),
+            shape((parent_rows, samples)),
+            shape((parent_rows, samples)),
+            shape((halo_rows, LANES)),
+            shape((halo_rows, LANES)),
             shape((leaves, slots)),
         ],
         scratch_shapes=[
@@ -451,10 +443,12 @@
         name="up",
     )(*[messages[d] for d in order], interp, phases, near_list)
 
-    across = lax.ppermute(
-        to_across, "box", [(i, (i + (1 if i % 2 else -1)) % nbox) for i in range(nbox)]
-    )
-    beside = lax.ppermute(parent_pat, "box", [(i, i ^ 1) for i in range(nbox)])
+    cross = [(i, (i + (1 if i % 2 else -1)) % nbox) for i in range(nbox)]
+    pair = [(i, i ^ 1) for i in range(nbox)]
+    across = lax.ppermute(to_across, "box", cross)
+    beside = lax.ppermute(parent_pat, "box", pair)
+    pass_across = lax.ppermute(pass_a, "box", cross)
+    pass_beside = lax.ppermute(pass_b, "box", pair)
 
     def near_half(late, args):
         return pl.pallas_call(
@@ -464,7 +458,6 @@
                 nsamp=nsamp,
                 total=total,
                 halo_rows=halo_rows,
-                parent_rows=parent_rows,
             ),
             in_specs=[whole_in(VM)] * (3 + len(args)),
             out_specs=whole_in(VM),
@@ -489,7 +482,7 @@
         lambda *refs: down_kernel(
             *refs, pieces=nsamp, boxes=boxes, parents=parents, parts=parts
         ),
-        in_specs=[whole_in(VM)] * 8,
+        in_specs=[whole_in(VM)] * 10,
         out_specs=[whole_in(VM)] * nsamp,
         out_shape=[shape((parts * boxes, LANES))] * nsamp,
         scratch_shapes=[
@@ -499,12 +492,12 @@
         ],
         compiler_params=PARAMS,
         name="down",
-    )(parent_pat, across, beside, dense, interp, phases, place_onehot, near_early)
+    )(parent_pat, across, beside, dense, interp, phases, place_onehot, near_early, pass_across, pass_beside)
 
     pieces = dict(zip(order, fields))
     partial = [pieces[0]] + [exchange(pieces[d], d) for d in reversed(range(1, nsamp))]
 
-    near_late = near_half(True, [fields[0], across, beside, *far_messages])
+    near_late = near_half(True, [fields[0], pass_across, pass_beside, *far_messages])
 
     return pl.pallas_call(
         lambda *refs: final_kernel(*refs, pieces=nsamp),

time: 27.7 us -> 27.7 us (level)
  starting transfers between devices: 11.9 us -> 13.5 us
  waiting for transfers between devices: 5.92 us -> 4.43 us
    ppermute x2 -> x4, starting transfers between devices: 1.67 us -> 3.28 us  [the longest x1 1.28 us: on_device(): beside = lax.ppermute(parent_pat, 'box', pair)]
    ppermute x2 -> x4, waiting for transfers between devices: 2.11 us -> 0.64 us  [the longest x1 0.63 us: on_device(): pass_across = lax.ppermute(pass_a, 'box', cross)]
  transfers between devices with their start and end apart: 8 -> 10, of which waited for: 4 -> 4; matrix products, arithmetic and copies ran while one was open for 0% -> 0% of each run, Pallas kernels for 19% -> 19%
where the time goes in v10:
time: 27.7 us; the launch traced here: 27.5 us
  starting transfers between devices  13.5 us (49%)
  Pallas kernels  9.51 us (34%)
  waiting for transfers between devices  4.43 us (16%)
    ppermute x6, starting transfers between devices, exchange(): return lax.ppermute(x, 'samp', [(i, i ^ d) for i in range(nsamp)])  10.2 us
    ppermute x6, waiting for transfers between devices, exchange(): return lax.ppermute(x, 'samp', [(i, i ^ d) for i in range(nsamp)])  3.79 us
    pallas_call x2, Pallas kernels, near_half(): pl.pallas_call(lambda *refs: near_kernel(*refs, late=late, nsamp=nsamp, t...  3.62 us
    pallas_call x1, Pallas kernels, on_device(): pl.pallas_call(lambda *refs: leaf_kernel(*refs, parents=parents), in_spec...  1.77 us
    pallas_call x1, Pallas kernels, on_device(): pl.pallas_call(lambda *refs: prep_kernel(*refs, parents=parents, all_pare...  1.6 us
    ppermute x1, starting transfers between devices, on_device(): beside = lax.ppermute(parent_pat, 'box', pair)  1.28 us
    ppermute x1, starting transfers between devices, on_device(): pass_across = lax.ppermute(pass_a, 'box', cross)  1.04 us
    pallas_call x1, Pallas kernels, on_device(): pl.pallas_call(lambda *refs: final_kernel(*refs, pieces=nsamp), in_specs=...  1.03 us
  transfers between devices with their start and end apart: 10, of which 4 were waited for; matrix products, arithmetic and copies ran while one was open for 0% of the time, Pallas kernels for 19%

profile of v10, /device:TPU:0, one launch (start us, length us, event | category | flops | bytes accessed | tf_op | source)
XLA Modules:
  0.0 27.5 jit_solution(13978418628276873993)
XLA Ops:
  0.0 0.0 copy-start
  0.0 1.8 %leaf.1 = (bf16[200,128]{1,0:T(8,128)(2,1)S(1)}, bf16[136,128]{1,0:T(8,128)(2,1)S(1)}, bf16[200,128]{1,0:T(8,128)(2,1)S(1)}, bf16[128,128]{1,0:T(8,128)(2,1)S(1)}) custom-call(s32[16]{0:T(128)} %refs_0_.2, s32[16]{0:T(128)} %refs_1_.2, bf16[16,2,4,128]{3,2,1,0:T(4,128)(2,1)} %refs_2_.3, bf16[16,2,128,128]{3,2,1,0:T(8,128)(2,1)} %refs_3_.2), custom_call_target="tpu_custom_call" | custom-call | tf_op jit(solution)/shard_map/leaf/pallas_call | solution.py:365
  1.8 5.1 %collective-permute-start = (bf16[200,128]{1,0:T(8,128)(2,1)S(1)}, bf16[200,128]{1,0:T(8,128)(2,1)S(1)}, u32[]{:S(2)}, u32[]{:S(2)}) collective-permute-start(bf16[200,128]{1,0:T(8,128)(2,1)S(1)} %get-tuple-element.21), channel_id=1, source_target_pairs={{0,3},{1,2},{2,1},{3,0},{4,7},{5,6},{6,5},{7,4},{8,11},{9,10},{10,... | collective-permute-start | bytes 153608 | tf_op jit(solution)/shard_map/ppermute | solution.py:388
  6.9 0.0 collective-permute-start.1
  6.9 0.6 %collective-permute-start.2 = (bf16[136,128]{1,0:T(8,128)(2,1)S(1)}, bf16[136,128]{1,0:T(8,128)(2,1)S(1)}, u32[]{:S(2)}, u32[]{:S(2)}) collective-permute-start(bf16[136,128]{1,0:T(8,128)(2,1)S(1)} %get-tuple-element.20.refs_0_), channel_id=1, source_target_pairs={{0,2},{1,3},{2,0},{3,1},{4,6},{5,7},{6,4},{7,5},{8,10},{9,11},{10,... | collective-permute-start | bytes 104456 | tf_op jit(solution)/shard_map/ppermute | solution.py:388
  7.5 1.6 %prep.1 = (f32[8,14,2,512]{3,2,1,0:T(2,128)S(1)}, s32[8,16]{1,0:T(8,128)S(1)}) custom-call(s32[8,14]{1,0:T(8,128)} %refs_0_.3, s32[8,14]{1,0:T(8,128)} %refs_1_.3, s32[8,16]{1,0:T(8,128)} %bitcast.1, f32[64,2,512]{2,1,0:T(2,128)} %refs_3_.3, bf16[16,8,2,128,128]{4,3,2,1,0:T(8,128)(2,1)} %refs_2_.5, bf16[128,128]{1,0:T(8,128)(2,1)S(1)} %get-tuple-element.23.refs_5_.refs_1_), custom_call_target="tpu_custom_call" | custom-call | bytes 8388608 | tf_op jit(solution)/shard_map/prep/pallas_call | solution.py:397
  9.1 2.7 %collective-permute-done.2.refs_3_ = bf16[136,128]{1,0:T(8,128)(2,1)S(1)} collective-permute-done((bf16[136,128]{1,0:T(8,128)(2,1)S(1)}, bf16[136,128]{1,0:T(8,128)(2,1)S(1)}, u32[]{:S(2)}, u32[]{:S(2)}) %collective-permute-start.2) | collective-permute-done | bytes 34848 | tf_op jit(solution)/shard_map/ppermute | solution.py:388
  11.9 0.0 collective-permute-done.refs_1_.refs_6_
  11.9 0.0 collective-permute-done.1.refs_2_.refs_4_
  11.9 0.0 copy-done.3
  11.9 0.0 copy-done.1
  11.9 0.7 %up.1 = (bf16[64,512]{1,0:T(8,128)(2,1)S(1)}, bf16[64,512]{1,0:T(8,128)(2,1)S(1)}, bf16[64,128]{1,0:T(8,128)(2,1)S(1)}, bf16[64,128]{1,0:T(8,128)(2,1)S(1)}, bf16[64,64]{1,0:T(8,128)(2,1)S(1)}) custom-call(bf16[136,128]{1,0:T(8,128)(2,1)S(1)} %get-tuple-element.20.refs_0_, bf16[200,128]{1,0:T(8,128)(2,1)S(1)} %collective-permute-done.refs_1_.refs_6_, ...), custom_call_target="tpu_custom_call" | custom-call | tf_op jit(solution)/shard_map/up/pallas_call | solution.py:425
  12.6 0.4 %collective-permute-start.3 = (bf16[64,512]{1,0:T(8,128)(2,1)S(1)}, bf16[64,512]{1,0:T(8,128)(2,1)S(1)}, u32[]{:S(2)}, u32[]{:S(2)}) collective-permute-start(bf16[64,512]{1,0:T(8,128)(2,1)S(1)} %get-tuple-element.26), channel_id=1, source_target_pairs={{0,28},{4,8},{8,4},{12,16},{16,12},{20,24},{24,20},{28,0},{1,29},{... | collective-permute-start | bytes 196616 | tf_op jit(solution)/shard_map/ppermute | solution.py:448
  13.0 1.3 %collective-permute-start.4 = (bf16[64,512]{1,0:T(8,128)(2,1)S(1)}, bf16[64,512]{1,0:T(8,128)(2,1)S(1)}, u32[]{:S(2)}, u32[]{:S(2)}) collective-permute-start(bf16[64,512]{1,0:T(8,128)(2,1)S(1)} %get-tuple-element.25.refs_0_), channel_id=1, source_target_pairs={{0,4},{4,0},{8,12},{12,8},{16,20},{20,16},{24,28},{28,24},{1,5},{5... | collective-permute-start | bytes 196616 | tf_op jit(solution)/shard_map/ppermute | solution.py:449
  14.2 1.0 %collective-permute-start.5 = (bf16[64,128]{1,0:T(8,128)(2,1)S(1)}, bf16[64,128]{1,0:T(8,128)(2,1)S(1)}, u32[]{:S(2)}, u32[]{:S(2)}) collective-permute-start(bf16[64,128]{1,0:T(8,128)(2,1)S(1)} %get-tuple-element.29), channel_id=1, source_target_pairs={{0,28},{4,8},{8,4},{12,16},{16,12},{20,24},{24,20},{28,0},{1,29},{... | collective-permute-start | bytes 49160 | tf_op jit(solution)/shard_map/ppermute | solution.py:450
  15.3 0.6 %collective-permute-start.6 = (bf16[64,128]{1,0:T(8,128)(2,1)S(1)}, bf16[64,128]{1,0:T(8,128)(2,1)S(1)}, u32[]{:S(2)}, u32[]{:S(2)}) collective-permute-start(bf16[64,128]{1,0:T(8,128)(2,1)S(1)} %get-tuple-element.30), channel_id=1, source_target_pairs={{0,4},{4,0},{8,12},{12,8},{16,20},{20,16},{24,28},{28,24},{1,5},{5... | collective-permute-start | bytes 49160 | tf_op jit(solution)/shard_map/ppermute | solution.py:451
  15.9 0.0 copy-done
  15.9 1.8 %near.2.refs_7_.refs_4_ = f32[8,8,128]{2,1,0:T(8,128)S(1)} custom-call(s32[8,16]{1,0:T(8,128)S(1)} %get-tuple-element.24.refs_6_.refs_0_, bf16[128,128]{1,0:T(8,128)(2,1)S(1)} %get-tuple-element.23.refs_5_.refs_1_, bf16[16,8,2,128,128]{4,3,2,1,0:T(8,128)(2,1)S(1)} %copy-done, bf16[64,64]{1,0:T(8,128)(2,1)S(1)} %get-tuple-element.28.refs_3_.refs_6_, ...), custom_call_target="tpu_custom_call" | custom-call | flops 33554432 | bytes 4194304 | tf_op jit(solution)/shard_map/near/pallas_call | solution.py:454
  17.7 0.6 %collective-permute-done.5.refs_8_.refs_4_ = bf16[64,128]{1,0:T(8,128)(2,1)S(1)} collective-permute-done((bf16[64,128]{1,0:T(8,128)(2,1)S(1)}, bf16[64,128]{1,0:T(8,128)(2,1)S(1)}, u32[]{:S(2)}, u32[]{:S(2)}) %collective-permute-start.5) | collective-permute-done | bytes 16416 | tf_op jit(solution)/shard_map/ppermute | solution.py:450
  18.3 0.0 collective-permute-done.6.refs_9_.refs_5_
  18.3 0.0 collective-permute-done.3.refs_1_
  18.3 0.0 collective-permute-done.4.refs_2_
  18.3 0.8 %down.1 = (bf16[128,128]{1,0:T(8,128)(2,1)S(1)}, bf16[128,128]{1,0:T(8,128)(2,1)S(1)}, bf16[128,128]{1,0:T(8,128)(2,1)S(1)}, bf16[128,128]{1,0:T(8,128)(2,1)S(1)}) custom-call(bf16[64,512]{1,0:T(8,128)(2,1)S(1)} %get-tuple-element.25.refs_0_, bf16[64,512]{1,0:T(8,128)(2,1)S(1)} %collective-permute-done.3.refs_1_, ...), custom_call_target="tpu_custom_call" | custom-call | tf_op jit(solution)/shard_map/down/pallas_call | solution.py:481
  19.2 1.7 %collective-permute-start.7 = (bf16[128,128]{1,0:T(8,128)(2,1)S(1)}, bf16[128,128]{1,0:T(8,128)(2,1)S(1)}, u32[]{:S(2)}, u32[]{:S(2)}) collective-permute-start(bf16[128,128]{1,0:T(8,128)(2,1)S(1)} %get-tuple-element.32), channel_id=1, source_target_pairs={{0,3},{1,2},{2,1},{3,0},{4,7},{5,6},{6,5},{7,4},{8,11},{9,10},{10,... | collective-permute-start | bytes 98312 | tf_op jit(solution)/shard_map/ppermute | solution.py:388
  20.9 1.7 %collective-permute-start.8 = (bf16[128,128]{1,0:T(8,128)(2,1)S(1)}, bf16[128,128]{1,0:T(8,128)(2,1)S(1)}, u32[]{:S(2)}, u32[]{:S(2)}) collective-permute-start(bf16[128,128]{1,0:T(8,128)(2,1)S(1)} %get-tuple-element.33), channel_id=1, source_target_pairs={{0,2},{1,3},{2,0},{3,1},{4,6},{5,7},{6,4},{7,5},{8,10},{9,11},{10,... | collective-permute-start | bytes 98312 | tf_op jit(solution)/shard_map/ppermute | solution.py:388
  22.6 1.0 %collective-permute-start.9 = (bf16[128,128]{1,0:T(8,128)(2,1)S(1)}, bf16[128,128]{1,0:T(8,128)(2,1)S(1)}, u32[]{:S(2)}, u32[]{:S(2)}) collective-permute-start(bf16[128,128]{1,0:T(8,128)(2,1)S(1)} %get-tuple-element.34), channel_id=1, source_target_pairs={{0,1},{1,0},{2,3},{3,2},{4,5},{5,4},{6,7},{7,6},{8,9},{9,8},{10,11... | collective-permute-start | bytes 98312 | tf_op jit(solution)/shard_map/ppermute | solution.py:388
  23.6 1.8 %near.3.refs_5_ = f32[8,8,128]{2,1,0:T(8,128)S(1)} custom-call(s32[8,16]{1,0:T(8,128)S(1)} %get-tuple-element.24.refs_6_.refs_0_, bf16[128,128]{1,0:T(8,128)(2,1)S(1)} %get-tuple-element.23.refs_5_.refs_1_, bf16[16,8,2,128,128]{4,3,2,1,0:T(8,128)(2,1)S(1)} %copy-done, bf16[128,128]{1,0:T(8,128)(2,1)S(1)} %get-tuple-element.31.refs_3_.refs_0_, ...), custom_call_target="tpu_custom_call" | custom-call | flops 33554432 | bytes 4194304 | tf_op jit(solution)/shard_map/near/pallas_call | solution.py:454
  25.4 0.0 collective-permute-done.7.refs_1_
  25.4 0.5 %collective-permute-done.8.refs_2_ = bf16[128,128]{1,0:T(8,128)(2,1)S(1)} collective-permute-done((bf16[128,128]{1,0:T(8,128)(2,1)S(1)}, bf16[128,128]{1,0:T(8,128)(2,1)S(1)}, u32[]{:S(2)}, u32[]{:S(2)}) %collective-permute-start.8) | collective-permute-done | bytes 32800 | tf_op jit(solution)/shard_map/ppermute | solution.py:388
  26.0 0.5 %collective-permute-done.9.refs_3_ = bf16[128,128]{1,0:T(8,128)(2,1)S(1)} collective-permute-done((bf16[128,128]{1,0:T(8,128)(2,1)S(1)}, bf16[128,128]{1,0:T(8,128)(2,1)S(1)}, u32[]{:S(2)}, u32[]{:S(2)}) %collective-permute-start.9) | collective-permute-done | bytes 32800 | tf_op jit(solution)/shard_map/ppermute | solution.py:388
  26.5 0.0 copy-done.2
  26.5 1.0 %final.1 = f32[16,2,4,128]{3,2,1,0:T(4,128)} custom-call(bf16[128,128]{1,0:T(8,128)(2,1)S(1)} %get-tuple-element.31.refs_3_.refs_0_, bf16[128,128]{1,0:T(8,128)(2,1)S(1)} %collective-permute-done.7.refs_1_, bf16[128,128]{1,0:T(8,128)(2,1)S(1)} %collective-permute-done.8.refs_2_, bf16[128,128]{1,0:T(8,128)(2,1)S(1)} %collective-permute-done.9.refs_3_, ...), custom_call_target="tpu_custom_call" | custom-call | tf_op jit(solution)/shard_map/final/pallas_call | solution.py:502
  (3 shorter events, 0.0 us)
Async XLA Ops:
  0.0 15.9 %copy-start = (bf16[16,8,2,128,128]{4,3,2,1,0:T(8,128)(2,1)S(1)}, bf16[16,8,2,128,128]{4,3,2,1,0:T(8,128)(2,1)}, u32[]{:S(2)}) copy-start(bf16[16,8,2,128,128]{4,3,2,1,0:T(8,128)(2,1)} %refs_2_.5) | copy-start | bytes 25165828
  0.0 11.9 %copy-start.3 = (f32[8,2,2048]{2,1,0:T(2,128)S(1)}, f32[8,2,2048]{2,1,0:T(2,128)}, u32[]{:S(2)}) copy-start(f32[8,2,2048]{2,1,0:T(2,128)} %refs_5_.3) | copy-start | bytes 393220
  0.0 11.9 %copy-start.1 = (bf16[2048,128]{1,0:T(8,128)(2,1)S(1)}, bf16[2048,128]{1,0:T(8,128)(2,1)}, u32[]{:S(2)}) copy-start(bf16[2048,128]{1,0:T(8,128)(2,1)} %refs_4_.5) | copy-start | bytes 1572868
  1.8 10.1 %collective-permute-start = (bf16[200,128]{1,0:T(8,128)(2,1)S(1)}, bf16[200,128]{1,0:T(8,128)(2,1)S(1)}, u32[]{:S(2)}, u32[]{:S(2)}) collective-permute-start(bf16[200,128]{1,0:T(8,128)(2,1)S(1)} %get-tuple-element.21), channel_id=1, source_target_pairs={{0,3},{1,2},{2,1},{3,0},{4,7},{5,6},{6,5},{7,4},{8,11},{9,10},{10,... | collective-permute-start | bytes 153608 | tf_op jit(solution)/shard_map/ppermute | solution.py:388
  6.9 5.0 %collective-permute-start.1 = (bf16[200,128]{1,0:T(8,128)(2,1)S(1)}, bf16[200,128]{1,0:T(8,128)(2,1)S(1)}, u32[]{:S(2)}, u32[]{:S(2)}) collective-permute-start(bf16[200,128]{1,0:T(8,128)(2,1)S(1)} %get-tuple-element.22), channel_id=1, source_target_pairs={{0,1},{1,0},{2,3},{3,2},{4,5},{5,4},{6,7},{7,6},{8,9},{9,8},{10,11... | collective-permute-start | bytes 153608 | tf_op jit(solution)/shard_map/ppermute | solution.py:388
  6.9 5.0 %collective-permute-start.2 = (bf16[136,128]{1,0:T(8,128)(2,1)S(1)}, bf16[136,128]{1,0:T(8,128)(2,1)S(1)}, u32[]{:S(2)}, u32[]{:S(2)}) collective-permute-start(bf16[136,128]{1,0:T(8,128)(2,1)S(1)} %get-tuple-element.20.refs_0_), channel_id=1, source_target_pairs={{0,2},{1,3},{2,0},{3,1},{4,6},{5,7},{6,4},{7,5},{8,10},{9,11},{10,... | collective-permute-start | bytes 104456 | tf_op jit(solution)/shard_map/ppermute | solution.py:388
  12.6 5.7 %collective-permute-start.3 = (bf16[64,512]{1,0:T(8,128)(2,1)S(1)}, bf16[64,512]{1,0:T(8,128)(2,1)S(1)}, u32[]{:S(2)}, u32[]{:S(2)}) collective-permute-start(bf16[64,512]{1,0:T(8,128)(2,1)S(1)} %get-tuple-element.26), channel_id=1, source_target_pairs={{0,28},{4,8},{8,4},{12,16},{16,12},{20,24},{24,20},{28,0},{1,29},{... | collective-permute-start | bytes 196616 | tf_op jit(solution)/shard_map/ppermute | solution.py:448
  13.0 5.4 %collective-permute-start.4 = (bf16[64,512]{1,0:T(8,128)(2,1)S(1)}, bf16[64,512]{1,0:T(8,128)(2,1)S(1)}, u32[]{:S(2)}, u32[]{:S(2)}) collective-permute-start(bf16[64,512]{1,0:T(8,128)(2,1)S(1)} %get-tuple-element.25.refs_0_), channel_id=1, source_target_pairs={{0,4},{4,0},{8,12},{12,8},{16,20},{20,16},{24,28},{28,24},{1,5},{5... | collective-permute-start | bytes 196616 | tf_op jit(solution)/shard_map/ppermute | solution.py:449
  14.2 4.1 %collective-permute-start.5 = (bf16[64,128]{1,0:T(8,128)(2,1)S(1)}, bf16[64,128]{1,0:T(8,128)(2,1)S(1)}, u32[]{:S(2)}, u32[]{:S(2)}) collective-permute-start(bf16[64,128]{1,0:T(8,128)(2,1)S(1)} %get-tuple-element.29), channel_id=1, source_target_pairs={{0,28},{4,8},{8,4},{12,16},{16,12},{20,24},{24,20},{28,0},{1,29},{... | collective-permute-start | bytes 49160 | tf_op jit(solution)/shard_map/ppermute | solution.py:450
  15.3 3.0 %collective-permute-start.6 = (bf16[64,128]{1,0:T(8,128)(2,1)S(1)}, bf16[64,128]{1,0:T(8,128)(2,1)S(1)}, u32[]{:S(2)}, u32[]{:S(2)}) collective-permute-start(bf16[64,128]{1,0:T(8,128)(2,1)S(1)} %get-tuple-element.30), channel_id=1, source_target_pairs={{0,4},{4,0},{8,12},{12,8},{16,20},{20,16},{24,28},{28,24},{1,5},{5... | collective-permute-start | bytes 49160 | tf_op jit(solution)/shard_map/ppermute | solution.py:451
  15.9 10.6 %copy-start.2 = (bf16[16,2,128,128]{3,2,1,0:T(8,128)(2,1)S(1)}, bf16[16,2,128,128]{3,2,1,0:T(8,128)(2,1)}, u32[]{:S(2)}) copy-start(bf16[16,2,128,128]{3,2,1,0:T(8,128)(2,1)} %refs_6_.1) | copy-start | bytes 3145732
  19.2 6.3 %collective-permute-start.7 = (bf16[128,128]{1,0:T(8,128)(2,1)S(1)}, bf16[128,128]{1,0:T(8,128)(2,1)S(1)}, u32[]{:S(2)}, u32[]{:S(2)}) collective-permute-start(bf16[128,128]{1,0:T(8,128)(2,1)S(1)} %get-tuple-element.32), channel_id=1, source_target_pairs={{0,3},{1,2},{2,1},{3,0},{4,7},{5,6},{6,5},{7,4},{8,11},{9,10},{10,... | collective-permute-start | bytes 98312 | tf_op jit(solution)/shard_map/ppermute | solution.py:388
  20.9 5.1 %collective-permute-start.8 = (bf16[128,128]{1,0:T(8,128)(2,1)S(1)}, bf16[128,128]{1,0:T(8,128)(2,1)S(1)}, u32[]{:S(2)}, u32[]{:S(2)}) collective-permute-start(bf16[128,128]{1,0:T(8,128)(2,1)S(1)} %get-tuple-element.33), channel_id=1, source_target_pairs={{0,2},{1,3},{2,0},{3,1},{4,6},{5,7},{6,4},{7,5},{8,10},{9,11},{10,... | collective-permute-start | bytes 98312 | tf_op jit(solution)/shard_map/ppermute | solution.py:388
  22.6 3.9 %collective-permute-start.9 = (bf16[128,128]{1,0:T(8,128)(2,1)S(1)}, bf16[128,128]{1,0:T(8,128)(2,1)S(1)}, u32[]{:S(2)}, u32[]{:S(2)}) collective-permute-start(bf16[128,128]{1,0:T(8,128)(2,1)S(1)} %get-tuple-element.34), channel_id=1, source_target_pairs={{0,1},{1,0},{2,3},{3,2},{4,5},{5,4},{6,7},{7,6},{8,9},{9,8},{10,11... | collective-permute-start | bytes 98312 | tf_op jit(solution)/shard_map/ppermute | solution.py:388

commit v11 on v7

--- a/solution.py
+++ b/solution.py
@@ -8,6 +8,7 @@
 F32 = jnp.float32
 BF16 = jnp.bfloat16
 LANES = 128
+CODE_ROWS = 8
 
 
 def nt_dot(a, b):
@@ -60,16 +61,16 @@
     for n in range(boxes):
         slot = (oct_s[n] * parents + lax.rem(par_s[n], parents)).astype(F32)
         codes = jnp.where(lane == n, slot, codes)
-    codes = codes.astype(BF16)
+    codes = codes[:CODE_ROWS].astype(BF16)
     x_rows[...] = jnp.concatenate(own, axis=0).astype(BF16)
     first = jnp.concatenate(own[:reach], axis=0)
     last = jnp.concatenate(own[reach:], axis=0)
     odd = lax.rem(lax.axis_index("samp"), 2) == 1
     at = parts * boxes
-    to_beside[at + boxes :] = jnp.where(odd, first, last).astype(BF16)
-    to_far[at + boxes :] = jnp.where(odd, last, first).astype(BF16)
+    to_beside[at + CODE_ROWS :] = jnp.where(odd, first, last).astype(BF16)
+    to_far[at + CODE_ROWS :] = jnp.where(odd, last, first).astype(BF16)
     for ref in (plain, to_beside, to_far):
-        ref[at : at + boxes] = codes
+        ref[at : at + CODE_ROWS] = codes
     for n in range(boxes):
         if n % per == 0:
             big[n // per].wait()
@@ -92,11 +93,11 @@
     at = parts * boxes
     tiles = []
     for t in range(0, pieces, per_tile):
-        lane = lax.broadcasted_iota(jnp.int32, (boxes, LANES), 1) // boxes
-        code = msgs[t][at : at + boxes].astype(F32)
+        lane = lax.broadcasted_iota(jnp.int32, (CODE_ROWS, LANES), 1) // boxes
+        code = msgs[t][at : at + CODE_ROWS].astype(F32)
         for d in range(1, min(per_tile, pieces - t)):
-            code = jnp.where(lane == d, msgs[t + d][at : at + boxes].astype(F32), code)
-        code = jnp.concatenate([code] * (slots // boxes), axis=0)
+            code = jnp.where(lane == d, msgs[t + d][at : at + CODE_ROWS].astype(F32), code)
+        code = jnp.concatenate([code] * (slots // CODE_ROWS), axis=0)
         want = lax.broadcasted_iota(jnp.int32, (slots, LANES), 0).astype(F32)
         width = min(per_tile, pieces - t) * boxes
         tiles.append(jnp.where(code == want, 1.0, 0.0)[:, :width])
@@ -111,10 +112,10 @@
         axis=1,
     )
     ordered = nn_dot(sorter, pats).astype(BF16)
-    for c in range(parts):
-        raised[c * slots : (c + 1) * slots] = nt_dot(
-            ordered[:, c * LANES : (c + 1) * LANES], mine
-        )
+    stacked = jnp.concatenate(
+        [ordered[:, c * LANES : (c + 1) * LANES] for c in range(parts)], axis=0
+    )
+    raised[...] = nt_dot(stacked, mine)
     half = parts // 2
     for t in range(samples // LANES):
         lanes = slice(t * LANES, (t + 1) * LANES)
@@ -201,6 +202,116 @@
     )
     offsets = zone(parents)
 
+    def one(p, t, source):
+        lanes = slice(t * LANES, (t + 1) * LANES)
+        acc_r = acc_i = None
+        for i, d in enumerate(offsets):
+            x = source(p + d)
+            yr = dense[p, i, 0:1, lanes] * x
+            yi = dense[p, i, 1:2, lanes] * x
+            acc_r = yr if acc_r is None else acc_r + yr
+            acc_i = yi if acc_i is None else acc_i + yi
+        got = (acc_r + times_i(acc_i)).astype(BF16).astype(F32)
+        incoming[t, pl.ds(p * parts, parts), :] = got
+
+    for t in range(samples // LANES):
+        lanes = slice(t * LANES, (t + 1) * LANES)
+        if parents <= 8:
+            held = [window[j, :, lanes] for j in range(3 * parents)]
+            for p in range(parents):
+                one(p, t, lambda j: held[parents + j])
+        else:
+            lax.fori_loop(
+                0,
+                parents,
+                lambda p, c: (one(p, t, lambda j: window[parents + j, :, lanes]), c)[1],
+                0,
+            )
+    for t in range(samples // LANES):
+        lanes = slice(t * LANES, (t + 1) * LANES)
+        here = pl.ds(pl.multiple_of(first + t * LANES, LANES), LANES)
+        for r in range(half):
+            re = im = None
+            for o in range(8):
+                ph_r = phase_ref[o, 0:1, here]
+                ph_i = phase_ref[o, 1:2, here]
+                base_r = r * slots + o * parents
+                base_i = (half + r) * slots + o * parents
+                xr = raised[base_r : base_r + parents, lanes]
+                xi = raised[base_i : base_i + parents, lanes]
+                dr = ph_r * xr - ph_i * xi
+                di = ph_r * xi + ph_i * xr
+                re = dr if re is None else re + dr
+                im = di if im is None else im + di
+            folded[t, r * parents : (r + 1) * parents] = re
+            folded[t, (half + r) * parents : (half + r + 1) * parents] = im
+        for p in range(0, parents, 2):
+            both = jnp.concatenate(
+                [folded[t, pl.ds(p + e, parts, stride=parents), :] for e in range(2)], axis=0
+            )
+            both = both.astype(BF16)
+            for ref in (out_ref, out_copy):
+                ref[p * parts : (p + 2) * parts, lanes] = both
+        extra = out_ref.shape[0] - parents * parts
+        start = forward.shape[0] - extra * (samples // LANES - t)
+        for ref in (out_ref, out_copy):
+            ref[parents * parts :, lanes] = forward[start : start + extra]
+
+
+def zone(parents):
+    return [d for d in range(-parents, parents + 1) if abs(d) >= 2]
+
+
+def prep_kernel(
+    inter, trans, neighbours, table_hbm, mats_hbm, after, dense, nbr, inter_s, trans_s, table, sems,
+    *, parents, all_parents,
+):
+    copies = [
+        pltpu.make_async_copy(inter, inter_s, sems.at[0]),
+        pltpu.make_async_copy(trans, trans_s, sems.at[1]),
+        pltpu.make_async_copy(table_hbm, table, sems.at[2]),
+        pltpu.make_async_copy(neighbours, nbr, sems.at[3]),
+    ]
+    for copy in copies:
+        copy.start()
+    for copy in copies[:3]:
+        copy.wait()
+    if len(zone(parents)) > inter.shape[1]:
+        dense[...] = jnp.zeros_like(dense)
+    first = lax.axis_index("box") * parents
+
+    def fill(p, carry):
+        for k in range(inter.shape[1]):
+            rel = lax.rem(inter_s[p, k] - first - p + parents + all_parents, all_parents)
+            at = jnp.where(rel < parents, rel, rel - 3)
+            dense[p, at] = table[trans_s[p, k]]
+        return carry
+
+    lax.fori_loop(0, parents, fill, 0)
+    copies[3].wait()
+
+
+def down_kernel(
+    own, across, beside, dense, interp_ref, phase_ref, place_ref, after, *refs, pieces, boxes, parents, parts
+):
+    outs = refs[:pieces]
+    window, incoming, shifted = refs[pieces:]
+    samples = window.shape[2]
+    first = lax.axis_index("samp") * samples
+    mine = interp_ref[pl.ds(pl.multiple_of(first, samples), samples)]
+    slots = 8 * parents
+    half = parts // 2
+    odd = lax.rem(lax.axis_index("box"), 2)
+    rows = parents * parts
+    window[parents : 2 * parents] = own[:rows].astype(F32).reshape(parents, parts, samples)
+    window[pl.ds(2 * parents * odd, parents)] = (
+        across[:rows].astype(F32).reshape(parents, parts, samples)
+    )
+    window[pl.ds(2 * parents * (1 - odd), parents)] = (
+        beside[:rows].astype(F32).reshape(parents, parts, samples)
+    )
+    offsets = zone(parents)
+
     def one(p):
         for t in range(samples // LANES):
             lanes = slice(t * LANES, (t + 1) * LANES)
@@ -366,12 +477,12 @@
     near_count = near_blocks.shape[1]
     halo_rows = reach * parts
     parent_rows = parents * parts
-    plain_rows = (parts + 1) * boxes
+    plain_rows = parts * boxes + CODE_ROWS
 
     def shape(dims, dtype=BF16):
         return jax.ShapeDtypeStruct(dims, dtype)
 
-    lift_chunks = 4
+    lift_chunks = 2
     to_far, plain, to_beside, x_rows = pl.pallas_call(
         lambda *refs: leaf_kernel(*refs, parents=parents),
         in_specs=[whole_in(HBM)] * 4,

time: 27.7 us -> 27.4 us (0.989)
  Pallas kernels: 9.67 us -> 9.36 us
where the time goes in v11:
time: 27.4 us; the launch traced here: 27.2 us
  starting transfers between devices  11.9 us (43%)
  Pallas kernels  9.36 us (34%)
  waiting for transfers between devices  5.89 us (21%)
    ppermute x6, starting transfers between devices, exchange(): return lax.ppermute(x, 'samp', [(i, i ^ d) for i in range(nsamp)])  10.2 us
    ppermute x6, waiting for transfers between devices, exchange(): return lax.ppermute(x, 'samp', [(i, i ^ d) for i in range(nsamp)])  3.79 us
    pallas_call x2, Pallas kernels, near_half(): pl.pallas_call(lambda *refs: near_kernel(*refs, late=late, nsamp=nsamp, t...  3.62 us
    ppermute x1, waiting for transfers between devices, on_device(): lax.ppermute(to_across, 'box', [(i, (i + (1 if i % 2 else -1)) % nbox) fo...  2.1 us
    pallas_call x1, Pallas kernels, on_device(): pl.pallas_call(lambda *refs: leaf_kernel(*refs, parents=parents), in_spec...  1.77 us
    pallas_call x1, Pallas kernels, on_device(): pl.pallas_call(lambda *refs: prep_kernel(*refs, parents=parents, all_pare...  1.6 us
    ppermute x1, starting transfers between devices, on_device(): beside = lax.ppermute(parent_pat, 'box', [(i, i ^ 1) for i in range(nbox)])  1.29 us
    pallas_call x1, Pallas kernels, on_device(): pl.pallas_call(lambda *refs: final_kernel(*refs, pieces=nsamp), in_specs=...  1.03 us
  transfers between devices with their start and end apart: 8, of which 4 were waited for; matrix products, arithmetic and copies ran while one was open for 0% of the time, Pallas kernels for 19%

profile of v11, /device:TPU:0, one launch (start us, length us, event | category | flops | bytes accessed | tf_op | source)
XLA Modules:
  0.0 27.2 jit_solution(3183383287191099369)
XLA Ops:
  0.0 0.0 copy-start
  0.0 0.0 copy-start.3
  0.0 0.0 copy-start.1
  0.0 1.8 %leaf.1 = (bf16[200,128]{1,0:T(8,128)(2,1)S(1)}, bf16[136,128]{1,0:T(8,128)(2,1)S(1)}, bf16[200,128]{1,0:T(8,128)(2,1)S(1)}, bf16[128,128]{1,0:T(8,128)(2,1)S(1)}) custom-call(s32[16]{0:T(128)} %refs_0_.2, s32[16]{0:T(128)} %refs_1_.2, bf16[16,2,4,128]{3,2,1,0:T(4,128)(2,1)} %refs_2_.3, bf16[16,2,128,128]{3,2,1,0:T(8,128)(2,1)} %refs_3_.2), custom_call_target="tpu_custom_call" | custom-call | tf_op jit(solution)/shard_map/leaf/pallas_call | solution.py:486
  1.8 5.1 %collective-permute-start = (bf16[200,128]{1,0:T(8,128)(2,1)S(1)}, bf16[200,128]{1,0:T(8,128)(2,1)S(1)}, u32[]{:S(2)}, u32[]{:S(2)}) collective-permute-start(bf16[200,128]{1,0:T(8,128)(2,1)S(1)} %get-tuple-element.19), channel_id=1, source_target_pairs={{0,3},{1,2},{2,1},{3,0},{4,7},{5,6},{6,5},{7,4},{8,11},{9,10},{10,... | collective-permute-start | bytes 153608 | tf_op jit(solution)/shard_map/ppermute | solution.py:509
  6.9 0.0 collective-permute-start.1
  6.9 0.6 %collective-permute-start.2 = (bf16[136,128]{1,0:T(8,128)(2,1)S(1)}, bf16[136,128]{1,0:T(8,128)(2,1)S(1)}, u32[]{:S(2)}, u32[]{:S(2)}) collective-permute-start(bf16[136,128]{1,0:T(8,128)(2,1)S(1)} %get-tuple-element.18.refs_0_), channel_id=1, source_target_pairs={{0,2},{1,3},{2,0},{3,1},{4,6},{5,7},{6,4},{7,5},{8,10},{9,11},{10,... | collective-permute-start | bytes 104456 | tf_op jit(solution)/shard_map/ppermute | solution.py:509
  7.5 1.6 %prep.1 = (f32[8,14,2,512]{3,2,1,0:T(2,128)S(1)}, s32[8,16]{1,0:T(8,128)S(1)}) custom-call(s32[8,14]{1,0:T(8,128)} %refs_0_.3, s32[8,14]{1,0:T(8,128)} %refs_1_.3, s32[8,16]{1,0:T(8,128)} %bitcast.1, f32[64,2,512]{2,1,0:T(2,128)} %refs_3_.3, bf16[16,8,2,128,128]{4,3,2,1,0:T(8,128)(2,1)} %refs_2_.5, bf16[128,128]{1,0:T(8,128)(2,1)S(1)} %get-tuple-element.21.refs_5_.refs_1_), custom_call_target="tpu_custom_call" | custom-call | bytes 8388608 | tf_op jit(solution)/shard_map/prep/pallas_call | solution.py:518
  9.1 2.7 %collective-permute-done.2.refs_3_ = bf16[136,128]{1,0:T(8,128)(2,1)S(1)} collective-permute-done((bf16[136,128]{1,0:T(8,128)(2,1)S(1)}, bf16[136,128]{1,0:T(8,128)(2,1)S(1)}, u32[]{:S(2)}, u32[]{:S(2)}) %collective-permute-start.2) | collective-permute-done | bytes 34848 | tf_op jit(solution)/shard_map/ppermute | solution.py:509
  11.9 0.0 collective-permute-done.refs_1_.refs_6_
  11.9 0.0 collective-permute-done.1.refs_2_.refs_4_
  11.9 0.0 copy-done.3
  11.9 0.0 copy-done.1
  11.9 0.5 %up.1 = (bf16[80,512]{1,0:T(8,128)(2,1)S(1)}, bf16[80,512]{1,0:T(8,128)(2,1)S(1)}, bf16[64,64]{1,0:T(8,128)(2,1)S(1)}) custom-call(bf16[136,128]{1,0:T(8,128)(2,1)S(1)} %get-tuple-element.18.refs_0_, bf16[200,128]{1,0:T(8,128)(2,1)S(1)} %collective-permute-done.refs_1_.refs_6_, bf16[200,128]{1,0:T(8,128)(2,1)S(1)} %collective-permute-done.1.refs_2_.refs_4_, ...), custom_call_target="tpu_custom_call" | custom-call | tf_op jit(solution)/shard_map/up/pallas_call | solution.py:546
  12.4 0.4 %collective-permute-start.3 = (bf16[80,512]{1,0:T(8,128)(2,1)S(1)}, bf16[80,512]{1,0:T(8,128)(2,1)S(1)}, u32[]{:S(2)}, u32[]{:S(2)}) collective-permute-start(bf16[80,512]{1,0:T(8,128)(2,1)S(1)} %get-tuple-element.24), channel_id=1, source_target_pairs={{0,28},{4,8},{8,4},{12,16},{16,12},{20,24},{24,20},{28,0},{1,29},{... | collective-permute-start | bytes 245768 | tf_op jit(solution)/shard_map/ppermute | solution.py:565
  12.8 1.3 %collective-permute-start.4 = (bf16[80,512]{1,0:T(8,128)(2,1)S(1)}, bf16[80,512]{1,0:T(8,128)(2,1)S(1)}, u32[]{:S(2)}, u32[]{:S(2)}) collective-permute-start(bf16[80,512]{1,0:T(8,128)(2,1)S(1)} %get-tuple-element.23.refs_0_), channel_id=1, source_target_pairs={{0,4},{4,0},{8,12},{12,8},{16,20},{20,16},{24,28},{28,24},{1,5},{5... | collective-permute-start | bytes 245768 | tf_op jit(solution)/shard_map/ppermute | solution.py:568
  14.1 0.0 copy-done
  14.1 0.0 copy-start.2
  14.1 1.8 %near.2.refs_7_.refs_4_ = f32[8,8,128]{2,1,0:T(8,128)S(1)} custom-call(s32[8,16]{1,0:T(8,128)S(1)} %get-tuple-element.22.refs_6_.refs_0_, bf16[128,128]{1,0:T(8,128)(2,1)S(1)} %get-tuple-element.21.refs_5_.refs_1_, bf16[16,8,2,128,128]{4,3,2,1,0:T(8,128)(2,1)S(1)} %copy-done, bf16[64,64]{1,0:T(8,128)(2,1)S(1)} %get-tuple-element.26.refs_3_.refs_6_, ...), custom_call_target="tpu_custom_call" | custom-call | flops 33554432 | bytes 4194304 | tf_op jit(solution)/shard_map/near/pallas_call | solution.py:571
  15.9 2.1 %collective-permute-done.3.refs_1_.refs_4_ = bf16[80,512]{1,0:T(8,128)(2,1)S(1)} collective-permute-done((bf16[80,512]{1,0:T(8,128)(2,1)S(1)}, bf16[80,512]{1,0:T(8,128)(2,1)S(1)}, u32[]{:S(2)}, u32[]{:S(2)}) %collective-permute-start.3) | collective-permute-done | bytes 81952 | tf_op jit(solution)/shard_map/ppermute | solution.py:565
  18.0 0.0 collective-permute-done.4.refs_2_.refs_5_
  18.0 0.8 %down.1 = (bf16[128,128]{1,0:T(8,128)(2,1)S(1)}, bf16[128,128]{1,0:T(8,128)(2,1)S(1)}, bf16[128,128]{1,0:T(8,128)(2,1)S(1)}, bf16[128,128]{1,0:T(8,128)(2,1)S(1)}) custom-call(bf16[80,512]{1,0:T(8,128)(2,1)S(1)} %get-tuple-element.23.refs_0_, bf16[80,512]{1,0:T(8,128)(2,1)S(1)} %collective-permute-done.3.refs_1_.refs_4_, ...), custom_call_target="tpu_custom_call" | custom-call | tf_op jit(solution)/shard_map/down/pallas_call | solution.py:599
  18.9 1.7 %collective-permute-start.5 = (bf16[128,128]{1,0:T(8,128)(2,1)S(1)}, bf16[128,128]{1,0:T(8,128)(2,1)S(1)}, u32[]{:S(2)}, u32[]{:S(2)}) collective-permute-start(bf16[128,128]{1,0:T(8,128)(2,1)S(1)} %get-tuple-element.28), channel_id=1, source_target_pairs={{0,3},{1,2},{2,1},{3,0},{4,7},{5,6},{6,5},{7,4},{8,11},{9,10},{10,... | collective-permute-start | bytes 98312 | tf_op jit(solution)/shard_map/ppermute | solution.py:509
  20.6 1.7 %collective-permute-start.6 = (bf16[128,128]{1,0:T(8,128)(2,1)S(1)}, bf16[128,128]{1,0:T(8,128)(2,1)S(1)}, u32[]{:S(2)}, u32[]{:S(2)}) collective-permute-start(bf16[128,128]{1,0:T(8,128)(2,1)S(1)} %get-tuple-element.29), channel_id=1, source_target_pairs={{0,2},{1,3},{2,0},{3,1},{4,6},{5,7},{6,4},{7,5},{8,10},{9,11},{10,... | collective-permute-start | bytes 98312 | tf_op jit(solution)/shard_map/ppermute | solution.py:509
  22.3 1.0 %collective-permute-start.7 = (bf16[128,128]{1,0:T(8,128)(2,1)S(1)}, bf16[128,128]{1,0:T(8,128)(2,1)S(1)}, u32[]{:S(2)}, u32[]{:S(2)}) collective-permute-start(bf16[128,128]{1,0:T(8,128)(2,1)S(1)} %get-tuple-element.30), channel_id=1, source_target_pairs={{0,1},{1,0},{2,3},{3,2},{4,5},{5,4},{6,7},{7,6},{8,9},{9,8},{10,11... | collective-permute-start | bytes 98312 | tf_op jit(solution)/shard_map/ppermute | solution.py:509
  23.3 1.8 %near.3.refs_5_ = f32[8,8,128]{2,1,0:T(8,128)S(1)} custom-call(s32[8,16]{1,0:T(8,128)S(1)} %get-tuple-element.22.refs_6_.refs_0_, bf16[128,128]{1,0:T(8,128)(2,1)S(1)} %get-tuple-element.21.refs_5_.refs_1_, bf16[16,8,2,128,128]{4,3,2,1,0:T(8,128)(2,1)S(1)} %copy-done, bf16[128,128]{1,0:T(8,128)(2,1)S(1)} %get-tuple-element.27.refs_3_.refs_0_, ...), custom_call_target="tpu_custom_call" | custom-call | flops 33554432 | bytes 4194304 | tf_op jit(solution)/shard_map/near/pallas_call | solution.py:571
  25.1 0.0 collective-permute-done.5.refs_1_
  25.1 0.4 %collective-permute-done.6.refs_2_ = bf16[128,128]{1,0:T(8,128)(2,1)S(1)} collective-permute-done((bf16[128,128]{1,0:T(8,128)(2,1)S(1)}, bf16[128,128]{1,0:T(8,128)(2,1)S(1)}, u32[]{:S(2)}, u32[]{:S(2)}) %collective-permute-start.6) | collective-permute-done | bytes 32800 | tf_op jit(solution)/shard_map/ppermute | solution.py:509
  25.5 0.7 %collective-permute-done.7.refs_3_ = bf16[128,128]{1,0:T(8,128)(2,1)S(1)} collective-permute-done((bf16[128,128]{1,0:T(8,128)(2,1)S(1)}, bf16[128,128]{1,0:T(8,128)(2,1)S(1)}, u32[]{:S(2)}, u32[]{:S(2)}) %collective-permute-start.7) | collective-permute-done | bytes 32800 | tf_op jit(solution)/shard_map/ppermute | solution.py:509
  26.2 0.0 copy-done.2
  26.2 1.0 %final.1 = f32[16,2,4,128]{3,2,1,0:T(4,128)} custom-call(bf16[128,128]{1,0:T(8,128)(2,1)S(1)} %get-tuple-element.27.refs_3_.refs_0_, bf16[128,128]{1,0:T(8,128)(2,1)S(1)} %collective-permute-done.5.refs_1_, bf16[128,128]{1,0:T(8,128)(2,1)S(1)} %collective-permute-done.6.refs_2_, bf16[128,128]{1,0:T(8,128)(2,1)S(1)} %collective-permute-done.7.refs_3_, ...), custom_call_target="tpu_custom_call" | custom-call | tf_op jit(solution)/shard_map/final/pallas_call | solution.py:620
Async XLA Ops:
  0.0 14.1 %copy-start = (bf16[16,8,2,128,128]{4,3,2,1,0:T(8,128)(2,1)S(1)}, bf16[16,8,2,128,128]{4,3,2,1,0:T(8,128)(2,1)}, u32[]{:S(2)}) copy-start(bf16[16,8,2,128,128]{4,3,2,1,0:T(8,128)(2,1)} %refs_2_.5) | copy-start | bytes 25165828
  0.0 11.9 %copy-start.3 = (f32[8,2,2048]{2,1,0:T(2,128)S(1)}, f32[8,2,2048]{2,1,0:T(2,128)}, u32[]{:S(2)}) copy-start(f32[8,2,2048]{2,1,0:T(2,128)} %refs_5_.3) | copy-start | bytes 393220
  0.0 11.9 %copy-start.1 = (bf16[2048,128]{1,0:T(8,128)(2,1)S(1)}, bf16[2048,128]{1,0:T(8,128)(2,1)}, u32[]{:S(2)}) copy-start(bf16[2048,128]{1,0:T(8,128)(2,1)} %refs_4_.5) | copy-start | bytes 1572868
  1.8 10.1 %collective-permute-start = (bf16[200,128]{1,0:T(8,128)(2,1)S(1)}, bf16[200,128]{1,0:T(8,128)(2,1)S(1)}, u32[]{:S(2)}, u32[]{:S(2)}) collective-permute-start(bf16[200,128]{1,0:T(8,128)(2,1)S(1)} %get-tuple-element.19), channel_id=1, source_target_pairs={{0,3},{1,2},{2,1},{3,0},{4,7},{5,6},{6,5},{7,4},{8,11},{9,10},{10,... | collective-permute-start | bytes 153608 | tf_op jit(solution)/shard_map/ppermute | solution.py:509
  6.9 5.0 %collective-permute-start.1 = (bf16[200,128]{1,0:T(8,128)(2,1)S(1)}, bf16[200,128]{1,0:T(8,128)(2,1)S(1)}, u32[]{:S(2)}, u32[]{:S(2)}) collective-permute-start(bf16[200,128]{1,0:T(8,128)(2,1)S(1)} %get-tuple-element.20), channel_id=1, source_target_pairs={{0,1},{1,0},{2,3},{3,2},{4,5},{5,4},{6,7},{7,6},{8,9},{9,8},{10,11... | collective-permute-start | bytes 153608 | tf_op jit(solution)/shard_map/ppermute | solution.py:509
  6.9 5.0 %collective-permute-start.2 = (bf16[136,128]{1,0:T(8,128)(2,1)S(1)}, bf16[136,128]{1,0:T(8,128)(2,1)S(1)}, u32[]{:S(2)}, u32[]{:S(2)}) collective-permute-start(bf16[136,128]{1,0:T(8,128)(2,1)S(1)} %get-tuple-element.18.refs_0_), channel_id=1, source_target_pairs={{0,2},{1,3},{2,0},{3,1},{4,6},{5,7},{6,4},{7,5},{8,10},{9,11},{10,... | collective-permute-start | bytes 104456 | tf_op jit(solution)/shard_map/ppermute | solution.py:509
  12.4 5.6 %collective-permute-start.3 = (bf16[80,512]{1,0:T(8,128)(2,1)S(1)}, bf16[80,512]{1,0:T(8,128)(2,1)S(1)}, u32[]{:S(2)}, u32[]{:S(2)}) collective-permute-start(bf16[80,512]{1,0:T(8,128)(2,1)S(1)} %get-tuple-element.24), channel_id=1, source_target_pairs={{0,28},{4,8},{8,4},{12,16},{16,12},{20,24},{24,20},{28,0},{1,29},{... | collective-permute-start | bytes 245768 | tf_op jit(solution)/shard_map/ppermute | solution.py:565
  12.8 5.2 %collective-permute-start.4 = (bf16[80,512]{1,0:T(8,128)(2,1)S(1)}, bf16[80,512]{1,0:T(8,128)(2,1)S(1)}, u32[]{:S(2)}, u32[]{:S(2)}) collective-permute-start(bf16[80,512]{1,0:T(8,128)(2,1)S(1)} %get-tuple-element.23.refs_0_), channel_id=1, source_target_pairs={{0,4},{4,0},{8,12},{12,8},{16,20},{20,16},{24,28},{28,24},{1,5},{5... | collective-permute-start | bytes 245768 | tf_op jit(solution)/shard_map/ppermute | solution.py:568
  14.1 12.1 %copy-start.2 = (bf16[16,2,128,128]{3,2,1,0:T(8,128)(2,1)S(1)}, bf16[16,2,128,128]{3,2,1,0:T(8,128)(2,1)}, u32[]{:S(2)}) copy-start(bf16[16,2,128,128]{3,2,1,0:T(8,128)(2,1)} %refs_6_.1) | copy-start | bytes 3145732
  18.9 6.3 %collective-permute-start.5 = (bf16[128,128]{1,0:T(8,128)(2,1)S(1)}, bf16[128,128]{1,0:T(8,128)(2,1)S(1)}, u32[]{:S(2)}, u32[]{:S(2)}) collective-permute-start(bf16[128,128]{1,0:T(8,128)(2,1)S(1)} %get-tuple-element.28), channel_id=1, source_target_pairs={{0,3},{1,2},{2,1},{3,0},{4,7},{5,6},{6,5},{7,4},{8,11},{9,10},{10,... | collective-permute-start | bytes 98312 | tf_op jit(solution)/shard_map/ppermute | solution.py:509
  20.6 4.9 %collective-permute-start.6 = (bf16[128,128]{1,0:T(8,128)(2,1)S(1)}, bf16[128,128]{1,0:T(8,128)(2,1)S(1)}, u32[]{:S(2)}, u32[]{:S(2)}) collective-permute-start(bf16[128,128]{1,0:T(8,128)(2,1)S(1)} %get-tuple-element.29), channel_id=1, source_target_pairs={{0,2},{1,3},{2,0},{3,1},{4,6},{5,7},{6,4},{7,5},{8,10},{9,11},{10,... | collective-permute-start | bytes 98312 | tf_op jit(solution)/shard_map/ppermute | solution.py:509
  22.3 3.9 %collective-permute-start.7 = (bf16[128,128]{1,0:T(8,128)(2,1)S(1)}, bf16[128,128]{1,0:T(8,128)(2,1)S(1)}, u32[]{:S(2)}, u32[]{:S(2)}) collective-permute-start(bf16[128,128]{1,0:T(8,128)(2,1)S(1)} %get-tuple-element.30), channel_id=1, source_target_pairs={{0,1},{1,0},{2,3},{3,2},{4,5},{5,4},{6,7},{7,6},{8,9},{9,8},{10,11... | collective-permute-start | bytes 98312 | tf_op jit(solution)/shard_map/ppermute | solution.py:509

commit v12 on v7

--- a/solution.py
+++ b/solution.py
@@ -8,6 +8,7 @@
 F32 = jnp.float32
 BF16 = jnp.bfloat16
 LANES = 128
+CODE_ROWS = 8
 
 
 def nt_dot(a, b):
@@ -28,8 +29,10 @@
 
 
 def leaf_kernel(
-    octant, parent, x_hbm, lift_hbm, to_far, plain, to_beside, x_rows,
-    x_ref, rows, lift, oct_s, par_s, sems, *, parents,
+    octant, parent, x_hbm, lift_hbm, inter, trans, table_hbm,
+    to_far, plain, to_beside, x_rows, dense,
+    x_ref, rows, lift, oct_s, par_s, sems, inter_s, trans_s, table, more,
+    *, parents, all_parents,
 ):
     boxes, halves, rhs, _ = x_ref.shape
     parts = halves * rhs
@@ -49,6 +52,10 @@
     ]
     for copy in small + big:
         copy.start()
+    start, finish = fill_dense(
+        dense, inter, trans, table_hbm, inter_s, trans_s, table, more, parents, all_parents
+    )
+    pl.when(odd_box())(start)
     for copy in small:
         copy.wait()
     own = [
@@ -60,16 +67,16 @@
     for n in range(boxes):
         slot = (oct_s[n] * parents + lax.rem(par_s[n], parents)).astype(F32)
         codes = jnp.where(lane == n, slot, codes)
-    codes = codes.astype(BF16)
+    codes = codes[:CODE_ROWS].astype(BF16)
     x_rows[...] = jnp.concatenate(own, axis=0).astype(BF16)
     first = jnp.concatenate(own[:reach], axis=0)
     last = jnp.concatenate(own[reach:], axis=0)
     odd = lax.rem(lax.axis_index("samp"), 2) == 1
     at = parts * boxes
-    to_beside[at + boxes :] = jnp.where(odd, first, last).astype(BF16)
-    to_far[at + boxes :] = jnp.where(odd, last, first).astype(BF16)
+    to_beside[at + CODE_ROWS :] = jnp.where(odd, first, last).astype(BF16)
+    to_far[at + CODE_ROWS :] = jnp.where(odd, last, first).astype(BF16)
     for ref in (plain, to_beside, to_far):
-        ref[at : at + boxes] = codes
+        ref[at : at + CODE_ROWS] = codes
     for n in range(boxes):
         if n % per == 0:
             big[n // per].wait()
@@ -78,6 +85,7 @@
     pattern = rows[...].astype(BF16)
     for ref in (plain, to_beside, to_far):
         ref[:at] = pattern
+    pl.when(odd_box())(finish)
 
 
 def up_kernel(*refs, pieces, boxes, parents, parts):
@@ -92,11 +100,11 @@
     at = parts * boxes
     tiles = []
     for t in range(0, pieces, per_tile):
-        lane = lax.broadcasted_iota(jnp.int32, (boxes, LANES), 1) // boxes
-        code = msgs[t][at : at + boxes].astype(F32)
+        lane = lax.broadcasted_iota(jnp.int32, (CODE_ROWS, LANES), 1) // boxes
+        code = msgs[t][at : at + CODE_ROWS].astype(F32)
         for d in range(1, min(per_tile, pieces - t)):
-            code = jnp.where(lane == d, msgs[t + d][at : at + boxes].astype(F32), code)
-        code = jnp.concatenate([code] * (slots // boxes), axis=0)
+            code = jnp.where(lane == d, msgs[t + d][at : at + CODE_ROWS].astype(F32), code)
+        code = jnp.concatenate([code] * (slots // CODE_ROWS), axis=0)
         want = lax.broadcasted_iota(jnp.int32, (slots, LANES), 0).astype(F32)
         width = min(per_tile, pieces - t) * boxes
         tiles.append(jnp.where(code == want, 1.0, 0.0)[:, :width])
@@ -111,10 +119,10 @@
         axis=1,
     )
     ordered = nn_dot(sorter, pats).astype(BF16)
-    for c in range(parts):
-        raised[c * slots : (c + 1) * slots] = nt_dot(
-            ordered[:, c * LANES : (c + 1) * LANES], mine
-        )
+    stacked = jnp.concatenate(
+        [ordered[:, c * LANES : (c + 1) * LANES] for c in range(parts)], axis=0
+    )
+    raised[...] = nt_dot(stacked, mine)
     half = parts // 2
     for t in range(samples // LANES):
         lanes = slice(t * LANES, (t + 1) * LANES)
@@ -151,33 +159,56 @@
     return [d for d in range(-parents, parents + 1) if abs(d) >= 2]
 
 
+def fill_dense(dense, inter_hbm, trans_hbm, table_hbm, inter, trans, table, sems, parents, all_parents):
+    copies = [
+        pltpu.make_async_copy(inter_hbm, inter, sems.at[0]),
+        pltpu.make_async_copy(trans_hbm, trans, sems.at[1]),
+        pltpu.make_async_copy(table_hbm, table, sems.at[2]),
+    ]
+    first = lax.axis_index("box") * parents
+
+    def start():
+        for copy in copies:
+            copy.start()
+
+    def finish():
+        for copy in copies:
+            copy.wait()
+        if len(zone(parents)) > inter.shape[1]:
+            dense[...] = jnp.zeros_like(dense)
+
+        def fill(p, carry):
+            for k in range(inter.shape[1]):
+                rel = lax.rem(inter[p, k] - first - p + parents + all_parents, all_parents)
+                at = jnp.where(rel < parents, rel, rel - 3)
+                dense[p, at] = table[trans[p, k]]
+            return carry
+
+        lax.fori_loop(0, parents, fill, 0)
+
+    return start, finish
+
+
+def odd_box():
+    return lax.rem(lax.axis_index("box"), 2) == 1
+
+
 def prep_kernel(
-    inter, trans, neighbours, table_hbm, mats_hbm, after, dense, nbr, inter_s, trans_s, table, sems,
-    *, parents, all_parents,
+    inter, trans, neighbours, table_hbm, mats_hbm, dense_in, after, dense, nbr,
+    inter_s, trans_s, table, sems, *, parents, all_parents,
 ):
-    copies = [
-        pltpu.make_async_copy(inter, inter_s, sems.at[0]),
-        pltpu.make_async_copy(trans, trans_s, sems.at[1]),
-        pltpu.make_async_copy(table_hbm, table, sems.at[2]),
-        pltpu.make_async_copy(neighbours, nbr, sems.at[3]),
-    ]
-    for copy in copies:
-        copy.start()
-    for copy in copies[:3]:
-        copy.wait()
-    if len(zone(parents)) > inter.shape[1]:
-        dense[...] = jnp.zeros_like(dense)
-    first = lax.axis_index("box") * parents
-
-    def fill(p, carry):
-        for k in range(inter.shape[1]):
-            rel = lax.rem(inter_s[p, k] - first - p + parents + all_parents, all_parents)
-            at = jnp.where(rel < parents, rel, rel - 3)
-            dense[p, at] = table[trans_s[p, k]]
-        return carry
-
-    lax.fori_loop(0, parents, fill, 0)
-    copies[3].wait()
+    copy = pltpu.make_async_copy(neighbours, nbr, sems.at[3])
+    copy.start()
+    start, finish = fill_dense(
+        dense, inter, trans, table_hbm, inter_s, trans_s, table, sems, parents, all_parents
+    )
+
+    @pl.when(jnp.logical_not(odd_box()))
+    def _():
+        start()
+        finish()
+
+    copy.wait()
 
 
 def down_kernel(
@@ -201,24 +232,31 @@
     )
     offsets = zone(parents)
 
-    def one(p):
-        for t in range(samples // LANES):
-            lanes = slice(t * LANES, (t + 1) * LANES)
-            acc_r = acc_i = None
-            for i, d in enumerate(offsets):
-                x = window[parents + p + d, :, lanes]
-                yr = dense[p, i, 0:1, lanes] * x
-                yi = dense[p, i, 1:2, lanes] * x
-                acc_r = yr if acc_r is None else acc_r + yr
-                acc_i = yi if acc_i is None else acc_i + yi
-            got = (acc_r + times_i(acc_i)).astype(BF16).astype(F32)
-            incoming[t, pl.ds(p * parts, parts), :] = got
-
-    if parents <= 8:
-        for p in range(parents):
-            one(p)
-    else:
-        lax.fori_loop(0, parents, lambda p, c: (one(p), c)[1], 0)
+    def one(p, t, source):
+        lanes = slice(t * LANES, (t + 1) * LANES)
+        acc_r = acc_i = None
+        for i, d in enumerate(offsets):
+            x = source(p + d)
+            yr = dense[p, i, 0:1, lanes] * x
+            yi = dense[p, i, 1:2, lanes] * x
+            acc_r = yr if acc_r is None else acc_r + yr
+            acc_i = yi if acc_i is None else acc_i + yi
+        got = (acc_r + times_i(acc_i)).astype(BF16).astype(F32)
+        incoming[t, pl.ds(p * parts, parts), :] = got
+
+    for t in range(samples // LANES):
+        lanes = slice(t * LANES, (t + 1) * LANES)
+        if parents <= 8:
+            held = [window[j, :, lanes] for j in range(3 * parents)]
+            for p in range(parents):
+                one(p, t, lambda j: held[parents + j])
+        else:
+            lax.fori_loop(
+                0,
+                parents,
+                lambda p, c: (one(p, t, lambda j: window[parents + j, :, lanes]), c)[1],
+                0,
+            )
     for t in range(samples // LANES):
         lanes = slice(t * LANES, (t + 1) * LANES)
         here = pl.ds(pl.multiple_of(first + t * LANES, LANES), LANES)
@@ -366,21 +404,22 @@
     near_count = near_blocks.shape[1]
     halo_rows = reach * parts
     parent_rows = parents * parts
-    plain_rows = (parts + 1) * boxes
+    plain_rows = parts * boxes + CODE_ROWS
 
     def shape(dims, dtype=BF16):
         return jax.ShapeDtypeStruct(dims, dtype)
 
-    lift_chunks = 4
-    to_far, plain, to_beside, x_rows = pl.pallas_call(
-        lambda *refs: leaf_kernel(*refs, parents=parents),
-        in_specs=[whole_in(HBM)] * 4,
-        out_specs=[whole_in(VM)] * 4,
+    lift_chunks = 2
+    to_far, plain, to_beside, x_rows, dense = pl.pallas_call(
+        lambda *refs: leaf_kernel(*refs, parents=parents, all_parents=all_parents),
+        in_specs=[whole_in(HBM)] * 7,
+        out_specs=[whole_in(VM)] * 5,
         out_shape=[
             shape((plain_rows + halo_rows, LANES)),
             shape((plain_rows, LANES)),
             shape((plain_rows + halo_rows, LANES)),
             shape((boxes * parts, LANES)),
+            shape((parents, len(zone(parents)), 2, samples), F32),
         ],
         scratch_shapes=[
             VM(xvec.shape, BF16),
@@ -389,10 +428,17 @@
             SM((boxes,), jnp.int32),
             SM((boxes,), jnp.int32),
             DMA((lift_chunks + 3,)),
+            SM(inter_list.shape, jnp.int32),
+            SM(trans_id.shape, jnp.int32),
+            VM(translators.shape, F32),
+            DMA((3,)),
         ],
         compiler_params=PARAMS,
         name="leaf",
-    )(*[stay(a) for a in (octant, leaf_parent_index, xvec, lift)])
+    )(
+        *[stay(a) for a in (octant, leaf_parent_index, xvec, lift)],
+        *[stay(a) for a in (inter_list, trans_id, translators)],
+    )
 
     def exchange(x, d):
         return lax.ppermute(x, "samp", [(i, i ^ d) for i in range(nsamp)])
@@ -406,8 +452,9 @@
 
     dense, near_list = pl.pallas_call(
         lambda *refs: prep_kernel(*refs, parents=parents, all_parents=all_parents),
-        in_specs=[whole_in(HBM)] * 5 + [whole_in(VM)],
+        in_specs=[whole_in(HBM)] * 5 + [whole_in(VM)] * 2,
         out_specs=[whole_in(VM)] * 2,
+        input_output_aliases={5: 0},
         out_shape=[
             shape((parents, len(zone(parents)), 2, samples), F32),
             shape((near_count, boxes), jnp.int32),
@@ -429,6 +476,7 @@
         stay(neighbours.T),
         stay(translators),
         stay(near_blocks),
+        dense,
         x_rows,
     )
 

time: 27.7 us -> 26.9 us (0.971)
  waiting for transfers between devices: 5.92 us -> 4.47 us
  starting transfers between devices: 11.9 us -> 12.8 us
  Pallas kernels: 9.67 us -> 9.39 us
    ppermute x1, starting transfers between devices: 0.36 us -> 2.55 us  [on_device(): lax.ppermute(to_across, 'box', [(i, (i + (1 if i % 2 else -1)) % nbox) fo...]
    ppermute x1, waiting for transfers between devices: 2.11 us -> 0.71 us  [on_device(): lax.ppermute(to_across, 'box', [(i, (i + (1 if i % 2 else -1)) % nbox) fo...]
    ppermute x1, starting transfers between devices: 1.31 us -> 0.07 us  [on_device(): beside = lax.ppermute(parent_pat, 'box', [(i, i ^ 1) for i in range(nbox)])]
  transfers between devices with their start and end apart: 8 -> 8, of which waited for: 4 -> 4; matrix products, arithmetic and copies ran while one was open for 0% -> 0% of each run, Pallas kernels for 19% -> 20%
where the time goes in v12:
time: 26.9 us; the launch traced here: 26.8 us
  starting transfers between devices  12.8 us (48%)
  Pallas kernels  9.39 us (35%)
  waiting for transfers between devices  4.47 us (17%)
    ppermute x6, starting transfers between devices, exchange(): return lax.ppermute(x, 'samp', [(i, i ^ d) for i in range(nsamp)])  10.2 us
    ppermute x6, waiting for transfers between devices, exchange(): return lax.ppermute(x, 'samp', [(i, i ^ d) for i in range(nsamp)])  3.76 us
    pallas_call x2, Pallas kernels, near_half(): pl.pallas_call(lambda *refs: near_kernel(*refs, late=late, nsamp=nsamp, t...  3.62 us
    ppermute x1, starting transfers between devices, on_device(): lax.ppermute(to_across, 'box', [(i, (i + (1 if i % 2 else -1)) % nbox) fo...  2.55 us
    pallas_call x1, Pallas kernels, on_device(): pl.pallas_call(lambda *refs: leaf_kernel(*refs, parents=parents, all_pare...  1.79 us
    pallas_call x1, Pallas kernels, on_device(): pl.pallas_call(lambda *refs: prep_kernel(*refs, parents=parents, all_pare...  1.61 us
    pallas_call x1, Pallas kernels, on_device(): pl.pallas_call(lambda *refs: final_kernel(*refs, pieces=nsamp), in_specs=...  1.03 us
    pallas_call x1, Pallas kernels, on_device(): pl.pallas_call(lambda *refs: down_kernel(*refs, pieces=nsamp, boxes=boxes...  0.81 us
  transfers between devices with their start and end apart: 8, of which 4 were waited for; matrix products, arithmetic and copies ran while one was open for 0% of the time, Pallas kernels for 20%

profile of v12, /device:TPU:0, one launch (start us, length us, event | category | flops | bytes accessed | tf_op | source)
XLA Modules:
  0.0 26.8 jit_solution(5105529049029655985)
XLA Ops:
  0.0 0.0 copy-start
  0.0 0.0 copy-start.1
  0.0 0.0 copy-start.3
  0.0 1.8 %leaf.1 = (bf16[200,128]{1,0:T(8,128)(2,1)S(1)}, bf16[136,128]{1,0:T(8,128)(2,1)S(1)}, bf16[200,128]{1,0:T(8,128)(2,1)S(1)}, bf16[128,128]{1,0:T(8,128)(2,1)S(1)}, f32[8,14,2,512]{3,2,1,0:T(2,128)S(1)}) custom-call(s32[16]{0:T(128)} %refs_0_.2, s32[16]{0:T(128)} %refs_1_.2, bf16[16,2,4,128]{3,2,1,0:T(4,128)(2,1)} %refs_2_.3, ...), custom_call_target="tpu_custom_call" | custom-call | tf_op jit(solution)/shard_map/leaf/pallas_call | solution.py:413
  1.8 5.1 %collective-permute-start = (bf16[200,128]{1,0:T(8,128)(2,1)S(1)}, bf16[200,128]{1,0:T(8,128)(2,1)S(1)}, u32[]{:S(2)}, u32[]{:S(2)}) collective-permute-start(bf16[200,128]{1,0:T(8,128)(2,1)S(1)} %get-tuple-element.20), channel_id=1, source_target_pairs={{0,3},{1,2},{2,1},{3,0},{4,7},{5,6},{6,5},{7,4},{8,11},{9,10},{10,... | collective-permute-start | bytes 153608 | tf_op jit(solution)/shard_map/ppermute | solution.py:444
  6.9 0.0 collective-permute-start.1
  6.9 0.6 %collective-permute-start.2 = (bf16[136,128]{1,0:T(8,128)(2,1)S(1)}, bf16[136,128]{1,0:T(8,128)(2,1)S(1)}, u32[]{:S(2)}, u32[]{:S(2)}) collective-permute-start(bf16[136,128]{1,0:T(8,128)(2,1)S(1)} %get-tuple-element.19.refs_0_), channel_id=1, source_target_pairs={{0,2},{1,3},{2,0},{3,1},{4,6},{5,7},{6,4},{7,5},{8,10},{9,11},{10,... | collective-permute-start | bytes 104456 | tf_op jit(solution)/shard_map/ppermute | solution.py:444
  7.6 1.6 %prep.1 = (f32[8,14,2,512]{3,2,1,0:T(2,128)S(1)}, s32[8,16]{1,0:T(8,128)S(1)}) custom-call(s32[8,14]{1,0:T(8,128)} %refs_0_.3, s32[8,14]{1,0:T(8,128)} %refs_1_.3, s32[8,16]{1,0:T(8,128)} %bitcast.1, f32[64,2,512]{2,1,0:T(2,128)} %refs_3_.3, bf16[16,8,2,128,128]{4,3,2,1,0:T(8,128)(2,1)} %refs_2_.5, ...), custom_call_target="tpu_custom_call", output_to_operand_aliasing={{0}: (5, {})} | custom-call | bytes 8388608 | tf_op jit(solution)/shard_map/prep/pallas_call | solution.py:453
  9.2 2.6 %collective-permute-done.2.refs_3_ = bf16[136,128]{1,0:T(8,128)(2,1)S(1)} collective-permute-done((bf16[136,128]{1,0:T(8,128)(2,1)S(1)}, bf16[136,128]{1,0:T(8,128)(2,1)S(1)}, u32[]{:S(2)}, u32[]{:S(2)}) %collective-permute-start.2) | collective-permute-done | bytes 34848 | tf_op jit(solution)/shard_map/ppermute | solution.py:444
  11.8 0.0 collective-permute-done.refs_1_.refs_6_
  11.8 0.0 collective-permute-done.1.refs_2_.refs_4_
  11.8 0.0 copy-done.1
  11.8 0.0 copy-done.3
  11.8 0.5 %up.1 = (bf16[80,512]{1,0:T(8,128)(2,1)S(1)}, bf16[80,512]{1,0:T(8,128)(2,1)S(1)}, bf16[64,64]{1,0:T(8,128)(2,1)S(1)}) custom-call(bf16[136,128]{1,0:T(8,128)(2,1)S(1)} %get-tuple-element.19.refs_0_, bf16[200,128]{1,0:T(8,128)(2,1)S(1)} %collective-permute-done.refs_1_.refs_6_, bf16[200,128]{1,0:T(8,128)(2,1)S(1)} %collective-permute-done.1.refs_2_.refs_4_, ...), custom_call_target="tpu_custom_call" | custom-call | tf_op jit(solution)/shard_map/up/pallas_call | solution.py:483
  12.3 0.1 collective-permute-start.4
  12.4 2.5 %collective-permute-start.3 = (bf16[80,512]{1,0:T(8,128)(2,1)S(1)}, bf16[80,512]{1,0:T(8,128)(2,1)S(1)}, u32[]{:S(2)}, u32[]{:S(2)}) collective-permute-start(bf16[80,512]{1,0:T(8,128)(2,1)S(1)} %get-tuple-element.26), channel_id=1, source_target_pairs={{0,28},{4,8},{8,4},{12,16},{16,12},{20,24},{24,20},{28,0},{1,29},{... | collective-permute-start | bytes 245768 | tf_op jit(solution)/shard_map/ppermute | solution.py:502
  15.0 0.0 copy-done
  15.0 0.0 copy-start.2
  15.0 1.8 %near.2.refs_7_.refs_4_ = f32[8,8,128]{2,1,0:T(8,128)S(1)} custom-call(s32[8,16]{1,0:T(8,128)S(1)} %get-tuple-element.24.refs_6_.refs_0_, bf16[128,128]{1,0:T(8,128)(2,1)S(1)} %get-tuple-element.23.refs_6_.refs_1_, bf16[16,8,2,128,128]{4,3,2,1,0:T(8,128)(2,1)S(1)} %copy-done, bf16[64,64]{1,0:T(8,128)(2,1)S(1)} %get-tuple-element.28.refs_3_.refs_6_, ...), custom_call_target="tpu_custom_call" | custom-call | flops 33554432 | bytes 4194304 | tf_op jit(solution)/shard_map/near/pallas_call | solution.py:508
  16.8 0.0 collective-permute-done.4.refs_2_.refs_5_
  16.8 0.7 %collective-permute-done.3.refs_1_.refs_4_ = bf16[80,512]{1,0:T(8,128)(2,1)S(1)} collective-permute-done((bf16[80,512]{1,0:T(8,128)(2,1)S(1)}, bf16[80,512]{1,0:T(8,128)(2,1)S(1)}, u32[]{:S(2)}, u32[]{:S(2)}) %collective-permute-start.3) | collective-permute-done | bytes 81952 | tf_op jit(solution)/shard_map/ppermute | solution.py:502
  17.5 0.8 %down.1 = (bf16[128,128]{1,0:T(8,128)(2,1)S(1)}, bf16[128,128]{1,0:T(8,128)(2,1)S(1)}, bf16[128,128]{1,0:T(8,128)(2,1)S(1)}, bf16[128,128]{1,0:T(8,128)(2,1)S(1)}) custom-call(bf16[80,512]{1,0:T(8,128)(2,1)S(1)} %get-tuple-element.25.refs_0_, bf16[80,512]{1,0:T(8,128)(2,1)S(1)} %collective-permute-done.3.refs_1_.refs_4_, ...), custom_call_target="tpu_custom_call" | custom-call | tf_op jit(solution)/shard_map/down/pallas_call | solution.py:536
  18.3 2.0 %collective-permute-start.5 = (bf16[128,128]{1,0:T(8,128)(2,1)S(1)}, bf16[128,128]{1,0:T(8,128)(2,1)S(1)}, u32[]{:S(2)}, u32[]{:S(2)}) collective-permute-start(bf16[128,128]{1,0:T(8,128)(2,1)S(1)} %get-tuple-element.30), channel_id=1, source_target_pairs={{0,3},{1,2},{2,1},{3,0},{4,7},{5,6},{6,5},{7,4},{8,11},{9,10},{10,... | collective-permute-start | bytes 98312 | tf_op jit(solution)/shard_map/ppermute | solution.py:444
  20.3 1.5 %collective-permute-start.6 = (bf16[128,128]{1,0:T(8,128)(2,1)S(1)}, bf16[128,128]{1,0:T(8,128)(2,1)S(1)}, u32[]{:S(2)}, u32[]{:S(2)}) collective-permute-start(bf16[128,128]{1,0:T(8,128)(2,1)S(1)} %get-tuple-element.31), channel_id=1, source_target_pairs={{0,2},{1,3},{2,0},{3,1},{4,6},{5,7},{6,4},{7,5},{8,10},{9,11},{10,... | collective-permute-start | bytes 98312 | tf_op jit(solution)/shard_map/ppermute | solution.py:444
  21.9 0.9 %collective-permute-start.7 = (bf16[128,128]{1,0:T(8,128)(2,1)S(1)}, bf16[128,128]{1,0:T(8,128)(2,1)S(1)}, u32[]{:S(2)}, u32[]{:S(2)}) collective-permute-start(bf16[128,128]{1,0:T(8,128)(2,1)S(1)} %get-tuple-element.32), channel_id=1, source_target_pairs={{0,1},{1,0},{2,3},{3,2},{4,5},{5,4},{6,7},{7,6},{8,9},{9,8},{10,11... | collective-permute-start | bytes 98312 | tf_op jit(solution)/shard_map/ppermute | solution.py:444
  22.8 1.8 %near.3.refs_5_ = f32[8,8,128]{2,1,0:T(8,128)S(1)} custom-call(s32[8,16]{1,0:T(8,128)S(1)} %get-tuple-element.24.refs_6_.refs_0_, bf16[128,128]{1,0:T(8,128)(2,1)S(1)} %get-tuple-element.23.refs_6_.refs_1_, bf16[16,8,2,128,128]{4,3,2,1,0:T(8,128)(2,1)S(1)} %copy-done, bf16[128,128]{1,0:T(8,128)(2,1)S(1)} %get-tuple-element.29.refs_3_.refs_0_, ...), custom_call_target="tpu_custom_call" | custom-call | flops 33554432 | bytes 4194304 | tf_op jit(solution)/shard_map/near/pallas_call | solution.py:508
  24.6 0.0 collective-permute-done.5.refs_1_
  24.6 0.8 %collective-permute-done.6.refs_2_ = bf16[128,128]{1,0:T(8,128)(2,1)S(1)} collective-permute-done((bf16[128,128]{1,0:T(8,128)(2,1)S(1)}, bf16[128,128]{1,0:T(8,128)(2,1)S(1)}, u32[]{:S(2)}, u32[]{:S(2)}) %collective-permute-start.6) | collective-permute-done | bytes 32800 | tf_op jit(solution)/shard_map/ppermute | solution.py:444
  25.4 0.4 %collective-permute-done.7.refs_3_ = bf16[128,128]{1,0:T(8,128)(2,1)S(1)} collective-permute-done((bf16[128,128]{1,0:T(8,128)(2,1)S(1)}, bf16[128,128]{1,0:T(8,128)(2,1)S(1)}, u32[]{:S(2)}, u32[]{:S(2)}) %collective-permute-start.7) | collective-permute-done | bytes 32800 | tf_op jit(solution)/shard_map/ppermute | solution.py:444
  25.8 0.0 copy-done.2
  25.8 1.0 %final.1 = f32[16,2,4,128]{3,2,1,0:T(4,128)} custom-call(bf16[128,128]{1,0:T(8,128)(2,1)S(1)} %get-tuple-element.29.refs_3_.refs_0_, bf16[128,128]{1,0:T(8,128)(2,1)S(1)} %collective-permute-done.5.refs_1_, bf16[128,128]{1,0:T(8,128)(2,1)S(1)} %collective-permute-done.6.refs_2_, bf16[128,128]{1,0:T(8,128)(2,1)S(1)} %collective-permute-done.7.refs_3_, ...), custom_call_target="tpu_custom_call" | custom-call | tf_op jit(solution)/shard_map/final/pallas_call | solution.py:557
Async XLA Ops:
  0.0 15.0 %copy-start = (bf16[16,8,2,128,128]{4,3,2,1,0:T(8,128)(2,1)S(1)}, bf16[16,8,2,128,128]{4,3,2,1,0:T(8,128)(2,1)}, u32[]{:S(2)}) copy-start(bf16[16,8,2,128,128]{4,3,2,1,0:T(8,128)(2,1)} %refs_2_.5) | copy-start | bytes 25165828
  0.0 11.8 %copy-start.1 = (bf16[2048,128]{1,0:T(8,128)(2,1)S(1)}, bf16[2048,128]{1,0:T(8,128)(2,1)}, u32[]{:S(2)}) copy-start(bf16[2048,128]{1,0:T(8,128)(2,1)} %refs_4_.7) | copy-start | bytes 1572868
  0.0 11.8 %copy-start.3 = (f32[8,2,2048]{2,1,0:T(2,128)S(1)}, f32[8,2,2048]{2,1,0:T(2,128)}, u32[]{:S(2)}) copy-start(f32[8,2,2048]{2,1,0:T(2,128)} %refs_5_.5) | copy-start | bytes 393220
  1.8 10.0 %collective-permute-start = (bf16[200,128]{1,0:T(8,128)(2,1)S(1)}, bf16[200,128]{1,0:T(8,128)(2,1)S(1)}, u32[]{:S(2)}, u32[]{:S(2)}) collective-permute-start(bf16[200,128]{1,0:T(8,128)(2,1)S(1)} %get-tuple-element.20), channel_id=1, source_target_pairs={{0,3},{1,2},{2,1},{3,0},{4,7},{5,6},{6,5},{7,4},{8,11},{9,10},{10,... | collective-permute-start | bytes 153608 | tf_op jit(solution)/shard_map/ppermute | solution.py:444
  6.9 4.9 %collective-permute-start.1 = (bf16[200,128]{1,0:T(8,128)(2,1)S(1)}, bf16[200,128]{1,0:T(8,128)(2,1)S(1)}, u32[]{:S(2)}, u32[]{:S(2)}) collective-permute-start(bf16[200,128]{1,0:T(8,128)(2,1)S(1)} %get-tuple-element.21), channel_id=1, source_target_pairs={{0,1},{1,0},{2,3},{3,2},{4,5},{5,4},{6,7},{7,6},{8,9},{9,8},{10,11... | collective-permute-start | bytes 153608 | tf_op jit(solution)/shard_map/ppermute | solution.py:444
  6.9 4.9 %collective-permute-start.2 = (bf16[136,128]{1,0:T(8,128)(2,1)S(1)}, bf16[136,128]{1,0:T(8,128)(2,1)S(1)}, u32[]{:S(2)}, u32[]{:S(2)}) collective-permute-start(bf16[136,128]{1,0:T(8,128)(2,1)S(1)} %get-tuple-element.19.refs_0_), channel_id=1, source_target_pairs={{0,2},{1,3},{2,0},{3,1},{4,6},{5,7},{6,4},{7,5},{8,10},{9,11},{10,... | collective-permute-start | bytes 104456 | tf_op jit(solution)/shard_map/ppermute | solution.py:444
  12.3 4.4 %collective-permute-start.4 = (bf16[80,512]{1,0:T(8,128)(2,1)S(1)}, bf16[80,512]{1,0:T(8,128)(2,1)S(1)}, u32[]{:S(2)}, u32[]{:S(2)}) collective-permute-start(bf16[80,512]{1,0:T(8,128)(2,1)S(1)} %get-tuple-element.25.refs_0_), channel_id=1, source_target_pairs={{0,4},{4,0},{8,12},{12,8},{16,20},{20,16},{24,28},{28,24},{1,5},{5... | collective-permute-start | bytes 245768 | tf_op jit(solution)/shard_map/ppermute | solution.py:505
  12.4 5.1 %collective-permute-start.3 = (bf16[80,512]{1,0:T(8,128)(2,1)S(1)}, bf16[80,512]{1,0:T(8,128)(2,1)S(1)}, u32[]{:S(2)}, u32[]{:S(2)}) collective-permute-start(bf16[80,512]{1,0:T(8,128)(2,1)S(1)} %get-tuple-element.26), channel_id=1, source_target_pairs={{0,28},{4,8},{8,4},{12,16},{16,12},{20,24},{24,20},{28,0},{1,29},{... | collective-permute-start | bytes 245768 | tf_op jit(solution)/shard_map/ppermute | solution.py:502
  15.0 10.8 %copy-start.2 = (bf16[16,2,128,128]{3,2,1,0:T(8,128)(2,1)S(1)}, bf16[16,2,128,128]{3,2,1,0:T(8,128)(2,1)}, u32[]{:S(2)}) copy-start(bf16[16,2,128,128]{3,2,1,0:T(8,128)(2,1)} %refs_6_.3) | copy-start | bytes 3145732
  18.3 6.3 %collective-permute-start.5 = (bf16[128,128]{1,0:T(8,128)(2,1)S(1)}, bf16[128,128]{1,0:T(8,128)(2,1)S(1)}, u32[]{:S(2)}, u32[]{:S(2)}) collective-permute-start(bf16[128,128]{1,0:T(8,128)(2,1)S(1)} %get-tuple-element.30), channel_id=1, source_target_pairs={{0,3},{1,2},{2,1},{3,0},{4,7},{5,6},{6,5},{7,4},{8,11},{9,10},{10,... | collective-permute-start | bytes 98312 | tf_op jit(solution)/shard_map/ppermute | solution.py:444
  20.3 5.1 %collective-permute-start.6 = (bf16[128,128]{1,0:T(8,128)(2,1)S(1)}, bf16[128,128]{1,0:T(8,128)(2,1)S(1)}, u32[]{:S(2)}, u32[]{:S(2)}) collective-permute-start(bf16[128,128]{1,0:T(8,128)(2,1)S(1)} %get-tuple-element.31), channel_id=1, source_target_pairs={{0,2},{1,3},{2,0},{3,1},{4,6},{5,7},{6,4},{7,5},{8,10},{9,11},{10,... | collective-permute-start | bytes 98312 | tf_op jit(solution)/shard_map/ppermute | solution.py:444
  21.9 3.9 %collective-permute-start.7 = (bf16[128,128]{1,0:T(8,128)(2,1)S(1)}, bf16[128,128]{1,0:T(8,128)(2,1)S(1)}, u32[]{:S(2)}, u32[]{:S(2)}) collective-permute-start(bf16[128,128]{1,0:T(8,128)(2,1)S(1)} %get-tuple-element.32), channel_id=1, source_target_pairs={{0,1},{1,0},{2,3},{3,2},{4,5},{5,4},{6,7},{7,6},{8,9},{9,8},{10,11... | collective-permute-start | bytes 98312 | tf_op jit(solution)/shard_map/ppermute | solution.py:444

commit v13 on v12

--- a/solution.py
+++ b/solution.py
@@ -91,7 +91,7 @@
 def up_kernel(*refs, pieces, boxes, parents, parts):
     msgs = refs[:pieces]
     interp_ref, phase_ref, after, out_ref, out_copy, place_ref, raised, folded = refs[pieces:]
-    forward = msgs[1]
+    forward = msgs[2]
     slots = 8 * parents
     samples = raised.shape[1]
     first = lax.axis_index("samp") * samples
@@ -443,7 +443,7 @@
     def exchange(x, d):
         return lax.ppermute(x, "samp", [(i, i ^ d) for i in range(nsamp)])
 
-    order = [0, nsamp - 1, *range(1, nsamp - 1)]
+    order = [0, 1, nsamp - 1, *range(2, nsamp - 1)]
     far = [(4 << i) - 1 for i in range(nsamp.bit_length() - 2)]
     messages = {0: plain}
     for d in order[1:]:

time: 26.9 us -> 27.7 us (1.030)
  waiting for transfers between devices: 4.47 us -> 5.29 us
    ppermute x6, waiting for transfers between devices: 3.76 us -> 4.58 us  [exchange(): return lax.ppermute(x, 'samp', [(i, i ^ d) for i in range(nsamp)])]
  transfers between devices with their start and end apart: 8 -> 8, of which waited for: 4 -> 3; matrix products, arithmetic and copies ran while one was open for 0% -> 0% of each run, Pallas kernels for 20% -> 19%
where the time goes in v13:
time: 27.7 us; the launch traced here: 27.5 us
  starting transfers between devices  12.8 us (46%)
  Pallas kernels  9.39 us (34%)
  waiting for transfers between devices  5.29 us (19%)
    ppermute x6, starting transfers between devices, exchange(): return lax.ppermute(x, 'samp', [(i, i ^ d) for i in range(nsamp)])  10.1 us
    ppermute x6, waiting for transfers between devices, exchange(): return lax.ppermute(x, 'samp', [(i, i ^ d) for i in range(nsamp)])  4.58 us
    pallas_call x2, Pallas kernels, near_half(): pl.pallas_call(lambda *refs: near_kernel(*refs, late=late, nsamp=nsamp, t...  3.62 us
    ppermute x1, starting transfers between devices, on_device(): lax.ppermute(to_across, 'box', [(i, (i + (1 if i % 2 else -1)) % nbox) fo...  2.55 us
    pallas_call x1, Pallas kernels, on_device(): pl.pallas_call(lambda *refs: leaf_kernel(*refs, parents=parents, all_pare...  1.79 us
    pallas_call x1, Pallas kernels, on_device(): pl.pallas_call(lambda *refs: prep_kernel(*refs, parents=parents, all_pare...  1.61 us
    pallas_call x1, Pallas kernels, on_device(): pl.pallas_call(lambda *refs: final_kernel(*refs, pieces=nsamp), in_specs=...  1.03 us
    pallas_call x1, Pallas kernels, on_device(): pl.pallas_call(lambda *refs: down_kernel(*refs, pieces=nsamp, boxes=boxes...  0.81 us
  transfers between devices with their start and end apart: 8, of which 3 were waited for; matrix products, arithmetic and copies ran while one was open for 0% of the time, Pallas kernels for 19%

profile of v13, /device:TPU:0, one launch (start us, length us, event | category | flops | bytes accessed | tf_op | source)
XLA Modules:
  0.0 27.5 jit_solution(5121747953292258678)
XLA Ops:
  0.0 0.0 copy-start
  0.0 0.0 copy-start.1
  0.0 0.0 copy-start.3
  0.0 1.8 %leaf.1 = (bf16[200,128]{1,0:T(8,128)(2,1)S(1)}, bf16[136,128]{1,0:T(8,128)(2,1)S(1)}, bf16[200,128]{1,0:T(8,128)(2,1)S(1)}, bf16[128,128]{1,0:T(8,128)(2,1)S(1)}, f32[8,14,2,512]{3,2,1,0:T(2,128)S(1)}) custom-call(s32[16]{0:T(128)} %refs_0_.2, s32[16]{0:T(128)} %refs_1_.2, bf16[16,2,4,128]{3,2,1,0:T(4,128)(2,1)} %refs_2_.3, ...), custom_call_target="tpu_custom_call" | custom-call | tf_op jit(solution)/shard_map/leaf/pallas_call | solution.py:413
  1.8 3.1 %collective-permute-start = (bf16[200,128]{1,0:T(8,128)(2,1)S(1)}, bf16[200,128]{1,0:T(8,128)(2,1)S(1)}, u32[]{:S(2)}, u32[]{:S(2)}) collective-permute-start(bf16[200,128]{1,0:T(8,128)(2,1)S(1)} %get-tuple-element.20), channel_id=1, source_target_pairs={{0,1},{1,0},{2,3},{3,2},{4,5},{5,4},{6,7},{7,6},{8,9},{9,8},{10,11... | collective-permute-start | bytes 153608 | tf_op jit(solution)/shard_map/ppermute | solution.py:444
  4.9 2.5 %collective-permute-start.1 = (bf16[200,128]{1,0:T(8,128)(2,1)S(1)}, bf16[200,128]{1,0:T(8,128)(2,1)S(1)}, u32[]{:S(2)}, u32[]{:S(2)}) collective-permute-start(bf16[200,128]{1,0:T(8,128)(2,1)S(1)} %get-tuple-element.21), channel_id=1, source_target_pairs={{0,3},{1,2},{2,1},{3,0},{4,7},{5,6},{6,5},{7,4},{8,11},{9,10},{10,... | collective-permute-start | bytes 153608 | tf_op jit(solution)/shard_map/ppermute | solution.py:444
  7.4 0.1 collective-permute-start.2
  7.5 1.6 %prep.1 = (f32[8,14,2,512]{3,2,1,0:T(2,128)S(1)}, s32[8,16]{1,0:T(8,128)S(1)}) custom-call(s32[8,14]{1,0:T(8,128)} %refs_0_.3, s32[8,14]{1,0:T(8,128)} %refs_1_.3, s32[8,16]{1,0:T(8,128)} %bitcast.1, f32[64,2,512]{2,1,0:T(2,128)} %refs_3_.3, bf16[16,8,2,128,128]{4,3,2,1,0:T(8,128)(2,1)} %refs_2_.5, ...), custom_call_target="tpu_custom_call", output_to_operand_aliasing={{0}: (5, {})} | custom-call | bytes 8388608 | tf_op jit(solution)/shard_map/prep/pallas_call | solution.py:453
  9.1 3.5 %collective-permute-done.2.refs_3_ = bf16[136,128]{1,0:T(8,128)(2,1)S(1)} collective-permute-done((bf16[136,128]{1,0:T(8,128)(2,1)S(1)}, bf16[136,128]{1,0:T(8,128)(2,1)S(1)}, u32[]{:S(2)}, u32[]{:S(2)}) %collective-permute-start.2) | collective-permute-done | bytes 34848 | tf_op jit(solution)/shard_map/ppermute | solution.py:444
  12.6 0.0 collective-permute-done.refs_1_.refs_4_
  12.6 0.0 collective-permute-done.1.refs_2_.refs_6_
  12.6 0.0 copy-done.1
  12.6 0.0 copy-done.3
  12.6 0.5 %up.1 = (bf16[80,512]{1,0:T(8,128)(2,1)S(1)}, bf16[80,512]{1,0:T(8,128)(2,1)S(1)}, bf16[64,64]{1,0:T(8,128)(2,1)S(1)}) custom-call(bf16[136,128]{1,0:T(8,128)(2,1)S(1)} %get-tuple-element.19.refs_0_, bf16[200,128]{1,0:T(8,128)(2,1)S(1)} %collective-permute-done.refs_1_.refs_4_, bf16[200,128]{1,0:T(8,128)(2,1)S(1)} %collective-permute-done.1.refs_2_.refs_6_, ...), custom_call_target="tpu_custom_call" | custom-call | tf_op jit(solution)/shard_map/up/pallas_call | solution.py:483
  13.1 0.1 collective-permute-start.4
  13.2 2.5 %collective-permute-start.3 = (bf16[80,512]{1,0:T(8,128)(2,1)S(1)}, bf16[80,512]{1,0:T(8,128)(2,1)S(1)}, u32[]{:S(2)}, u32[]{:S(2)}) collective-permute-start(bf16[80,512]{1,0:T(8,128)(2,1)S(1)} %get-tuple-element.26), channel_id=1, source_target_pairs={{0,28},{4,8},{8,4},{12,16},{16,12},{20,24},{24,20},{28,0},{1,29},{... | collective-permute-start | bytes 245768 | tf_op jit(solution)/shard_map/ppermute | solution.py:502
  15.8 0.0 copy-done
  15.8 0.0 copy-start.2
  15.8 1.8 %near.2.refs_7_.refs_4_ = f32[8,8,128]{2,1,0:T(8,128)S(1)} custom-call(s32[8,16]{1,0:T(8,128)S(1)} %get-tuple-element.24.refs_6_.refs_0_, bf16[128,128]{1,0:T(8,128)(2,1)S(1)} %get-tuple-element.23.refs_6_.refs_1_, bf16[16,8,2,128,128]{4,3,2,1,0:T(8,128)(2,1)S(1)} %copy-done, bf16[64,64]{1,0:T(8,128)(2,1)S(1)} %get-tuple-element.28.refs_3_.refs_6_, ...), custom_call_target="tpu_custom_call" | custom-call | flops 33554432 | bytes 4194304 | tf_op jit(solution)/shard_map/near/pallas_call | solution.py:508
  17.6 0.0 collective-permute-done.4.refs_2_.refs_5_
  17.6 0.7 %collective-permute-done.3.refs_1_.refs_4_ = bf16[80,512]{1,0:T(8,128)(2,1)S(1)} collective-permute-done((bf16[80,512]{1,0:T(8,128)(2,1)S(1)}, bf16[80,512]{1,0:T(8,128)(2,1)S(1)}, u32[]{:S(2)}, u32[]{:S(2)}) %collective-permute-start.3) | collective-permute-done | bytes 81952 | tf_op jit(solution)/shard_map/ppermute | solution.py:502
  18.3 0.8 %down.1 = (bf16[128,128]{1,0:T(8,128)(2,1)S(1)}, bf16[128,128]{1,0:T(8,128)(2,1)S(1)}, bf16[128,128]{1,0:T(8,128)(2,1)S(1)}, bf16[128,128]{1,0:T(8,128)(2,1)S(1)}) custom-call(bf16[80,512]{1,0:T(8,128)(2,1)S(1)} %get-tuple-element.25.refs_0_, bf16[80,512]{1,0:T(8,128)(2,1)S(1)} %collective-permute-done.3.refs_1_.refs_4_, ...), custom_call_target="tpu_custom_call" | custom-call | tf_op jit(solution)/shard_map/down/pallas_call | solution.py:536
  19.1 2.6 %collective-permute-start.5 = (bf16[128,128]{1,0:T(8,128)(2,1)S(1)}, bf16[128,128]{1,0:T(8,128)(2,1)S(1)}, u32[]{:S(2)}, u32[]{:S(2)}) collective-permute-start(bf16[128,128]{1,0:T(8,128)(2,1)S(1)} %get-tuple-element.30), channel_id=1, source_target_pairs={{0,3},{1,2},{2,1},{3,0},{4,7},{5,6},{6,5},{7,4},{8,11},{9,10},{10,... | collective-permute-start | bytes 98312 | tf_op jit(solution)/shard_map/ppermute | solution.py:444
  21.7 0.0 collective-permute-start.6
  21.7 1.9 %collective-permute-start.7 = (bf16[128,128]{1,0:T(8,128)(2,1)S(1)}, bf16[128,128]{1,0:T(8,128)(2,1)S(1)}, u32[]{:S(2)}, u32[]{:S(2)}) collective-permute-start(bf16[128,128]{1,0:T(8,128)(2,1)S(1)} %get-tuple-element.32), channel_id=1, source_target_pairs={{0,1},{1,0},{2,3},{3,2},{4,5},{5,4},{6,7},{7,6},{8,9},{9,8},{10,11... | collective-permute-start | bytes 98312 | tf_op jit(solution)/shard_map/ppermute | solution.py:444
  23.6 1.8 %near.3.refs_5_ = f32[8,8,128]{2,1,0:T(8,128)S(1)} custom-call(s32[8,16]{1,0:T(8,128)S(1)} %get-tuple-element.24.refs_6_.refs_0_, bf16[128,128]{1,0:T(8,128)(2,1)S(1)} %get-tuple-element.23.refs_6_.refs_1_, bf16[16,8,2,128,128]{4,3,2,1,0:T(8,128)(2,1)S(1)} %copy-done, bf16[128,128]{1,0:T(8,128)(2,1)S(1)} %get-tuple-element.29.refs_3_.refs_0_, ...), custom_call_target="tpu_custom_call" | custom-call | flops 33554432 | bytes 4194304 | tf_op jit(solution)/shard_map/near/pallas_call | solution.py:508
  25.4 0.0 collective-permute-done.5.refs_1_
  25.4 1.1 %collective-permute-done.6.refs_2_ = bf16[128,128]{1,0:T(8,128)(2,1)S(1)} collective-permute-done((bf16[128,128]{1,0:T(8,128)(2,1)S(1)}, bf16[128,128]{1,0:T(8,128)(2,1)S(1)}, u32[]{:S(2)}, u32[]{:S(2)}) %collective-permute-start.6) | collective-permute-done | bytes 32800 | tf_op jit(solution)/shard_map/ppermute | solution.py:444
  26.5 0.0 collective-permute-done.7.refs_3_
  26.5 0.0 copy-done.2
  26.5 1.0 %final.1 = f32[16,2,4,128]{3,2,1,0:T(4,128)} custom-call(bf16[128,128]{1,0:T(8,128)(2,1)S(1)} %get-tuple-element.29.refs_3_.refs_0_, bf16[128,128]{1,0:T(8,128)(2,1)S(1)} %collective-permute-done.5.refs_1_, bf16[128,128]{1,0:T(8,128)(2,1)S(1)} %collective-permute-done.6.refs_2_, bf16[128,128]{1,0:T(8,128)(2,1)S(1)} %collective-permute-done.7.refs_3_, ...), custom_call_target="tpu_custom_call" | custom-call | tf_op jit(solution)/shard_map/final/pallas_call | solution.py:557
Async XLA Ops:
  0.0 15.8 %copy-start = (bf16[16,8,2,128,128]{4,3,2,1,0:T(8,128)(2,1)S(1)}, bf16[16,8,2,128,128]{4,3,2,1,0:T(8,128)(2,1)}, u32[]{:S(2)}) copy-start(bf16[16,8,2,128,128]{4,3,2,1,0:T(8,128)(2,1)} %refs_2_.5) | copy-start | bytes 25165828
  0.0 12.6 %copy-start.1 = (bf16[2048,128]{1,0:T(8,128)(2,1)S(1)}, bf16[2048,128]{1,0:T(8,128)(2,1)}, u32[]{:S(2)}) copy-start(bf16[2048,128]{1,0:T(8,128)(2,1)} %refs_4_.7) | copy-start | bytes 1572868
  0.0 12.6 %copy-start.3 = (f32[8,2,2048]{2,1,0:T(2,128)S(1)}, f32[8,2,2048]{2,1,0:T(2,128)}, u32[]{:S(2)}) copy-start(f32[8,2,2048]{2,1,0:T(2,128)} %refs_5_.5) | copy-start | bytes 393220
  1.8 10.8 %collective-permute-start = (bf16[200,128]{1,0:T(8,128)(2,1)S(1)}, bf16[200,128]{1,0:T(8,128)(2,1)S(1)}, u32[]{:S(2)}, u32[]{:S(2)}) collective-permute-start(bf16[200,128]{1,0:T(8,128)(2,1)S(1)} %get-tuple-element.20), channel_id=1, source_target_pairs={{0,1},{1,0},{2,3},{3,2},{4,5},{5,4},{6,7},{7,6},{8,9},{9,8},{10,11... | collective-permute-start | bytes 153608 | tf_op jit(solution)/shard_map/ppermute | solution.py:444
  4.9 7.7 %collective-permute-start.1 = (bf16[200,128]{1,0:T(8,128)(2,1)S(1)}, bf16[200,128]{1,0:T(8,128)(2,1)S(1)}, u32[]{:S(2)}, u32[]{:S(2)}) collective-permute-start(bf16[200,128]{1,0:T(8,128)(2,1)S(1)} %get-tuple-element.21), channel_id=1, source_target_pairs={{0,3},{1,2},{2,1},{3,0},{4,7},{5,6},{6,5},{7,4},{8,11},{9,10},{10,... | collective-permute-start | bytes 153608 | tf_op jit(solution)/shard_map/ppermute | solution.py:444
  7.4 5.2 %collective-permute-start.2 = (bf16[136,128]{1,0:T(8,128)(2,1)S(1)}, bf16[136,128]{1,0:T(8,128)(2,1)S(1)}, u32[]{:S(2)}, u32[]{:S(2)}) collective-permute-start(bf16[136,128]{1,0:T(8,128)(2,1)S(1)} %get-tuple-element.19.refs_0_), channel_id=1, source_target_pairs={{0,2},{1,3},{2,0},{3,1},{4,6},{5,7},{6,4},{7,5},{8,10},{9,11},{10,... | collective-permute-start | bytes 104456 | tf_op jit(solution)/shard_map/ppermute | solution.py:444
  13.1 4.4 %collective-permute-start.4 = (bf16[80,512]{1,0:T(8,128)(2,1)S(1)}, bf16[80,512]{1,0:T(8,128)(2,1)S(1)}, u32[]{:S(2)}, u32[]{:S(2)}) collective-permute-start(bf16[80,512]{1,0:T(8,128)(2,1)S(1)} %get-tuple-element.25.refs_0_), channel_id=1, source_target_pairs={{0,4},{4,0},{8,12},{12,8},{16,20},{20,16},{24,28},{28,24},{1,5},{5... | collective-permute-start | bytes 245768 | tf_op jit(solution)/shard_map/ppermute | solution.py:505
  13.2 5.1 %collective-permute-start.3 = (bf16[80,512]{1,0:T(8,128)(2,1)S(1)}, bf16[80,512]{1,0:T(8,128)(2,1)S(1)}, u32[]{:S(2)}, u32[]{:S(2)}) collective-permute-start(bf16[80,512]{1,0:T(8,128)(2,1)S(1)} %get-tuple-element.26), channel_id=1, source_target_pairs={{0,28},{4,8},{8,4},{12,16},{16,12},{20,24},{24,20},{28,0},{1,29},{... | collective-permute-start | bytes 245768 | tf_op jit(solution)/shard_map/ppermute | solution.py:502
  15.8 10.7 %copy-start.2 = (bf16[16,2,128,128]{3,2,1,0:T(8,128)(2,1)S(1)}, bf16[16,2,128,128]{3,2,1,0:T(8,128)(2,1)}, u32[]{:S(2)}) copy-start(bf16[16,2,128,128]{3,2,1,0:T(8,128)(2,1)} %refs_6_.3) | copy-start | bytes 3145732
  19.1 6.3 %collective-permute-start.5 = (bf16[128,128]{1,0:T(8,128)(2,1)S(1)}, bf16[128,128]{1,0:T(8,128)(2,1)S(1)}, u32[]{:S(2)}, u32[]{:S(2)}) collective-permute-start(bf16[128,128]{1,0:T(8,128)(2,1)S(1)} %get-tuple-element.30), channel_id=1, source_target_pairs={{0,3},{1,2},{2,1},{3,0},{4,7},{5,6},{6,5},{7,4},{8,11},{9,10},{10,... | collective-permute-start | bytes 98312 | tf_op jit(solution)/shard_map/ppermute | solution.py:444
  21.7 4.8 %collective-permute-start.6 = (bf16[128,128]{1,0:T(8,128)(2,1)S(1)}, bf16[128,128]{1,0:T(8,128)(2,1)S(1)}, u32[]{:S(2)}, u32[]{:S(2)}) collective-permute-start(bf16[128,128]{1,0:T(8,128)(2,1)S(1)} %get-tuple-element.31), channel_id=1, source_target_pairs={{0,2},{1,3},{2,0},{3,1},{4,6},{5,7},{6,4},{7,5},{8,10},{9,11},{10,... | collective-permute-start | bytes 98312 | tf_op jit(solution)/shard_map/ppermute | solution.py:444
  21.7 4.8 %collective-permute-start.7 = (bf16[128,128]{1,0:T(8,128)(2,1)S(1)}, bf16[128,128]{1,0:T(8,128)(2,1)S(1)}, u32[]{:S(2)}, u32[]{:S(2)}) collective-permute-start(bf16[128,128]{1,0:T(8,128)(2,1)S(1)} %get-tuple-element.32), channel_id=1, source_target_pairs={{0,1},{1,0},{2,3},{3,2},{4,5},{5,4},{6,7},{7,6},{8,9},{9,8},{10,11... | collective-permute-start | bytes 98312 | tf_op jit(solution)/shard_map/ppermute | solution.py:444

commit v14 on v12

--- a/solution.py
+++ b/solution.py
@@ -30,7 +30,7 @@
 
 def leaf_kernel(
     octant, parent, x_hbm, lift_hbm, inter, trans, table_hbm,
-    to_far, plain, to_beside, x_rows, dense,
+    message, plain, x_rows, dense,
     x_ref, rows, lift, oct_s, par_s, sems, inter_s, trans_s, table, more,
     *, parents, all_parents,
 ):
@@ -71,11 +71,11 @@
     x_rows[...] = jnp.concatenate(own, axis=0).astype(BF16)
     first = jnp.concatenate(own[:reach], axis=0)
     last = jnp.concatenate(own[reach:], axis=0)
-    odd = lax.rem(lax.axis_index("samp"), 2) == 1
     at = parts * boxes
-    to_beside[at + CODE_ROWS :] = jnp.where(odd, first, last).astype(BF16)
-    to_far[at + CODE_ROWS :] = jnp.where(odd, last, first).astype(BF16)
-    for ref in (plain, to_beside, to_far):
+    halo = first.shape[0]
+    message[at + CODE_ROWS : at + CODE_ROWS + halo] = first.astype(BF16)
+    message[at + CODE_ROWS + halo :] = last.astype(BF16)
+    for ref in (plain, message):
         ref[at : at + CODE_ROWS] = codes
     for n in range(boxes):
         if n % per == 0:
@@ -83,7 +83,7 @@
         mat = jnp.concatenate([lift[n, 0], lift[n, 1]], axis=1)
         rows[pl.ds(n, parts, stride=boxes), :] = nt_dot(widen(own[n]).astype(BF16), mat)
     pattern = rows[...].astype(BF16)
-    for ref in (plain, to_beside, to_far):
+    for ref in (plain, message):
         ref[:at] = pattern
     pl.when(odd_box())(finish)
 
@@ -410,14 +410,13 @@
         return jax.ShapeDtypeStruct(dims, dtype)
 
     lift_chunks = 2
-    to_far, plain, to_beside, x_rows, dense = pl.pallas_call(
+    message, plain, x_rows, dense = pl.pallas_call(
         lambda *refs: leaf_kernel(*refs, parents=parents, all_parents=all_parents),
         in_specs=[whole_in(HBM)] * 7,
-        out_specs=[whole_in(VM)] * 5,
+        out_specs=[whole_in(VM)] * 4,
         out_shape=[
-            shape((plain_rows + halo_rows, LANES)),
+            shape((plain_rows + 2 * halo_rows, LANES)),
             shape((plain_rows, LANES)),
-            shape((plain_rows + halo_rows, LANES)),
             shape((boxes * parts, LANES)),
             shape((parents, len(zone(parents)), 2, samples), F32),
         ],
@@ -445,9 +444,19 @@
 
     order = [0, nsamp - 1, *range(1, nsamp - 1)]
     far = [(4 << i) - 1 for i in range(nsamp.bit_length() - 2)]
+    gathered = lax.all_gather(message, "samp")
+    samp = lax.axis_index("samp").astype(jnp.int32)
     messages = {0: plain}
     for d in order[1:]:
-        messages[d] = exchange(to_beside if d == 1 else to_far if d in far else plain, d)
+        got = lax.dynamic_index_in_dim(gathered, samp ^ d, 0, keepdims=False)
+        if d == 1 or d in far:
+            sender_odd = (samp ^ d) % 2
+            take_last = 1 - sender_odd if d == 1 else sender_odd
+            halo = lax.dynamic_slice_in_dim(got, plain_rows + halo_rows * take_last, halo_rows, 0)
+            got = jnp.concatenate([got[:plain_rows], halo], axis=0)
+        else:
+            got = got[:plain_rows]
+        messages[d] = got
     far_messages = [messages[d] for d in far]
 
     dense, near_list = pl.pallas_call(

time: 26.9 us -> 36.3 us (1.35)
  blocking collectives: 0 us -> 15.8 us
  starting transfers between devices: 12.8 us -> 6.24 us
    all_gather x0 -> x1, blocking collectives: none -> 15.8 us  [on_device(): gathered = lax.all_gather(message, 'samp')]
    ppermute x6 -> x3, starting transfers between devices: 10.2 us -> 4.57 us  [exchange(): return lax.ppermute(x, 'samp', [(i, i ^ d) for i in range(nsamp)])]
    ppermute x1, starting transfers between devices: 2.55 us -> 0.07 us  [on_device(): lax.ppermute(to_across, 'box', [(i, (i + (1 if i % 2 else -1)) % nbox) fo...]
    ppermute x1, starting transfers between devices: 0.07 us -> 1.59 us  [on_device(): beside = lax.ppermute(parent_pat, 'box', [(i, i ^ 1) for i in range(nbox)])]
    ppermute x6 -> x3, waiting for transfers between devices: 3.76 us -> 2.35 us  [exchange(): return lax.ppermute(x, 'samp', [(i, i ^ d) for i in range(nsamp)])]
    ppermute x1, waiting for transfers between devices: 0.71 us -> 2.11 us  [on_device(): lax.ppermute(to_across, 'box', [(i, (i + (1 if i % 2 else -1)) % nbox) fo...]
  transfers between devices with their start and end apart: 8 -> 5, of which waited for: 4 -> 2; matrix products, arithmetic and copies ran while one was open for 0% -> 0% of each run, Pallas kernels for 20% -> 10%
where the time goes in v14:
time: 36.3 us; the launch traced here: 36.1 us
  blocking collectives  15.8 us (44%)
  Pallas kernels  9.45 us (26%)
  starting transfers between devices  6.24 us (17%)
  waiting for transfers between devices  4.46 us (12%)
    all_gather x1, blocking collectives, on_device(): gathered = lax.all_gather(message, 'samp')  15.8 us
    ppermute x3, starting transfers between devices, exchange(): return lax.ppermute(x, 'samp', [(i, i ^ d) for i in range(nsamp)])  4.57 us
    pallas_call x2, Pallas kernels, near_half(): pl.pallas_call(lambda *refs: near_kernel(*refs, late=late, nsamp=nsamp, t...  3.62 us
    ppermute x3, waiting for transfers between devices, exchange(): return lax.ppermute(x, 'samp', [(i, i ^ d) for i in range(nsamp)])  2.35 us
    ppermute x1, waiting for transfers between devices, on_device(): lax.ppermute(to_across, 'box', [(i, (i + (1 if i % 2 else -1)) % nbox) fo...  2.11 us
    pallas_call x1, Pallas kernels, on_device(): pl.pallas_call(lambda *refs: prep_kernel(*refs, parents=parents, all_pare...  1.77 us
    pallas_call x1, Pallas kernels, on_device(): pl.pallas_call(lambda *refs: leaf_kernel(*refs, parents=parents, all_pare...  1.71 us
    ppermute x1, starting transfers between devices, on_device(): beside = lax.ppermute(parent_pat, 'box', [(i, i ^ 1) for i in range(nbox)])  1.59 us
  transfers between devices with their start and end apart: 5, of which 2 were waited for; matrix products, arithmetic and copies ran while one was open for 0% of the time, Pallas kernels for 10%

profile of v14, /device:TPU:0, one launch (start us, length us, event | category | flops | bytes accessed | tf_op | source)
XLA Modules:
  0.0 36.1 jit_solution(18169367025068133183)
XLA Ops:
  0.0 0.0 copy-start.3
  0.0 0.0 copy-start.1
  0.0 1.7 %leaf.1 = (bf16[264,128]{1,0:T(8,128)(2,1)S(1)}, bf16[136,128]{1,0:T(8,128)(2,1)S(1)}, bf16[128,128]{1,0:T(8,128)(2,1)S(1)}, f32[8,14,2,512]{3,2,1,0:T(2,128)S(1)}) custom-call(s32[16]{0:T(128)} %refs_0_.2, s32[16]{0:T(128)} %refs_1_.2, bf16[16,2,4,128]{3,2,1,0:T(4,128)(2,1)} %refs_2_.3, bf16[16,2,128,128]{3,2,1,0:T(8,128)(2,1)} %refs_3_.2, ...), custom_call_target="tpu_custom_call" | custom-call | tf_op jit(solution)/shard_map/leaf/pallas_call | solution.py:413
  1.7 15.8 %all-gather = bf16[1056,128]{1,0:T(8,128)(2,1)S(1)} all-gather(bf16[264,128]{1,0:T(8,128)(2,1)S(1)} %get-tuple-element.19), channel_id=2, replica_groups=mesh['box'=8,'samp'=4] {'samp'}, dimensions={0}, use_global_device_ids=true | all-gather | bytes 337920 | tf_op jit(solution)/shard_map/all_gather | solution.py:447
  17.5 0.0 copy-start
  17.6 1.8 %prep.1 = (f32[8,14,2,512]{3,2,1,0:T(2,128)S(1)}, s32[8,16]{1,0:T(8,128)S(1)}) custom-call(s32[8,14]{1,0:T(8,128)} %refs_0_.3, s32[8,14]{1,0:T(8,128)} %refs_1_.3, s32[8,16]{1,0:T(8,128)} %bitcast.14, f32[64,2,512]{2,1,0:T(2,128)} %refs_3_.3, bf16[16,8,2,128,128]{4,3,2,1,0:T(8,128)(2,1)} %refs_2_.5, ...), custom_call_target="tpu_custom_call", output_to_operand_aliasing={{0}: (5, {})} | custom-call | bytes 8388608 | tf_op jit(solution)/shard_map/prep/pallas_call | solution.py:462
  19.3 0.0 copy-done.3
  19.4 0.0 copy-done.1
  19.4 0.5 %up.1 = (bf16[80,512]{1,0:T(8,128)(2,1)S(1)}, bf16[80,512]{1,0:T(8,128)(2,1)S(1)}, bf16[64,64]{1,0:T(8,128)(2,1)S(1)}) custom-call(bf16[136,128]{1,0:T(8,128)(2,1)S(1)} %get-tuple-element.18.refs_0_, bf16[200,128]{1,0:T(8,128)(2,1)S(1)} %get-tuple-element.36.refs_1_.refs_6_, bf16[200,128]{1,0:T(8,128)(2,1)S(1)} %get-tuple-element.37.refs_2_.refs_4_, ...), custom_call_target="tpu_custom_call" | custom-call | tf_op jit(solution)/shard_map/up/pallas_call | solution.py:492
  19.9 0.1 collective-permute-start
  20.0 1.6 %collective-permute-start.1 = (bf16[80,512]{1,0:T(8,128)(2,1)S(1)}, bf16[80,512]{1,0:T(8,128)(2,1)S(1)}, u32[]{:S(2)}, u32[]{:S(2)}) collective-permute-start(bf16[80,512]{1,0:T(8,128)(2,1)S(1)} %get-tuple-element.23.refs_0_), channel_id=1, source_target_pairs={{0,4},{4,0},{8,12},{12,8},{16,20},{20,16},{24,28},{28,24},{1,5},{5... | collective-permute-start | bytes 245768 | tf_op jit(solution)/shard_map/ppermute | solution.py:514
  21.6 0.0 copy-done
  21.6 0.0 copy-start.2
  21.6 1.8 %near.2.refs_7_.refs_4_ = f32[8,8,128]{2,1,0:T(8,128)S(1)} custom-call(s32[8,16]{1,0:T(8,128)S(1)} %get-tuple-element.22.refs_6_.refs_0_, bf16[128,128]{1,0:T(8,128)(2,1)S(1)} %get-tuple-element.21.refs_6_.refs_1_, bf16[16,8,2,128,128]{4,3,2,1,0:T(8,128)(2,1)S(1)} %copy-done, bf16[64,64]{1,0:T(8,128)(2,1)S(1)} %get-tuple-element.26.refs_3_.refs_6_, ...), custom_call_target="tpu_custom_call" | custom-call | flops 33554432 | bytes 4194304 | tf_op jit(solution)/shard_map/near/pallas_call | solution.py:517
  23.4 2.1 %collective-permute-done.refs_1_.refs_4_ = bf16[80,512]{1,0:T(8,128)(2,1)S(1)} collective-permute-done((bf16[80,512]{1,0:T(8,128)(2,1)S(1)}, bf16[80,512]{1,0:T(8,128)(2,1)S(1)}, u32[]{:S(2)}, u32[]{:S(2)}) %collective-permute-start) | collective-permute-done | bytes 81952 | tf_op jit(solution)/shard_map/ppermute | solution.py:511
  25.5 0.0 collective-permute-done.1.refs_2_.refs_5_
  25.5 0.8 %down.1 = (bf16[128,128]{1,0:T(8,128)(2,1)S(1)}, bf16[128,128]{1,0:T(8,128)(2,1)S(1)}, bf16[128,128]{1,0:T(8,128)(2,1)S(1)}, bf16[128,128]{1,0:T(8,128)(2,1)S(1)}) custom-call(bf16[80,512]{1,0:T(8,128)(2,1)S(1)} %get-tuple-element.23.refs_0_, bf16[80,512]{1,0:T(8,128)(2,1)S(1)} %collective-permute-done.refs_1_.refs_4_, ...), custom_call_target="tpu_custom_call" | custom-call | tf_op jit(solution)/shard_map/down/pallas_call | solution.py:545
  26.3 3.9 %collective-permute-start.2 = (bf16[128,128]{1,0:T(8,128)(2,1)S(1)}, bf16[128,128]{1,0:T(8,128)(2,1)S(1)}, u32[]{:S(2)}, u32[]{:S(2)}) collective-permute-start(bf16[128,128]{1,0:T(8,128)(2,1)S(1)} %get-tuple-element.28), channel_id=1, source_target_pairs={{0,3},{1,2},{2,1},{3,0},{4,7},{5,6},{6,5},{7,4},{8,11},{9,10},{10,... | collective-permute-start | bytes 98312 | tf_op jit(solution)/shard_map/ppermute | solution.py:443
  30.3 0.0 collective-permute-start.3
  30.3 0.6 %collective-permute-start.4 = (bf16[128,128]{1,0:T(8,128)(2,1)S(1)}, bf16[128,128]{1,0:T(8,128)(2,1)S(1)}, u32[]{:S(2)}, u32[]{:S(2)}) collective-permute-start(bf16[128,128]{1,0:T(8,128)(2,1)S(1)} %get-tuple-element.30), channel_id=1, source_target_pairs={{0,1},{1,0},{2,3},{3,2},{4,5},{5,4},{6,7},{7,6},{8,9},{9,8},{10,11... | collective-permute-start | bytes 98312 | tf_op jit(solution)/shard_map/ppermute | solution.py:443
  30.9 1.8 %near.3.refs_5_ = f32[8,8,128]{2,1,0:T(8,128)S(1)} custom-call(s32[8,16]{1,0:T(8,128)S(1)} %get-tuple-element.22.refs_6_.refs_0_, bf16[128,128]{1,0:T(8,128)(2,1)S(1)} %get-tuple-element.21.refs_6_.refs_1_, bf16[16,8,2,128,128]{4,3,2,1,0:T(8,128)(2,1)S(1)} %copy-done, bf16[128,128]{1,0:T(8,128)(2,1)S(1)} %get-tuple-element.27.refs_3_.refs_0_, ...), custom_call_target="tpu_custom_call" | custom-call | flops 33554432 | bytes 4194304 | tf_op jit(solution)/shard_map/near/pallas_call | solution.py:517
  32.7 0.0 collective-permute-done.2.refs_1_
  32.7 2.3 %collective-permute-done.3.refs_2_ = bf16[128,128]{1,0:T(8,128)(2,1)S(1)} collective-permute-done((bf16[128,128]{1,0:T(8,128)(2,1)S(1)}, bf16[128,128]{1,0:T(8,128)(2,1)S(1)}, u32[]{:S(2)}, u32[]{:S(2)}) %collective-permute-start.3) | collective-permute-done | bytes 32800 | tf_op jit(solution)/shard_map/ppermute | solution.py:443
  35.1 0.0 collective-permute-done.4.refs_3_
  35.1 0.0 copy-done.2
  35.1 1.0 %final.1 = f32[16,2,4,128]{3,2,1,0:T(4,128)} custom-call(bf16[128,128]{1,0:T(8,128)(2,1)S(1)} %get-tuple-element.27.refs_3_.refs_0_, bf16[128,128]{1,0:T(8,128)(2,1)S(1)} %collective-permute-done.2.refs_1_, bf16[128,128]{1,0:T(8,128)(2,1)S(1)} %collective-permute-done.3.refs_2_, bf16[128,128]{1,0:T(8,128)(2,1)S(1)} %collective-permute-done.4.refs_3_, ...), custom_call_target="tpu_custom_call" | custom-call | tf_op jit(solution)/shard_map/final/pallas_call | solution.py:566
  (3 shorter events, 0.1 us)
Async XLA Ops:
  0.0 19.4 %copy-start.3 = (f32[8,2,2048]{2,1,0:T(2,128)S(1)}, f32[8,2,2048]{2,1,0:T(2,128)}, u32[]{:S(2)}) copy-start(f32[8,2,2048]{2,1,0:T(2,128)} %refs_5_.5) | copy-start | bytes 393220
  0.0 19.4 %copy-start.1 = (bf16[2048,128]{1,0:T(8,128)(2,1)S(1)}, bf16[2048,128]{1,0:T(8,128)(2,1)}, u32[]{:S(2)}) copy-start(bf16[2048,128]{1,0:T(8,128)(2,1)} %refs_4_.7) | copy-start | bytes 1572868
  17.5 4.1 %copy-start = (bf16[16,8,2,128,128]{4,3,2,1,0:T(8,128)(2,1)S(1)}, bf16[16,8,2,128,128]{4,3,2,1,0:T(8,128)(2,1)}, u32[]{:S(2)}) copy-start(bf16[16,8,2,128,128]{4,3,2,1,0:T(8,128)(2,1)} %refs_2_.5) | copy-start | bytes 25165828
  19.9 5.6 %collective-permute-start = (bf16[80,512]{1,0:T(8,128)(2,1)S(1)}, bf16[80,512]{1,0:T(8,128)(2,1)S(1)}, u32[]{:S(2)}, u32[]{:S(2)}) collective-permute-start(bf16[80,512]{1,0:T(8,128)(2,1)S(1)} %get-tuple-element.24), channel_id=1, source_target_pairs={{0,28},{4,8},{8,4},{12,16},{16,12},{20,24},{24,20},{28,0},{1,29},{... | collective-permute-start | bytes 245768 | tf_op jit(solution)/shard_map/ppermute | solution.py:511
  20.0 5.5 %collective-permute-start.1 = (bf16[80,512]{1,0:T(8,128)(2,1)S(1)}, bf16[80,512]{1,0:T(8,128)(2,1)S(1)}, u32[]{:S(2)}, u32[]{:S(2)}) collective-permute-start(bf16[80,512]{1,0:T(8,128)(2,1)S(1)} %get-tuple-element.23.refs_0_), channel_id=1, source_target_pairs={{0,4},{4,0},{8,12},{12,8},{16,20},{20,16},{24,28},{28,24},{1,5},{5... | collective-permute-start | bytes 245768 | tf_op jit(solution)/shard_map/ppermute | solution.py:514
  21.6 13.5 %copy-start.2 = (bf16[16,2,128,128]{3,2,1,0:T(8,128)(2,1)S(1)}, bf16[16,2,128,128]{3,2,1,0:T(8,128)(2,1)}, u32[]{:S(2)}) copy-start(bf16[16,2,128,128]{3,2,1,0:T(8,128)(2,1)} %refs_6_.3) | copy-start | bytes 3145732
  26.3 6.4 %collective-permute-start.2 = (bf16[128,128]{1,0:T(8,128)(2,1)S(1)}, bf16[128,128]{1,0:T(8,128)(2,1)S(1)}, u32[]{:S(2)}, u32[]{:S(2)}) collective-permute-start(bf16[128,128]{1,0:T(8,128)(2,1)S(1)} %get-tuple-element.28), channel_id=1, source_target_pairs={{0,3},{1,2},{2,1},{3,0},{4,7},{5,6},{6,5},{7,4},{8,11},{9,10},{10,... | collective-permute-start | bytes 98312 | tf_op jit(solution)/shard_map/ppermute | solution.py:443
  30.3 4.8 %collective-permute-start.3 = (bf16[128,128]{1,0:T(8,128)(2,1)S(1)}, bf16[128,128]{1,0:T(8,128)(2,1)S(1)}, u32[]{:S(2)}, u32[]{:S(2)}) collective-permute-start(bf16[128,128]{1,0:T(8,128)(2,1)S(1)} %get-tuple-element.29), channel_id=1, source_target_pairs={{0,2},{1,3},{2,0},{3,1},{4,6},{5,7},{6,4},{7,5},{8,10},{9,11},{10,... | collective-permute-start | bytes 98312 | tf_op jit(solution)/shard_map/ppermute | solution.py:443
  30.3 4.8 %collective-permute-start.4 = (bf16[128,128]{1,0:T(8,128)(2,1)S(1)}, bf16[128,128]{1,0:T(8,128)(2,1)S(1)}, u32[]{:S(2)}, u32[]{:S(2)}) collective-permute-start(bf16[128,128]{1,0:T(8,128)(2,1)S(1)} %get-tuple-element.30), channel_id=1, source_target_pairs={{0,1},{1,0},{2,3},{3,2},{4,5},{5,4},{6,7},{7,6},{8,9},{9,8},{10,11... | collective-permute-start | bytes 98312 | tf_op jit(solution)/shard_map/ppermute | solution.py:443

commit v15 on v12

--- a/solution.py
+++ b/solution.py
@@ -17,6 +17,18 @@
 
 def nn_dot(a, b):
     return lax.dot_general(a, b, (((1,), (0,)), ((), ())), preferred_element_type=F32)
+
+
+def pair_dot(x0, x1, a0, a1):
+    both = nt_dot(
+        jnp.concatenate([x0, x1], axis=0).astype(BF16), jnp.concatenate([a0, a1], axis=0)
+    )
+    rows, cols = x0.shape[0], a0.shape[0]
+    return both[:rows, :cols], both[rows:, cols:]
+
+
+def abreast(a):
+    return jnp.concatenate([a[0], a[1]], axis=1)
 
 
 def times_i(v):
@@ -77,11 +89,12 @@
     to_far[at + CODE_ROWS :] = jnp.where(odd, last, first).astype(BF16)
     for ref in (plain, to_beside, to_far):
         ref[at : at + CODE_ROWS] = codes
-    for n in range(boxes):
+    for n in range(0, boxes, 2):
         if n % per == 0:
             big[n // per].wait()
-        mat = jnp.concatenate([lift[n, 0], lift[n, 1]], axis=1)
-        rows[pl.ds(n, parts, stride=boxes), :] = nt_dot(widen(own[n]).astype(BF16), mat)
+        y0, y1 = pair_dot(widen(own[n]), widen(own[n + 1]), abreast(lift[n]), abreast(lift[n + 1]))
+        rows[pl.ds(n, parts, stride=boxes), :] = y0
+        rows[pl.ds(n + 1, parts, stride=boxes), :] = y1
     pattern = rows[...].astype(BF16)
     for ref in (plain, to_beside, to_far):
         ref[:at] = pattern
@@ -332,10 +345,14 @@
     base = (box * nsamp + samp) * boxes
     for i in range(count):
         acc = None
-        for k in range(near_count):
-            j = lax.rem(nbr[k, first + i] - base + count + total, total)
-            mat = jnp.concatenate([mats[first + i, k, 0], mats[first + i, k, 1]], axis=1)
-            y = nt_dot(window[j].astype(BF16), mat)
+        for k in range(0, near_count, 2):
+            j0, j1 = (
+                lax.rem(nbr[k + e, first + i] - base + count + total, total) for e in range(2)
+            )
+            y0, y1 = pair_dot(
+                window[j0], window[j1], abreast(mats[first + i, k]), abreast(mats[first + i, k + 1])
+            )
+            y = y0 + y1
             acc = y if acc is None else acc + y
         out_ref[i] = acc
 
@@ -351,14 +368,14 @@
     for m in parts_in[1:]:
         total += m[...].astype(F32)
     field[...] = total.astype(BF16).astype(F32)
-    for n in range(boxes):
-        v = field[pl.ds(n, parts, stride=boxes), :]
-        wide = jnp.concatenate([v, times_i(v)], axis=1).astype(BF16)
-        y = nt_dot(wide, jnp.concatenate([mats[n, 0], mats[n, 1]], axis=1))
-        i = n % half
-        y = y + jnp.where(odd == (n < half), near_early[i], near_late[i])
-        out_ref[n, 0] = y[:rhs]
-        out_ref[n, 1] = y[rhs:]
+    for n in range(0, boxes, 2):
+        wide = [field[pl.ds(n + e, parts, stride=boxes), :] for e in range(2)]
+        wide = [widen(v) for v in wide]
+        for e, y in enumerate(pair_dot(*wide, abreast(mats[n]), abreast(mats[n + 1]))):
+            i = (n + e) % half
+            y = y + jnp.where(odd == (n < half), near_early[i], near_late[i])
+            out_ref[n + e, 0] = y[:rhs]
+            out_ref[n + e, 1] = y[rhs:]
 
 
 def whole_in(kind):

time: 26.9 us -> 26.9 us (level)
  no operation moved by 1% of the time
where the time goes in v15:
time: 26.9 us; the launch traced here: 26.8 us
  starting transfers between devices  12.8 us (48%)
  Pallas kernels  9.4 us (35%)
  waiting for transfers between devices  4.45 us (17%)
    ppermute x6, starting transfers between devices, exchange(): return lax.ppermute(x, 'samp', [(i, i ^ d) for i in range(nsamp)])  10.2 us
    ppermute x6, waiting for transfers between devices, exchange(): return lax.ppermute(x, 'samp', [(i, i ^ d) for i in range(nsamp)])  3.76 us
    pallas_call x2, Pallas kernels, near_half(): pl.pallas_call(lambda *refs: near_kernel(*refs, late=late, nsamp=nsamp, t...  3.64 us
    ppermute x1, starting transfers between devices, on_device(): lax.ppermute(to_across, 'box', [(i, (i + (1 if i % 2 else -1)) % nbox) fo...  2.55 us
    pallas_call x1, Pallas kernels, on_device(): pl.pallas_call(lambda *refs: leaf_kernel(*refs, parents=parents, all_pare...  1.8 us
    pallas_call x1, Pallas kernels, on_device(): pl.pallas_call(lambda *refs: prep_kernel(*refs, parents=parents, all_pare...  1.61 us
    pallas_call x1, Pallas kernels, on_device(): pl.pallas_call(lambda *refs: final_kernel(*refs, pieces=nsamp), in_specs=...  1.02 us
    pallas_call x1, Pallas kernels, on_device(): pl.pallas_call(lambda *refs: down_kernel(*refs, pieces=nsamp, boxes=boxes...  0.81 us
  transfers between devices with their start and end apart: 8, of which 4 were waited for; matrix products, arithmetic and copies ran while one was open for 0% of the time, Pallas kernels for 20%

profile of v15, /device:TPU:0, one launch (start us, length us, event | category | flops | bytes accessed | tf_op | source)
XLA Modules:
  0.0 26.8 jit_solution(2300435949123433635)
XLA Ops:
  0.0 0.0 copy-start
  0.0 0.0 copy-start.1
  0.0 0.0 copy-start.3
  0.0 1.8 %leaf.1 = (bf16[200,128]{1,0:T(8,128)(2,1)S(1)}, bf16[136,128]{1,0:T(8,128)(2,1)S(1)}, bf16[200,128]{1,0:T(8,128)(2,1)S(1)}, bf16[128,128]{1,0:T(8,128)(2,1)S(1)}, f32[8,14,2,512]{3,2,1,0:T(2,128)S(1)}) custom-call(s32[16]{0:T(128)} %refs_0_.2, s32[16]{0:T(128)} %refs_1_.2, bf16[16,2,4,128]{3,2,1,0:T(4,128)(2,1)} %refs_2_.3, ...), custom_call_target="tpu_custom_call" | custom-call | tf_op jit(solution)/shard_map/leaf/pallas_call | solution.py:430
  1.8 5.1 %collective-permute-start = (bf16[200,128]{1,0:T(8,128)(2,1)S(1)}, bf16[200,128]{1,0:T(8,128)(2,1)S(1)}, u32[]{:S(2)}, u32[]{:S(2)}) collective-permute-start(bf16[200,128]{1,0:T(8,128)(2,1)S(1)} %get-tuple-element.20), channel_id=1, source_target_pairs={{0,3},{1,2},{2,1},{3,0},{4,7},{5,6},{6,5},{7,4},{8,11},{9,10},{10,... | collective-permute-start | bytes 153608 | tf_op jit(solution)/shard_map/ppermute | solution.py:461
  6.9 0.0 collective-permute-start.1
  6.9 0.6 %collective-permute-start.2 = (bf16[136,128]{1,0:T(8,128)(2,1)S(1)}, bf16[136,128]{1,0:T(8,128)(2,1)S(1)}, u32[]{:S(2)}, u32[]{:S(2)}) collective-permute-start(bf16[136,128]{1,0:T(8,128)(2,1)S(1)} %get-tuple-element.19.refs_0_), channel_id=1, source_target_pairs={{0,2},{1,3},{2,0},{3,1},{4,6},{5,7},{6,4},{7,5},{8,10},{9,11},{10,... | collective-permute-start | bytes 104456 | tf_op jit(solution)/shard_map/ppermute | solution.py:461
  7.6 1.6 %prep.1 = (f32[8,14,2,512]{3,2,1,0:T(2,128)S(1)}, s32[8,16]{1,0:T(8,128)S(1)}) custom-call(s32[8,14]{1,0:T(8,128)} %refs_0_.3, s32[8,14]{1,0:T(8,128)} %refs_1_.3, s32[8,16]{1,0:T(8,128)} %bitcast.1, f32[64,2,512]{2,1,0:T(2,128)} %refs_3_.3, bf16[16,8,2,128,128]{4,3,2,1,0:T(8,128)(2,1)} %refs_2_.5, ...), custom_call_target="tpu_custom_call", output_to_operand_aliasing={{0}: (5, {})} | custom-call | bytes 8388608 | tf_op jit(solution)/shard_map/prep/pallas_call | solution.py:470
  9.2 2.6 %collective-permute-done.2.refs_3_ = bf16[136,128]{1,0:T(8,128)(2,1)S(1)} collective-permute-done((bf16[136,128]{1,0:T(8,128)(2,1)S(1)}, bf16[136,128]{1,0:T(8,128)(2,1)S(1)}, u32[]{:S(2)}, u32[]{:S(2)}) %collective-permute-start.2) | collective-permute-done | bytes 34848 | tf_op jit(solution)/shard_map/ppermute | solution.py:461
  11.8 0.0 collective-permute-done.refs_1_.refs_6_
  11.8 0.0 collective-permute-done.1.refs_2_.refs_4_
  11.8 0.0 copy-done.1
  11.8 0.0 copy-done.3
  11.8 0.5 %up.1 = (bf16[80,512]{1,0:T(8,128)(2,1)S(1)}, bf16[80,512]{1,0:T(8,128)(2,1)S(1)}, bf16[64,64]{1,0:T(8,128)(2,1)S(1)}) custom-call(bf16[136,128]{1,0:T(8,128)(2,1)S(1)} %get-tuple-element.19.refs_0_, bf16[200,128]{1,0:T(8,128)(2,1)S(1)} %collective-permute-done.refs_1_.refs_6_, bf16[200,128]{1,0:T(8,128)(2,1)S(1)} %collective-permute-done.1.refs_2_.refs_4_, ...), custom_call_target="tpu_custom_call" | custom-call | tf_op jit(solution)/shard_map/up/pallas_call | solution.py:500
  12.3 0.1 collective-permute-start.4
  12.4 2.6 %collective-permute-start.3 = (bf16[80,512]{1,0:T(8,128)(2,1)S(1)}, bf16[80,512]{1,0:T(8,128)(2,1)S(1)}, u32[]{:S(2)}, u32[]{:S(2)}) collective-permute-start(bf16[80,512]{1,0:T(8,128)(2,1)S(1)} %get-tuple-element.26), channel_id=1, source_target_pairs={{0,28},{4,8},{8,4},{12,16},{16,12},{20,24},{24,20},{28,0},{1,29},{... | collective-permute-start | bytes 245768 | tf_op jit(solution)/shard_map/ppermute | solution.py:519
  15.0 0.0 copy-done
  15.0 0.0 copy-start.2
  15.0 1.8 %near.2.refs_7_.refs_4_ = f32[8,8,128]{2,1,0:T(8,128)S(1)} custom-call(s32[8,16]{1,0:T(8,128)S(1)} %get-tuple-element.24.refs_6_.refs_0_, bf16[128,128]{1,0:T(8,128)(2,1)S(1)} %get-tuple-element.23.refs_6_.refs_1_, bf16[16,8,2,128,128]{4,3,2,1,0:T(8,128)(2,1)S(1)} %copy-done, bf16[64,64]{1,0:T(8,128)(2,1)S(1)} %get-tuple-element.28.refs_3_.refs_6_, ...), custom_call_target="tpu_custom_call" | custom-call | flops 33554432 | bytes 4194304 | tf_op jit(solution)/shard_map/near/pallas_call | solution.py:525
  16.8 0.0 collective-permute-done.4.refs_2_.refs_5_
  16.8 0.7 %collective-permute-done.3.refs_1_.refs_4_ = bf16[80,512]{1,0:T(8,128)(2,1)S(1)} collective-permute-done((bf16[80,512]{1,0:T(8,128)(2,1)S(1)}, bf16[80,512]{1,0:T(8,128)(2,1)S(1)}, u32[]{:S(2)}, u32[]{:S(2)}) %collective-permute-start.3) | collective-permute-done | bytes 81952 | tf_op jit(solution)/shard_map/ppermute | solution.py:519
  17.5 0.8 %down.1 = (bf16[128,128]{1,0:T(8,128)(2,1)S(1)}, bf16[128,128]{1,0:T(8,128)(2,1)S(1)}, bf16[128,128]{1,0:T(8,128)(2,1)S(1)}, bf16[128,128]{1,0:T(8,128)(2,1)S(1)}) custom-call(bf16[80,512]{1,0:T(8,128)(2,1)S(1)} %get-tuple-element.25.refs_0_, bf16[80,512]{1,0:T(8,128)(2,1)S(1)} %collective-permute-done.3.refs_1_.refs_4_, ...), custom_call_target="tpu_custom_call" | custom-call | tf_op jit(solution)/shard_map/down/pallas_call | solution.py:553
  18.3 2.0 %collective-permute-start.5 = (bf16[128,128]{1,0:T(8,128)(2,1)S(1)}, bf16[128,128]{1,0:T(8,128)(2,1)S(1)}, u32[]{:S(2)}, u32[]{:S(2)}) collective-permute-start(bf16[128,128]{1,0:T(8,128)(2,1)S(1)} %get-tuple-element.30), channel_id=1, source_target_pairs={{0,3},{1,2},{2,1},{3,0},{4,7},{5,6},{6,5},{7,4},{8,11},{9,10},{10,... | collective-permute-start | bytes 98312 | tf_op jit(solution)/shard_map/ppermute | solution.py:461
  20.3 1.5 %collective-permute-start.6 = (bf16[128,128]{1,0:T(8,128)(2,1)S(1)}, bf16[128,128]{1,0:T(8,128)(2,1)S(1)}, u32[]{:S(2)}, u32[]{:S(2)}) collective-permute-start(bf16[128,128]{1,0:T(8,128)(2,1)S(1)} %get-tuple-element.31), channel_id=1, source_target_pairs={{0,2},{1,3},{2,0},{3,1},{4,6},{5,7},{6,4},{7,5},{8,10},{9,11},{10,... | collective-permute-start | bytes 98312 | tf_op jit(solution)/shard_map/ppermute | solution.py:461
  21.9 0.9 %collective-permute-start.7 = (bf16[128,128]{1,0:T(8,128)(2,1)S(1)}, bf16[128,128]{1,0:T(8,128)(2,1)S(1)}, u32[]{:S(2)}, u32[]{:S(2)}) collective-permute-start(bf16[128,128]{1,0:T(8,128)(2,1)S(1)} %get-tuple-element.32), channel_id=1, source_target_pairs={{0,1},{1,0},{2,3},{3,2},{4,5},{5,4},{6,7},{7,6},{8,9},{9,8},{10,11... | collective-permute-start | bytes 98312 | tf_op jit(solution)/shard_map/ppermute | solution.py:461
  22.8 1.8 %near.3.refs_5_ = f32[8,8,128]{2,1,0:T(8,128)S(1)} custom-call(s32[8,16]{1,0:T(8,128)S(1)} %get-tuple-element.24.refs_6_.refs_0_, bf16[128,128]{1,0:T(8,128)(2,1)S(1)} %get-tuple-element.23.refs_6_.refs_1_, bf16[16,8,2,128,128]{4,3,2,1,0:T(8,128)(2,1)S(1)} %copy-done, bf16[128,128]{1,0:T(8,128)(2,1)S(1)} %get-tuple-element.29.refs_3_.refs_0_, ...), custom_call_target="tpu_custom_call" | custom-call | flops 33554432 | bytes 4194304 | tf_op jit(solution)/shard_map/near/pallas_call | solution.py:525
  24.6 0.0 collective-permute-done.5.refs_1_
  24.6 0.8 %collective-permute-done.6.refs_2_ = bf16[128,128]{1,0:T(8,128)(2,1)S(1)} collective-permute-done((bf16[128,128]{1,0:T(8,128)(2,1)S(1)}, bf16[128,128]{1,0:T(8,128)(2,1)S(1)}, u32[]{:S(2)}, u32[]{:S(2)}) %collective-permute-start.6) | collective-permute-done | bytes 32800 | tf_op jit(solution)/shard_map/ppermute | solution.py:461
  25.4 0.4 %collective-permute-done.7.refs_3_ = bf16[128,128]{1,0:T(8,128)(2,1)S(1)} collective-permute-done((bf16[128,128]{1,0:T(8,128)(2,1)S(1)}, bf16[128,128]{1,0:T(8,128)(2,1)S(1)}, u32[]{:S(2)}, u32[]{:S(2)}) %collective-permute-start.7) | collective-permute-done | bytes 32800 | tf_op jit(solution)/shard_map/ppermute | solution.py:461
  25.8 0.0 copy-done.2
  25.8 1.0 %final.1 = f32[16,2,4,128]{3,2,1,0:T(4,128)} custom-call(bf16[128,128]{1,0:T(8,128)(2,1)S(1)} %get-tuple-element.29.refs_3_.refs_0_, bf16[128,128]{1,0:T(8,128)(2,1)S(1)} %collective-permute-done.5.refs_1_, bf16[128,128]{1,0:T(8,128)(2,1)S(1)} %collective-permute-done.6.refs_2_, bf16[128,128]{1,0:T(8,128)(2,1)S(1)} %collective-permute-done.7.refs_3_, ...), custom_call_target="tpu_custom_call" | custom-call | tf_op jit(solution)/shard_map/final/pallas_call | solution.py:574
Async XLA Ops:
  0.0 15.0 %copy-start = (bf16[16,8,2,128,128]{4,3,2,1,0:T(8,128)(2,1)S(1)}, bf16[16,8,2,128,128]{4,3,2,1,0:T(8,128)(2,1)}, u32[]{:S(2)}) copy-start(bf16[16,8,2,128,128]{4,3,2,1,0:T(8,128)(2,1)} %refs_2_.5) | copy-start | bytes 25165828
  0.0 11.8 %copy-start.1 = (bf16[2048,128]{1,0:T(8,128)(2,1)S(1)}, bf16[2048,128]{1,0:T(8,128)(2,1)}, u32[]{:S(2)}) copy-start(bf16[2048,128]{1,0:T(8,128)(2,1)} %refs_4_.7) | copy-start | bytes 1572868
  0.0 11.8 %copy-start.3 = (f32[8,2,2048]{2,1,0:T(2,128)S(1)}, f32[8,2,2048]{2,1,0:T(2,128)}, u32[]{:S(2)}) copy-start(f32[8,2,2048]{2,1,0:T(2,128)} %refs_5_.5) | copy-start | bytes 393220
  1.8 10.0 %collective-permute-start = (bf16[200,128]{1,0:T(8,128)(2,1)S(1)}, bf16[200,128]{1,0:T(8,128)(2,1)S(1)}, u32[]{:S(2)}, u32[]{:S(2)}) collective-permute-start(bf16[200,128]{1,0:T(8,128)(2,1)S(1)} %get-tuple-element.20), channel_id=1, source_target_pairs={{0,3},{1,2},{2,1},{3,0},{4,7},{5,6},{6,5},{7,4},{8,11},{9,10},{10,... | collective-permute-start | bytes 153608 | tf_op jit(solution)/shard_map/ppermute | solution.py:461
  6.9 4.9 %collective-permute-start.1 = (bf16[200,128]{1,0:T(8,128)(2,1)S(1)}, bf16[200,128]{1,0:T(8,128)(2,1)S(1)}, u32[]{:S(2)}, u32[]{:S(2)}) collective-permute-start(bf16[200,128]{1,0:T(8,128)(2,1)S(1)} %get-tuple-element.21), channel_id=1, source_target_pairs={{0,1},{1,0},{2,3},{3,2},{4,5},{5,4},{6,7},{7,6},{8,9},{9,8},{10,11... | collective-permute-start | bytes 153608 | tf_op jit(solution)/shard_map/ppermute | solution.py:461
  6.9 4.9 %collective-permute-start.2 = (bf16[136,128]{1,0:T(8,128)(2,1)S(1)}, bf16[136,128]{1,0:T(8,128)(2,1)S(1)}, u32[]{:S(2)}, u32[]{:S(2)}) collective-permute-start(bf16[136,128]{1,0:T(8,128)(2,1)S(1)} %get-tuple-element.19.refs_0_), channel_id=1, source_target_pairs={{0,2},{1,3},{2,0},{3,1},{4,6},{5,7},{6,4},{7,5},{8,10},{9,11},{10,... | collective-permute-start | bytes 104456 | tf_op jit(solution)/shard_map/ppermute | solution.py:461
  12.3 4.5 %collective-permute-start.4 = (bf16[80,512]{1,0:T(8,128)(2,1)S(1)}, bf16[80,512]{1,0:T(8,128)(2,1)S(1)}, u32[]{:S(2)}, u32[]{:S(2)}) collective-permute-start(bf16[80,512]{1,0:T(8,128)(2,1)S(1)} %get-tuple-element.25.refs_0_), channel_id=1, source_target_pairs={{0,4},{4,0},{8,12},{12,8},{16,20},{20,16},{24,28},{28,24},{1,5},{5... | collective-permute-start | bytes 245768 | tf_op jit(solution)/shard_map/ppermute | solution.py:522
  12.4 5.1 %collective-permute-start.3 = (bf16[80,512]{1,0:T(8,128)(2,1)S(1)}, bf16[80,512]{1,0:T(8,128)(2,1)S(1)}, u32[]{:S(2)}, u32[]{:S(2)}) collective-permute-start(bf16[80,512]{1,0:T(8,128)(2,1)S(1)} %get-tuple-element.26), channel_id=1, source_target_pairs={{0,28},{4,8},{8,4},{12,16},{16,12},{20,24},{24,20},{28,0},{1,29},{... | collective-permute-start | bytes 245768 | tf_op jit(solution)/shard_map/ppermute | solution.py:519
  15.0 10.8 %copy-start.2 = (bf16[16,2,128,128]{3,2,1,0:T(8,128)(2,1)S(1)}, bf16[16,2,128,128]{3,2,1,0:T(8,128)(2,1)}, u32[]{:S(2)}) copy-start(bf16[16,2,128,128]{3,2,1,0:T(8,128)(2,1)} %refs_6_.3) | copy-start | bytes 3145732
  18.3 6.3 %collective-permute-start.5 = (bf16[128,128]{1,0:T(8,128)(2,1)S(1)}, bf16[128,128]{1,0:T(8,128)(2,1)S(1)}, u32[]{:S(2)}, u32[]{:S(2)}) collective-permute-start(bf16[128,128]{1,0:T(8,128)(2,1)S(1)} %get-tuple-element.30), channel_id=1, source_target_pairs={{0,3},{1,2},{2,1},{3,0},{4,7},{5,6},{6,5},{7,4},{8,11},{9,10},{10,... | collective-permute-start | bytes 98312 | tf_op jit(solution)/shard_map/ppermute | solution.py:461
  20.3 5.1 %collective-permute-start.6 = (bf16[128,128]{1,0:T(8,128)(2,1)S(1)}, bf16[128,128]{1,0:T(8,128)(2,1)S(1)}, u32[]{:S(2)}, u32[]{:S(2)}) collective-permute-start(bf16[128,128]{1,0:T(8,128)(2,1)S(1)} %get-tuple-element.31), channel_id=1, source_target_pairs={{0,2},{1,3},{2,0},{3,1},{4,6},{5,7},{6,4},{7,5},{8,10},{9,11},{10,... | collective-permute-start | bytes 98312 | tf_op jit(solution)/shard_map/ppermute | solution.py:461
  21.9 3.9 %collective-permute-start.7 = (bf16[128,128]{1,0:T(8,128)(2,1)S(1)}, bf16[128,128]{1,0:T(8,128)(2,1)S(1)}, u32[]{:S(2)}, u32[]{:S(2)}) collective-permute-start(bf16[128,128]{1,0:T(8,128)(2,1)S(1)} %get-tuple-element.32), channel_id=1, source_target_pairs={{0,1},{1,0},{2,3},{3,2},{4,5},{5,4},{6,7},{7,6},{8,9},{9,8},{10,11... | collective-permute-start | bytes 98312 | tf_op jit(solution)/shard_map/ppermute | solution.py:461

commit v16 on v15

--- a/solution.py
+++ b/solution.py
@@ -225,10 +225,13 @@
 
 
 def down_kernel(
-    own, across, beside, dense, interp_ref, phase_ref, place_ref, after, *refs, pieces, boxes, parents, parts
+    own, across, beside, dense, interp_ref, phase_ref, place_ref, after,
+    neighbours, x_rows, mats, *refs, pieces, boxes, parents, parts, sizes
 ):
+    far = len(refs) - pieces - 7
+    from_far, refs = refs[:far], refs[far:]
     outs = refs[:pieces]
-    window, incoming, shifted = refs[pieces:]
+    near_out, window, incoming, shifted, near_window, nbr, sems = refs[pieces:]
     samples = window.shape[2]
     first = lax.axis_index("samp") * samples
     mine = interp_ref[pl.ds(pl.multiple_of(first, samples), samples)]
@@ -295,9 +298,13 @@
                 d * boxes : (d + 1) * boxes, c * LANES : (c + 1) * LANES
             ]
 
-
-def near_kernel(*refs, late, nsamp, total, halo_rows, parent_rows):
-    neighbours, own, mats, after, *halos, out_ref, window, nbr, sems = refs
+    @pl.when(odd_box())
+    def _():
+        halos = (across, beside, *from_far)
+        near_half_of(True, neighbours, x_rows, mats, halos, near_out, near_window, nbr, sems, **sizes)
+
+
+def near_half_of(late, neighbours, own, mats, halos, out_ref, window, nbr, sems, nsamp, total, halo_rows, parent_rows):
     if late:
         across, beside, *from_far = halos
     else:
@@ -357,6 +364,18 @@
         out_ref[i] = acc
 
 
+def near_kernel(*refs, late, **sizes):
+    if not late:
+        neighbours, own, mats, after, *halos, out_ref, window, nbr, sems = refs
+        near_half_of(late, neighbours, own, mats, halos, out_ref, window, nbr, sems, **sizes)
+        return
+    neighbours, own, mats, done_in, *halos, out_ref, window, nbr, sems = refs
+
+    @pl.when(jnp.logical_not(odd_box()))
+    def _():
+        near_half_of(late, neighbours, own, mats, halos, out_ref, window, nbr, sems, **sizes)
+
+
 def final_kernel(*refs, pieces):
     parts_in = refs[:pieces]
     near_early, near_late, mats, out_ref, field = refs[pieces:]
@@ -521,24 +540,21 @@
     )
     beside = lax.ppermute(parent_pat, "box", [(i, i ^ 1) for i in range(nbox)])
 
+    sizes = dict(nsamp=nsamp, total=total, halo_rows=halo_rows, parent_rows=parent_rows)
+    near_scratch = [
+        VM((boxes + 2 * reach, parts, 2 * unknowns), F32),
+        SM((near_count, boxes), jnp.int32),
+        DMA((1,)),
+    ]
+
     def near_half(late, args):
         return pl.pallas_call(
-            lambda *refs: near_kernel(
-                *refs,
-                late=late,
-                nsamp=nsamp,
-                total=total,
-                halo_rows=halo_rows,
-                parent_rows=parent_rows,
-            ),
+            lambda *refs: near_kernel(*refs, late=late, **sizes),
             in_specs=[whole_in(VM)] * (3 + len(args)),
             out_specs=whole_in(VM),
             out_shape=shape((reach, parts, unknowns), F32),
-            scratch_shapes=[
-                VM((boxes + 2 * reach, parts, 2 * unknowns), F32),
-                SM((near_count, boxes), jnp.int32),
-                DMA((1,)),
-            ],
+            input_output_aliases={3: 0} if late else {},
+            scratch_shapes=near_scratch,
             compiler_params=PARAMS,
             cost_estimate=pl.CostEstimate(
                 flops=parts * near_blocks.size,
@@ -550,26 +566,41 @@
 
     near_early = near_half(False, [place_onehot, messages[1]])
 
-    fields = pl.pallas_call(
+    *fields, near_done = pl.pallas_call(
         lambda *refs: down_kernel(
-            *refs, pieces=nsamp, boxes=boxes, parents=parents, parts=parts
+            *refs, pieces=nsamp, boxes=boxes, parents=parents, parts=parts, sizes=sizes
         ),
-        in_specs=[whole_in(VM)] * 8,
-        out_specs=[whole_in(VM)] * nsamp,
-        out_shape=[shape((parts * boxes, LANES))] * nsamp,
+        in_specs=[whole_in(VM)] * (11 + len(far_messages)),
+        out_specs=[whole_in(VM)] * (nsamp + 1),
+        out_shape=[shape((parts * boxes, LANES))] * nsamp
+        + [shape((reach, parts, unknowns), F32)],
         scratch_shapes=[
             VM((3 * parents, parts, samples), F32),
             VM((samples // LANES, parent_rows, LANES), F32),
             VM((parts * slots, samples), BF16),
+            *near_scratch,
         ],
         compiler_params=PARAMS,
         name="down",
-    )(parent_pat, across, beside, dense, interp, phases, place_onehot, near_early)
+    )(
+        parent_pat,
+        across,
+        beside,
+        dense,
+        interp,
+        phases,
+        place_onehot,
+        near_early,
+        near_list,
+        x_rows,
+        near_blocks,
+        *far_messages,
+    )
 
     pieces = dict(zip(order, fields))
     partial = [pieces[0]] + [exchange(pieces[d], d) for d in reversed(range(1, nsamp))]
 
-    near_late = near_half(True, [fields[0], across, beside, *far_messages])
+    near_late = near_half(True, [near_done, across, beside, *far_messages])
 
     return pl.pallas_call(
         lambda *refs: final_kernel(*refs, pieces=nsamp),

time: 26.9 us -> 27.7 us (1.030)
  waiting for transfers between devices: 4.45 us -> 5.2 us
    ppermute x6, waiting for transfers between devices: 3.76 us -> 4.49 us  [exchange(): return lax.ppermute(x, 'samp', [(i, i ^ d) for i in range(nsamp)])]
  transfers between devices with their start and end apart: 8 -> 8, of which waited for: 4 -> 4; matrix products, arithmetic and copies ran while one was open for 0% -> 0% of each run, Pallas kernels for 20% -> 19%
where the time goes in v16:
time: 27.7 us; the launch traced here: 27.6 us
  starting transfers between devices  12.8 us (46%)
  Pallas kernels  9.46 us (34%)
  waiting for transfers between devices  5.2 us (19%)
    ppermute x6, starting transfers between devices, exchange(): return lax.ppermute(x, 'samp', [(i, i ^ d) for i in range(nsamp)])  10.2 us
    ppermute x6, waiting for transfers between devices, exchange(): return lax.ppermute(x, 'samp', [(i, i ^ d) for i in range(nsamp)])  4.49 us
    pallas_call x2, Pallas kernels, near_half(): pl.pallas_call(lambda *refs: near_kernel(*refs, late=late, **sizes), in_s...  3.64 us
    ppermute x1, starting transfers between devices, on_device(): lax.ppermute(to_across, 'box', [(i, (i + (1 if i % 2 else -1)) % nbox) fo...  2.55 us
    pallas_call x1, Pallas kernels, on_device(): pl.pallas_call(lambda *refs: leaf_kernel(*refs, parents=parents, all_pare...  1.8 us
    pallas_call x1, Pallas kernels, on_device(): pl.pallas_call(lambda *refs: prep_kernel(*refs, parents=parents, all_pare...  1.61 us
    pallas_call x1, Pallas kernels, on_device(): pl.pallas_call(lambda *refs: final_kernel(*refs, pieces=nsamp), in_specs=...  1.03 us
    pallas_call x1, Pallas kernels, on_device(): pl.pallas_call(lambda *refs: down_kernel(*refs, pieces=nsamp, boxes=boxes...  0.85 us
  transfers between devices with their start and end apart: 8, of which 4 were waited for; matrix products, arithmetic and copies ran while one was open for 0% of the time, Pallas kernels for 19%

profile of v16, /device:TPU:0, one launch (start us, length us, event | category | flops | bytes accessed | tf_op | source)
XLA Modules:
  0.0 27.6 jit_solution(4998955271386341876)
XLA Ops:
  0.0 0.0 copy-start
  0.0 0.0 copy-start.1
  0.0 0.0 copy-start.3
  0.0 1.8 %leaf.1 = (bf16[200,128]{1,0:T(8,128)(2,1)S(1)}, bf16[136,128]{1,0:T(8,128)(2,1)S(1)}, bf16[200,128]{1,0:T(8,128)(2,1)S(1)}, bf16[128,128]{1,0:T(8,128)(2,1)S(1)}, f32[8,14,2,512]{3,2,1,0:T(2,128)S(1)}) custom-call(s32[16]{0:T(128)} %refs_0_.2, s32[16]{0:T(128)} %refs_1_.2, bf16[16,2,4,128]{3,2,1,0:T(4,128)(2,1)} %refs_2_.3, ...), custom_call_target="tpu_custom_call" | custom-call | tf_op jit(solution)/shard_map/leaf/pallas_call | solution.py:449
  1.8 5.1 %collective-permute-start = (bf16[200,128]{1,0:T(8,128)(2,1)S(1)}, bf16[200,128]{1,0:T(8,128)(2,1)S(1)}, u32[]{:S(2)}, u32[]{:S(2)}) collective-permute-start(bf16[200,128]{1,0:T(8,128)(2,1)S(1)} %get-tuple-element.21), channel_id=1, source_target_pairs={{0,3},{1,2},{2,1},{3,0},{4,7},{5,6},{6,5},{7,4},{8,11},{9,10},{10,... | collective-permute-start | bytes 153608 | tf_op jit(solution)/shard_map/ppermute | solution.py:480
  6.9 0.0 collective-permute-start.1
  6.9 0.6 %collective-permute-start.2 = (bf16[136,128]{1,0:T(8,128)(2,1)S(1)}, bf16[136,128]{1,0:T(8,128)(2,1)S(1)}, u32[]{:S(2)}, u32[]{:S(2)}) collective-permute-start(bf16[136,128]{1,0:T(8,128)(2,1)S(1)} %get-tuple-element.20.refs_0_), channel_id=1, source_target_pairs={{0,2},{1,3},{2,0},{3,1},{4,6},{5,7},{6,4},{7,5},{8,10},{9,11},{10,... | collective-permute-start | bytes 104456 | tf_op jit(solution)/shard_map/ppermute | solution.py:480
  7.6 1.6 %prep.1 = (f32[8,14,2,512]{3,2,1,0:T(2,128)S(1)}, s32[8,16]{1,0:T(8,128)S(1)}) custom-call(s32[8,14]{1,0:T(8,128)} %refs_0_.3, s32[8,14]{1,0:T(8,128)} %refs_1_.3, s32[8,16]{1,0:T(8,128)} %bitcast.1, f32[64,2,512]{2,1,0:T(2,128)} %refs_3_.3, bf16[16,8,2,128,128]{4,3,2,1,0:T(8,128)(2,1)} %refs_2_.5, ...), custom_call_target="tpu_custom_call", output_to_operand_aliasing={{0}: (5, {})} | custom-call | bytes 8388608 | tf_op jit(solution)/shard_map/prep/pallas_call | solution.py:489
  9.2 2.6 %collective-permute-done.2.refs_3_ = bf16[136,128]{1,0:T(8,128)(2,1)S(1)} collective-permute-done((bf16[136,128]{1,0:T(8,128)(2,1)S(1)}, bf16[136,128]{1,0:T(8,128)(2,1)S(1)}, u32[]{:S(2)}, u32[]{:S(2)}) %collective-permute-start.2) | collective-permute-done | bytes 34848 | tf_op jit(solution)/shard_map/ppermute | solution.py:480
  11.8 0.0 collective-permute-done.refs_1_.refs_11_.refs_6_
  11.8 0.0 collective-permute-done.1.refs_2_.refs_4_
  11.8 0.0 copy-done.1
  11.8 0.0 copy-done.3
  11.8 0.5 %up.1 = (bf16[80,512]{1,0:T(8,128)(2,1)S(1)}, bf16[80,512]{1,0:T(8,128)(2,1)S(1)}, bf16[64,64]{1,0:T(8,128)(2,1)S(1)}) custom-call(bf16[136,128]{1,0:T(8,128)(2,1)S(1)} %get-tuple-element.20.refs_0_, bf16[200,128]{1,0:T(8,128)(2,1)S(1)} %collective-permute-done.refs_1_.refs_11_.refs_6_, bf16[200,128]{1,0:T(8,128)(2,1)S(1)} %collective-permute-done.1.refs_2_.refs_4_, ...), custom_call_target="tpu_custom_call" | custom-call | tf_op jit(solution)/shard_map/up/pallas_call | solution.py:519
  12.4 0.1 collective-permute-start.4
  12.4 2.5 %collective-permute-start.3 = (bf16[80,512]{1,0:T(8,128)(2,1)S(1)}, bf16[80,512]{1,0:T(8,128)(2,1)S(1)}, u32[]{:S(2)}, u32[]{:S(2)}) collective-permute-start(bf16[80,512]{1,0:T(8,128)(2,1)S(1)} %get-tuple-element.27), channel_id=1, source_target_pairs={{0,28},{4,8},{8,4},{12,16},{16,12},{20,24},{24,20},{28,0},{1,29},{... | collective-permute-start | bytes 245768 | tf_op jit(solution)/shard_map/ppermute | solution.py:538
  15.0 0.0 copy-done
  15.0 1.8 %near.2.refs_7_.refs_4_ = f32[8,8,128]{2,1,0:T(8,128)S(1)} custom-call(s32[8,16]{1,0:T(8,128)S(1)} %get-tuple-element.25.refs_6_.refs_0_.refs_8_, bf16[128,128]{1,0:T(8,128)(2,1)S(1)} %get-tuple-element.24.refs_6_.refs_1_.refs_9_, bf16[16,8,2,128,128]{4,3,2,1,0:T(8,128)(2,1)S(1)} %copy-done, bf16[64,64]{1,0:T(8,128)(2,1)S(1)} %get-tuple-element.29.refs_3_.refs_6_, ...), custom_call_target="tpu_custom_call" | custom-call | flops 33554432 | bytes 4194304 | tf_op jit(solution)/shard_map/near/pallas_call | solution.py:551
  16.8 0.0 collective-permute-done.4.refs_2_.refs_5_
  16.8 0.7 %collective-permute-done.3.refs_1_.refs_4_ = bf16[80,512]{1,0:T(8,128)(2,1)S(1)} collective-permute-done((bf16[80,512]{1,0:T(8,128)(2,1)S(1)}, bf16[80,512]{1,0:T(8,128)(2,1)S(1)}, u32[]{:S(2)}, u32[]{:S(2)}) %collective-permute-start.3) | collective-permute-done | bytes 81952 | tf_op jit(solution)/shard_map/ppermute | solution.py:538
  17.5 0.0 copy-start.2
  17.5 0.8 %down.1 = (bf16[128,128]{1,0:T(8,128)(2,1)S(1)}, bf16[128,128]{1,0:T(8,128)(2,1)S(1)}, bf16[128,128]{1,0:T(8,128)(2,1)S(1)}, bf16[128,128]{1,0:T(8,128)(2,1)S(1)}, f32[8,8,128]{2,1,0:T(8,128)S(1)}) custom-call(bf16[80,512]{1,0:T(8,128)(2,1)S(1)} %get-tuple-element.26.refs_0_, bf16[80,512]{1,0:T(8,128)(2,1)S(1)} %collective-permute-done.3.refs_1_.refs_4_, ...), custom_call_target="tpu_custom_call" | custom-call | tf_op jit(solution)/shard_map/down/pallas_call | solution.py:569
  18.4 2.0 %collective-permute-start.5 = (bf16[128,128]{1,0:T(8,128)(2,1)S(1)}, bf16[128,128]{1,0:T(8,128)(2,1)S(1)}, u32[]{:S(2)}, u32[]{:S(2)}) collective-permute-start(bf16[128,128]{1,0:T(8,128)(2,1)S(1)} %get-tuple-element.31), channel_id=1, source_target_pairs={{0,3},{1,2},{2,1},{3,0},{4,7},{5,6},{6,5},{7,4},{8,11},{9,10},{10,... | collective-permute-start | bytes 98312 | tf_op jit(solution)/shard_map/ppermute | solution.py:480
  20.3 1.6 %collective-permute-start.6 = (bf16[128,128]{1,0:T(8,128)(2,1)S(1)}, bf16[128,128]{1,0:T(8,128)(2,1)S(1)}, u32[]{:S(2)}, u32[]{:S(2)}) collective-permute-start(bf16[128,128]{1,0:T(8,128)(2,1)S(1)} %get-tuple-element.32), channel_id=1, source_target_pairs={{0,2},{1,3},{2,0},{3,1},{4,6},{5,7},{6,4},{7,5},{8,10},{9,11},{10,... | collective-permute-start | bytes 98312 | tf_op jit(solution)/shard_map/ppermute | solution.py:480
  21.9 0.9 %collective-permute-start.7 = (bf16[128,128]{1,0:T(8,128)(2,1)S(1)}, bf16[128,128]{1,0:T(8,128)(2,1)S(1)}, u32[]{:S(2)}, u32[]{:S(2)}) collective-permute-start(bf16[128,128]{1,0:T(8,128)(2,1)S(1)} %get-tuple-element.33), channel_id=1, source_target_pairs={{0,1},{1,0},{2,3},{3,2},{4,5},{5,4},{6,7},{7,6},{8,9},{9,8},{10,11... | collective-permute-start | bytes 98312 | tf_op jit(solution)/shard_map/ppermute | solution.py:480
  22.8 1.8 %near.3.refs_5_ = f32[8,8,128]{2,1,0:T(8,128)S(1)} custom-call(s32[8,16]{1,0:T(8,128)S(1)} %get-tuple-element.25.refs_6_.refs_0_.refs_8_, bf16[128,128]{1,0:T(8,128)(2,1)S(1)} %get-tuple-element.24.refs_6_.refs_1_.refs_9_, bf16[16,8,2,128,128]{4,3,2,1,0:T(8,128)(2,1)S(1)} %copy-done, ...), custom_call_target="tpu_custom_call", output_to_operand_aliasing={{}: (3, {})} | custom-call | flops 33554432 | bytes 4194304 | tf_op jit(solution)/shard_map/near/pallas_call | solution.py:551
  24.7 0.0 collective-permute-done.5.refs_1_
  24.7 1.8 %collective-permute-done.6.refs_2_ = bf16[128,128]{1,0:T(8,128)(2,1)S(1)} collective-permute-done((bf16[128,128]{1,0:T(8,128)(2,1)S(1)}, bf16[128,128]{1,0:T(8,128)(2,1)S(1)}, u32[]{:S(2)}, u32[]{:S(2)}) %collective-permute-start.6) | collective-permute-done | bytes 32800 | tf_op jit(solution)/shard_map/ppermute | solution.py:480
  26.5 0.1 collective-permute-done.7.refs_3_
  26.6 0.0 copy-done.2
  26.6 1.0 %final.1 = f32[16,2,4,128]{3,2,1,0:T(4,128)} custom-call(bf16[128,128]{1,0:T(8,128)(2,1)S(1)} %get-tuple-element.30.refs_0_, bf16[128,128]{1,0:T(8,128)(2,1)S(1)} %collective-permute-done.5.refs_1_, bf16[128,128]{1,0:T(8,128)(2,1)S(1)} %collective-permute-done.6.refs_2_, bf16[128,128]{1,0:T(8,128)(2,1)S(1)} %collective-permute-done.7.refs_3_, ...), custom_call_target="tpu_custom_call" | custom-call | tf_op jit(solution)/shard_map/final/pallas_call | solution.py:605
Async XLA Ops:
  0.0 15.0 %copy-start = (bf16[16,8,2,128,128]{4,3,2,1,0:T(8,128)(2,1)S(1)}, bf16[16,8,2,128,128]{4,3,2,1,0:T(8,128)(2,1)}, u32[]{:S(2)}) copy-start(bf16[16,8,2,128,128]{4,3,2,1,0:T(8,128)(2,1)} %refs_2_.5) | copy-start | bytes 25165828
  0.0 11.8 %copy-start.1 = (bf16[2048,128]{1,0:T(8,128)(2,1)S(1)}, bf16[2048,128]{1,0:T(8,128)(2,1)}, u32[]{:S(2)}) copy-start(bf16[2048,128]{1,0:T(8,128)(2,1)} %refs_4_.7) | copy-start | bytes 1572868
  0.0 11.8 %copy-start.3 = (f32[8,2,2048]{2,1,0:T(2,128)S(1)}, f32[8,2,2048]{2,1,0:T(2,128)}, u32[]{:S(2)}) copy-start(f32[8,2,2048]{2,1,0:T(2,128)} %refs_5_.5) | copy-start | bytes 393220
  1.8 10.0 %collective-permute-start = (bf16[200,128]{1,0:T(8,128)(2,1)S(1)}, bf16[200,128]{1,0:T(8,128)(2,1)S(1)}, u32[]{:S(2)}, u32[]{:S(2)}) collective-permute-start(bf16[200,128]{1,0:T(8,128)(2,1)S(1)} %get-tuple-element.21), channel_id=1, source_target_pairs={{0,3},{1,2},{2,1},{3,0},{4,7},{5,6},{6,5},{7,4},{8,11},{9,10},{10,... | collective-permute-start | bytes 153608 | tf_op jit(solution)/shard_map/ppermute | solution.py:480
  6.9 4.9 %collective-permute-start.1 = (bf16[200,128]{1,0:T(8,128)(2,1)S(1)}, bf16[200,128]{1,0:T(8,128)(2,1)S(1)}, u32[]{:S(2)}, u32[]{:S(2)}) collective-permute-start(bf16[200,128]{1,0:T(8,128)(2,1)S(1)} %get-tuple-element.22), channel_id=1, source_target_pairs={{0,1},{1,0},{2,3},{3,2},{4,5},{5,4},{6,7},{7,6},{8,9},{9,8},{10,11... | collective-permute-start | bytes 153608 | tf_op jit(solution)/shard_map/ppermute | solution.py:480
  6.9 4.9 %collective-permute-start.2 = (bf16[136,128]{1,0:T(8,128)(2,1)S(1)}, bf16[136,128]{1,0:T(8,128)(2,1)S(1)}, u32[]{:S(2)}, u32[]{:S(2)}) collective-permute-start(bf16[136,128]{1,0:T(8,128)(2,1)S(1)} %get-tuple-element.20.refs_0_), channel_id=1, source_target_pairs={{0,2},{1,3},{2,0},{3,1},{4,6},{5,7},{6,4},{7,5},{8,10},{9,11},{10,... | collective-permute-start | bytes 104456 | tf_op jit(solution)/shard_map/ppermute | solution.py:480
  12.4 4.5 %collective-permute-start.4 = (bf16[80,512]{1,0:T(8,128)(2,1)S(1)}, bf16[80,512]{1,0:T(8,128)(2,1)S(1)}, u32[]{:S(2)}, u32[]{:S(2)}) collective-permute-start(bf16[80,512]{1,0:T(8,128)(2,1)S(1)} %get-tuple-element.26.refs_0_), channel_id=1, source_target_pairs={{0,4},{4,0},{8,12},{12,8},{16,20},{20,16},{24,28},{28,24},{1,5},{5... | collective-permute-start | bytes 245768 | tf_op jit(solution)/shard_map/ppermute | solution.py:541
  12.4 5.1 %collective-permute-start.3 = (bf16[80,512]{1,0:T(8,128)(2,1)S(1)}, bf16[80,512]{1,0:T(8,128)(2,1)S(1)}, u32[]{:S(2)}, u32[]{:S(2)}) collective-permute-start(bf16[80,512]{1,0:T(8,128)(2,1)S(1)} %get-tuple-element.27), channel_id=1, source_target_pairs={{0,28},{4,8},{8,4},{12,16},{16,12},{20,24},{24,20},{28,0},{1,29},{... | collective-permute-start | bytes 245768 | tf_op jit(solution)/shard_map/ppermute | solution.py:538
  17.5 9.0 %copy-start.2 = (bf16[16,2,128,128]{3,2,1,0:T(8,128)(2,1)S(1)}, bf16[16,2,128,128]{3,2,1,0:T(8,128)(2,1)}, u32[]{:S(2)}) copy-start(bf16[16,2,128,128]{3,2,1,0:T(8,128)(2,1)} %refs_6_.3) | copy-start | bytes 3145732
  18.4 6.3 %collective-permute-start.5 = (bf16[128,128]{1,0:T(8,128)(2,1)S(1)}, bf16[128,128]{1,0:T(8,128)(2,1)S(1)}, u32[]{:S(2)}, u32[]{:S(2)}) collective-permute-start(bf16[128,128]{1,0:T(8,128)(2,1)S(1)} %get-tuple-element.31), channel_id=1, source_target_pairs={{0,3},{1,2},{2,1},{3,0},{4,7},{5,6},{6,5},{7,4},{8,11},{9,10},{10,... | collective-permute-start | bytes 98312 | tf_op jit(solution)/shard_map/ppermute | solution.py:480
  20.3 6.1 %collective-permute-start.6 = (bf16[128,128]{1,0:T(8,128)(2,1)S(1)}, bf16[128,128]{1,0:T(8,128)(2,1)S(1)}, u32[]{:S(2)}, u32[]{:S(2)}) collective-permute-start(bf16[128,128]{1,0:T(8,128)(2,1)S(1)} %get-tuple-element.32), channel_id=1, source_target_pairs={{0,2},{1,3},{2,0},{3,1},{4,6},{5,7},{6,4},{7,5},{8,10},{9,11},{10,... | collective-permute-start | bytes 98312 | tf_op jit(solution)/shard_map/ppermute | solution.py:480
  21.9 4.7 %collective-permute-start.7 = (bf16[128,128]{1,0:T(8,128)(2,1)S(1)}, bf16[128,128]{1,0:T(8,128)(2,1)S(1)}, u32[]{:S(2)}, u32[]{:S(2)}) collective-permute-start(bf16[128,128]{1,0:T(8,128)(2,1)S(1)} %get-tuple-element.33), channel_id=1, source_target_pairs={{0,1},{1,0},{2,3},{3,2},{4,5},{5,4},{6,7},{7,6},{8,9},{9,8},{10,11... | collective-permute-start | bytes 98312 | tf_op jit(solution)/shard_map/ppermute | solution.py:480

commit v17 on v15

--- a/solution.py
+++ b/solution.py
@@ -8,7 +8,7 @@
 F32 = jnp.float32
 BF16 = jnp.bfloat16
 LANES = 128
-CODE_ROWS = 8
+CODE_ROWS = 16
 
 
 def nt_dot(a, b):

time: 26.9 us -> 27 us (level)
  no operation moved by 1% of the time
where the time goes in v17:
time: 27 us; the launch traced here: 26.8 us
  starting transfers between devices  12.8 us (47%)
  Pallas kernels  9.4 us (35%)
  waiting for transfers between devices  4.49 us (17%)
    ppermute x6, starting transfers between devices, exchange(): return lax.ppermute(x, 'samp', [(i, i ^ d) for i in range(nsamp)])  10.2 us
    ppermute x6, waiting for transfers between devices, exchange(): return lax.ppermute(x, 'samp', [(i, i ^ d) for i in range(nsamp)])  3.79 us
    pallas_call x2, Pallas kernels, near_half(): pl.pallas_call(lambda *refs: near_kernel(*refs, late=late, nsamp=nsamp, t...  3.64 us
    ppermute x1, starting transfers between devices, on_device(): lax.ppermute(to_across, 'box', [(i, (i + (1 if i % 2 else -1)) % nbox) fo...  2.55 us
    pallas_call x1, Pallas kernels, on_device(): pl.pallas_call(lambda *refs: leaf_kernel(*refs, parents=parents, all_pare...  1.8 us
    pallas_call x1, Pallas kernels, on_device(): pl.pallas_call(lambda *refs: prep_kernel(*refs, parents=parents, all_pare...  1.61 us
    pallas_call x1, Pallas kernels, on_device(): pl.pallas_call(lambda *refs: final_kernel(*refs, pieces=nsamp), in_specs=...  1.02 us
    pallas_call x1, Pallas kernels, on_device(): pl.pallas_call(lambda *refs: down_kernel(*refs, pieces=nsamp, boxes=boxes...  0.81 us
  transfers between devices with their start and end apart: 8, of which 4 were waited for; matrix products, arithmetic and copies ran while one was open for 0% of the time, Pallas kernels for 20%

profile of v17, /device:TPU:0, one launch (start us, length us, event | category | flops | bytes accessed | tf_op | source)
XLA Modules:
  0.0 26.8 jit_solution(16506045698179283251)
XLA Ops:
  0.0 0.0 copy-start
  0.0 0.0 copy-start.1
  0.0 0.0 copy-start.3
  0.0 1.8 %leaf.1 = (bf16[208,128]{1,0:T(8,128)(2,1)S(1)}, bf16[144,128]{1,0:T(8,128)(2,1)S(1)}, bf16[208,128]{1,0:T(8,128)(2,1)S(1)}, bf16[128,128]{1,0:T(8,128)(2,1)S(1)}, f32[8,14,2,512]{3,2,1,0:T(2,128)S(1)}) custom-call(s32[16]{0:T(128)} %refs_0_.2, s32[16]{0:T(128)} %refs_1_.2, bf16[16,2,4,128]{3,2,1,0:T(4,128)(2,1)} %refs_2_.3, ...), custom_call_target="tpu_custom_call" | custom-call | tf_op jit(solution)/shard_map/leaf/pallas_call | solution.py:430
  1.8 5.1 %collective-permute-start = (bf16[208,128]{1,0:T(8,128)(2,1)S(1)}, bf16[208,128]{1,0:T(8,128)(2,1)S(1)}, u32[]{:S(2)}, u32[]{:S(2)}) collective-permute-start(bf16[208,128]{1,0:T(8,128)(2,1)S(1)} %get-tuple-element.20), channel_id=1, source_target_pairs={{0,3},{1,2},{2,1},{3,0},{4,7},{5,6},{6,5},{7,4},{8,11},{9,10},{10,... | collective-permute-start | bytes 159752 | tf_op jit(solution)/shard_map/ppermute | solution.py:461
  6.9 0.0 collective-permute-start.1
  6.9 0.6 %collective-permute-start.2 = (bf16[144,128]{1,0:T(8,128)(2,1)S(1)}, bf16[144,128]{1,0:T(8,128)(2,1)S(1)}, u32[]{:S(2)}, u32[]{:S(2)}) collective-permute-start(bf16[144,128]{1,0:T(8,128)(2,1)S(1)} %get-tuple-element.19.refs_0_), channel_id=1, source_target_pairs={{0,2},{1,3},{2,0},{3,1},{4,6},{5,7},{6,4},{7,5},{8,10},{9,11},{10,... | collective-permute-start | bytes 110600 | tf_op jit(solution)/shard_map/ppermute | solution.py:461
  7.6 1.6 %prep.1 = (f32[8,14,2,512]{3,2,1,0:T(2,128)S(1)}, s32[8,16]{1,0:T(8,128)S(1)}) custom-call(s32[8,14]{1,0:T(8,128)} %refs_0_.3, s32[8,14]{1,0:T(8,128)} %refs_1_.3, s32[8,16]{1,0:T(8,128)} %bitcast.1, f32[64,2,512]{2,1,0:T(2,128)} %refs_3_.3, bf16[16,8,2,128,128]{4,3,2,1,0:T(8,128)(2,1)} %refs_2_.5, ...), custom_call_target="tpu_custom_call", output_to_operand_aliasing={{0}: (5, {})} | custom-call | bytes 8388608 | tf_op jit(solution)/shard_map/prep/pallas_call | solution.py:470
  9.2 2.6 %collective-permute-done.2.refs_3_ = bf16[144,128]{1,0:T(8,128)(2,1)S(1)} collective-permute-done((bf16[144,128]{1,0:T(8,128)(2,1)S(1)}, bf16[144,128]{1,0:T(8,128)(2,1)S(1)}, u32[]{:S(2)}, u32[]{:S(2)}) %collective-permute-start.2) | collective-permute-done | bytes 36896 | tf_op jit(solution)/shard_map/ppermute | solution.py:461
  11.8 0.0 collective-permute-done.refs_1_.refs_6_
  11.8 0.0 collective-permute-done.1.refs_2_.refs_4_
  11.9 0.0 copy-done.1
  11.9 0.0 copy-done.3
  11.9 0.5 %up.1 = (bf16[80,512]{1,0:T(8,128)(2,1)S(1)}, bf16[80,512]{1,0:T(8,128)(2,1)S(1)}, bf16[64,64]{1,0:T(8,128)(2,1)S(1)}) custom-call(bf16[144,128]{1,0:T(8,128)(2,1)S(1)} %get-tuple-element.19.refs_0_, bf16[208,128]{1,0:T(8,128)(2,1)S(1)} %collective-permute-done.refs_1_.refs_6_, bf16[208,128]{1,0:T(8,128)(2,1)S(1)} %collective-permute-done.1.refs_2_.refs_4_, ...), custom_call_target="tpu_custom_call" | custom-call | tf_op jit(solution)/shard_map/up/pallas_call | solution.py:500
  12.4 0.1 collective-permute-start.4
  12.5 2.6 %collective-permute-start.3 = (bf16[80,512]{1,0:T(8,128)(2,1)S(1)}, bf16[80,512]{1,0:T(8,128)(2,1)S(1)}, u32[]{:S(2)}, u32[]{:S(2)}) collective-permute-start(bf16[80,512]{1,0:T(8,128)(2,1)S(1)} %get-tuple-element.26), channel_id=1, source_target_pairs={{0,28},{4,8},{8,4},{12,16},{16,12},{20,24},{24,20},{28,0},{1,29},{... | collective-permute-start | bytes 245768 | tf_op jit(solution)/shard_map/ppermute | solution.py:519
  15.0 0.0 copy-done
  15.0 0.0 copy-start.2
  15.0 1.8 %near.2.refs_7_.refs_4_ = f32[8,8,128]{2,1,0:T(8,128)S(1)} custom-call(s32[8,16]{1,0:T(8,128)S(1)} %get-tuple-element.24.refs_6_.refs_0_, bf16[128,128]{1,0:T(8,128)(2,1)S(1)} %get-tuple-element.23.refs_6_.refs_1_, bf16[16,8,2,128,128]{4,3,2,1,0:T(8,128)(2,1)S(1)} %copy-done, bf16[64,64]{1,0:T(8,128)(2,1)S(1)} %get-tuple-element.28.refs_3_.refs_6_, ...), custom_call_target="tpu_custom_call" | custom-call | flops 33554432 | bytes 4194304 | tf_op jit(solution)/shard_map/near/pallas_call | solution.py:525
  16.9 0.0 collective-permute-done.4.refs_2_.refs_5_
  16.9 0.7 %collective-permute-done.3.refs_1_.refs_4_ = bf16[80,512]{1,0:T(8,128)(2,1)S(1)} collective-permute-done((bf16[80,512]{1,0:T(8,128)(2,1)S(1)}, bf16[80,512]{1,0:T(8,128)(2,1)S(1)}, u32[]{:S(2)}, u32[]{:S(2)}) %collective-permute-start.3) | collective-permute-done | bytes 81952 | tf_op jit(solution)/shard_map/ppermute | solution.py:519
  17.6 0.8 %down.1 = (bf16[128,128]{1,0:T(8,128)(2,1)S(1)}, bf16[128,128]{1,0:T(8,128)(2,1)S(1)}, bf16[128,128]{1,0:T(8,128)(2,1)S(1)}, bf16[128,128]{1,0:T(8,128)(2,1)S(1)}) custom-call(bf16[80,512]{1,0:T(8,128)(2,1)S(1)} %get-tuple-element.25.refs_0_, bf16[80,512]{1,0:T(8,128)(2,1)S(1)} %collective-permute-done.3.refs_1_.refs_4_, ...), custom_call_target="tpu_custom_call" | custom-call | tf_op jit(solution)/shard_map/down/pallas_call | solution.py:553
  18.4 2.0 %collective-permute-start.5 = (bf16[128,128]{1,0:T(8,128)(2,1)S(1)}, bf16[128,128]{1,0:T(8,128)(2,1)S(1)}, u32[]{:S(2)}, u32[]{:S(2)}) collective-permute-start(bf16[128,128]{1,0:T(8,128)(2,1)S(1)} %get-tuple-element.30), channel_id=1, source_target_pairs={{0,3},{1,2},{2,1},{3,0},{4,7},{5,6},{6,5},{7,4},{8,11},{9,10},{10,... | collective-permute-start | bytes 98312 | tf_op jit(solution)/shard_map/ppermute | solution.py:461
  20.4 1.5 %collective-permute-start.6 = (bf16[128,128]{1,0:T(8,128)(2,1)S(1)}, bf16[128,128]{1,0:T(8,128)(2,1)S(1)}, u32[]{:S(2)}, u32[]{:S(2)}) collective-permute-start(bf16[128,128]{1,0:T(8,128)(2,1)S(1)} %get-tuple-element.31), channel_id=1, source_target_pairs={{0,2},{1,3},{2,0},{3,1},{4,6},{5,7},{6,4},{7,5},{8,10},{9,11},{10,... | collective-permute-start | bytes 98312 | tf_op jit(solution)/shard_map/ppermute | solution.py:461
  21.9 0.9 %collective-permute-start.7 = (bf16[128,128]{1,0:T(8,128)(2,1)S(1)}, bf16[128,128]{1,0:T(8,128)(2,1)S(1)}, u32[]{:S(2)}, u32[]{:S(2)}) collective-permute-start(bf16[128,128]{1,0:T(8,128)(2,1)S(1)} %get-tuple-element.32), channel_id=1, source_target_pairs={{0,1},{1,0},{2,3},{3,2},{4,5},{5,4},{6,7},{7,6},{8,9},{9,8},{10,11... | collective-permute-start | bytes 98312 | tf_op jit(solution)/shard_map/ppermute | solution.py:461
  22.8 1.8 %near.3.refs_5_ = f32[8,8,128]{2,1,0:T(8,128)S(1)} custom-call(s32[8,16]{1,0:T(8,128)S(1)} %get-tuple-element.24.refs_6_.refs_0_, bf16[128,128]{1,0:T(8,128)(2,1)S(1)} %get-tuple-element.23.refs_6_.refs_1_, bf16[16,8,2,128,128]{4,3,2,1,0:T(8,128)(2,1)S(1)} %copy-done, bf16[128,128]{1,0:T(8,128)(2,1)S(1)} %get-tuple-element.29.refs_3_.refs_0_, ...), custom_call_target="tpu_custom_call" | custom-call | flops 33554432 | bytes 4194304 | tf_op jit(solution)/shard_map/near/pallas_call | solution.py:525
  24.7 0.0 collective-permute-done.5.refs_1_
  24.7 0.7 %collective-permute-done.6.refs_2_ = bf16[128,128]{1,0:T(8,128)(2,1)S(1)} collective-permute-done((bf16[128,128]{1,0:T(8,128)(2,1)S(1)}, bf16[128,128]{1,0:T(8,128)(2,1)S(1)}, u32[]{:S(2)}, u32[]{:S(2)}) %collective-permute-start.6) | collective-permute-done | bytes 32800 | tf_op jit(solution)/shard_map/ppermute | solution.py:461
  25.4 0.4 %collective-permute-done.7.refs_3_ = bf16[128,128]{1,0:T(8,128)(2,1)S(1)} collective-permute-done((bf16[128,128]{1,0:T(8,128)(2,1)S(1)}, bf16[128,128]{1,0:T(8,128)(2,1)S(1)}, u32[]{:S(2)}, u32[]{:S(2)}) %collective-permute-start.7) | collective-permute-done | bytes 32800 | tf_op jit(solution)/shard_map/ppermute | solution.py:461
  25.8 0.0 copy-done.2
  25.8 1.0 %final.1 = f32[16,2,4,128]{3,2,1,0:T(4,128)} custom-call(bf16[128,128]{1,0:T(8,128)(2,1)S(1)} %get-tuple-element.29.refs_3_.refs_0_, bf16[128,128]{1,0:T(8,128)(2,1)S(1)} %collective-permute-done.5.refs_1_, bf16[128,128]{1,0:T(8,128)(2,1)S(1)} %collective-permute-done.6.refs_2_, bf16[128,128]{1,0:T(8,128)(2,1)S(1)} %collective-permute-done.7.refs_3_, ...), custom_call_target="tpu_custom_call" | custom-call | tf_op jit(solution)/shard_map/final/pallas_call | solution.py:574
Async XLA Ops:
  0.0 15.0 %copy-start = (bf16[16,8,2,128,128]{4,3,2,1,0:T(8,128)(2,1)S(1)}, bf16[16,8,2,128,128]{4,3,2,1,0:T(8,128)(2,1)}, u32[]{:S(2)}) copy-start(bf16[16,8,2,128,128]{4,3,2,1,0:T(8,128)(2,1)} %refs_2_.5) | copy-start | bytes 25165828
  0.0 11.9 %copy-start.1 = (bf16[2048,128]{1,0:T(8,128)(2,1)S(1)}, bf16[2048,128]{1,0:T(8,128)(2,1)}, u32[]{:S(2)}) copy-start(bf16[2048,128]{1,0:T(8,128)(2,1)} %refs_4_.7) | copy-start | bytes 1572868
  0.0 11.9 %copy-start.3 = (f32[8,2,2048]{2,1,0:T(2,128)S(1)}, f32[8,2,2048]{2,1,0:T(2,128)}, u32[]{:S(2)}) copy-start(f32[8,2,2048]{2,1,0:T(2,128)} %refs_5_.5) | copy-start | bytes 393220
  1.8 10.0 %collective-permute-start = (bf16[208,128]{1,0:T(8,128)(2,1)S(1)}, bf16[208,128]{1,0:T(8,128)(2,1)S(1)}, u32[]{:S(2)}, u32[]{:S(2)}) collective-permute-start(bf16[208,128]{1,0:T(8,128)(2,1)S(1)} %get-tuple-element.20), channel_id=1, source_target_pairs={{0,3},{1,2},{2,1},{3,0},{4,7},{5,6},{6,5},{7,4},{8,11},{9,10},{10,... | collective-permute-start | bytes 159752 | tf_op jit(solution)/shard_map/ppermute | solution.py:461
  6.9 4.9 %collective-permute-start.1 = (bf16[208,128]{1,0:T(8,128)(2,1)S(1)}, bf16[208,128]{1,0:T(8,128)(2,1)S(1)}, u32[]{:S(2)}, u32[]{:S(2)}) collective-permute-start(bf16[208,128]{1,0:T(8,128)(2,1)S(1)} %get-tuple-element.21), channel_id=1, source_target_pairs={{0,1},{1,0},{2,3},{3,2},{4,5},{5,4},{6,7},{7,6},{8,9},{9,8},{10,11... | collective-permute-start | bytes 159752 | tf_op jit(solution)/shard_map/ppermute | solution.py:461
  6.9 4.9 %collective-permute-start.2 = (bf16[144,128]{1,0:T(8,128)(2,1)S(1)}, bf16[144,128]{1,0:T(8,128)(2,1)S(1)}, u32[]{:S(2)}, u32[]{:S(2)}) collective-permute-start(bf16[144,128]{1,0:T(8,128)(2,1)S(1)} %get-tuple-element.19.refs_0_), channel_id=1, source_target_pairs={{0,2},{1,3},{2,0},{3,1},{4,6},{5,7},{6,4},{7,5},{8,10},{9,11},{10,... | collective-permute-start | bytes 110600 | tf_op jit(solution)/shard_map/ppermute | solution.py:461
  12.4 4.5 %collective-permute-start.4 = (bf16[80,512]{1,0:T(8,128)(2,1)S(1)}, bf16[80,512]{1,0:T(8,128)(2,1)S(1)}, u32[]{:S(2)}, u32[]{:S(2)}) collective-permute-start(bf16[80,512]{1,0:T(8,128)(2,1)S(1)} %get-tuple-element.25.refs_0_), channel_id=1, source_target_pairs={{0,4},{4,0},{8,12},{12,8},{16,20},{20,16},{24,28},{28,24},{1,5},{5... | collective-permute-start | bytes 245768 | tf_op jit(solution)/shard_map/ppermute | solution.py:522
  12.5 5.1 %collective-permute-start.3 = (bf16[80,512]{1,0:T(8,128)(2,1)S(1)}, bf16[80,512]{1,0:T(8,128)(2,1)S(1)}, u32[]{:S(2)}, u32[]{:S(2)}) collective-permute-start(bf16[80,512]{1,0:T(8,128)(2,1)S(1)} %get-tuple-element.26), channel_id=1, source_target_pairs={{0,28},{4,8},{8,4},{12,16},{16,12},{20,24},{24,20},{28,0},{1,29},{... | collective-permute-start | bytes 245768 | tf_op jit(solution)/shard_map/ppermute | solution.py:519
  15.0 10.8 %copy-start.2 = (bf16[16,2,128,128]{3,2,1,0:T(8,128)(2,1)S(1)}, bf16[16,2,128,128]{3,2,1,0:T(8,128)(2,1)}, u32[]{:S(2)}) copy-start(bf16[16,2,128,128]{3,2,1,0:T(8,128)(2,1)} %refs_6_.3) | copy-start | bytes 3145732
  18.4 6.3 %collective-permute-start.5 = (bf16[128,128]{1,0:T(8,128)(2,1)S(1)}, bf16[128,128]{1,0:T(8,128)(2,1)S(1)}, u32[]{:S(2)}, u32[]{:S(2)}) collective-permute-start(bf16[128,128]{1,0:T(8,128)(2,1)S(1)} %get-tuple-element.30), channel_id=1, source_target_pairs={{0,3},{1,2},{2,1},{3,0},{4,7},{5,6},{6,5},{7,4},{8,11},{9,10},{10,... | collective-permute-start | bytes 98312 | tf_op jit(solution)/shard_map/ppermute | solution.py:461
  20.4 5.0 %collective-permute-start.6 = (bf16[128,128]{1,0:T(8,128)(2,1)S(1)}, bf16[128,128]{1,0:T(8,128)(2,1)S(1)}, u32[]{:S(2)}, u32[]{:S(2)}) collective-permute-start(bf16[128,128]{1,0:T(8,128)(2,1)S(1)} %get-tuple-element.31), channel_id=1, source_target_pairs={{0,2},{1,3},{2,0},{3,1},{4,6},{5,7},{6,4},{7,5},{8,10},{9,11},{10,... | collective-permute-start | bytes 98312 | tf_op jit(solution)/shard_map/ppermute | solution.py:461
  21.9 3.9 %collective-permute-start.7 = (bf16[128,128]{1,0:T(8,128)(2,1)S(1)}, bf16[128,128]{1,0:T(8,128)(2,1)S(1)}, u32[]{:S(2)}, u32[]{:S(2)}) collective-permute-start(bf16[128,128]{1,0:T(8,128)(2,1)S(1)} %get-tuple-element.32), channel_id=1, source_target_pairs={{0,1},{1,0},{2,3},{3,2},{4,5},{5,4},{6,7},{7,6},{8,9},{9,8},{10,11... | collective-permute-start | bytes 98312 | tf_op jit(solution)/shard_map/ppermute | solution.py:461

commit v18 on v17

--- a/solution.py
+++ b/solution.py
@@ -62,7 +62,7 @@
         )
         for i in range(chunks)
     ]
-    for copy in small + big:
+    for copy in big + small:
         copy.start()
     start, finish = fill_dense(
         dense, inter, trans, table_hbm, inter_s, trans_s, table, more, parents, all_parents

time: 27 us -> 27.1 us (level)
  no operation moved by 1% of the time
where the time goes in v18:
time: 27.1 us; the launch traced here: 26.9 us
  starting transfers between devices  12.8 us (47%)
  Pallas kernels  9.5 us (35%)
  waiting for transfers between devices  4.49 us (17%)
    ppermute x6, starting transfers between devices, exchange(): return lax.ppermute(x, 'samp', [(i, i ^ d) for i in range(nsamp)])  10.2 us
    ppermute x6, waiting for transfers between devices, exchange(): return lax.ppermute(x, 'samp', [(i, i ^ d) for i in range(nsamp)])  3.79 us
    pallas_call x2, Pallas kernels, near_half(): pl.pallas_call(lambda *refs: near_kernel(*refs, late=late, nsamp=nsamp, t...  3.64 us
    ppermute x1, starting transfers between devices, on_device(): lax.ppermute(to_across, 'box', [(i, (i + (1 if i % 2 else -1)) % nbox) fo...  2.55 us
    pallas_call x1, Pallas kernels, on_device(): pl.pallas_call(lambda *refs: leaf_kernel(*refs, parents=parents, all_pare...  1.89 us
    pallas_call x1, Pallas kernels, on_device(): pl.pallas_call(lambda *refs: prep_kernel(*refs, parents=parents, all_pare...  1.61 us
    pallas_call x1, Pallas kernels, on_device(): pl.pallas_call(lambda *refs: final_kernel(*refs, pieces=nsamp), in_specs=...  1.02 us
    pallas_call x1, Pallas kernels, on_device(): pl.pallas_call(lambda *refs: down_kernel(*refs, pieces=nsamp, boxes=boxes...  0.81 us
  transfers between devices with their start and end apart: 8, of which 4 were waited for; matrix products, arithmetic and copies ran while one was open for 0% of the time, Pallas kernels for 20%

profile of v18, /device:TPU:0, one launch (start us, length us, event | category | flops | bytes accessed | tf_op | source)
XLA Modules:
  0.0 26.9 jit_solution(6560468654852496464)
XLA Ops:
  0.0 0.0 copy-start
  0.0 0.0 copy-start.1
  0.0 0.0 copy-start.3
  0.0 1.9 %leaf.1 = (bf16[208,128]{1,0:T(8,128)(2,1)S(1)}, bf16[144,128]{1,0:T(8,128)(2,1)S(1)}, bf16[208,128]{1,0:T(8,128)(2,1)S(1)}, bf16[128,128]{1,0:T(8,128)(2,1)S(1)}, f32[8,14,2,512]{3,2,1,0:T(2,128)S(1)}) custom-call(s32[16]{0:T(128)} %refs_0_.2, s32[16]{0:T(128)} %refs_1_.2, bf16[16,2,4,128]{3,2,1,0:T(4,128)(2,1)} %refs_2_.3, ...), custom_call_target="tpu_custom_call" | custom-call | tf_op jit(solution)/shard_map/leaf/pallas_call | solution.py:430
  1.9 5.1 %collective-permute-start = (bf16[208,128]{1,0:T(8,128)(2,1)S(1)}, bf16[208,128]{1,0:T(8,128)(2,1)S(1)}, u32[]{:S(2)}, u32[]{:S(2)}) collective-permute-start(bf16[208,128]{1,0:T(8,128)(2,1)S(1)} %get-tuple-element.20), channel_id=1, source_target_pairs={{0,3},{1,2},{2,1},{3,0},{4,7},{5,6},{6,5},{7,4},{8,11},{9,10},{10,... | collective-permute-start | bytes 159752 | tf_op jit(solution)/shard_map/ppermute | solution.py:461
  7.0 0.0 collective-permute-start.1
  7.0 0.6 %collective-permute-start.2 = (bf16[144,128]{1,0:T(8,128)(2,1)S(1)}, bf16[144,128]{1,0:T(8,128)(2,1)S(1)}, u32[]{:S(2)}, u32[]{:S(2)}) collective-permute-start(bf16[144,128]{1,0:T(8,128)(2,1)S(1)} %get-tuple-element.19.refs_0_), channel_id=1, source_target_pairs={{0,2},{1,3},{2,0},{3,1},{4,6},{5,7},{6,4},{7,5},{8,10},{9,11},{10,... | collective-permute-start | bytes 110600 | tf_op jit(solution)/shard_map/ppermute | solution.py:461
  7.7 1.6 %prep.1 = (f32[8,14,2,512]{3,2,1,0:T(2,128)S(1)}, s32[8,16]{1,0:T(8,128)S(1)}) custom-call(s32[8,14]{1,0:T(8,128)} %refs_0_.3, s32[8,14]{1,0:T(8,128)} %refs_1_.3, s32[8,16]{1,0:T(8,128)} %bitcast.1, f32[64,2,512]{2,1,0:T(2,128)} %refs_3_.3, bf16[16,8,2,128,128]{4,3,2,1,0:T(8,128)(2,1)} %refs_2_.5, ...), custom_call_target="tpu_custom_call", output_to_operand_aliasing={{0}: (5, {})} | custom-call | bytes 8388608 | tf_op jit(solution)/shard_map/prep/pallas_call | solution.py:470
  9.3 2.6 %collective-permute-done.2.refs_3_ = bf16[144,128]{1,0:T(8,128)(2,1)S(1)} collective-permute-done((bf16[144,128]{1,0:T(8,128)(2,1)S(1)}, bf16[144,128]{1,0:T(8,128)(2,1)S(1)}, u32[]{:S(2)}, u32[]{:S(2)}) %collective-permute-start.2) | collective-permute-done | bytes 36896 | tf_op jit(solution)/shard_map/ppermute | solution.py:461
  11.9 0.0 collective-permute-done.refs_1_.refs_6_
  11.9 0.0 collective-permute-done.1.refs_2_.refs_4_
  12.0 0.0 copy-done.1
  12.0 0.0 copy-done.3
  12.0 0.5 %up.1 = (bf16[80,512]{1,0:T(8,128)(2,1)S(1)}, bf16[80,512]{1,0:T(8,128)(2,1)S(1)}, bf16[64,64]{1,0:T(8,128)(2,1)S(1)}) custom-call(bf16[144,128]{1,0:T(8,128)(2,1)S(1)} %get-tuple-element.19.refs_0_, bf16[208,128]{1,0:T(8,128)(2,1)S(1)} %collective-permute-done.refs_1_.refs_6_, bf16[208,128]{1,0:T(8,128)(2,1)S(1)} %collective-permute-done.1.refs_2_.refs_4_, ...), custom_call_target="tpu_custom_call" | custom-call | tf_op jit(solution)/shard_map/up/pallas_call | solution.py:500
  12.5 0.1 collective-permute-start.4
  12.6 2.6 %collective-permute-start.3 = (bf16[80,512]{1,0:T(8,128)(2,1)S(1)}, bf16[80,512]{1,0:T(8,128)(2,1)S(1)}, u32[]{:S(2)}, u32[]{:S(2)}) collective-permute-start(bf16[80,512]{1,0:T(8,128)(2,1)S(1)} %get-tuple-element.26), channel_id=1, source_target_pairs={{0,28},{4,8},{8,4},{12,16},{16,12},{20,24},{24,20},{28,0},{1,29},{... | collective-permute-start | bytes 245768 | tf_op jit(solution)/shard_map/ppermute | solution.py:519
  15.1 0.0 copy-done
  15.1 0.0 copy-start.2
  15.1 1.8 %near.2.refs_7_.refs_4_ = f32[8,8,128]{2,1,0:T(8,128)S(1)} custom-call(s32[8,16]{1,0:T(8,128)S(1)} %get-tuple-element.24.refs_6_.refs_0_, bf16[128,128]{1,0:T(8,128)(2,1)S(1)} %get-tuple-element.23.refs_6_.refs_1_, bf16[16,8,2,128,128]{4,3,2,1,0:T(8,128)(2,1)S(1)} %copy-done, bf16[64,64]{1,0:T(8,128)(2,1)S(1)} %get-tuple-element.28.refs_3_.refs_6_, ...), custom_call_target="tpu_custom_call" | custom-call | flops 33554432 | bytes 4194304 | tf_op jit(solution)/shard_map/near/pallas_call | solution.py:525
  17.0 0.0 collective-permute-done.4.refs_2_.refs_5_
  17.0 0.7 %collective-permute-done.3.refs_1_.refs_4_ = bf16[80,512]{1,0:T(8,128)(2,1)S(1)} collective-permute-done((bf16[80,512]{1,0:T(8,128)(2,1)S(1)}, bf16[80,512]{1,0:T(8,128)(2,1)S(1)}, u32[]{:S(2)}, u32[]{:S(2)}) %collective-permute-start.3) | collective-permute-done | bytes 81952 | tf_op jit(solution)/shard_map/ppermute | solution.py:519
  17.7 0.8 %down.1 = (bf16[128,128]{1,0:T(8,128)(2,1)S(1)}, bf16[128,128]{1,0:T(8,128)(2,1)S(1)}, bf16[128,128]{1,0:T(8,128)(2,1)S(1)}, bf16[128,128]{1,0:T(8,128)(2,1)S(1)}) custom-call(bf16[80,512]{1,0:T(8,128)(2,1)S(1)} %get-tuple-element.25.refs_0_, bf16[80,512]{1,0:T(8,128)(2,1)S(1)} %collective-permute-done.3.refs_1_.refs_4_, ...), custom_call_target="tpu_custom_call" | custom-call | tf_op jit(solution)/shard_map/down/pallas_call | solution.py:553
  18.5 2.0 %collective-permute-start.5 = (bf16[128,128]{1,0:T(8,128)(2,1)S(1)}, bf16[128,128]{1,0:T(8,128)(2,1)S(1)}, u32[]{:S(2)}, u32[]{:S(2)}) collective-permute-start(bf16[128,128]{1,0:T(8,128)(2,1)S(1)} %get-tuple-element.30), channel_id=1, source_target_pairs={{0,3},{1,2},{2,1},{3,0},{4,7},{5,6},{6,5},{7,4},{8,11},{9,10},{10,... | collective-permute-start | bytes 98312 | tf_op jit(solution)/shard_map/ppermute | solution.py:461
  20.5 1.5 %collective-permute-start.6 = (bf16[128,128]{1,0:T(8,128)(2,1)S(1)}, bf16[128,128]{1,0:T(8,128)(2,1)S(1)}, u32[]{:S(2)}, u32[]{:S(2)}) collective-permute-start(bf16[128,128]{1,0:T(8,128)(2,1)S(1)} %get-tuple-element.31), channel_id=1, source_target_pairs={{0,2},{1,3},{2,0},{3,1},{4,6},{5,7},{6,4},{7,5},{8,10},{9,11},{10,... | collective-permute-start | bytes 98312 | tf_op jit(solution)/shard_map/ppermute | solution.py:461
  22.0 0.9 %collective-permute-start.7 = (bf16[128,128]{1,0:T(8,128)(2,1)S(1)}, bf16[128,128]{1,0:T(8,128)(2,1)S(1)}, u32[]{:S(2)}, u32[]{:S(2)}) collective-permute-start(bf16[128,128]{1,0:T(8,128)(2,1)S(1)} %get-tuple-element.32), channel_id=1, source_target_pairs={{0,1},{1,0},{2,3},{3,2},{4,5},{5,4},{6,7},{7,6},{8,9},{9,8},{10,11... | collective-permute-start | bytes 98312 | tf_op jit(solution)/shard_map/ppermute | solution.py:461
  22.9 1.8 %near.3.refs_5_ = f32[8,8,128]{2,1,0:T(8,128)S(1)} custom-call(s32[8,16]{1,0:T(8,128)S(1)} %get-tuple-element.24.refs_6_.refs_0_, bf16[128,128]{1,0:T(8,128)(2,1)S(1)} %get-tuple-element.23.refs_6_.refs_1_, bf16[16,8,2,128,128]{4,3,2,1,0:T(8,128)(2,1)S(1)} %copy-done, bf16[128,128]{1,0:T(8,128)(2,1)S(1)} %get-tuple-element.29.refs_3_.refs_0_, ...), custom_call_target="tpu_custom_call" | custom-call | flops 33554432 | bytes 4194304 | tf_op jit(solution)/shard_map/near/pallas_call | solution.py:525
  24.8 0.0 collective-permute-done.5.refs_1_
  24.8 0.7 %collective-permute-done.6.refs_2_ = bf16[128,128]{1,0:T(8,128)(2,1)S(1)} collective-permute-done((bf16[128,128]{1,0:T(8,128)(2,1)S(1)}, bf16[128,128]{1,0:T(8,128)(2,1)S(1)}, u32[]{:S(2)}, u32[]{:S(2)}) %collective-permute-start.6) | collective-permute-done | bytes 32800 | tf_op jit(solution)/shard_map/ppermute | solution.py:461
  25.5 0.4 %collective-permute-done.7.refs_3_ = bf16[128,128]{1,0:T(8,128)(2,1)S(1)} collective-permute-done((bf16[128,128]{1,0:T(8,128)(2,1)S(1)}, bf16[128,128]{1,0:T(8,128)(2,1)S(1)}, u32[]{:S(2)}, u32[]{:S(2)}) %collective-permute-start.7) | collective-permute-done | bytes 32800 | tf_op jit(solution)/shard_map/ppermute | solution.py:461
  25.9 0.0 copy-done.2
  25.9 1.0 %final.1 = f32[16,2,4,128]{3,2,1,0:T(4,128)} custom-call(bf16[128,128]{1,0:T(8,128)(2,1)S(1)} %get-tuple-element.29.refs_3_.refs_0_, bf16[128,128]{1,0:T(8,128)(2,1)S(1)} %collective-permute-done.5.refs_1_, bf16[128,128]{1,0:T(8,128)(2,1)S(1)} %collective-permute-done.6.refs_2_, bf16[128,128]{1,0:T(8,128)(2,1)S(1)} %collective-permute-done.7.refs_3_, ...), custom_call_target="tpu_custom_call" | custom-call | tf_op jit(solution)/shard_map/final/pallas_call | solution.py:574
Async XLA Ops:
  0.0 15.1 %copy-start = (bf16[16,8,2,128,128]{4,3,2,1,0:T(8,128)(2,1)S(1)}, bf16[16,8,2,128,128]{4,3,2,1,0:T(8,128)(2,1)}, u32[]{:S(2)}) copy-start(bf16[16,8,2,128,128]{4,3,2,1,0:T(8,128)(2,1)} %refs_2_.5) | copy-start | bytes 25165828
  0.0 12.0 %copy-start.1 = (bf16[2048,128]{1,0:T(8,128)(2,1)S(1)}, bf16[2048,128]{1,0:T(8,128)(2,1)}, u32[]{:S(2)}) copy-start(bf16[2048,128]{1,0:T(8,128)(2,1)} %refs_4_.7) | copy-start | bytes 1572868
  0.0 12.0 %copy-start.3 = (f32[8,2,2048]{2,1,0:T(2,128)S(1)}, f32[8,2,2048]{2,1,0:T(2,128)}, u32[]{:S(2)}) copy-start(f32[8,2,2048]{2,1,0:T(2,128)} %refs_5_.5) | copy-start | bytes 393220
  1.9 10.0 %collective-permute-start = (bf16[208,128]{1,0:T(8,128)(2,1)S(1)}, bf16[208,128]{1,0:T(8,128)(2,1)S(1)}, u32[]{:S(2)}, u32[]{:S(2)}) collective-permute-start(bf16[208,128]{1,0:T(8,128)(2,1)S(1)} %get-tuple-element.20), channel_id=1, source_target_pairs={{0,3},{1,2},{2,1},{3,0},{4,7},{5,6},{6,5},{7,4},{8,11},{9,10},{10,... | collective-permute-start | bytes 159752 | tf_op jit(solution)/shard_map/ppermute | solution.py:461
  7.0 4.9 %collective-permute-start.1 = (bf16[208,128]{1,0:T(8,128)(2,1)S(1)}, bf16[208,128]{1,0:T(8,128)(2,1)S(1)}, u32[]{:S(2)}, u32[]{:S(2)}) collective-permute-start(bf16[208,128]{1,0:T(8,128)(2,1)S(1)} %get-tuple-element.21), channel_id=1, source_target_pairs={{0,1},{1,0},{2,3},{3,2},{4,5},{5,4},{6,7},{7,6},{8,9},{9,8},{10,11... | collective-permute-start | bytes 159752 | tf_op jit(solution)/shard_map/ppermute | solution.py:461
  7.0 4.9 %collective-permute-start.2 = (bf16[144,128]{1,0:T(8,128)(2,1)S(1)}, bf16[144,128]{1,0:T(8,128)(2,1)S(1)}, u32[]{:S(2)}, u32[]{:S(2)}) collective-permute-start(bf16[144,128]{1,0:T(8,128)(2,1)S(1)} %get-tuple-element.19.refs_0_), channel_id=1, source_target_pairs={{0,2},{1,3},{2,0},{3,1},{4,6},{5,7},{6,4},{7,5},{8,10},{9,11},{10,... | collective-permute-start | bytes 110600 | tf_op jit(solution)/shard_map/ppermute | solution.py:461
  12.5 4.5 %collective-permute-start.4 = (bf16[80,512]{1,0:T(8,128)(2,1)S(1)}, bf16[80,512]{1,0:T(8,128)(2,1)S(1)}, u32[]{:S(2)}, u32[]{:S(2)}) collective-permute-start(bf16[80,512]{1,0:T(8,128)(2,1)S(1)} %get-tuple-element.25.refs_0_), channel_id=1, source_target_pairs={{0,4},{4,0},{8,12},{12,8},{16,20},{20,16},{24,28},{28,24},{1,5},{5... | collective-permute-start | bytes 245768 | tf_op jit(solution)/shard_map/ppermute | solution.py:522
  12.6 5.1 %collective-permute-start.3 = (bf16[80,512]{1,0:T(8,128)(2,1)S(1)}, bf16[80,512]{1,0:T(8,128)(2,1)S(1)}, u32[]{:S(2)}, u32[]{:S(2)}) collective-permute-start(bf16[80,512]{1,0:T(8,128)(2,1)S(1)} %get-tuple-element.26), channel_id=1, source_target_pairs={{0,28},{4,8},{8,4},{12,16},{16,12},{20,24},{24,20},{28,0},{1,29},{... | collective-permute-start | bytes 245768 | tf_op jit(solution)/shard_map/ppermute | solution.py:519
  15.1 10.8 %copy-start.2 = (bf16[16,2,128,128]{3,2,1,0:T(8,128)(2,1)S(1)}, bf16[16,2,128,128]{3,2,1,0:T(8,128)(2,1)}, u32[]{:S(2)}) copy-start(bf16[16,2,128,128]{3,2,1,0:T(8,128)(2,1)} %refs_6_.3) | copy-start | bytes 3145732
  18.5 6.3 %collective-permute-start.5 = (bf16[128,128]{1,0:T(8,128)(2,1)S(1)}, bf16[128,128]{1,0:T(8,128)(2,1)S(1)}, u32[]{:S(2)}, u32[]{:S(2)}) collective-permute-start(bf16[128,128]{1,0:T(8,128)(2,1)S(1)} %get-tuple-element.30), channel_id=1, source_target_pairs={{0,3},{1,2},{2,1},{3,0},{4,7},{5,6},{6,5},{7,4},{8,11},{9,10},{10,... | collective-permute-start | bytes 98312 | tf_op jit(solution)/shard_map/ppermute | solution.py:461
  20.5 5.0 %collective-permute-start.6 = (bf16[128,128]{1,0:T(8,128)(2,1)S(1)}, bf16[128,128]{1,0:T(8,128)(2,1)S(1)}, u32[]{:S(2)}, u32[]{:S(2)}) collective-permute-start(bf16[128,128]{1,0:T(8,128)(2,1)S(1)} %get-tuple-element.31), channel_id=1, source_target_pairs={{0,2},{1,3},{2,0},{3,1},{4,6},{5,7},{6,4},{7,5},{8,10},{9,11},{10,... | collective-permute-start | bytes 98312 | tf_op jit(solution)/shard_map/ppermute | solution.py:461
  22.0 3.9 %collective-permute-start.7 = (bf16[128,128]{1,0:T(8,128)(2,1)S(1)}, bf16[128,128]{1,0:T(8,128)(2,1)S(1)}, u32[]{:S(2)}, u32[]{:S(2)}) collective-permute-start(bf16[128,128]{1,0:T(8,128)(2,1)S(1)} %get-tuple-element.32), channel_id=1, source_target_pairs={{0,1},{1,0},{2,3},{3,2},{4,5},{5,4},{6,7},{7,6},{8,9},{9,8},{10,11... | collective-permute-start | bytes 98312 | tf_op jit(solution)/shard_map/ppermute | solution.py:461
